TPU v7x, 768 devices: a whole 4x8x12 slice. The times are simulated.
768 devices in a mesh: row: 4 (over y_lo, core), col: 192 (over y_hi, x, z).
Axes of the slice: x: 4, y: 8 (y_hi: 4, y_lo: 2; y = y_hi * 2 + y_lo), z: 12, core: 2. Of those that a mesh axis runs over, the one named last changes fastest.
Arguments:
- features: bfloat16 [98304, 128], P(('row', 'col')), may hold values from -6 to 6
- tile_rows: int32 [4, 192, 48], P('row', 'col'), may hold values from 0 to 7, as said below
- tile_cols: int32 [4, 192, 48], P('row', 'col'), may hold values from 0 to 191, as said below
- tile_counts: int32 [4, 192], P('row', 'col'), may hold values from 1 to 48, as said below
- tile_values: bfloat16 [4, 192, 48, 64, 128], P('row', 'col'), may hold values from 0 to 0.049804688
- weight: bfloat16 [128, 256], replicated, may hold values from -0.5 to 0.5
- bias: float32 [256], replicated, may hold values from -3 to 3
- cotangent: bfloat16 [98304, 256], P(('row', 'col')), may hold values from -6 to 6
Outputs:
- hidden_out: bfloat16 [98304, 256], P(('row', 'col'))
- features_grad: float32 [98304, 128], P(('row', 'col'))
- weight_grad: float32 [128, 256], replicated
- bias_grad: float32 [256], replicated
Inputs may be any that keep to these rules, and one draw needn't show every extreme that they name: `tile_cols`: within each block the live slots (k < tile_counts) are ordered by tile column, then tile row; slots past the count hold 0. `tile_rows`: slots past the count hold 0. `tile_counts`: some block is full in every draw.
All inputs are finite; a program needn't handle non-finite values.
Results may differ from a plain program's by a relative error of at most 0.0075.
Values may be sent and summed in bfloat16 or wider, within the bound.
No kernel may reach another device: no remote copies, remote signals or barrier semaphores. Data moves between devices by JAX's collectives and lax.ppermute only.
A program may use at most 32 MiB of HBM per device.

v0:
```python
import math

import jax
import jax.numpy as jnp
from jax import lax
from jax.sharding import PartitionSpec as P

far_start = 1 << 30


def gelu_tanh(values):
    return jax.nn.gelu(values, approximate=True)


def local(features, tile_rows, tile_cols, tile_counts, tile_values, weight, bias, cotangent):
    rows_dev, feat_width = features.shape
    tile_height = tile_values.shape[3]
    slab_width = tile_values.shape[4]
    slot_total = tile_values.shape[2]
    group_rows = lax.axis_size("row")
    group_cols = lax.axis_size("col")
    sub_width = min(slab_width, rows_dev)
    parts_per = slab_width // sub_width
    rows_index = tile_rows[0, 0]
    cols_index = tile_cols[0, 0]
    live_count = tile_counts[0, 0]
    values = tile_values[0, 0]
    item_ids = jnp.arange(slot_total * parts_per, dtype=jnp.int32)
    item_slot = item_ids // parts_per
    item_sub = item_ids % parts_per
    item_start = cols_index[item_slot] * slab_width + item_sub * sub_width
    sort_keys = jnp.where(item_slot < live_count, item_start, far_start)
    ordering = jnp.argsort(sort_keys, stable=True)
    sorted_start = sort_keys[ordering]
    live_items = live_count * parts_per

    def tile_part(position):
        item = ordering[position]
        slot_id = item // parts_per
        block = values[slot_id]
        return (slot_id, block)

    empty_rows = jnp.zeros((group_rows * rows_dev, feat_width), jnp.float32)
    piece = lax.all_gather(features, "col", axis=0, tiled=True)
    start = jnp.int32(0)
    length = piece.shape[0]
    begin_at = jnp.sum(sorted_start < start)
    end_at = jnp.sum(sorted_start + sub_width <= start + length)

    def one_item(position, accum):
        slot_id, block = tile_part(position)
        slab = lax.dynamic_slice_in_dim(piece, sorted_start[position], sub_width, 0)
        product = jnp.dot(block, slab, preferred_element_type=jnp.float32)
        top_row = rows_index[slot_id] * tile_height
        current = lax.dynamic_slice_in_dim(accum, top_row, tile_height, 0)
        return lax.dynamic_update_slice_in_dim(accum, current + product, top_row, 0)

    partial_value = lax.fori_loop(begin_at, end_at, one_item, empty_rows)
    aggregate = lax.psum_scatter(partial_value, "row", scatter_dimension=0, tiled=True)
    pre = jnp.dot(aggregate, weight.astype(jnp.float32), precision=lax.Precision.HIGHEST) + bias
    activated, pullback = jax.vjp(gelu_tanh, pre)
    hidden_out = activated.astype(jnp.bfloat16)
    slope = pullback(cotangent.astype(jnp.float32))[0].astype(jnp.bfloat16)
    slope_wide = slope.astype(jnp.float32)
    weight_part = lax.dot_general(
        aggregate, slope_wide, (((0,), (0,)), ((), ())), precision=lax.Precision.HIGHEST
    )
    bias_part = jnp.sum(slope_wide, axis=0)
    whole_slope = lax.all_gather(slope, "row", axis=0, tiled=True)
    whole_spread = lax.dot_general(
        whole_slope, weight, (((1,), (1,)), ((), ())), preferred_element_type=jnp.float32
    ).astype(jnp.bfloat16)

    def back_item(position, accum):
        slot_id, block = tile_part(position)
        picked = lax.dynamic_slice_in_dim(
            whole_spread, rows_index[slot_id] * tile_height, tile_height, 0
        )
        contrib = lax.dot_general(
            block, picked, (((0,), (0,)), ((), ())), preferred_element_type=jnp.float32
        )
        column_at = sorted_start[position]
        current = lax.dynamic_slice_in_dim(accum, column_at, sub_width, 0)
        return lax.dynamic_update_slice_in_dim(accum, current + contrib, column_at, 0)

    empty_cols = jnp.zeros((group_cols * rows_dev, feat_width), jnp.float32)
    column_part = lax.fori_loop(0, live_items, back_item, empty_cols)
    features_grad = lax.psum_scatter(column_part, "col", scatter_dimension=0, tiled=True)
    weight_sum, bias_sum = lax.psum((weight_part, bias_part), ("row", "col"))
    factor = 1.0 / math.sqrt(rows_dev * group_rows * group_cols)
    return (hidden_out, features_grad, weight_sum * factor, bias_sum * factor)


def solution(mesh):
    in_specs = (
        P(("row", "col"), None),
        P("row", "col", None),
        P("row", "col", None),
        P("row", "col"),
        P("row", "col", None, None, None),
        P(),
        P(),
        P(("row", "col"), None),
    )
    out_specs = (P(("row", "col"), None), P(("row", "col"), None), P(), P())
    return jax.shard_map(local, mesh=mesh, in_specs=in_specs, out_specs=out_specs, check_vma=False)
```

profile of v0, /device:TPU:8, one launch (start us, length us, event | category | flops | bytes accessed | tf_op | source)
XLA Modules:
  0.0 2356.9 jit_solution(4873659488663962794)
XLA Ops:
  8.6 1.4 gather_fusion
  10.1 2.0 sort.17
  13.5 192.6 %all-gather.2.cloned.1.call-done = bf16[24576,128]{1,0:T(8,128)(2,1)} async-done(((bf16[128,128]{1,0:T(8,128)(2,1)}), bf16[24576,128]{1,0:T(8,128)(2,1)}) %all-gather.2.cloned.1.call-update) | async-done | bytes 6291472 | tf_op jit(solution)/shard_map/all_gather | solution.py:44
  206.1 115.3 %while.24 = (s32[]{:T(128)}, f32[512,128]{1,0:T(8,128)S(1)}, s32[]{:T(128)}, s32[48]{0:T(128)S(1)}, s32[48]{0:T(128)}, /*index=5*/bf16[48,64,128]{2,1,0:T(8,128)...) while((s32[]{:T(128)}, f32[512,128]{1,0:T(8,128)S(1)}, ...), condition=%wide.region_4.5_spmd, body=%wide.region_3.4_spmd.sunk | while | flops 2105359 | bytes 115025 | solution.py:58
  210.6 1.2 dynamic_slice.102
  221.0 1.2 dynamic_slice.102
  231.3 1.2 dynamic_slice.102
  241.7 1.2 dynamic_slice.102
  252.1 1.2 dynamic_slice.102
  272.8 1.2 dynamic_slice.102
  283.1 1.2 dynamic_slice.102
  293.5 1.2 dynamic_slice.102
  322.2 394.6 %reduce-scatter.3.cloned.1.call-done = f32[128,128]{1,0:T(8,128)} async-done(((f32[512,128]{1,0:T(8,128)}), f32[128,128]{1,0:T(8,128)}) %reduce-scatter.3.cloned.1.call-update) | async-done | bytes 65552 | tf_op jit(solution)/shard_map/reduce_scatter | solution.py:59
  716.8 1.8 convert_reduce_fusion
  718.6 6.6 all_gather.7
  725.2 1.8 fusion.22
  727.3 4.8 broadcast_in_dim.18
  732.1 106.5 %while.25 = (s32[]{:T(128)}, f32[24576,128]{1,0:T(8,128)}, s32[]{:T(128)}, s32[48]{0:T(128)S(1)}, s32[48]{0:T(128)S(1)}, /*index=5*/bf16[48,64,128]{2,1,0:T(8,12...) while((s32[]{:T(128)}, f32[24576,128]{1,0:T(8,128)}, ...), condition=%wide.region_7.8_spmd, body=%wide.region_6.7_spmd.sunk | while | flops 2113551 | bytes 295253 | solution.py:87
  740.2 1.5 dynamic_update_slice.16
  749.8 1.5 dynamic_update_slice.16
  759.4 1.5 dynamic_update_slice.16
  769.0 1.5 dynamic_update_slice.16
  778.7 1.5 dynamic_update_slice.16
  788.3 1.5 dynamic_update_slice.16
  797.9 1.5 dynamic_update_slice.16
  807.5 1.5 dynamic_update_slice.16
  817.1 1.5 dynamic_update_slice.16
  826.8 1.5 dynamic_update_slice.16
  836.4 1.5 dynamic_update_slice.16
  838.6 462.7 %psum.15 = f32[256]{0:T(256)S(1)} all-reduce(f32[256]{0:T(256)S(1)} %get-tuple-element.254), channel_id=1, replica_groups=mesh['row'=4,'col'=192] {'row','col'}, use_global_device_ids=true, to_apply=%region_11.12 | all-reduce | flops 256 | bytes 2048 | tf_op jit(solution)/shard_map/psum | solution.py:89
  1301.8 1.6 broadcast_multiply_fusion
  1303.4 1047.0 %reduce-scatter.5.cloned.1.call-done = f32[128,128]{1,0:T(8,128)} async-done(((f32[24576,128]{1,0:T(8,128)}), f32[128,128]{1,0:T(8,128)}) %reduce-scatter.5.cloned.1.call-update) | async-done | bytes 65552 | tf_op jit(solution)/shard_map/reduce_scatter | solution.py:88
  (106 shorter events, 62.1 us)
Async XLA Ops:
  7.2 709.6 %copy-start = (bf16[128,256]{1,0:T(8,128)(2,1)S(1)}, bf16[128,256]{1,0:T(8,128)(2,1)}, u32[]{:S(2)}) copy-start(bf16[128,256]{1,0:T(8,128)(2,1)} %param.17) | copy-start | bytes 196612
  7.2 198.9 %all-gather.2.cloned.1.call-start = ((), (), s32[]{:S(2)}) async-start(), calls=%async_computation.2 | async-start | bytes 6324224 | tf_op jit(solution)/shard_map/all_gather | solution.py:44
  7.9 708.9 %reduce-scatter.3.cloned.1.call-start = ((), (), s32[]{:S(2)}) async-start(), calls=%async_computation.3 | async-start | bytes 327680 | tf_op jit(solution)/shard_map/reduce_scatter | solution.py:59
  321.4 0.7 copy-start.1
  321.4 410.7 %copy-start.2 = (s32[48]{0:T(128)S(1)}, s32[48]{0:T(128)}, u32[]{:S(2)}) copy-start(s32[48]{0:T(128)} %get-tuple-element.459) | copy-start | bytes 580
  322.1 979.7 %all-reduce.2.cloned.1.call-start = ((), (), s32[]{:S(2)}) async-start(), calls=%async_computation.5 | async-start | bytes 262144 | tf_op jit(solution)/shard_map/psum | solution.py:89
  727.0 1623.4 %reduce-scatter.5.cloned.1.call-start = ((), (), s32[]{:S(2)}) async-start(), calls=%async_computation.4 | async-start | bytes 12648448 | tf_op jit(solution)/shard_map/reduce_scatter | solution.py:88
Sparse Core Ops, SparseCore 0:
  13.4 192.6 all-gather.1
  322.2 394.5 reduce-scatter.2
  727.1 458.8 all-reduce.1
  1189.5 1160.8 reduce-scatter.4
where the time goes:
time: 2370 us; the launch traced here: 2360 us
  waiting for transfers between devices  1630 us (69%)
  blocking collectives  469 us (20%)
  loops' own time  137 us (6%)
  local copies, waits for them, and re-layouts  70.7 us (3%)
  matrix products  26 us (1%)
    reduce_scatter x1, waiting for transfers between devices, local(): lax.psum_scatter(column_part, 'col', scatter_dimension=0, tiled=True)  1050 us
    psum x1, blocking collectives, local(): weight_sum, bias_sum = lax.psum((weight_part, bias_part), ('row', 'col'))  463 us
    reduce_scatter x1, waiting for transfers between devices, local(): lax.psum_scatter(partial_value, 'row', scatter_dimension=0, tiled=True)  395 us
    all_gather x1, waiting for transfers between devices, local(): piece = lax.all_gather(features, 'col', axis=0, tiled=True)  193 us
    another operation x1, loops' own time, local(): partial_value = lax.fori_loop(begin_at, end_at, one_item, empty_rows)  78.5 us
    another operation x1, loops' own time, local(): column_part = lax.fori_loop(0, live_items, back_item, empty_cols)  58 us
  transfers between devices with their start and end apart: 4, of which 3 were waited for; matrix products, arithmetic and copies ran while one was open for 3% of the time, Pallas kernels for 0%

commit v1 on v0

v1 whole, which is shorter than its diff:
```python
import math

import jax
import jax.numpy as jnp
from jax import lax
from jax.experimental import pallas as pl
from jax.experimental.pallas import tpu as pltpu
from jax.sharding import Mesh, PartitionSpec as P

row_split = (2, 2)
col_split = (4, 4, 12)
axis_names = ("ylo", "core", "yhi", "x", "z")
row_axes = ("ylo", "core")
col_axes = ("yhi", "x", "z")
team_axes = ("ylo", "core", "x")
group = 4
lanes = 128
vmem_bytes = 32 * 1024 * 1024
root_two_over_pi = math.sqrt(2.0 / math.pi)
cubic = 0.044715


def spread_out(value, axes, count):
    copies = jnp.broadcast_to(value[None], (count,) + value.shape)
    return lax.all_to_all(copies, axes, 0, 0, tiled=True)


def pick_tiles(codes, counts, tile_refs, chosen, picked, slots, height, dummy):
    total = jnp.int32(0)
    for source, tiles in enumerate(tile_refs):

        def body(step, total, source=source, tiles=tiles):
            for sub in range(group):
                slot = step * group + sub
                code = codes[source * slots + slot]
                top = pl.multiple_of(slot * height, height)
                chosen[total] = tiles[pl.ds(top, height), :]
                picked[total] = code
                total = total + jnp.where(code >= 0, 1, 0)
            return total

        total = lax.fori_loop(0, (counts[source] + group - 1) // group, body, total)
    for sub in range(group):
        picked[total + sub] = dummy
    return total


def forward_kernel(codes, counts, slabs, *refs, slots, height, blocks):
    tile_refs = refs[: -4]
    out, chosen, totals, picked = refs[-4:]
    slab_count = slabs.shape[0]
    dummy = slab_count * 64 + blocks
    totals[...] = jnp.zeros_like(totals)
    total = pick_tiles(codes, counts, tile_refs, chosen, picked, slots, height, dummy)

    def body(step, carry):
        products = []
        for sub in range(group):
            code = picked[step * group + sub]
            slab = jnp.minimum(code >> 6, slab_count - 1)
            product = jnp.dot(
                chosen[step * group + sub], slabs[slab], preferred_element_type=jnp.float32
            )
            products.append((code & 63, product))
        for block, product in products:
            totals[block] += product
        return carry

    lax.fori_loop(0, (total + group - 1) // group, body, 0)
    halves = out.shape[1] // height
    for block in range(blocks):
        out[block // halves, pl.ds((block % halves) * height, height), :] = totals[block]


def split_wide(value):
    high = value.astype(jnp.bfloat16).astype(jnp.float32)
    return high, value - high


def bias_rows(pieces):
    rows = lax.broadcasted_iota(jnp.int32, (16, lanes), 0)
    block = jnp.zeros((16, lanes), jnp.float32)
    for index, piece in enumerate(pieces):
        block = jnp.where(rows == index, jnp.broadcast_to(piece, (16, lanes)), block)
    return block


def dense_kernel(partials, weight, bias, cotangent, hidden, message):
    members = partials.shape[0]
    nodes = partials.shape[1]
    aggregate = partials[0]
    for member in range(1, members):
        aggregate = aggregate + partials[member]
    weight_wide = weight[...].astype(jnp.float32)
    pre = (
        jnp.dot(
            aggregate,
            weight_wide,
            precision=lax.Precision.HIGHEST,
            preferred_element_type=jnp.float32,
        )
        + bias[...]
    )
    square = pre * pre
    angle = jnp.tanh(root_two_over_pi * (pre + cubic * (square * pre)))
    gate = 0.5 * (1.0 + angle)
    hidden[...] = (pre * gate).astype(jnp.bfloat16)
    inner = root_two_over_pi * (1.0 + 3.0 * cubic * square)
    gradient = gate + 0.5 * pre * (1.0 - angle * angle) * inner
    slope = (cotangent[...].astype(jnp.float32) * gradient).astype(jnp.bfloat16)
    slope_wide = slope.astype(jnp.float32)
    spread = lax.dot_general(
        slope, weight[...], (((1,), (1,)), ((), ())), preferred_element_type=jnp.float32
    ).astype(jnp.bfloat16)
    weight_part = lax.dot_general(
        aggregate,
        slope_wide,
        (((0,), (0,)), ((), ())),
        precision=lax.Precision.HIGHEST,
        preferred_element_type=jnp.float32,
    )
    bias_part = jnp.sum(slope_wide, axis=0, keepdims=True)
    high, low = split_wide(bias_part)
    bias_block = bias_rows([high[:, :lanes], high[:, lanes:], low[:, :lanes], low[:, lanes:]])
    bias_block = bias_block.astype(jnp.bfloat16)
    share = weight_part.shape[0] // members
    for member in range(members):
        message[member, pl.ds(0, nodes), :] = spread
        part = weight_part[member * share : (member + 1) * share]
        part = jnp.concatenate([part[:, :lanes], part[:, lanes:]], axis=0)
        high, low = split_wide(part)
        message[member, pl.ds(nodes, 2 * share), :] = high.astype(jnp.bfloat16)
        message[member, pl.ds(nodes + 2 * share, 2 * share), :] = low.astype(jnp.bfloat16)
        message[member, pl.ds(nodes + 4 * share, 16), :] = bias_block


def sum_rows(ref, start, size):
    value = ref[0, pl.ds(start, size), :].astype(jnp.float32)
    for index in range(1, ref.shape[0]):
        value = value + ref[index, pl.ds(start, size), :].astype(jnp.float32)
    return value


def sum_bias(ref, start):
    block = sum_rows(ref, start, 16)
    return [block[0:1] + block[2:3], block[1:2] + block[3:4]]


def pack_bias(values):
    parts = [split_wide(value) for value in values]
    return bias_rows([parts[0][0], parts[1][0], parts[0][1], parts[1][1]]).astype(jnp.bfloat16)


def backward_kernel(
    codes, counts, spreads, *refs, slots, height, blocks, nodes, share
):
    tile_refs = refs[: -4]
    out, chosen, totals, picked = refs[-4:]
    slab_count = totals.shape[0] - 1
    halves = nodes // height
    dummy = slab_count * 64 + blocks
    totals[...] = jnp.zeros_like(totals)
    total = pick_tiles(codes, counts, tile_refs, chosen, picked, slots, height, dummy)

    def body(step, carry):
        products = []
        for sub in range(group):
            code = picked[step * group + sub]
            block = jnp.minimum(code & 63, blocks - 1)
            top = pl.multiple_of((block % halves) * height, height)
            product = lax.dot_general(
                chosen[step * group + sub],
                spreads[block // halves, pl.ds(top, height), :],
                (((0,), (0,)), ((), ())),
                preferred_element_type=jnp.float32,
            )
            products.append((code >> 6, product))
        for slab, product in products:
            totals[slab] += product
        return carry

    lax.fori_loop(0, (total + group - 1) // group, body, 0)
    far = out.shape[0]
    near = slab_count // far
    width = totals.shape[1]
    for slab in range(slab_count):
        out[slab // near, pl.ds((slab % near) * width, width), :] = totals[slab].astype(
            jnp.bfloat16
        )
    weight_sum = sum_rows(spreads, nodes, 2 * share) + sum_rows(spreads, nodes + 2 * share, 2 * share)
    high, low = split_wide(weight_sum)
    bias_block = pack_bias(sum_bias(spreads, nodes + 4 * share))
    for index in range(far):
        out[index, pl.ds(near * width, 2 * share), :] = high.astype(jnp.bfloat16)
        out[index, pl.ds(near * width + 2 * share, 2 * share), :] = low.astype(jnp.bfloat16)
        out[index, pl.ds(near * width + 4 * share, 16), :] = bias_block


def middle_kernel(arrived, out, *, share):
    near = out.shape[0]
    rows = arrived.shape[1] - 4 * share - 16
    width = rows // near
    weight_sum = sum_rows(arrived, rows, 2 * share) + sum_rows(arrived, rows + 2 * share, 2 * share)
    bias_block = pack_bias(sum_bias(arrived, rows + 4 * share))
    for index in range(near):
        out[index, pl.ds(0, width), :] = sum_rows(arrived, index * width, width).astype(jnp.bfloat16)
        out[index, pl.ds(width, 2 * share), :] = weight_sum.astype(jnp.bfloat16)
        out[index, pl.ds(width + 2 * share, 16), :] = bias_block


def last_kernel(arrived, grad, weight_share, bias_grad, *, share, factor):
    width = grad.shape[0]
    grad[...] = sum_rows(arrived, 0, width)
    weight_share[...] = sum_rows(arrived, width, 2 * share) * factor
    low, high = sum_bias(arrived, width + 2 * share)
    bias_grad[:, pl.ds(0, lanes)] = low * factor
    bias_grad[:, pl.ds(lanes, lanes)] = high * factor


def in_vmem():
    return pl.BlockSpec(memory_space=pltpu.VMEM)


def in_smem():
    return pl.BlockSpec(memory_space=pltpu.SMEM)


def local(features, tile_rows, tile_cols, tile_counts, tile_values, weight, bias, cotangent):
    nodes, width = features.shape
    slots, height, tile_width = tile_values.shape[2:]
    hidden = weight.shape[1]
    far = lax.axis_size("yhi")
    across = lax.axis_size("x")
    near = lax.axis_size("z")
    members = lax.axis_size(team_axes)
    group_rows = lax.axis_size(row_axes)
    here = lax.axis_index("x")
    params = pltpu.CompilerParams(vmem_limit_bytes=vmem_bytes)

    live = jnp.arange(slots, dtype=jnp.int32) < tile_counts[0, 0]
    places = jnp.stack([tile_cols[0, 0], tile_rows[0, 0], live.astype(jnp.int32)])
    places = jnp.pad(places, ((0, 13), (0, lanes - slots))).astype(jnp.bfloat16)
    own = jnp.concatenate([tile_values[0, 0].reshape(slots * height, tile_width), places], axis=0)
    buffers = [own]
    for shift in range(1, across):
        hops = [(start, (start + shift) % across) for start in range(across)]
        buffers.append(lax.ppermute(own, "x", hops))

    line = spread_out(features, "z", near)
    slabs = spread_out(line, "yhi", far).reshape(far * near, nodes, width)

    halves = nodes // height
    blocks = members * halves
    tops = jnp.stack([buffer[slots * height :, :slots] for buffer in buffers]).astype(jnp.int32)
    columns, rows, alive = tops[:, 0], tops[:, 1], tops[:, 2]
    owner = (here - jnp.arange(across, dtype=jnp.int32)[:, None]) % across
    slab = (columns // (across * near)) * near + columns % near
    block = ((rows // halves) * across + owner) * halves + rows % halves
    mine = (alive > 0) & ((columns // near) % across == here)
    codes = jnp.where(mine, slab * 64 + block, -1).reshape(-1)
    counts = jnp.sum(alive, axis=1)

    scratch_tiles = pltpu.VMEM((across * slots + group, height, tile_width), jnp.bfloat16)
    scratch_list = pltpu.SMEM((across * slots + group,), jnp.int32)
    partial = pl.pallas_call(
        lambda *refs: forward_kernel(*refs, slots=slots, height=height, blocks=blocks),
        out_shape=jax.ShapeDtypeStruct((members, nodes, width), jnp.float32),
        in_specs=[in_smem(), in_smem(), in_vmem()] + [in_vmem()] * across,
        out_specs=in_vmem(),
        scratch_shapes=[
            scratch_tiles,
            pltpu.VMEM((blocks + 1, height, width), jnp.float32),
            scratch_list,
        ],
        compiler_params=params,
        name="forward_tiles",
    )(codes, counts, slabs, *buffers)
    partials = lax.all_to_all(partial, team_axes, 0, 0, tiled=True)

    share = width // members
    hidden_out, message = pl.pallas_call(
        dense_kernel,
        out_shape=(
            jax.ShapeDtypeStruct((nodes, hidden), jnp.bfloat16),
            jax.ShapeDtypeStruct((members, nodes + 4 * share + 16, width), jnp.bfloat16),
        ),
        in_specs=[in_vmem()] * 4,
        out_specs=(in_vmem(), in_vmem()),
        compiler_params=params,
        name="dense_layer",
    )(partials, weight, bias.reshape(1, hidden), cotangent)
    spreads = lax.all_to_all(message, team_axes, 0, 0, tiled=True)

    column_part = pl.pallas_call(
        lambda *refs: backward_kernel(
            *refs, slots=slots, height=height, blocks=blocks, nodes=nodes, share=share
        ),
        out_shape=jax.ShapeDtypeStruct((far, near * nodes + 4 * share + 16, width), jnp.bfloat16),
        in_specs=[in_smem(), in_smem(), in_vmem()] + [in_vmem()] * across,
        out_specs=in_vmem(),
        scratch_shapes=[
            scratch_tiles,
            pltpu.VMEM((far * near + 1, nodes, width), jnp.float32),
            scratch_list,
        ],
        compiler_params=params,
        name="backward_tiles",
    )(codes, counts, spreads, *buffers)
    arrived = lax.all_to_all(column_part, "yhi", 0, 0, tiled=True)
    line_part = pl.pallas_call(
        lambda *refs: middle_kernel(*refs, share=share),
        out_shape=jax.ShapeDtypeStruct((near, nodes + 2 * share + 16, width), jnp.bfloat16),
        in_specs=[in_vmem()],
        out_specs=in_vmem(),
        compiler_params=params,
        name="sum_far",
    )(arrived)
    arrived = lax.all_to_all(line_part, "z", 0, 0, tiled=True)
    factor = 1.0 / math.sqrt(nodes * group_rows * far * across * near)
    features_grad, weight_share, bias_grad = pl.pallas_call(
        lambda *refs: last_kernel(*refs, share=share, factor=factor),
        out_shape=(
            jax.ShapeDtypeStruct((nodes, width), jnp.float32),
            jax.ShapeDtypeStruct((2 * share, lanes), jnp.float32),
            jax.ShapeDtypeStruct((1, hidden), jnp.float32),
        ),
        in_specs=[in_vmem()],
        out_specs=(in_vmem(), in_vmem(), in_vmem()),
        compiler_params=params,
        name="sum_near",
    )(arrived)
    shares = spread_out(weight_share, team_axes, members)
    weight_grad = shares.reshape(members, 2, share, lanes).transpose(0, 2, 1, 3)
    weight_grad = weight_grad.reshape(width, hidden)
    return (hidden_out, features_grad, weight_grad, bias_grad.reshape(hidden))


def solution(mesh):
    fine = Mesh(mesh.devices.reshape(row_split + col_split), axis_names)
    nodes_spec = P(row_axes + col_axes, None)
    in_specs = (
        nodes_spec,
        P(row_axes, col_axes, None),
        P(row_axes, col_axes, None),
        P(row_axes, col_axes),
        P(row_axes, col_axes, None, None, None),
        P(),
        P(),
        nodes_spec,
    )
    out_specs = (nodes_spec, nodes_spec, P(), P())
    return jax.shard_map(local, mesh=fine, in_specs=in_specs, out_specs=out_specs, check_vma=False)
```

time: 2370 us -> 219 us (0.09)
  the two profiles are of different devices: /device:TPU:8 before, /device:TPU:1 now
where the time goes in v1:
time: 219 us; the launch traced here: 218 us
  blocking collectives  119 us (54%)
  waiting for transfers between devices  51.5 us (24%)
  starting transfers between devices  32 us (15%)
  Pallas kernels  7.38 us (3%)
  local copies, waits for them, and re-layouts  5.89 us (3%)
    all_to_all x1, blocking collectives, local(): arrived = lax.all_to_all(column_part, 'yhi', 0, 0, tiled=True)  45.4 us
    ppermute x3, waiting for transfers between devices, local(): buffers.append(lax.ppermute(own, 'x', hops))  34.2 us
    all_to_all x1, blocking collectives, local(): arrived = lax.all_to_all(line_part, 'z', 0, 0, tiled=True)  25.9 us
    all_to_all x2, starting transfers between devices, spread_out(): return lax.all_to_all(copies, axes, 0, 0, tiled=True)  22.6 us
    all_to_all x1, blocking collectives, local(): partials = lax.all_to_all(partial, team_axes, 0, 0, tiled=True)  19.4 us
    all_to_all x2, waiting for transfers between devices, spread_out(): return lax.all_to_all(copies, axes, 0, 0, tiled=True)  17.3 us
    all_to_all x1, blocking collectives, local(): spreads = lax.all_to_all(message, team_axes, 0, 0, tiled=True)  15.8 us
    all_to_all x1, blocking collectives, spread_out(): return lax.all_to_all(copies, axes, 0, 0, tiled=True)  12.4 us
  transfers between devices with their start and end apart: 5, of which 4 were waited for; matrix products, arithmetic and copies ran while one was open for 1% of the time, Pallas kernels for 0%

profile of v1, /device:TPU:1, one launch (start us, length us, event | category | flops | bytes accessed | tf_op | source)
XLA Modules:
  0.0 218.2 jit_solution(7991303839406388348)
XLA Ops:
  0.6 1.6 broadcast_in_dim.7
  2.2 15.7 %all-to-all-start = ((bf16[12,128,128]{2,1,0:T(8,128)(2,1)}), bf16[12,128,128]{2,1,0:T(8,128)(2,1)S(1)}, u32[]{:S(2)}, u32[]{:S(2)}) async-start(bf16[12,128,128]{2,1,0:T(8,128)(2,1)} %broadcast_in_dim.7), calls=%async_computation | async-start | bytes 786432 | tf_op jit(solution)/shard_map/all_to_all | solution.py:25
  18.6 0.7 convert_bitcast_fusion
  19.3 17.3 %all-to-all-done = bf16[12,128,128]{2,1,0:T(8,128)(2,1)S(1)} async-done(((bf16[12,128,128]{2,1,0:T(8,128)(2,1)}), bf16[12,128,128]{2,1,0:T(8,128)(2,1)S(1)}, u32[]{:S(2)}, u32[]{:S(2)}) %all-to-all-start) | async-done | bytes 393248 | tf_op jit(solution)/shard_map/all_to_all | solution.py:25
  36.6 1.5 broadcast_in_dim.8
  38.1 6.9 %all-to-all-start.1 = ((bf16[4,12,128,128]{3,2,1,0:T(8,128)(2,1)}), bf16[4,12,128,128]{3,2,1,0:T(8,128)(2,1)S(1)}, u32[]{:S(2)}, u32[]{:S(2)}) async-start(bf16[4,12,128,128]{3,2,1,0:T(8,128)(2,1)} %broadcast_in_dim.8), calls=%async_computation.1 | async-start | bytes 3145728 | tf_op jit(solution)/shard_map/all_to_all | solution.py:25
  45.1 4.4 %collective-permute-start.2 = (bf16[3088,128]{1,0:T(8,128)(2,1)S(1)}, bf16[3088,128]{1,0:T(8,128)(2,1)S(1)}, u32[]{:S(2)}, u32[]{:S(2)}) collective-permute-start(bf16[3088,128]{1,0:T(8,128)(2,1)S(1)} %pad_maximum_fusion.refs_3_), channel_id=1, source_target_pairs={{0,36},{12,0},{24,12},{36,24},{1,37},{13,1},{25,13},{37,25},{2,38}... | collective-permute-start | bytes 2371592 | tf_op jit(solution)/shard_map/ppermute | solution.py:247
  49.5 2.4 %collective-permute-start.1 = (bf16[3088,128]{1,0:T(8,128)(2,1)S(1)}, bf16[3088,128]{1,0:T(8,128)(2,1)}, u32[]{:S(2)}, u32[]{:S(2)}) collective-permute-start(bf16[3088,128]{1,0:T(8,128)(2,1)S(1)} %pad_maximum_fusion.refs_3_), channel_id=1, source_target_pairs={{0,24},{12,36},{24,0},{36,12},{1,25},{13,37},{25,1},{37,13},{2,26}... | collective-permute-start | bytes 2371592 | tf_op jit(solution)/shard_map/ppermute | solution.py:247
  52.0 2.5 %collective-permute-start = (bf16[3088,128]{1,0:T(8,128)(2,1)S(1)}, bf16[3088,128]{1,0:T(8,128)(2,1)}, u32[]{:S(2)}, u32[]{:S(2)}) collective-permute-start(bf16[3088,128]{1,0:T(8,128)(2,1)S(1)} %pad_maximum_fusion.refs_3_), channel_id=1, source_target_pairs={{0,12},{12,24},{24,36},{36,0},{1,13},{13,25},{25,37},{37,1},{2,14}... | collective-permute-start | bytes 2371592 | tf_op jit(solution)/shard_map/ppermute | solution.py:247
  54.6 0.1 add.64
  54.7 10.2 %collective-permute-done.2.refs_6_ = bf16[3088,128]{1,0:T(8,128)(2,1)S(1)} collective-permute-done((bf16[3088,128]{1,0:T(8,128)(2,1)S(1)}, bf16[3088,128]{1,0:T(8,128)(2,1)S(1)}, u32[]{:S(2)}, u32[]{:S(2)}) %collective-permute-start.2) | collective-permute-done | bytes 790560 | tf_op jit(solution)/shard_map/ppermute | solution.py:247
  64.9 4.7 %collective-permute-done.1.refs_5_ = bf16[3088,128]{1,0:T(8,128)(2,1)} collective-permute-done((bf16[3088,128]{1,0:T(8,128)(2,1)S(1)}, bf16[3088,128]{1,0:T(8,128)(2,1)}, u32[]{:S(2)}, u32[]{:S(2)}) %collective-permute-start.1) | collective-permute-done | bytes 790560 | tf_op jit(solution)/shard_map/ppermute | solution.py:247
  69.6 0.7 slice_bitcast_fusion.1
  70.3 19.2 %collective-permute-done.refs_4_ = bf16[3088,128]{1,0:T(8,128)(2,1)} collective-permute-done((bf16[3088,128]{1,0:T(8,128)(2,1)S(1)}, bf16[3088,128]{1,0:T(8,128)(2,1)}, u32[]{:S(2)}, u32[]{:S(2)}) %collective-permute-start) | collective-permute-done | bytes 790560 | tf_op jit(solution)/shard_map/ppermute | solution.py:247
  89.5 0.7 slice_bitcast_fusion.2
  90.2 0.2 convert_reduce_fusion
  90.4 0.1 gt.14
  90.5 0.1 ne.86
  90.6 0.1 ne.82
  90.7 0.1 squeeze.9
  90.8 0.1 div.29
  91.1 2.5 %forward_tiles.1 = f32[16,128,128]{2,1,0:T(8,128)S(1)} custom-call(s32[192]{0:T(256)S(1)} %and_select_fusion.5.refs_0_, s32[4]{0:T(128)S(1)} %get-tuple-element.19.refs_1_, bf16[48,128,128]{2,1,0:T(8,128)(2,1)S(1)} %bitcast.23, bf16[3088,128]{1,0:T(8,128)(2,1)S(1)} %pad_maximum_fusion.refs_3_, bf16[3088,128]{1,0:T(8,128)(2,1)} %collective-permute-done.refs_4_, ...), custom_call_target="tpu_custom_call" | custom-call | tf_op jit(solution)/shard_map/forward_tiles/pallas_call | solution.py:265
  93.7 19.4 %all_to_all.35.partials = f32[16,128,128]{2,1,0:T(8,128)S(1)} all-to-all(f32[16,128,128]{2,1,0:T(8,128)S(1)} %forward_tiles.1), channel_id=1, replica_groups=mesh['ylo'=2,'core'=2,'yhi'=4,'x'=4,'z'=12] {'ylo','core','x'}, dimensions={0} | all-to-all | bytes 2097152 | tf_op jit(solution)/shard_map/all_to_all | solution.py:278
  113.1 1.1 dense_layer.1
  114.1 15.8 %all_to_all.36.refs_2_ = bf16[16,176,128]{2,1,0:T(8,128)(2,1)S(1)} all-to-all(bf16[16,176,128]{2,1,0:T(8,128)(2,1)S(1)} %get-tuple-element.10), channel_id=1, replica_groups=mesh['ylo'=2,'core'=2,'yhi'=4,'x'=4,'z'=12] {'ylo','core','x'}, dimensions={0} | all-to-all | bytes 1441792 | tf_op jit(solution)/shard_map/all_to_all | solution.py:292
  129.9 2.9 %backward_tiles.1 = bf16[4,1584,128]{2,1,0:T(8,128)(2,1)S(1)} custom-call(s32[192]{0:T(256)S(1)} %and_select_fusion.5.refs_0_, s32[4]{0:T(128)S(1)} %get-tuple-element.19.refs_1_, bf16[16,176,128]{2,1,0:T(8,128)(2,1)S(1)} %all_to_all.36.refs_2_, bf16[3088,128]{1,0:T(8,128)(2,1)S(1)} %pad_maximum_fusion.refs_3_, ...), custom_call_target="tpu_custom_call" | custom-call | tf_op jit(solution)/shard_map/backward_tiles/pallas_call | solution.py:294
  132.8 45.4 %all_to_all.37.refs_0_ = bf16[4,1584,128]{2,1,0:T(8,128)(2,1)S(1)} all-to-all(bf16[4,1584,128]{2,1,0:T(8,128)(2,1)S(1)} %backward_tiles.1), channel_id=1, replica_groups=mesh['ylo'=2,'core'=2,'yhi'=4,'x'=4,'z'=12] {'yhi'}, dimensions={0} | all-to-all | bytes 3244032 | tf_op jit(solution)/shard_map/all_to_all | solution.py:309
  178.2 0.2 sum_far.1
  178.4 25.9 %all_to_all.38.refs_0_ = bf16[12,160,128]{2,1,0:T(8,128)(2,1)S(1)} all-to-all(bf16[12,160,128]{2,1,0:T(8,128)(2,1)S(1)} %sum_far.1), channel_id=1, replica_groups=mesh['ylo'=2,'core'=2,'yhi'=4,'x'=4,'z'=12] {'z'}, dimensions={0} | all-to-all | bytes 983040 | tf_op jit(solution)/shard_map/all_to_all | solution.py:318
  204.4 0.7 sum_near.1
  205.1 12.4 %all_to_all.39 = f32[16,16,128]{2,1,0:T(8,128)S(1)} all-to-all(f32[16,16,128]{2,1,0:T(8,128)S(1)} %broadcast_in_dim.9), channel_id=1, replica_groups=mesh['ylo'=2,'core'=2,'yhi'=4,'x'=4,'z'=12] {'ylo','core','x'}, dimensions={0} | all-to-all | bytes 262144 | tf_op jit(solution)/shard_map/all_to_all | solution.py:25
  217.5 0.7 copy.14
  (23 shorter events, 0.5 us)
Async XLA Ops:
  2.2 34.4 %all-to-all-start = ((bf16[12,128,128]{2,1,0:T(8,128)(2,1)}), bf16[12,128,128]{2,1,0:T(8,128)(2,1)S(1)}, u32[]{:S(2)}, u32[]{:S(2)}) async-start(bf16[12,128,128]{2,1,0:T(8,128)(2,1)} %broadcast_in_dim.7), calls=%async_computation | async-start | bytes 786432 | tf_op jit(solution)/shard_map/all_to_all | solution.py:25
  38.1 7.0 %copy-start.3 = (bf16[1,1,48,64,128]{4,3,2,1,0:T(8,128)(2,1)S(1)}, bf16[1,1,48,64,128]{4,3,2,1,0:T(8,128)(2,1)}, u32[]{:S(2)}) copy-start(bf16[1,1,48,64,128]{4,3,2,1,0:T(8,128)(2,1)} %param.12) | copy-start | bytes 2359300
  38.1 53.0 %all-to-all-start.1 = ((bf16[4,12,128,128]{3,2,1,0:T(8,128)(2,1)}), bf16[4,12,128,128]{3,2,1,0:T(8,128)(2,1)S(1)}, u32[]{:S(2)}, u32[]{:S(2)}) async-start(bf16[4,12,128,128]{3,2,1,0:T(8,128)(2,1)} %broadcast_in_dim.8), calls=%async_computation.1 | async-start | bytes 3145728 | tf_op jit(solution)/shard_map/all_to_all | solution.py:25
  45.1 19.8 %collective-permute-start.2 = (bf16[3088,128]{1,0:T(8,128)(2,1)S(1)}, bf16[3088,128]{1,0:T(8,128)(2,1)S(1)}, u32[]{:S(2)}, u32[]{:S(2)}) collective-permute-start(bf16[3088,128]{1,0:T(8,128)(2,1)S(1)} %pad_maximum_fusion.refs_3_), channel_id=1, source_target_pairs={{0,36},{12,0},{24,12},{36,24},{1,37},{13,1},{25,13},{37,25},{2,38}... | collective-permute-start | bytes 2371592 | tf_op jit(solution)/shard_map/ppermute | solution.py:247
  49.5 20.1 %collective-permute-start.1 = (bf16[3088,128]{1,0:T(8,128)(2,1)S(1)}, bf16[3088,128]{1,0:T(8,128)(2,1)}, u32[]{:S(2)}, u32[]{:S(2)}) collective-permute-start(bf16[3088,128]{1,0:T(8,128)(2,1)S(1)} %pad_maximum_fusion.refs_3_), channel_id=1, source_target_pairs={{0,24},{12,36},{24,0},{36,12},{1,25},{13,37},{25,1},{37,13},{2,26}... | collective-permute-start | bytes 2371592 | tf_op jit(solution)/shard_map/ppermute | solution.py:247
  52.0 37.6 %collective-permute-start = (bf16[3088,128]{1,0:T(8,128)(2,1)S(1)}, bf16[3088,128]{1,0:T(8,128)(2,1)}, u32[]{:S(2)}, u32[]{:S(2)}) collective-permute-start(bf16[3088,128]{1,0:T(8,128)(2,1)S(1)} %pad_maximum_fusion.refs_3_), channel_id=1, source_target_pairs={{0,12},{12,24},{24,36},{36,0},{1,13},{13,25},{25,37},{37,1},{2,14}... | collective-permute-start | bytes 2371592 | tf_op jit(solution)/shard_map/ppermute | solution.py:247
  93.6 19.4 %copy-start = (bf16[128,256]{1,0:T(8,128)(2,1)S(1)}, bf16[128,256]{1,0:T(8,128)(2,1)}, u32[]{:S(2)}) copy-start(bf16[128,256]{1,0:T(8,128)(2,1)} %weight.1) | copy-start | bytes 196612
  93.6 19.4 %copy-start.1 = (bf16[128,256]{1,0:T(8,128)(2,1)S(1)}, bf16[128,256]{1,0:T(8,128)(2,1)}, u32[]{:S(2)}) copy-start(bf16[128,256]{1,0:T(8,128)(2,1)} %cotangent.1) | copy-start | bytes 196612
  93.6 19.4 %copy-start.2 = (f32[256]{0:T(256)S(1)}, f32[256]{0:T(256)}, u32[]{:S(2)}) copy-start(f32[256]{0:T(256)} %param.14) | copy-start | bytes 3076

commit v2 on v1

v2 whole, which is shorter than its diff:
```python
import math

import jax
import jax.numpy as jnp
from jax import lax
from jax.experimental import pallas as pl
from jax.experimental.pallas import tpu as pltpu
from jax.sharding import Mesh, PartitionSpec as P

row_split = (2, 2)
col_split = (4, 4, 12)
axis_names = ("ylo", "core", "yhi", "x", "z")
row_axes = ("ylo", "core")
col_axes = ("yhi", "x", "z")
team_axes = ("ylo", "core", "x")
thirds = 3
group = 4
lanes = 128
vmem_bytes = 12 * 1024 * 1024
small_vmem_bytes = 2 * 1024 * 1024
root_two_over_pi = math.sqrt(2.0 / math.pi)
cubic = 0.044715


def spread_out(value, axes, count):
    copies = jnp.broadcast_to(value[None], (count,) + value.shape)
    return lax.all_to_all(copies, axes, 0, 0, tiled=True)


def pick_tiles(codes, tile_refs, chosen, picked, slots, height, dummy):
    total = jnp.int32(0)
    for source, tiles in enumerate(tile_refs):

        def body(step, total, source=source, tiles=tiles):
            for sub in range(group):
                slot = step * group + sub
                code = codes[source, slot]
                top = pl.multiple_of(slot * height, height)
                chosen[total] = tiles[pl.ds(top, height), :]
                picked[total] = code
                total = total + jnp.where(code >= 0, 1, 0)
            return total

        total = lax.fori_loop(0, (codes[source, slots] + group - 1) // group, body, total)
    for sub in range(group):
        picked[total + sub] = dummy
    return total


def forward_kernel(codes, slabs, *refs, slots, height, blocks):
    tile_refs = refs[: -4]
    out, chosen, totals, picked = refs[-4:]
    slab_count = slabs.shape[0]
    dummy = slab_count * 64 + blocks
    totals[...] = jnp.zeros_like(totals)
    total = pick_tiles(codes, tile_refs, chosen, picked, slots, height, dummy)

    def body(step, carry):
        products = []
        for sub in range(group):
            code = picked[step * group + sub]
            slab = jnp.minimum(code >> 6, slab_count - 1)
            product = jnp.dot(
                chosen[step * group + sub], slabs[slab], preferred_element_type=jnp.float32
            )
            products.append((code & 63, product))
        for block, product in products:
            totals[block] += product
        return carry

    lax.fori_loop(0, (total + group - 1) // group, body, 0)
    halves = out.shape[1] // height
    for block in range(blocks):
        out[block // halves, pl.ds((block % halves) * height, height), :] = totals[block].astype(
            jnp.bfloat16
        )


def split_wide(value):
    high = value.astype(jnp.bfloat16).astype(jnp.float32)
    return high, value - high


def bias_rows(pieces):
    rows = lax.broadcasted_iota(jnp.int32, (16, lanes), 0)
    block = jnp.zeros((16, lanes), jnp.float32)
    for index, piece in enumerate(pieces):
        block = jnp.where(rows == index, jnp.broadcast_to(piece, (16, lanes)), block)
    return block


def sum_rows(ref, start, size):
    value = ref[0, pl.ds(start, size), :].astype(jnp.float32)
    for index in range(1, ref.shape[0]):
        value = value + ref[index, pl.ds(start, size), :].astype(jnp.float32)
    return value


def dense_kernel(partials, weight, bias, cotangent, hidden, message):
    members = partials.shape[0]
    nodes = partials.shape[1]
    aggregate = sum_rows(partials, 0, nodes)
    weight_wide = weight[...].astype(jnp.float32)
    pre = (
        jnp.dot(
            aggregate,
            weight_wide,
            precision=lax.Precision.HIGHEST,
            preferred_element_type=jnp.float32,
        )
        + bias[...]
    )
    square = pre * pre
    angle = jnp.tanh(root_two_over_pi * (pre + cubic * (square * pre)))
    gate = 0.5 * (1.0 + angle)
    hidden[...] = (pre * gate).astype(jnp.bfloat16)
    inner = root_two_over_pi * (1.0 + 3.0 * cubic * square)
    gradient = gate + 0.5 * pre * (1.0 - angle * angle) * inner
    slope = (cotangent[...].astype(jnp.float32) * gradient).astype(jnp.bfloat16)
    slope_wide = slope.astype(jnp.float32)
    spread = lax.dot_general(
        slope, weight[...], (((1,), (1,)), ((), ())), preferred_element_type=jnp.float32
    ).astype(jnp.bfloat16)
    weight_part = lax.dot_general(
        aggregate,
        slope_wide,
        (((0,), (0,)), ((), ())),
        precision=lax.Precision.HIGHEST,
        preferred_element_type=jnp.float32,
    )
    bias_part = jnp.sum(slope_wide, axis=0, keepdims=True)
    high, low = split_wide(bias_part)
    bias_block = bias_rows([high[:, :lanes], high[:, lanes:], low[:, :lanes], low[:, lanes:]])
    bias_block = bias_block.astype(jnp.bfloat16)
    share = weight_part.shape[0] // members
    for member in range(members):
        message[member, pl.ds(0, nodes), :] = spread
        part = weight_part[member * share : (member + 1) * share]
        part = jnp.concatenate([part[:, :lanes], part[:, lanes:]], axis=0)
        high, low = split_wide(part)
        message[member, pl.ds(nodes, 2 * share), :] = high.astype(jnp.bfloat16)
        message[member, pl.ds(nodes + 2 * share, 2 * share), :] = low.astype(jnp.bfloat16)
        message[member, pl.ds(nodes + 4 * share, 16), :] = bias_block


def backward_kernel(codes, spreads, *refs, slots, height, blocks, nodes, share):
    tile_refs = refs[:-5]
    out, small, chosen, totals, picked = refs[-5:]
    slab_count = totals.shape[0] - 1
    halves = nodes // height
    dummy = slab_count * 64 + blocks
    totals[...] = jnp.zeros_like(totals)
    total = pick_tiles(codes, tile_refs, chosen, picked, slots, height, dummy)

    def body(step, carry):
        products = []
        for sub in range(group):
            code = picked[step * group + sub]
            block = jnp.minimum(code & 63, blocks - 1)
            top = pl.multiple_of((block % halves) * height, height)
            product = lax.dot_general(
                chosen[step * group + sub],
                spreads[block // halves, pl.ds(top, height), :],
                (((0,), (0,)), ((), ())),
                preferred_element_type=jnp.float32,
            )
            products.append((code >> 6, product))
        for slab, product in products:
            totals[slab] += product
        return carry

    lax.fori_loop(0, (total + group - 1) // group, body, 0)
    far = out.shape[0]
    near = slab_count // far
    width = totals.shape[1]
    for slab in range(slab_count):
        out[slab // near, pl.ds((slab % near) * width, width), :] = totals[slab].astype(
            jnp.bfloat16
        )
    small[pl.ds(0, 2 * share), :] = sum_rows(spreads, nodes, 2 * share) + sum_rows(
        spreads, nodes + 2 * share, 2 * share
    )
    block = sum_rows(spreads, nodes + 4 * share, 16)[0:8]
    small[pl.ds(2 * share, 8), :] = jnp.concatenate(
        [block[0:2] + block[2:4], jnp.zeros((6, lanes), jnp.float32)], axis=0
    )


def sum_kernel(arrived, unused, out):
    width = out.shape[1]
    for index in range(out.shape[0]):
        out[index] = sum_rows(arrived, index * width, width).astype(jnp.bfloat16)


def last_kernel(arrived, grad):
    grad[...] = sum_rows(arrived, 0, grad.shape[0])


def copies_kernel(value, *refs):
    out = refs[-1]
    for index in range(out.shape[0]):
        out[index] = value[...]


def ordered_kernel(place, *refs):
    stack, out = refs[-1], refs[-2]
    count = len(refs) - 2
    for shift in range(count):
        stack[lax.rem(place[0] - shift + count, count)] = refs[shift][...]
    total = stack[0]
    for index in range(1, count):
        total = total + stack[index]
    out[...] = total


def assemble_kernel(place, *refs, across, share, factor):
    out = refs[-1]
    for flip, shares in enumerate(refs[:-1]):
        row = place[0] ^ flip
        for shift in range(across):
            member = row * across + lax.rem(place[1] - shift + across, across)
            top = pl.multiple_of(member * share, share)
            out[pl.ds(top, share), pl.ds(0, lanes)] = shares[shift, pl.ds(0, share), :] * factor
            out[pl.ds(top, share), pl.ds(lanes, lanes)] = (
                shares[shift, pl.ds(share, share), :] * factor
            )


def in_vmem():
    return pl.BlockSpec(memory_space=pltpu.VMEM)


def in_smem():
    return pl.BlockSpec(memory_space=pltpu.SMEM)


def ordered_sum(value, axis, size, hops, place):
    pieces = [value] + [lax.ppermute(value, axis, hops(shift)) for shift in range(1, size)]
    return pl.pallas_call(
        ordered_kernel,
        out_shape=jax.ShapeDtypeStruct(value.shape, value.dtype),
        in_specs=[in_smem()] + [in_vmem()] * size,
        out_specs=in_vmem(),
        scratch_shapes=[pltpu.VMEM((size,) + value.shape, value.dtype)],
        compiler_params=pltpu.CompilerParams(vmem_limit_bytes=small_vmem_bytes),
        name="ordered_sum",
    )(place.reshape(1), *pieces)


def local(features, tile_rows, tile_cols, tile_counts, tile_values, weight, bias, cotangent):
    nodes, width = features.shape
    slots, height, tile_width = tile_values.shape[2:]
    hidden = weight.shape[1]
    far = lax.axis_size("yhi")
    across = lax.axis_size("x")
    near = lax.axis_size("z")
    members = lax.axis_size(team_axes)
    group_rows = lax.axis_size(row_axes)
    here = lax.axis_index("x")
    params = pltpu.CompilerParams(vmem_limit_bytes=vmem_bytes)
    halves = nodes // height
    blocks = members * halves

    def any_place():
        return pl.BlockSpec(memory_space=pl.ANY)

    live = jnp.arange(slots, dtype=jnp.int32) < tile_counts[0, 0]
    columns, rows = tile_cols[0, 0], tile_rows[0, 0]
    owner = jnp.where(live, (columns // near) % across, 255)
    slab = (columns // (across * near)) * near + columns % near
    block = ((rows // halves) * across + here) * halves + rows % halves
    places = jnp.stack([owner, slab, block])
    ends = jnp.stack([jnp.int32(254), jnp.int32(0), tile_counts[0, 0]])[:, None]
    places = jnp.concatenate([places, ends], axis=1)
    places = jnp.pad(places, ((0, 13), (0, lanes - slots - 1))).astype(jnp.bfloat16)
    own = jnp.concatenate([tile_values[0, 0].reshape(slots * height, tile_width), places], axis=0)

    up = [(start, (start + 1) % across) for start in range(across)]
    down = [(end, start) for start, end in up]
    buffers = [own, lax.ppermute(own, "x", up)]

    line = spread_out(features, "z", near).reshape(near * nodes, width)
    copies = pl.pallas_call(
        copies_kernel,
        out_shape=jax.ShapeDtypeStruct((far, near * nodes, width), jnp.bfloat16),
        in_specs=[in_vmem(), any_place()],
        out_specs=in_vmem(),
        compiler_params=params,
        name="line_copies",
    )(line, buffers[1])
    if across > 2:
        back = lax.ppermute(own, "x", down)
        for shift in range(2, across - 1):
            buffers.append(lax.ppermute(buffers[-1], "x", up))
        buffers.append(back)
    slabs = lax.all_to_all(copies, "yhi", 0, 0, tiled=True).reshape(far * near, nodes, width)

    tables = []
    for buffer in buffers:
        top = buffer[slots * height :].astype(jnp.int32)
        mine = (top[0] == here) | (top[0] == 254)
        tables.append(jnp.where(mine, top[1] * 64 + top[2], -1))
    codes = jnp.stack(tables)

    scratch_tiles = pltpu.VMEM((across * slots + group, height, tile_width), jnp.bfloat16)
    scratch_list = pltpu.SMEM((across * slots + group,), jnp.int32)
    partial = pl.pallas_call(
        lambda *refs: forward_kernel(*refs, slots=slots, height=height, blocks=blocks),
        out_shape=jax.ShapeDtypeStruct((members, nodes, width), jnp.bfloat16),
        in_specs=[in_smem(), in_vmem()] + [in_vmem()] * across,
        out_specs=in_vmem(),
        scratch_shapes=[
            scratch_tiles,
            pltpu.VMEM((blocks + 1, height, width), jnp.float32),
            scratch_list,
        ],
        compiler_params=params,
        name="forward_tiles",
    )(codes, slabs, *buffers)
    partials = lax.all_to_all(partial, team_axes, 0, 0, tiled=True)

    share = width // members
    hidden_out, message = pl.pallas_call(
        dense_kernel,
        out_shape=(
            jax.ShapeDtypeStruct((nodes, hidden), jnp.bfloat16),
            jax.ShapeDtypeStruct((members, nodes + 4 * share + 16, width), jnp.bfloat16),
        ),
        in_specs=[in_vmem()] * 4,
        out_specs=(in_vmem(), in_vmem()),
        compiler_params=params,
        name="dense_layer",
    )(partials, weight, bias.reshape(1, hidden), cotangent)
    spreads = lax.all_to_all(message, team_axes, 0, 0, tiled=True)

    column_part, small = pl.pallas_call(
        lambda *refs: backward_kernel(
            *refs, slots=slots, height=height, blocks=blocks, nodes=nodes, share=share
        ),
        out_shape=(
            jax.ShapeDtypeStruct((far, near * nodes, width), jnp.bfloat16),
            jax.ShapeDtypeStruct((2 * share + 8, lanes), jnp.float32),
        ),
        in_specs=[in_smem(), in_vmem()] + [in_vmem()] * across,
        out_specs=(in_vmem(), in_vmem()),
        scratch_shapes=[
            scratch_tiles,
            pltpu.VMEM((far * near + 1, nodes, width), jnp.float32),
            scratch_list,
        ],
        compiler_params=params,
        name="backward_tiles",
    )(codes, spreads, *buffers)
    def ring(size):
        return lambda shift: [(start, (start + shift) % size) for start in range(size)]

    depth = lax.axis_index("z")
    strip = near // thirds
    small = ordered_sum(small, "yhi", far, ring(far), lax.axis_index("yhi"))
    small = ordered_sum(
        small,
        "z",
        thirds,
        lambda shift: [(start, (start + shift * strip) % near) for start in range(near)],
        depth // strip,
    )
    small = ordered_sum(
        small,
        "z",
        strip,
        lambda shift: [
            (start, start // strip * strip + (start + shift) % strip) for start in range(near)
        ],
        depth % strip,
    )
    arrived = lax.all_to_all(column_part, "yhi", 0, 0, tiled=True)
    line_part = pl.pallas_call(
        sum_kernel,
        out_shape=jax.ShapeDtypeStruct((near, nodes, width), jnp.bfloat16),
        in_specs=[in_vmem(), any_place()],
        out_specs=in_vmem(),
        compiler_params=params,
        name="sum_far",
    )(arrived, small)
    arrived = lax.all_to_all(line_part, "z", 0, 0, tiled=True)
    features_grad = pl.pallas_call(
        last_kernel,
        out_shape=jax.ShapeDtypeStruct((nodes, width), jnp.float32),
        in_specs=[in_vmem()],
        out_specs=in_vmem(),
        compiler_params=params,
        name="sum_near",
    )(arrived)

    weight_share = small[: 2 * share]
    pieces = [weight_share]
    for shift in range(1, across):
        pieces.append(lax.ppermute(weight_share, "x", ring(across)(shift)))
    shares = jnp.stack(pieces)
    pieces = [shares]
    for flip in range(1, group_rows):
        pieces.append(
            lax.ppermute(shares, row_axes, [(start, start ^ flip) for start in range(group_rows)])
        )
    factor = 1.0 / math.sqrt(nodes * group_rows * far * across * near)
    place = jnp.stack([lax.axis_index(row_axes), here])
    weight_grad = pl.pallas_call(
        lambda *refs: assemble_kernel(*refs, across=across, share=share, factor=factor),
        out_shape=jax.ShapeDtypeStruct((width, hidden), jnp.float32),
        in_specs=[in_smem()] + [in_vmem()] * group_rows,
        out_specs=in_vmem(),
        compiler_params=pltpu.CompilerParams(vmem_limit_bytes=small_vmem_bytes),
        name="weight_grad",
    )(place, *pieces)
    bias_grad = small[2 * share : 2 * share + 2].reshape(hidden) * factor
    return (hidden_out, features_grad, weight_grad, bias_grad)


def solution(mesh):
    fine = Mesh(mesh.devices.reshape(row_split + col_split), axis_names)
    nodes_spec = P(row_axes + col_axes, None)
    in_specs = (
        nodes_spec,
        P(row_axes, col_axes, None),
        P(row_axes, col_axes, None),
        P(row_axes, col_axes),
        P(row_axes, col_axes, None, None, None),
        P(),
        P(),
        nodes_spec,
    )
    out_specs = (nodes_spec, nodes_spec, P(), P())
    return jax.shard_map(local, mesh=fine, in_specs=in_specs, out_specs=out_specs, check_vma=False)
```

time: 219 us -> 234 us (1.068)
  blocking collectives: 119 us -> 32 us
  starting transfers between devices: 32 us -> 99.3 us
  waiting for transfers between devices: 51.5 us -> 81 us
  Pallas kernels: 7.38 us -> 10.2 us
    all_to_all x3 -> x0, blocking collectives: 83.8 us -> none  [the longest x1 45.4 us: local(): arrived = lax.all_to_all(column_part, 'yhi', 0, 0, tiled=True)]
    ppermute x3 -> x17, starting transfers between devices: 9.33 us -> 68.6 us  [the longest x8 35.4 us: ordered_sum(): lax.ppermute(value, axis, hops(shift))]
    ppermute x3 -> x17, waiting for transfers between devices: 34.2 us -> 67.6 us  [the longest x8 30.3 us: ordered_sum(): lax.ppermute(value, axis, hops(shift))]
    all_to_all x2 -> x1, waiting for transfers between devices: 17.3 us -> 0.01 us  [spread_out(): return lax.all_to_all(copies, axes, 0, 0, tiled=True)]
    all_to_all x0 -> x3, starting transfers between devices: none -> 14.9 us  [the longest x1 6.81 us: local(): lax.all_to_all(copies, 'yhi', 0, 0, tiled=True)]
    all_to_all x0 -> x3, waiting for transfers between devices: none -> 13.4 us  [the longest x1 13.4 us: local(): lax.all_to_all(copies, 'yhi', 0, 0, tiled=True)]
    all_to_all x2 -> x1, starting transfers between devices: 22.6 us -> 15.7 us  [spread_out(): return lax.all_to_all(copies, axes, 0, 0, tiled=True)]
    unnamed x9 -> x22, local copies, waits for them, and re-layouts: 0.68 us -> 5.25 us
  transfers between devices with their start and end apart: 5 -> 21, of which waited for: 4 -> 10; matrix products, arithmetic and copies ran while one was open for 1% -> 1% of each run, Pallas kernels for 0% -> 1%
where the time goes in v2:
time: 234 us; the launch traced here: 233 us
  starting transfers between devices  99.3 us (42%)
  waiting for transfers between devices  81 us (35%)
  blocking collectives  32 us (14%)
  Pallas kernels  10.2 us (4%)
  local copies, waits for them, and re-layouts  7.01 us (3%)
    ppermute x8, starting transfers between devices, ordered_sum(): lax.ppermute(value, axis, hops(shift))  35.4 us
    ppermute x8, waiting for transfers between devices, ordered_sum(): lax.ppermute(value, axis, hops(shift))  30.3 us
    ppermute x1, waiting for transfers between devices, local(): buffers = [own, lax.ppermute(own, 'x', up)]  18.2 us
    all_to_all x1, blocking collectives, local(): partials = lax.all_to_all(partial, team_axes, 0, 0, tiled=True)  16.2 us
    all_to_all x1, blocking collectives, local(): spreads = lax.all_to_all(message, team_axes, 0, 0, tiled=True)  15.8 us
    all_to_all x1, starting transfers between devices, spread_out(): return lax.all_to_all(copies, axes, 0, 0, tiled=True)  15.7 us
    ppermute x3, starting transfers between devices, local(): lax.ppermute(shares, row_axes, [(start, start ^ flip) for start in range(...  15.6 us
    ppermute x1, waiting for transfers between devices, local(): back = lax.ppermute(own, 'x', down)  13.5 us
  transfers between devices with their start and end apart: 21, of which 10 were waited for; matrix products, arithmetic and copies ran while one was open for 1% of the time, Pallas kernels for 1%

profile of v2, /device:TPU:1, one launch (start us, length us, event | category | flops | bytes accessed | tf_op | source)
XLA Modules:
  0.0 232.8 jit_solution(11563657355579163231)
XLA Ops:
  2.3 15.7 %all-to-all-start = ((bf16[12,128,128]{2,1,0:T(8,128)(2,1)}), bf16[12,128,128]{2,1,0:T(8,128)(2,1)S(1)}, u32[]{:S(2)}, u32[]{:S(2)}) async-start(bf16[12,128,128]{2,1,0:T(8,128)(2,1)} %broadcast_in_dim.24), calls=%async_computation | async-start | bytes 786432 | tf_op jit(solution)/shard_map/all_to_all | solution.py:27
  19.7 3.1 %collective-permute-start = (bf16[3088,128]{1,0:T(8,128)(2,1)S(1)}, bf16[3088,128]{1,0:T(8,128)(2,1)S(1)}, u32[]{:S(2)}, u32[]{:S(2)}) collective-permute-start(bf16[3088,128]{1,0:T(8,128)(2,1)S(1)} %pad_maximum_fusion.refs_2_), channel_id=1, source_target_pairs={{0,12},{12,24},{24,36},{36,0},{1,13},{13,25},{25,37},{37,1},{2,14}... | collective-permute-start | bytes 2371592 | tf_op jit(solution)/shard_map/ppermute | solution.py:280
  22.8 18.2 %collective-permute-done.refs_0_.refs_3_ = bf16[3088,128]{1,0:T(8,128)(2,1)S(1)} collective-permute-done((bf16[3088,128]{1,0:T(8,128)(2,1)S(1)}, bf16[3088,128]{1,0:T(8,128)(2,1)S(1)}, u32[]{:S(2)}, u32[]{:S(2)}) %collective-permute-start) | collective-permute-done | bytes 790560 | tf_op jit(solution)/shard_map/ppermute | solution.py:280
  42.4 6.8 %all-to-all-start.1 = ((bf16[4,1536,128]{2,1,0:T(8,128)(2,1)}), bf16[4,1536,128]{2,1,0:T(8,128)(2,1)S(1)}, u32[]{:S(2)}, u32[]{:S(2)}) async-start(bf16[4,1536,128]{2,1,0:T(8,128)(2,1)} %copy-done), calls=%async_computation.1 | async-start | bytes 3145728 | tf_op jit(solution)/shard_map/all_to_all | solution.py:296
  49.2 3.2 %collective-permute-start.2 = (bf16[3088,128]{1,0:T(8,128)(2,1)S(1)}, bf16[3088,128]{1,0:T(8,128)(2,1)S(1)}, u32[]{:S(2)}, u32[]{:S(2)}) collective-permute-start(bf16[3088,128]{1,0:T(8,128)(2,1)S(1)} %pad_maximum_fusion.refs_2_), channel_id=1, source_target_pairs={{12,0},{24,12},{36,24},{0,36},{13,1},{25,13},{37,25},{1,37},{14,2}... | collective-permute-start | bytes 2371592 | tf_op jit(solution)/shard_map/ppermute | solution.py:292
  52.4 2.1 collective-permute-start.1
  54.5 13.5 %collective-permute-done.2.refs_5_ = bf16[3088,128]{1,0:T(8,128)(2,1)S(1)} collective-permute-done((bf16[3088,128]{1,0:T(8,128)(2,1)S(1)}, bf16[3088,128]{1,0:T(8,128)(2,1)S(1)}, u32[]{:S(2)}, u32[]{:S(2)}) %collective-permute-start.2) | collective-permute-done | bytes 790560 | tf_op jit(solution)/shard_map/ppermute | solution.py:292
  69.0 3.2 %collective-permute-done.1.refs_4_ = bf16[3088,128]{1,0:T(8,128)(2,1)S(1)} collective-permute-done((bf16[3088,128]{1,0:T(8,128)(2,1)S(1)}, bf16[3088,128]{1,0:T(8,128)(2,1)S(1)}, u32[]{:S(2)}, u32[]{:S(2)}) %collective-permute-start.1) | collective-permute-done | bytes 790560 | tf_op jit(solution)/shard_map/ppermute | solution.py:294
  73.1 13.4 %all-to-all-done.1 = bf16[4,1536,128]{2,1,0:T(8,128)(2,1)S(1)} async-done(((bf16[4,1536,128]{2,1,0:T(8,128)(2,1)}), bf16[4,1536,128]{2,1,0:T(8,128)(2,1)S(1)}, u32[]{:S(2)}, u32[]{:S(2)}) %all-to-all-start.1) | async-done | bytes 1572896 | tf_op jit(solution)/shard_map/all_to_all | solution.py:296
  88.8 2.2 forward_tiles.1
  91.0 16.2 %all_to_all.30.partials = bf16[16,128,128]{2,1,0:T(8,128)(2,1)S(1)} all-to-all(bf16[16,128,128]{2,1,0:T(8,128)(2,1)S(1)} %forward_tiles.1), channel_id=1, replica_groups=mesh['ylo'=2,'core'=2,'yhi'=4,'x'=4,'z'=12] {'ylo','core','x'}, dimensions={0} | all-to-all | bytes 1048576 | tf_op jit(solution)/shard_map/all_to_all | solution.py:320
  108.3 15.8 %all_to_all.31.refs_1_ = bf16[16,176,128]{2,1,0:T(8,128)(2,1)S(1)} all-to-all(bf16[16,176,128]{2,1,0:T(8,128)(2,1)S(1)} %get-tuple-element.9), channel_id=1, replica_groups=mesh['ylo'=2,'core'=2,'yhi'=4,'x'=4,'z'=12] {'ylo','core','x'}, dimensions={0} | all-to-all | bytes 1441792 | tf_op jit(solution)/shard_map/all_to_all | solution.py:334
  124.1 3.9 %backward_tiles.1 = (bf16[4,1536,128]{2,1,0:T(8,128)(2,1)}, f32[24,128]{1,0:T(8,128)S(1)}) custom-call(s32[4,128]{1,0:T(4,128)S(1)} %pad_add_fusion.refs_0_, bf16[16,176,128]{2,1,0:T(8,128)(2,1)S(1)} %all_to_all.31.refs_1_, bf16[3088,128]{1,0:T(8,128)(2,1)S(1)} %pad_maximum_fusion.refs_2_, bf16[3088,128]{1,0:T(8,128)(2,1)S(1)} %collective-permute-done.refs_0_.refs_3_, ...), custom_call_target="tpu_custom_call" | custom-call | tf_op jit(solution)/shard_map/backward_tiles/pallas_call | solution.py:336
  127.9 3.6 %all-to-all-start.4 = ((bf16[4,1536,128]{2,1,0:T(8,128)(2,1)}), bf16[4,1536,128]{2,1,0:T(8,128)(2,1)S(1)}, u32[]{:S(2)}, u32[]{:S(2)}) async-start(bf16[4,1536,128]{2,1,0:T(8,128)(2,1)} %get-tuple-element.10), calls=%async_computation.4 | async-start | bytes 3145728 | tf_op jit(solution)/shard_map/all_to_all | solution.py:376
  131.5 4.2 %collective-permute-start.3 = (f32[24,128]{1,0:T(8,128)S(1)}, f32[24,128]{1,0:T(8,128)S(1)}, u32[]{:S(2)}, u32[]{:S(2)}) collective-permute-start(f32[24,128]{1,0:T(8,128)S(1)} %get-tuple-element.11.refs_0_), channel_id=1, source_target_pairs={{0,48},{48,96},{96,144},{144,0},{1,49},{49,97},{97,145},{145,1},{2... | collective-permute-start | bytes 36872 | tf_op jit(solution)/shard_map/ppermute | solution.py:238
  135.7 5.2 %collective-permute-start.4 = (f32[24,128]{1,0:T(8,128)S(1)}, f32[24,128]{1,0:T(8,128)S(1)}, u32[]{:S(2)}, u32[]{:S(2)}) collective-permute-start(f32[24,128]{1,0:T(8,128)S(1)} %get-tuple-element.11.refs_0_), channel_id=1, source_target_pairs={{0,96},{48,144},{96,0},{144,48},{1,97},{49,145},{97,1},{145,49},{2... | collective-permute-start | bytes 36872 | tf_op jit(solution)/shard_map/ppermute | solution.py:238
  140.9 5.2 %collective-permute-start.5 = (f32[24,128]{1,0:T(8,128)S(1)}, f32[24,128]{1,0:T(8,128)S(1)}, u32[]{:S(2)}, u32[]{:S(2)}) collective-permute-start(f32[24,128]{1,0:T(8,128)S(1)} %get-tuple-element.11.refs_0_), channel_id=1, source_target_pairs={{0,144},{48,0},{96,48},{144,96},{1,145},{49,1},{97,49},{145,97},{2... | collective-permute-start | bytes 36872 | tf_op jit(solution)/shard_map/ppermute | solution.py:238
  146.2 23.6 %collective-permute-done.3.refs_1_ = f32[24,128]{1,0:T(8,128)S(1)} collective-permute-done((f32[24,128]{1,0:T(8,128)S(1)}, f32[24,128]{1,0:T(8,128)S(1)}, u32[]{:S(2)}, u32[]{:S(2)}) %collective-permute-start.3) | collective-permute-done | bytes 12320 | tf_op jit(solution)/shard_map/ppermute | solution.py:238
  169.8 1.9 collective-permute-start.6
  171.7 7.3 %collective-permute-start.7 = (f32[24,128]{1,0:T(8,128)S(1)}, f32[24,128]{1,0:T(8,128)S(1)}, u32[]{:S(2)}, u32[]{:S(2)}) collective-permute-start(f32[24,128]{1,0:T(8,128)S(1)} %ordered_sum.3.refs_0_), channel_id=1, source_target_pairs={{0,8},{1,9},{2,10},{3,11},{4,0},{5,1},{6,2},{7,3},{8,4},{9,5},{10,... | collective-permute-start | bytes 36872 | tf_op jit(solution)/shard_map/ppermute | solution.py:238
  179.0 3.6 %collective-permute-done.7.refs_2_ = f32[24,128]{1,0:T(8,128)S(1)} collective-permute-done((f32[24,128]{1,0:T(8,128)S(1)}, f32[24,128]{1,0:T(8,128)S(1)}, u32[]{:S(2)}, u32[]{:S(2)}) %collective-permute-start.7) | collective-permute-done | bytes 12320 | tf_op jit(solution)/shard_map/ppermute | solution.py:238
  182.6 7.4 %collective-permute-start.10 = (f32[24,128]{1,0:T(8,128)S(1)}, f32[24,128]{1,0:T(8,128)S(1)}, u32[]{:S(2)}, u32[]{:S(2)}) collective-permute-start(f32[24,128]{1,0:T(8,128)S(1)} %ordered_sum.4.refs_0_), channel_id=1, source_target_pairs={{0,3},{1,0},{2,1},{3,2},{4,7},{5,4},{6,5},{7,6},{8,11},{9,8},{10,9... | collective-permute-start | bytes 36872 | tf_op jit(solution)/shard_map/ppermute | solution.py:238
  190.0 1.9 collective-permute-start.8
  191.9 2.2 collective-permute-start.9
  194.2 2.0 collective-permute-done.8.refs_1_
  198.3 4.6 %all-to-all-start.5 = ((bf16[12,128,128]{2,1,0:T(8,128)(2,1)}), bf16[12,128,128]{2,1,0:T(8,128)(2,1)S(1)}, u32[]{:S(2)}, u32[]{:S(2)}) async-start(bf16[12,128,128]{2,1,0:T(8,128)(2,1)} %sum_far.1), calls=%async_computation.5 | async-start | bytes 786432 | tf_op jit(solution)/shard_map/all_to_all | solution.py:385
  202.8 1.9 collective-permute-start.11
  204.8 3.3 %collective-permute-start.12 = (f32[16,128]{1,0:T(8,128)S(1)}, f32[16,128]{1,0:T(8,128)S(1)}, u32[]{:S(2)}, u32[]{:S(2)}) collective-permute-start(f32[16,128]{1,0:T(8,128)S(1)} %get-tuple-element.15), channel_id=1, source_target_pairs={{0,24},{12,36},{24,0},{36,12},{1,25},{13,37},{25,1},{37,13},{2,26}... | collective-permute-start | bytes 24584 | tf_op jit(solution)/shard_map/ppermute | solution.py:398
  208.1 4.0 %collective-permute-start.13 = (f32[16,128]{1,0:T(8,128)S(1)}, f32[16,128]{1,0:T(8,128)S(1)}, u32[]{:S(2)}, u32[]{:S(2)}) collective-permute-start(f32[16,128]{1,0:T(8,128)S(1)} %get-tuple-element.15), channel_id=1, source_target_pairs={{0,36},{12,0},{24,12},{36,24},{1,37},{13,1},{25,13},{37,25},{2,38}... | collective-permute-start | bytes 24584 | tf_op jit(solution)/shard_map/ppermute | solution.py:398
  212.9 10.2 %collective-permute-start.14 = (f32[4,16,128]{2,1,0:T(8,128)S(1)}, f32[4,16,128]{2,1,0:T(8,128)S(1)}, u32[]{:S(2)}, u32[]{:S(2)}) collective-permute-start(f32[4,16,128]{2,1,0:T(8,128)S(1)} %pad_maximum_fusion.1.refs_1_), channel_id=1, source_target_pairs={{0,192},{192,0},{384,576},{576,384},{1,193},{193,1},{385,577},{577... | collective-permute-start | bytes 98312 | tf_op jit(solution)/shard_map/ppermute | solution.py:403
  223.1 2.5 %collective-permute-start.15 = (f32[4,16,128]{2,1,0:T(8,128)S(1)}, f32[4,16,128]{2,1,0:T(8,128)S(1)}, u32[]{:S(2)}, u32[]{:S(2)}) collective-permute-start(f32[4,16,128]{2,1,0:T(8,128)S(1)} %pad_maximum_fusion.1.refs_1_), channel_id=1, source_target_pairs={{0,384},{192,576},{384,0},{576,192},{1,385},{193,577},{385,1},{577... | collective-permute-start | bytes 98312 | tf_op jit(solution)/shard_map/ppermute | solution.py:403
  225.6 2.9 %collective-permute-start.16 = (f32[4,16,128]{2,1,0:T(8,128)S(1)}, f32[4,16,128]{2,1,0:T(8,128)S(1)}, u32[]{:S(2)}, u32[]{:S(2)}) collective-permute-start(f32[4,16,128]{2,1,0:T(8,128)S(1)} %pad_maximum_fusion.1.refs_1_), channel_id=1, source_target_pairs={{0,576},{192,384},{384,192},{576,0},{1,577},{193,385},{385,193},{5... | collective-permute-start | bytes 98312 | tf_op jit(solution)/shard_map/ppermute | solution.py:403
  (62 shorter events, 16.3 us)
Async XLA Ops:
  0.6 19.0 %copy-start.10 = (bf16[1,1,48,64,128]{4,3,2,1,0:T(8,128)(2,1)S(1)}, bf16[1,1,48,64,128]{4,3,2,1,0:T(8,128)(2,1)}, u32[]{:S(2)}) copy-start(bf16[1,1,48,64,128]{4,3,2,1,0:T(8,128)(2,1)} %param.12) | copy-start | bytes 2359300
  2.3 38.7 %all-to-all-start = ((bf16[12,128,128]{2,1,0:T(8,128)(2,1)}), bf16[12,128,128]{2,1,0:T(8,128)(2,1)S(1)}, u32[]{:S(2)}, u32[]{:S(2)}) async-start(bf16[12,128,128]{2,1,0:T(8,128)(2,1)} %broadcast_in_dim.24), calls=%async_computation | async-start | bytes 786432 | tf_op jit(solution)/shard_map/all_to_all | solution.py:27
  19.7 21.3 %collective-permute-start = (bf16[3088,128]{1,0:T(8,128)(2,1)S(1)}, bf16[3088,128]{1,0:T(8,128)(2,1)S(1)}, u32[]{:S(2)}, u32[]{:S(2)}) collective-permute-start(bf16[3088,128]{1,0:T(8,128)(2,1)S(1)} %pad_maximum_fusion.refs_2_), channel_id=1, source_target_pairs={{0,12},{12,24},{24,36},{36,0},{1,13},{13,25},{25,37},{37,1},{2,14}... | collective-permute-start | bytes 2371592 | tf_op jit(solution)/shard_map/ppermute | solution.py:280
  41.2 1.2 copy-start
  42.4 44.1 %all-to-all-start.1 = ((bf16[4,1536,128]{2,1,0:T(8,128)(2,1)}), bf16[4,1536,128]{2,1,0:T(8,128)(2,1)S(1)}, u32[]{:S(2)}, u32[]{:S(2)}) async-start(bf16[4,1536,128]{2,1,0:T(8,128)(2,1)} %copy-done), calls=%async_computation.1 | async-start | bytes 3145728 | tf_op jit(solution)/shard_map/all_to_all | solution.py:296
  49.2 18.9 %collective-permute-start.2 = (bf16[3088,128]{1,0:T(8,128)(2,1)S(1)}, bf16[3088,128]{1,0:T(8,128)(2,1)S(1)}, u32[]{:S(2)}, u32[]{:S(2)}) collective-permute-start(bf16[3088,128]{1,0:T(8,128)(2,1)S(1)} %pad_maximum_fusion.refs_2_), channel_id=1, source_target_pairs={{12,0},{24,12},{36,24},{0,36},{13,1},{25,13},{37,25},{1,37},{14,2}... | collective-permute-start | bytes 2371592 | tf_op jit(solution)/shard_map/ppermute | solution.py:292
  52.4 19.8 %collective-permute-start.1 = (bf16[3088,128]{1,0:T(8,128)(2,1)S(1)}, bf16[3088,128]{1,0:T(8,128)(2,1)S(1)}, u32[]{:S(2)}, u32[]{:S(2)}) collective-permute-start(bf16[3088,128]{1,0:T(8,128)(2,1)S(1)} %collective-permute-done.refs_0_.refs_3_), channel_id=1, source_target_pairs={{0,12},{12,24},{24,36},{36,0},{1,13},{13,25},{25,37},{37,1},{2,14}... | collective-permute-start | bytes 2371592 | tf_op jit(solution)/shard_map/ppermute | solution.py:294
  68.1 0.9 copy-start.1
  72.2 0.9 copy-start.4
  86.5 1.1 copy-start.2
  87.6 1.1 copy-start.5
  88.8 18.4 %copy-start.7 = (bf16[128,256]{1,0:T(8,128)(2,1)S(1)}, bf16[128,256]{1,0:T(8,128)(2,1)}, u32[]{:S(2)}) copy-start(bf16[128,256]{1,0:T(8,128)(2,1)} %weight.1) | copy-start | bytes 196612
  88.8 18.4 %copy-start.8 = (bf16[128,256]{1,0:T(8,128)(2,1)S(1)}, bf16[128,256]{1,0:T(8,128)(2,1)}, u32[]{:S(2)}) copy-start(bf16[128,256]{1,0:T(8,128)(2,1)} %cotangent.1) | copy-start | bytes 196612
  88.8 18.4 %copy-start.9 = (f32[256]{0:T(256)S(1)}, f32[256]{0:T(256)}, u32[]{:S(2)}) copy-start(f32[256]{0:T(256)} %param.14) | copy-start | bytes 3076
  91.0 33.1 %copy-start.3 = (bf16[3088,128]{1,0:T(8,128)(2,1)S(1)}, bf16[3088,128]{1,0:T(8,128)(2,1)}, u32[]{:S(2)}) copy-start(bf16[3088,128]{1,0:T(8,128)(2,1)} %copy-done.1) | copy-start | bytes 2371588
  91.0 33.1 %copy-start.6 = (bf16[3088,128]{1,0:T(8,128)(2,1)S(1)}, bf16[3088,128]{1,0:T(8,128)(2,1)}, u32[]{:S(2)}) copy-start(bf16[3088,128]{1,0:T(8,128)(2,1)} %copy-done.4) | copy-start | bytes 2371588
  127.9 69.4 %all-to-all-start.4 = ((bf16[4,1536,128]{2,1,0:T(8,128)(2,1)}), bf16[4,1536,128]{2,1,0:T(8,128)(2,1)S(1)}, u32[]{:S(2)}, u32[]{:S(2)}) async-start(bf16[4,1536,128]{2,1,0:T(8,128)(2,1)} %get-tuple-element.10), calls=%async_computation.4 | async-start | bytes 3145728 | tf_op jit(solution)/shard_map/all_to_all | solution.py:376
  131.5 38.3 %collective-permute-start.3 = (f32[24,128]{1,0:T(8,128)S(1)}, f32[24,128]{1,0:T(8,128)S(1)}, u32[]{:S(2)}, u32[]{:S(2)}) collective-permute-start(f32[24,128]{1,0:T(8,128)S(1)} %get-tuple-element.11.refs_0_), channel_id=1, source_target_pairs={{0,48},{48,96},{96,144},{144,0},{1,49},{49,97},{97,145},{145,1},{2... | collective-permute-start | bytes 36872 | tf_op jit(solution)/shard_map/ppermute | solution.py:238
  135.7 34.0 %collective-permute-start.4 = (f32[24,128]{1,0:T(8,128)S(1)}, f32[24,128]{1,0:T(8,128)S(1)}, u32[]{:S(2)}, u32[]{:S(2)}) collective-permute-start(f32[24,128]{1,0:T(8,128)S(1)} %get-tuple-element.11.refs_0_), channel_id=1, source_target_pairs={{0,96},{48,144},{96,0},{144,48},{1,97},{49,145},{97,1},{145,49},{2... | collective-permute-start | bytes 36872 | tf_op jit(solution)/shard_map/ppermute | solution.py:238
  140.9 28.8 %collective-permute-start.5 = (f32[24,128]{1,0:T(8,128)S(1)}, f32[24,128]{1,0:T(8,128)S(1)}, u32[]{:S(2)}, u32[]{:S(2)}) collective-permute-start(f32[24,128]{1,0:T(8,128)S(1)} %get-tuple-element.11.refs_0_), channel_id=1, source_target_pairs={{0,144},{48,0},{96,48},{144,96},{1,145},{49,1},{97,49},{145,97},{2... | collective-permute-start | bytes 36872 | tf_op jit(solution)/shard_map/ppermute | solution.py:238
  169.8 9.2 %collective-permute-start.6 = (f32[24,128]{1,0:T(8,128)S(1)}, f32[24,128]{1,0:T(8,128)S(1)}, u32[]{:S(2)}, u32[]{:S(2)}) collective-permute-start(f32[24,128]{1,0:T(8,128)S(1)} %ordered_sum.3.refs_0_), channel_id=1, source_target_pairs={{0,4},{1,5},{2,6},{3,7},{4,8},{5,9},{6,10},{7,11},{8,0},{9,1},{10,... | collective-permute-start | bytes 36872 | tf_op jit(solution)/shard_map/ppermute | solution.py:238
  171.7 10.9 %collective-permute-start.7 = (f32[24,128]{1,0:T(8,128)S(1)}, f32[24,128]{1,0:T(8,128)S(1)}, u32[]{:S(2)}, u32[]{:S(2)}) collective-permute-start(f32[24,128]{1,0:T(8,128)S(1)} %ordered_sum.3.refs_0_), channel_id=1, source_target_pairs={{0,8},{1,9},{2,10},{3,11},{4,0},{5,1},{6,2},{7,3},{8,4},{9,5},{10,... | collective-permute-start | bytes 36872 | tf_op jit(solution)/shard_map/ppermute | solution.py:238
  182.6 11.6 %collective-permute-start.10 = (f32[24,128]{1,0:T(8,128)S(1)}, f32[24,128]{1,0:T(8,128)S(1)}, u32[]{:S(2)}, u32[]{:S(2)}) collective-permute-start(f32[24,128]{1,0:T(8,128)S(1)} %ordered_sum.4.refs_0_), channel_id=1, source_target_pairs={{0,3},{1,0},{2,1},{3,2},{4,7},{5,4},{6,5},{7,6},{8,11},{9,8},{10,9... | collective-permute-start | bytes 36872 | tf_op jit(solution)/shard_map/ppermute | solution.py:238
  190.0 6.2 %collective-permute-start.8 = (f32[24,128]{1,0:T(8,128)S(1)}, f32[24,128]{1,0:T(8,128)S(1)}, u32[]{:S(2)}, u32[]{:S(2)}) collective-permute-start(f32[24,128]{1,0:T(8,128)S(1)} %ordered_sum.4.refs_0_), channel_id=1, source_target_pairs={{0,1},{1,2},{2,3},{3,0},{4,5},{5,6},{6,7},{7,4},{8,9},{9,10},{10,1... | collective-permute-start | bytes 36872 | tf_op jit(solution)/shard_map/ppermute | solution.py:238
  191.9 5.3 %collective-permute-start.9 = (f32[24,128]{1,0:T(8,128)S(1)}, f32[24,128]{1,0:T(8,128)S(1)}, u32[]{:S(2)}, u32[]{:S(2)}) collective-permute-start(f32[24,128]{1,0:T(8,128)S(1)} %ordered_sum.4.refs_0_), channel_id=1, source_target_pairs={{0,2},{1,3},{2,0},{3,1},{4,6},{5,7},{6,4},{7,5},{8,10},{9,11},{10,... | collective-permute-start | bytes 36872 | tf_op jit(solution)/shard_map/ppermute | solution.py:238
  198.3 33.8 %all-to-all-start.5 = ((bf16[12,128,128]{2,1,0:T(8,128)(2,1)}), bf16[12,128,128]{2,1,0:T(8,128)(2,1)S(1)}, u32[]{:S(2)}, u32[]{:S(2)}) async-start(bf16[12,128,128]{2,1,0:T(8,128)(2,1)} %sum_far.1), calls=%async_computation.5 | async-start | bytes 786432 | tf_op jit(solution)/shard_map/all_to_all | solution.py:385
  202.8 9.3 %collective-permute-start.11 = (f32[16,128]{1,0:T(8,128)S(1)}, f32[16,128]{1,0:T(8,128)S(1)}, u32[]{:S(2)}, u32[]{:S(2)}) collective-permute-start(f32[16,128]{1,0:T(8,128)S(1)} %get-tuple-element.15), channel_id=1, source_target_pairs={{0,12},{12,24},{24,36},{36,0},{1,13},{13,25},{25,37},{37,1},{2,14}... | collective-permute-start | bytes 24584 | tf_op jit(solution)/shard_map/ppermute | solution.py:398
  204.8 7.4 %collective-permute-start.12 = (f32[16,128]{1,0:T(8,128)S(1)}, f32[16,128]{1,0:T(8,128)S(1)}, u32[]{:S(2)}, u32[]{:S(2)}) collective-permute-start(f32[16,128]{1,0:T(8,128)S(1)} %get-tuple-element.15), channel_id=1, source_target_pairs={{0,24},{12,36},{24,0},{36,12},{1,25},{13,37},{25,1},{37,13},{2,26}... | collective-permute-start | bytes 24584 | tf_op jit(solution)/shard_map/ppermute | solution.py:398
  208.1 4.8 %collective-permute-start.13 = (f32[16,128]{1,0:T(8,128)S(1)}, f32[16,128]{1,0:T(8,128)S(1)}, u32[]{:S(2)}, u32[]{:S(2)}) collective-permute-start(f32[16,128]{1,0:T(8,128)S(1)} %get-tuple-element.15), channel_id=1, source_target_pairs={{0,36},{12,0},{24,12},{36,24},{1,37},{13,1},{25,13},{37,25},{2,38}... | collective-permute-start | bytes 24584 | tf_op jit(solution)/shard_map/ppermute | solution.py:398
  212.9 16.2 %collective-permute-start.14 = (f32[4,16,128]{2,1,0:T(8,128)S(1)}, f32[4,16,128]{2,1,0:T(8,128)S(1)}, u32[]{:S(2)}, u32[]{:S(2)}) collective-permute-start(f32[4,16,128]{2,1,0:T(8,128)S(1)} %pad_maximum_fusion.1.refs_1_), channel_id=1, source_target_pairs={{0,192},{192,0},{384,576},{576,384},{1,193},{193,1},{385,577},{577... | collective-permute-start | bytes 98312 | tf_op jit(solution)/shard_map/ppermute | solution.py:403
  223.1 6.0 %collective-permute-start.15 = (f32[4,16,128]{2,1,0:T(8,128)S(1)}, f32[4,16,128]{2,1,0:T(8,128)S(1)}, u32[]{:S(2)}, u32[]{:S(2)}) collective-permute-start(f32[4,16,128]{2,1,0:T(8,128)S(1)} %pad_maximum_fusion.1.refs_1_), channel_id=1, source_target_pairs={{0,384},{192,576},{384,0},{576,192},{1,385},{193,577},{385,1},{577... | collective-permute-start | bytes 98312 | tf_op jit(solution)/shard_map/ppermute | solution.py:403
  225.6 5.2 %collective-permute-start.16 = (f32[4,16,128]{2,1,0:T(8,128)S(1)}, f32[4,16,128]{2,1,0:T(8,128)S(1)}, u32[]{:S(2)}, u32[]{:S(2)}) collective-permute-start(f32[4,16,128]{2,1,0:T(8,128)S(1)} %pad_maximum_fusion.1.refs_1_), channel_id=1, source_target_pairs={{0,576},{192,384},{384,192},{576,0},{1,577},{193,385},{385,193},{5... | collective-permute-start | bytes 98312 | tf_op jit(solution)/shard_map/ppermute | solution.py:403

commit v3 on v1

v3 whole, which is shorter than its diff:
```python
import math

import jax
import jax.numpy as jnp
from jax import lax
from jax.experimental import pallas as pl
from jax.experimental.pallas import tpu as pltpu
from jax.sharding import Mesh, PartitionSpec as P

row_split = (2, 2)
col_split = (4, 4, 12)
axis_names = ("ylo", "core", "yhi", "x", "z")
row_axes = ("ylo", "core")
col_axes = ("yhi", "x", "z")
team_axes = ("ylo", "core", "x")
ahead_rows = 80
back_rows = 96
group = 4
lanes = 128
vmem_bytes = 12 * 1024 * 1024
root_two_over_pi = math.sqrt(2.0 / math.pi)
cubic = 0.044715


def spread_out(value, axes, count):
    copies = jnp.broadcast_to(value[None], (count,) + value.shape)
    return lax.all_to_all(copies, axes, 0, 0, tiled=True)


def pick_tiles(codes, tile_refs, chosen, picked, slots, height, dummy):
    total = jnp.int32(0)
    for source, tiles in enumerate(tile_refs):

        def body(step, total, source=source, tiles=tiles):
            for sub in range(group):
                slot = step * group + sub
                code = codes[source, slot]
                top = pl.multiple_of(slot * height, height)
                chosen[total] = tiles[pl.ds(top, height), :]
                picked[total] = code
                total = total + jnp.where(code >= 0, 1, 0)
            return total

        total = lax.fori_loop(0, (codes[source, slots] + group - 1) // group, body, total)
    for sub in range(group):
        picked[total + sub] = dummy
    return total


def forward_kernel(codes, *refs, slots, height, blocks, far, across):
    lines, columns = refs[:far], refs[far]
    tile_refs = refs[far + 1 : far + 1 + across]
    out, slabs, chosen, totals, picked = refs[far + 1 + across :]
    slab_count, nodes = slabs.shape[:2]
    near = columns.shape[0]
    ahead = lines[0].shape[0] // near
    rest = nodes - ahead
    for shift in range(far):
        for index in range(near):
            slab = shift * near + index
            slabs[slab, pl.ds(0, ahead), :] = lines[shift][pl.ds(index * ahead, ahead), :]
            slabs[slab, pl.ds(ahead, rest), :] = columns[index, pl.ds(shift * rest, rest), :]
    dummy = slab_count * 64 + blocks
    totals[...] = jnp.zeros_like(totals)
    total = pick_tiles(codes, tile_refs, chosen, picked, slots, height, dummy)

    def body(step, carry):
        products = []
        for sub in range(group):
            code = picked[step * group + sub]
            slab = jnp.minimum(code >> 6, slab_count - 1)
            product = jnp.dot(
                chosen[step * group + sub], slabs[slab], preferred_element_type=jnp.float32
            )
            products.append((code & 63, product))
        for block, product in products:
            totals[block] += product
        return carry

    lax.fori_loop(0, (total + group - 1) // group, body, 0)
    halves = out.shape[1] // height
    for block in range(blocks):
        out[block // halves, pl.ds((block % halves) * height, height), :] = totals[block].astype(
            jnp.bfloat16
        )


def split_wide(value):
    high = value.astype(jnp.bfloat16).astype(jnp.float32)
    return high, value - high


def bias_rows(pieces):
    rows = lax.broadcasted_iota(jnp.int32, (16, lanes), 0)
    block = jnp.zeros((16, lanes), jnp.float32)
    for index, piece in enumerate(pieces):
        block = jnp.where(rows == index, jnp.broadcast_to(piece, (16, lanes)), block)
    return block


def sum_rows(ref, start, size):
    value = ref[0, pl.ds(start, size), :].astype(jnp.float32)
    for index in range(1, ref.shape[0]):
        value = value + ref[index, pl.ds(start, size), :].astype(jnp.float32)
    return value


def dense_kernel(partials, weight, bias, cotangent, hidden, message):
    members = partials.shape[0]
    nodes = partials.shape[1]
    aggregate = sum_rows(partials, 0, nodes)
    weight_wide = weight[...].astype(jnp.float32)
    pre = (
        jnp.dot(
            aggregate,
            weight_wide,
            precision=lax.Precision.HIGHEST,
            preferred_element_type=jnp.float32,
        )
        + bias[...]
    )
    square = pre * pre
    angle = jnp.tanh(root_two_over_pi * (pre + cubic * (square * pre)))
    gate = 0.5 * (1.0 + angle)
    hidden[...] = (pre * gate).astype(jnp.bfloat16)
    inner = root_two_over_pi * (1.0 + 3.0 * cubic * square)
    gradient = gate + 0.5 * pre * (1.0 - angle * angle) * inner
    slope = (cotangent[...].astype(jnp.float32) * gradient).astype(jnp.bfloat16)
    slope_wide = slope.astype(jnp.float32)
    spread = lax.dot_general(
        slope, weight[...], (((1,), (1,)), ((), ())), preferred_element_type=jnp.float32
    ).astype(jnp.bfloat16)
    weight_part = lax.dot_general(
        aggregate,
        slope_wide,
        (((0,), (0,)), ((), ())),
        precision=lax.Precision.HIGHEST,
        preferred_element_type=jnp.float32,
    )
    bias_part = jnp.sum(slope_wide, axis=0, keepdims=True)
    high, low = split_wide(bias_part)
    bias_block = bias_rows([high[:, :lanes], high[:, lanes:], low[:, :lanes], low[:, lanes:]])
    bias_block = bias_block.astype(jnp.bfloat16)
    share = weight_part.shape[0] // members
    for member in range(members):
        message[member, pl.ds(0, nodes), :] = spread
        part = weight_part[member * share : (member + 1) * share]
        part = jnp.concatenate([part[:, :lanes], part[:, lanes:]], axis=0)
        high, low = split_wide(part)
        message[member, pl.ds(nodes, 2 * share), :] = high.astype(jnp.bfloat16)
        message[member, pl.ds(nodes + 2 * share, 2 * share), :] = low.astype(jnp.bfloat16)
        message[member, pl.ds(nodes + 4 * share, 16), :] = bias_block


def sum_bias(ref, start):
    block = sum_rows(ref, start, 16)
    return [block[0:1] + block[2:3], block[1:2] + block[3:4]]


def pack_bias(values):
    parts = [split_wide(value) for value in values]
    return bias_rows([parts[0][0], parts[1][0], parts[0][1], parts[1][1]]).astype(jnp.bfloat16)


def backward_kernel(codes, spreads, *refs, slots, height, blocks, nodes, share, far, across):
    tile_refs, outs = refs[:across], refs[across : across + far]
    columns, chosen, totals, picked = refs[across + far :]
    slab_count = totals.shape[0] - 1
    halves = nodes // height
    dummy = slab_count * 64 + blocks
    totals[...] = jnp.zeros_like(totals)
    total = pick_tiles(codes, tile_refs, chosen, picked, slots, height, dummy)

    def body(step, carry):
        products = []
        for sub in range(group):
            code = picked[step * group + sub]
            block = jnp.minimum(code & 63, blocks - 1)
            top = pl.multiple_of((block % halves) * height, height)
            product = lax.dot_general(
                chosen[step * group + sub],
                spreads[block // halves, pl.ds(top, height), :],
                (((0,), (0,)), ((), ())),
                preferred_element_type=jnp.float32,
            )
            products.append((code >> 6, product))
        for slab, product in products:
            totals[slab] += product
        return carry

    lax.fori_loop(0, (total + group - 1) // group, body, 0)
    near = slab_count // far
    ahead = outs[0].shape[0] // near
    rest = nodes - ahead
    for shift in range(far):
        for index in range(near):
            total = totals[shift * near + index].astype(jnp.bfloat16)
            outs[shift][pl.ds(index * ahead, ahead), :] = total[:ahead]
            columns[index, pl.ds(shift * rest, rest), :] = total[ahead:]
    weight_sum = sum_rows(spreads, nodes, 2 * share) + sum_rows(spreads, nodes + 2 * share, 2 * share)
    weight_sum = weight_sum.astype(jnp.bfloat16)
    bias_block = pack_bias(sum_bias(spreads, nodes + 4 * share))
    for index in range(near):
        columns[index, pl.ds(far * rest, 2 * share), :] = weight_sum
        columns[index, pl.ds(far * rest + 2 * share, 16), :] = bias_block


def middle_kernel(arrived, *refs, share, far):
    lines, outs, line = refs[:far], refs[far : 2 * far], refs[2 * far]
    near, ahead = line.shape[:2]
    rest = outs[0].shape[0] - 4 * share - 16
    for index in range(near):
        total = lines[0][pl.ds(index * ahead, ahead), :].astype(jnp.float32)
        for other in lines[1:]:
            total = total + other[pl.ds(index * ahead, ahead), :].astype(jnp.float32)
        line[index] = total.astype(jnp.bfloat16)
    high, low = split_wide(sum_rows(arrived, far * rest, 2 * share))
    bias_block = pack_bias(sum_bias(arrived, far * rest + 2 * share))
    for shift, out in enumerate(outs):
        out[pl.ds(0, rest), :] = sum_rows(arrived, shift * rest, rest).astype(jnp.bfloat16)
        out[pl.ds(rest, 2 * share), :] = high.astype(jnp.bfloat16)
        out[pl.ds(rest + 2 * share, 2 * share), :] = low.astype(jnp.bfloat16)
        out[pl.ds(rest + 4 * share, 16), :] = bias_block


def last_kernel(place, arrived, *refs, share, far, factor):
    pieces = refs[:far]
    grad, weight_share, bias_grad, stack = refs[far:]
    ahead = arrived.shape[1]
    rest = grad.shape[0] - ahead
    grad[pl.ds(0, ahead), :] = sum_rows(arrived, 0, ahead)
    for shift, piece in enumerate(pieces):
        stack[lax.rem(place[0] + shift, far)] = piece[...]
    grad[pl.ds(ahead, rest), :] = sum_rows(stack, 0, rest)
    weight_sum = sum_rows(stack, rest, 2 * share) + sum_rows(stack, rest + 2 * share, 2 * share)
    weight_share[...] = weight_sum * factor
    low, high = sum_bias(stack, rest + 4 * share)
    bias_grad[:, pl.ds(0, lanes)] = low * factor
    bias_grad[:, pl.ds(lanes, lanes)] = high * factor


def copies_kernel(*refs, count):
    out = refs[-1]
    rows = refs[0].shape[0]
    for index in range(out.shape[0]):
        for shift in range(count):
            out[index, pl.ds(shift * rows, rows), :] = refs[shift][...]


def in_vmem():
    return pl.BlockSpec(memory_space=pltpu.VMEM)


def in_smem():
    return pl.BlockSpec(memory_space=pltpu.SMEM)


def local(features, tile_rows, tile_cols, tile_counts, tile_values, weight, bias, cotangent):
    nodes, width = features.shape
    slots, height, tile_width = tile_values.shape[2:]
    hidden = weight.shape[1]
    far = lax.axis_size("yhi")
    across = lax.axis_size("x")
    near = lax.axis_size("z")
    members = lax.axis_size(team_axes)
    group_rows = lax.axis_size(row_axes)
    here = lax.axis_index("x")
    params = pltpu.CompilerParams(vmem_limit_bytes=vmem_bytes)
    halves = nodes // height
    blocks = members * halves

    def any_place():
        return pl.BlockSpec(memory_space=pl.ANY)

    live = jnp.arange(slots, dtype=jnp.int32) < tile_counts[0, 0]
    columns, rows = tile_cols[0, 0], tile_rows[0, 0]
    owner = jnp.where(live, (columns // near) % across, 255)
    distance = (lax.axis_index("yhi") - columns // (across * near)) % far
    slab = distance * near + columns % near
    block = ((rows // halves) * across + here) * halves + rows % halves
    places = jnp.stack([owner, slab, block])
    ends = jnp.stack([jnp.int32(254), jnp.int32(0), tile_counts[0, 0]])[:, None]
    places = jnp.concatenate([places, ends], axis=1)
    places = jnp.pad(places, ((0, 13), (0, lanes - slots - 1))).astype(jnp.bfloat16)
    own = jnp.concatenate([tile_values[0, 0].reshape(slots * height, tile_width), places], axis=0)

    def ring(size, shift):
        return [(start, (start + shift) % size) for start in range(size)]

    buffers = [own, lax.ppermute(own, "x", ring(across, 1))]
    if across > 2:
        buffers.append(lax.ppermute(own, "x", ring(across, -1)))
    early = buffers[1:]
    for shift in range(2, across - 1):
        buffers.append(lax.ppermute(buffers[1 if shift == 2 else -1], "x", ring(across, 1)))

    columns = [features[ahead_rows:]]
    for shift in range(1, far):
        columns.append(lax.ppermute(columns[0], "yhi", ring(far, shift)))
    lines = [spread_out(features[:ahead_rows], "z", near).reshape(near * ahead_rows, width)]
    copies = pl.pallas_call(
        lambda *refs: copies_kernel(*refs, count=far),
        out_shape=jax.ShapeDtypeStruct((near, far * (nodes - ahead_rows), width), jnp.bfloat16),
        in_specs=[in_vmem()] * far + [any_place()] * (1 + len(early)),
        out_specs=in_vmem(),
        compiler_params=params,
        name="column_copies",
    )(*columns, lines[0], *early)
    for shift in range(1, far):
        lines.append(lax.ppermute(lines[0], "yhi", ring(far, shift)))
    columns = lax.all_to_all(copies, "z", 0, 0, tiled=True)

    tables = []
    for buffer in buffers:
        top = buffer[slots * height :].astype(jnp.int32)
        mine = (top[0] == here) | (top[0] == 254)
        tables.append(jnp.where(mine, top[1] * 64 + top[2], -1))
    codes = jnp.stack(tables)

    scratch_tiles = pltpu.VMEM((across * slots + group, height, tile_width), jnp.bfloat16)
    scratch_list = pltpu.SMEM((across * slots + group,), jnp.int32)
    partial = pl.pallas_call(
        lambda *refs: forward_kernel(*refs, slots=slots, height=height, blocks=blocks, far=far, across=across),
        out_shape=jax.ShapeDtypeStruct((members, nodes, width), jnp.bfloat16),
        in_specs=[in_smem()] + [in_vmem()] * (far + 1 + across),
        out_specs=in_vmem(),
        scratch_shapes=[
            pltpu.VMEM((far * near, nodes, width), jnp.bfloat16),
            scratch_tiles,
            pltpu.VMEM((blocks + 1, height, width), jnp.float32),
            scratch_list,
        ],
        compiler_params=params,
        name="forward_tiles",
    )(codes, *lines, columns, *buffers)
    partials = lax.all_to_all(partial, team_axes, 0, 0, tiled=True)

    share = width // members
    hidden_out, message = pl.pallas_call(
        dense_kernel,
        out_shape=(
            jax.ShapeDtypeStruct((nodes, hidden), jnp.bfloat16),
            jax.ShapeDtypeStruct((members, nodes + 4 * share + 16, width), jnp.bfloat16),
        ),
        in_specs=[in_vmem()] * 4,
        out_specs=(in_vmem(), in_vmem()),
        compiler_params=params,
        name="dense_layer",
    )(partials, weight, bias.reshape(1, hidden), cotangent)
    spreads = lax.all_to_all(message, team_axes, 0, 0, tiled=True)

    rest = nodes - back_rows
    shared_rows = 2 * share + 16
    outs = pl.pallas_call(
        lambda *refs: backward_kernel(
            *refs,
            slots=slots,
            height=height,
            blocks=blocks,
            nodes=nodes,
            share=share,
            far=far,
            across=across,
        ),
        out_shape=(jax.ShapeDtypeStruct((near * back_rows, width), jnp.bfloat16),) * far
        + (jax.ShapeDtypeStruct((near, far * rest + shared_rows, width), jnp.bfloat16),),
        in_specs=[in_smem(), in_vmem()] + [in_vmem()] * across,
        out_specs=(in_vmem(),) * (far + 1),
        scratch_shapes=[
            scratch_tiles,
            pltpu.VMEM((far * near + 1, nodes, width), jnp.float32),
            scratch_list,
        ],
        compiler_params=params,
        name="backward_tiles",
    )(codes, spreads, *buffers)

    lines = [outs[0]]
    for shift in range(1, far):
        lines.append(lax.ppermute(outs[shift], "yhi", ring(far, -shift)))
    arrived = lax.all_to_all(outs[far], "z", 0, 0, tiled=True)
    outs = pl.pallas_call(
        lambda *refs: middle_kernel(*refs, share=share, far=far),
        out_shape=(jax.ShapeDtypeStruct((rest + 2 * share + shared_rows, width), jnp.bfloat16),) * far
        + (jax.ShapeDtypeStruct((near, back_rows, width), jnp.bfloat16),),
        in_specs=[in_vmem()] * (far + 1),
        out_specs=(in_vmem(),) * (far + 1),
        compiler_params=params,
        name="middle_sums",
    )(arrived, *lines)
    pieces = [outs[0]]
    for shift in range(1, far):
        pieces.append(lax.ppermute(outs[shift], "yhi", ring(far, -shift)))
    arrived = lax.all_to_all(outs[far], "z", 0, 0, tiled=True)
    factor = 1.0 / math.sqrt(nodes * group_rows * far * across * near)
    features_grad, weight_share, bias_grad = pl.pallas_call(
        lambda *refs: last_kernel(*refs, share=share, far=far, factor=factor),
        out_shape=(
            jax.ShapeDtypeStruct((nodes, width), jnp.float32),
            jax.ShapeDtypeStruct((2 * share, lanes), jnp.float32),
            jax.ShapeDtypeStruct((1, hidden), jnp.float32),
        ),
        in_specs=[in_smem()] + [in_vmem()] * (far + 1),
        out_specs=(in_vmem(), in_vmem(), in_vmem()),
        scratch_shapes=[pltpu.VMEM((far,) + pieces[0].shape, jnp.bfloat16)],
        compiler_params=params,
        name="last_sums",
    )(lax.axis_index("yhi").reshape(1), arrived, *pieces)
    shares = spread_out(weight_share, team_axes, members)
    weight_grad = shares.reshape(members, 2, share, lanes).transpose(0, 2, 1, 3)
    weight_grad = weight_grad.reshape(width, hidden)
    return (hidden_out, features_grad, weight_grad, bias_grad.reshape(hidden))


def solution(mesh):
    fine = Mesh(mesh.devices.reshape(row_split + col_split), axis_names)
    nodes_spec = P(row_axes + col_axes, None)
    in_specs = (
        nodes_spec,
        P(row_axes, col_axes, None),
        P(row_axes, col_axes, None),
        P(row_axes, col_axes),
        P(row_axes, col_axes, None, None, None),
        P(),
        P(),
        nodes_spec,
    )
    out_specs = (nodes_spec, nodes_spec, P(), P())
    return jax.shard_map(local, mesh=fine, in_specs=in_specs, out_specs=out_specs, check_vma=False)
```

time: 219 us -> 216 us (0.986)
  starting transfers between devices: 32 us -> 99.9 us
  blocking collectives: 119 us -> 54.8 us
  waiting for transfers between devices: 51.5 us -> 39.1 us
  local copies, waits for them, and re-layouts: 5.89 us -> 10.1 us
    all_to_all x2 -> x0, blocking collectives: 71.3 us -> none  [the longest x1 45.4 us: local(): arrived = lax.all_to_all(column_part, 'yhi', 0, 0, tiled=True)]
    ppermute x3 -> x15, starting transfers between devices: 9.33 us -> 57.1 us  [the longest x3 13.6 us: local(): columns.append(lax.ppermute(columns[0], 'yhi', ring(far, shift)))]
    all_to_all x0 -> x3, starting transfers between devices: none -> 27.9 us  [the longest x2 18.8 us: local(): arrived = lax.all_to_all(outs[far], 'z', 0, 0, tiled=True)]
    all_to_all x2 -> x1, waiting for transfers between devices: 17.3 us -> 0.01 us  [spread_out(): return lax.all_to_all(copies, axes, 0, 0, tiled=True)]
    unnamed x9 -> x37, local copies, waits for them, and re-layouts: 0.68 us -> 9.25 us
    all_to_all x2 -> x1, starting transfers between devices: 22.6 us -> 14.9 us  [spread_out(): return lax.all_to_all(copies, axes, 0, 0, tiled=True)]
    all_to_all x1, blocking collectives: 12.4 us -> 20.1 us  [spread_out(): return lax.all_to_all(copies, axes, 0, 0, tiled=True)]
    ppermute x3 -> x15, waiting for transfers between devices: 34.2 us -> 39.1 us  [the longest x3 17.7 us: local(): lines.append(lax.ppermute(outs[shift], 'yhi', ring(far, -shift)))]
  transfers between devices with their start and end apart: 5 -> 19, of which waited for: 4 -> 7; matrix products, arithmetic and copies ran while one was open for 1% -> 0% of each run, Pallas kernels for 0% -> 0%
where the time goes in v3:
time: 216 us; the launch traced here: 215 us
  starting transfers between devices  99.9 us (46%)
  blocking collectives  54.8 us (25%)
  waiting for transfers between devices  39.1 us (18%)
  local copies, waits for them, and re-layouts  10.1 us (5%)
  Pallas kernels  7.03 us (3%)
    all_to_all x1, blocking collectives, spread_out(): return lax.all_to_all(copies, axes, 0, 0, tiled=True)  20.1 us
    all_to_all x1, blocking collectives, local(): partials = lax.all_to_all(partial, team_axes, 0, 0, tiled=True)  18.9 us
    all_to_all x2, starting transfers between devices, local(): arrived = lax.all_to_all(outs[far], 'z', 0, 0, tiled=True)  18.8 us
    ppermute x3, waiting for transfers between devices, local(): lines.append(lax.ppermute(outs[shift], 'yhi', ring(far, -shift)))  17.7 us
    all_to_all x1, blocking collectives, local(): spreads = lax.all_to_all(message, team_axes, 0, 0, tiled=True)  15.8 us
    ppermute x1, waiting for transfers between devices, local(): lax.ppermute(buffers[1 if shift == 2 else -1], 'x', ring(across, 1))  15.7 us
    all_to_all x1, starting transfers between devices, spread_out(): return lax.all_to_all(copies, axes, 0, 0, tiled=True)  14.9 us
    ppermute x3, starting transfers between devices, local(): columns.append(lax.ppermute(columns[0], 'yhi', ring(far, shift)))  13.6 us
  transfers between devices with their start and end apart: 19, of which 7 were waited for; matrix products, arithmetic and copies ran while one was open for 0% of the time, Pallas kernels for 0%

profile of v3, /device:TPU:1, one launch (start us, length us, event | category | flops | bytes accessed | tf_op | source)
XLA Modules:
  0.0 214.6 jit_solution(4137297870852702644)
XLA Ops:
  2.3 1.2 pad_maximum_fusion.refs_6_.refs_2_
  3.5 5.2 %collective-permute-start.1 = (bf16[3088,128]{1,0:T(8,128)(2,1)S(1)}, bf16[3088,128]{1,0:T(8,128)(2,1)S(1)}, u32[]{:S(2)}, u32[]{:S(2)}) collective-permute-start(bf16[3088,128]{1,0:T(8,128)(2,1)S(1)} %pad_maximum_fusion.refs_6_.refs_2_), channel_id=1, source_target_pairs={{0,36},{12,0},{24,12},{36,24},{1,37},{13,1},{25,13},{37,25},{2,38}... | collective-permute-start | bytes 2371592 | tf_op jit(solution)/shard_map/ppermute | solution.py:292
  8.7 1.9 collective-permute-start
  11.4 14.9 %all-to-all-start = ((bf16[12,80,128]{2,1,0:T(8,128)(2,1)}), bf16[12,80,128]{2,1,0:T(8,128)(2,1)S(1)}, u32[]{:S(2)}, u32[]{:S(2)}) async-start(bf16[12,80,128]{2,1,0:T(8,128)(2,1)} %broadcast_in_dim.30), calls=%async_computation | async-start | bytes 491520 | tf_op jit(solution)/shard_map/all_to_all | solution.py:27
  26.3 5.9 %collective-permute-start.8 = (bf16[48,128]{1,0:T(8,128)(2,1)S(1)}, bf16[48,128]{1,0:T(8,128)(2,1)S(1)}, u32[]{:S(2)}, u32[]{:S(2)}) collective-permute-start(bf16[48,128]{1,0:T(8,128)(2,1)S(1)} %slice.71.refs_0_), channel_id=1, source_target_pairs={{0,144},{48,0},{96,48},{144,96},{1,145},{49,1},{97,49},{145,97},{2... | collective-permute-start | bytes 36872 | tf_op jit(solution)/shard_map/ppermute | solution.py:299
  32.2 3.5 %collective-permute-start.7 = (bf16[48,128]{1,0:T(8,128)(2,1)S(1)}, bf16[48,128]{1,0:T(8,128)(2,1)S(1)}, u32[]{:S(2)}, u32[]{:S(2)}) collective-permute-start(bf16[48,128]{1,0:T(8,128)(2,1)S(1)} %slice.71.refs_0_), channel_id=1, source_target_pairs={{0,96},{48,144},{96,0},{144,48},{1,97},{49,145},{97,1},{145,49},{2... | collective-permute-start | bytes 36872 | tf_op jit(solution)/shard_map/ppermute | solution.py:299
  35.7 4.2 %collective-permute-start.6 = (bf16[48,128]{1,0:T(8,128)(2,1)S(1)}, bf16[48,128]{1,0:T(8,128)(2,1)S(1)}, u32[]{:S(2)}, u32[]{:S(2)}) collective-permute-start(bf16[48,128]{1,0:T(8,128)(2,1)S(1)} %slice.71.refs_0_), channel_id=1, source_target_pairs={{0,48},{48,96},{96,144},{144,0},{1,49},{49,97},{97,145},{145,1},{2... | collective-permute-start | bytes 36872 | tf_op jit(solution)/shard_map/ppermute | solution.py:299
  40.8 1.7 collective-permute-done.6.refs_1_
  43.5 9.1 %all-to-all-start.1 = ((bf16[12,192,128]{2,1,0:T(8,128)(2,1)}), bf16[12,192,128]{2,1,0:T(8,128)(2,1)}, u32[]{:S(2)}, u32[]{:S(2)}) async-start(bf16[12,192,128]{2,1,0:T(8,128)(2,1)} %column_copies.1), calls=%async_computation.1 | async-start | bytes 1179648 | tf_op jit(solution)/shard_map/all_to_all | solution.py:311
  52.5 2.1 collective-permute-start.5
  54.6 5.8 %collective-permute-start.4 = (bf16[960,128]{1,0:T(8,128)(2,1)S(1)}, bf16[960,128]{1,0:T(8,128)(2,1)S(1)}, u32[]{:S(2)}, u32[]{:S(2)}) collective-permute-start(bf16[960,128]{1,0:T(8,128)(2,1)S(1)} %bitcast.68), channel_id=1, source_target_pairs={{0,96},{48,144},{96,0},{144,48},{1,97},{49,145},{97,1},{145,49},{2... | collective-permute-start | bytes 737288 | tf_op jit(solution)/shard_map/ppermute | solution.py:310
  60.5 3.6 %collective-permute-start.3 = (bf16[960,128]{1,0:T(8,128)(2,1)S(1)}, bf16[960,128]{1,0:T(8,128)(2,1)S(1)}, u32[]{:S(2)}, u32[]{:S(2)}) collective-permute-start(bf16[960,128]{1,0:T(8,128)(2,1)S(1)} %bitcast.69), channel_id=1, source_target_pairs={{0,48},{48,96},{96,144},{144,0},{1,49},{49,97},{97,145},{145,1},{2... | collective-permute-start | bytes 737288 | tf_op jit(solution)/shard_map/ppermute | solution.py:310
  64.1 2.1 collective-permute-start.2
  66.3 15.7 %collective-permute-done.2.refs_9_.refs_5_ = bf16[3088,128]{1,0:T(8,128)(2,1)S(1)} collective-permute-done((bf16[3088,128]{1,0:T(8,128)(2,1)S(1)}, bf16[3088,128]{1,0:T(8,128)(2,1)S(1)}, u32[]{:S(2)}, u32[]{:S(2)}) %collective-permute-start.2) | collective-permute-done | bytes 790560 | tf_op jit(solution)/shard_map/ppermute | solution.py:295
  87.0 1.9 forward_tiles.1
  88.9 18.9 %all_to_all.35.partials = bf16[16,128,128]{2,1,0:T(8,128)(2,1)S(1)} all-to-all(bf16[16,128,128]{2,1,0:T(8,128)(2,1)S(1)} %forward_tiles.1), channel_id=1, replica_groups=mesh['ylo'=2,'core'=2,'yhi'=4,'x'=4,'z'=12] {'ylo','core','x'}, dimensions={0} | all-to-all | bytes 1048576 | tf_op jit(solution)/shard_map/all_to_all | solution.py:336
  107.8 1.1 dense_layer.1
  108.9 15.8 %all_to_all.36.refs_1_ = bf16[16,176,128]{2,1,0:T(8,128)(2,1)S(1)} all-to-all(bf16[16,176,128]{2,1,0:T(8,128)(2,1)S(1)} %get-tuple-element.20), channel_id=1, replica_groups=mesh['ylo'=2,'core'=2,'yhi'=4,'x'=4,'z'=12] {'ylo','core','x'}, dimensions={0} | all-to-all | bytes 1441792 | tf_op jit(solution)/shard_map/all_to_all | solution.py:350
  124.6 1.6 backward_tiles.1
  129.9 10.1 %all-to-all-start.4 = ((bf16[12,160,128]{2,1,0:T(8,128)(2,1)}), bf16[12,160,128]{2,1,0:T(8,128)(2,1)S(1)}, u32[]{:S(2)}, u32[]{:S(2)}) async-start(bf16[12,160,128]{2,1,0:T(8,128)(2,1)} %copy-done), calls=%async_computation.4 | async-start | bytes 983040 | tf_op jit(solution)/shard_map/all_to_all | solution.py:381
  140.0 4.0 %collective-permute-start.9 = (bf16[1152,128]{1,0:T(8,128)(2,1)}, bf16[1152,128]{1,0:T(8,128)(2,1)S(1)}, u32[]{:S(2)}, u32[]{:S(2)}) collective-permute-start(bf16[1152,128]{1,0:T(8,128)(2,1)} %copy-done.16), channel_id=1, source_target_pairs={{0,144},{48,0},{96,48},{144,96},{1,145},{49,1},{97,49},{145,97},{2... | collective-permute-start | bytes 884744 | tf_op jit(solution)/shard_map/ppermute | solution.py:380
  144.1 3.5 %collective-permute-start.10 = (bf16[1152,128]{1,0:T(8,128)(2,1)S(1)}, bf16[1152,128]{1,0:T(8,128)(2,1)S(1)}, u32[]{:S(2)}, u32[]{:S(2)}) collective-permute-start(bf16[1152,128]{1,0:T(8,128)(2,1)S(1)} %copy-done.15), channel_id=1, source_target_pairs={{0,96},{48,144},{96,0},{144,48},{1,97},{49,145},{97,1},{145,49},{2... | collective-permute-start | bytes 884744 | tf_op jit(solution)/shard_map/ppermute | solution.py:380
  147.6 3.5 %collective-permute-start.11 = (bf16[1152,128]{1,0:T(8,128)(2,1)S(1)}, bf16[1152,128]{1,0:T(8,128)(2,1)S(1)}, u32[]{:S(2)}, u32[]{:S(2)}) collective-permute-start(bf16[1152,128]{1,0:T(8,128)(2,1)S(1)} %copy-done.13), channel_id=1, source_target_pairs={{0,48},{48,96},{96,144},{144,0},{1,49},{49,97},{97,145},{145,1},{2... | collective-permute-start | bytes 884744 | tf_op jit(solution)/shard_map/ppermute | solution.py:380
  151.1 15.5 %collective-permute-done.9.refs_2_ = bf16[1152,128]{1,0:T(8,128)(2,1)S(1)} collective-permute-done((bf16[1152,128]{1,0:T(8,128)(2,1)}, bf16[1152,128]{1,0:T(8,128)(2,1)S(1)}, u32[]{:S(2)}, u32[]{:S(2)}) %collective-permute-start.9) | collective-permute-done | bytes 294944 | tf_op jit(solution)/shard_map/ppermute | solution.py:380
  166.6 2.2 %collective-permute-done.11.refs_4_ = bf16[1152,128]{1,0:T(8,128)(2,1)S(1)} collective-permute-done((bf16[1152,128]{1,0:T(8,128)(2,1)S(1)}, bf16[1152,128]{1,0:T(8,128)(2,1)S(1)}, u32[]{:S(2)}, u32[]{:S(2)}) %collective-permute-start.11) | collective-permute-done | bytes 294944 | tf_op jit(solution)/shard_map/ppermute | solution.py:380
  169.7 8.7 %all-to-all-start.5 = ((bf16[12,96,128]{2,1,0:T(8,128)(2,1)}), bf16[12,96,128]{2,1,0:T(8,128)(2,1)S(1)}, u32[]{:S(2)}, u32[]{:S(2)}) async-start(bf16[12,96,128]{2,1,0:T(8,128)(2,1)} %get-tuple-element.26), calls=%async_computation.5 | async-start | bytes 589824 | tf_op jit(solution)/shard_map/all_to_all | solution.py:394
  178.4 4.3 %collective-permute-start.12 = (bf16[80,128]{1,0:T(8,128)(2,1)S(1)}, bf16[80,128]{1,0:T(8,128)(2,1)S(1)}, u32[]{:S(2)}, u32[]{:S(2)}) collective-permute-start(bf16[80,128]{1,0:T(8,128)(2,1)S(1)} %get-tuple-element.28), channel_id=1, source_target_pairs={{0,144},{48,0},{96,48},{144,96},{1,145},{49,1},{97,49},{145,97},{2... | collective-permute-start | bytes 61448 | tf_op jit(solution)/shard_map/ppermute | solution.py:393
  182.7 3.5 %collective-permute-start.13 = (bf16[80,128]{1,0:T(8,128)(2,1)S(1)}, bf16[80,128]{1,0:T(8,128)(2,1)S(1)}, u32[]{:S(2)}, u32[]{:S(2)}) collective-permute-start(bf16[80,128]{1,0:T(8,128)(2,1)S(1)} %get-tuple-element.29), channel_id=1, source_target_pairs={{0,96},{48,144},{96,0},{144,48},{1,97},{49,145},{97,1},{145,49},{2... | collective-permute-start | bytes 61448 | tf_op jit(solution)/shard_map/ppermute | solution.py:393
  186.2 3.9 %collective-permute-start.14 = (bf16[80,128]{1,0:T(8,128)(2,1)S(1)}, bf16[80,128]{1,0:T(8,128)(2,1)S(1)}, u32[]{:S(2)}, u32[]{:S(2)}) collective-permute-start(bf16[80,128]{1,0:T(8,128)(2,1)S(1)} %get-tuple-element.30), channel_id=1, source_target_pairs={{0,48},{48,96},{96,144},{144,0},{1,49},{49,97},{97,145},{145,1},{2... | collective-permute-start | bytes 61448 | tf_op jit(solution)/shard_map/ppermute | solution.py:393
  190.1 1.1 collective-permute-done.13.refs_4_
  191.2 1.9 collective-permute-done.14.refs_5_
  193.8 20.1 %all_to_all.37 = f32[16,16,128]{2,1,0:T(8,128)S(1)} all-to-all(f32[16,16,128]{2,1,0:T(8,128)S(1)} %broadcast_in_dim.31), channel_id=1, replica_groups=mesh['ylo'=2,'core'=2,'yhi'=4,'x'=4,'z'=12] {'ylo','core','x'}, dimensions={0} | all-to-all | bytes 262144 | tf_op jit(solution)/shard_map/all_to_all | solution.py:27
  (70 shorter events, 14.4 us)
Async XLA Ops:
  2.3 8.4 %slice-start = ((bf16[128,128]{1,0:T(8,128)(2,1)}), bf16[80,128]{1,0:T(8,128)(2,1)S(1)}, s32[]{:S(2)}) async-start(bf16[128,128]{1,0:T(8,128)(2,1)} %param.8), calls=%async_computation.7 | async-start | bytes 40960 | tf_op jit(solution)/shard_map/slice | solution.py:300
  3.5 22.8 %copy-start.17 = (bf16[128,128]{1,0:T(8,128)(2,1)S(1)}, bf16[128,128]{1,0:T(8,128)(2,1)}, u32[]{:S(2)}) copy-start(bf16[128,128]{1,0:T(8,128)(2,1)} %param.8) | copy-start | bytes 98308
  3.5 39.1 %collective-permute-start.1 = (bf16[3088,128]{1,0:T(8,128)(2,1)S(1)}, bf16[3088,128]{1,0:T(8,128)(2,1)S(1)}, u32[]{:S(2)}, u32[]{:S(2)}) collective-permute-start(bf16[3088,128]{1,0:T(8,128)(2,1)S(1)} %pad_maximum_fusion.refs_6_.refs_2_), channel_id=1, source_target_pairs={{0,36},{12,0},{24,12},{36,24},{1,37},{13,1},{25,13},{37,25},{2,38}... | collective-permute-start | bytes 2371592 | tf_op jit(solution)/shard_map/ppermute | solution.py:292
  8.7 33.9 %collective-permute-start = (bf16[3088,128]{1,0:T(8,128)(2,1)S(1)}, bf16[3088,128]{1,0:T(8,128)(2,1)S(1)}, u32[]{:S(2)}, u32[]{:S(2)}) collective-permute-start(bf16[3088,128]{1,0:T(8,128)(2,1)S(1)} %pad_maximum_fusion.refs_6_.refs_2_), channel_id=1, source_target_pairs={{0,12},{12,24},{24,36},{36,0},{1,13},{13,25},{25,37},{37,1},{2,14}... | collective-permute-start | bytes 2371592 | tf_op jit(solution)/shard_map/ppermute | solution.py:290
  11.4 31.2 %all-to-all-start = ((bf16[12,80,128]{2,1,0:T(8,128)(2,1)}), bf16[12,80,128]{2,1,0:T(8,128)(2,1)S(1)}, u32[]{:S(2)}, u32[]{:S(2)}) async-start(bf16[12,80,128]{2,1,0:T(8,128)(2,1)} %broadcast_in_dim.30), calls=%async_computation | async-start | bytes 491520 | tf_op jit(solution)/shard_map/all_to_all | solution.py:27
  26.3 13.7 %collective-permute-start.8 = (bf16[48,128]{1,0:T(8,128)(2,1)S(1)}, bf16[48,128]{1,0:T(8,128)(2,1)S(1)}, u32[]{:S(2)}, u32[]{:S(2)}) collective-permute-start(bf16[48,128]{1,0:T(8,128)(2,1)S(1)} %slice.71.refs_0_), channel_id=1, source_target_pairs={{0,144},{48,0},{96,48},{144,96},{1,145},{49,1},{97,49},{145,97},{2... | collective-permute-start | bytes 36872 | tf_op jit(solution)/shard_map/ppermute | solution.py:299
  32.2 8.6 %collective-permute-start.7 = (bf16[48,128]{1,0:T(8,128)(2,1)S(1)}, bf16[48,128]{1,0:T(8,128)(2,1)S(1)}, u32[]{:S(2)}, u32[]{:S(2)}) collective-permute-start(bf16[48,128]{1,0:T(8,128)(2,1)S(1)} %slice.71.refs_0_), channel_id=1, source_target_pairs={{0,96},{48,144},{96,0},{144,48},{1,97},{49,145},{97,1},{145,49},{2... | collective-permute-start | bytes 36872 | tf_op jit(solution)/shard_map/ppermute | solution.py:299
  35.7 6.8 %collective-permute-start.6 = (bf16[48,128]{1,0:T(8,128)(2,1)S(1)}, bf16[48,128]{1,0:T(8,128)(2,1)S(1)}, u32[]{:S(2)}, u32[]{:S(2)}) collective-permute-start(bf16[48,128]{1,0:T(8,128)(2,1)S(1)} %slice.71.refs_0_), channel_id=1, source_target_pairs={{0,48},{48,96},{96,144},{144,0},{1,49},{49,97},{97,145},{145,1},{2... | collective-permute-start | bytes 36872 | tf_op jit(solution)/shard_map/ppermute | solution.py:299
  43.5 40.7 %all-to-all-start.1 = ((bf16[12,192,128]{2,1,0:T(8,128)(2,1)}), bf16[12,192,128]{2,1,0:T(8,128)(2,1)}, u32[]{:S(2)}, u32[]{:S(2)}) async-start(bf16[12,192,128]{2,1,0:T(8,128)(2,1)} %column_copies.1), calls=%async_computation.1 | async-start | bytes 1179648 | tf_op jit(solution)/shard_map/all_to_all | solution.py:311
  52.5 29.5 %collective-permute-start.5 = (bf16[960,128]{1,0:T(8,128)(2,1)S(1)}, bf16[960,128]{1,0:T(8,128)(2,1)S(1)}, u32[]{:S(2)}, u32[]{:S(2)}) collective-permute-start(bf16[960,128]{1,0:T(8,128)(2,1)S(1)} %bitcast.67), channel_id=1, source_target_pairs={{0,144},{48,0},{96,48},{144,96},{1,145},{49,1},{97,49},{145,97},{2... | collective-permute-start | bytes 737288 | tf_op jit(solution)/shard_map/ppermute | solution.py:310
  54.6 28.1 %collective-permute-start.4 = (bf16[960,128]{1,0:T(8,128)(2,1)S(1)}, bf16[960,128]{1,0:T(8,128)(2,1)S(1)}, u32[]{:S(2)}, u32[]{:S(2)}) collective-permute-start(bf16[960,128]{1,0:T(8,128)(2,1)S(1)} %bitcast.68), channel_id=1, source_target_pairs={{0,96},{48,144},{96,0},{144,48},{1,97},{49,145},{97,1},{145,49},{2... | collective-permute-start | bytes 737288 | tf_op jit(solution)/shard_map/ppermute | solution.py:310
  60.5 23.0 %collective-permute-start.3 = (bf16[960,128]{1,0:T(8,128)(2,1)S(1)}, bf16[960,128]{1,0:T(8,128)(2,1)S(1)}, u32[]{:S(2)}, u32[]{:S(2)}) collective-permute-start(bf16[960,128]{1,0:T(8,128)(2,1)S(1)} %bitcast.69), channel_id=1, source_target_pairs={{0,48},{48,96},{96,144},{144,0},{1,49},{49,97},{97,145},{145,1},{2... | collective-permute-start | bytes 737288 | tf_op jit(solution)/shard_map/ppermute | solution.py:310
  64.1 17.9 %collective-permute-start.2 = (bf16[3088,128]{1,0:T(8,128)(2,1)S(1)}, bf16[3088,128]{1,0:T(8,128)(2,1)S(1)}, u32[]{:S(2)}, u32[]{:S(2)}) collective-permute-start(bf16[3088,128]{1,0:T(8,128)(2,1)S(1)} %collective-permute-done.refs_5_.refs_7_.refs_3_), channel_id=1, source_target_pairs={{0,12},{12,24},{24,36},{36,0},{1,13},{13,25},{25,37},{37,1},{2,14}... | collective-permute-start | bytes 2371592 | tf_op jit(solution)/shard_map/ppermute | solution.py:295
  84.1 0.9 copy-start.4
  85.1 0.9 copy-start.6
  86.0 0.9 copy-start.8
  88.8 18.9 %copy-start.9 = (bf16[128,256]{1,0:T(8,128)(2,1)S(1)}, bf16[128,256]{1,0:T(8,128)(2,1)}, u32[]{:S(2)}) copy-start(bf16[128,256]{1,0:T(8,128)(2,1)} %weight.1) | copy-start | bytes 196612
  88.8 18.9 %copy-start.10 = (bf16[128,256]{1,0:T(8,128)(2,1)S(1)}, bf16[128,256]{1,0:T(8,128)(2,1)}, u32[]{:S(2)}) copy-start(bf16[128,256]{1,0:T(8,128)(2,1)} %cotangent.1) | copy-start | bytes 196612
  88.9 18.9 %copy-start.11 = (f32[256]{0:T(256)S(1)}, f32[256]{0:T(256)}, u32[]{:S(2)}) copy-start(f32[256]{0:T(256)} %param.14) | copy-start | bytes 3076
  126.3 0.8 copy-start
  127.1 0.7 copy-start.1
  129.9 14.1 %copy-start.15 = (bf16[1152,128]{1,0:T(8,128)(2,1)S(1)}, bf16[1152,128]{1,0:T(8,128)(2,1)}, u32[]{:S(2)}) copy-start(bf16[1152,128]{1,0:T(8,128)(2,1)} %copy-done.14) | copy-start | bytes 884740
  129.9 17.7 %copy-start.13 = (bf16[1152,128]{1,0:T(8,128)(2,1)S(1)}, bf16[1152,128]{1,0:T(8,128)(2,1)}, u32[]{:S(2)}) copy-start(bf16[1152,128]{1,0:T(8,128)(2,1)} %copy-done.12) | copy-start | bytes 884740
  129.9 38.9 %copy-start.2 = (bf16[1152,128]{1,0:T(8,128)(2,1)S(1)}, bf16[1152,128]{1,0:T(8,128)(2,1)}, u32[]{:S(2)}) copy-start(bf16[1152,128]{1,0:T(8,128)(2,1)} %copy-done.1) | copy-start | bytes 884740
  129.9 38.9 %all-to-all-start.4 = ((bf16[12,160,128]{2,1,0:T(8,128)(2,1)}), bf16[12,160,128]{2,1,0:T(8,128)(2,1)S(1)}, u32[]{:S(2)}, u32[]{:S(2)}) async-start(bf16[12,160,128]{2,1,0:T(8,128)(2,1)} %copy-done), calls=%async_computation.4 | async-start | bytes 983040 | tf_op jit(solution)/shard_map/all_to_all | solution.py:381
  140.0 26.6 %collective-permute-start.9 = (bf16[1152,128]{1,0:T(8,128)(2,1)}, bf16[1152,128]{1,0:T(8,128)(2,1)S(1)}, u32[]{:S(2)}, u32[]{:S(2)}) collective-permute-start(bf16[1152,128]{1,0:T(8,128)(2,1)} %copy-done.16), channel_id=1, source_target_pairs={{0,144},{48,0},{96,48},{144,96},{1,145},{49,1},{97,49},{145,97},{2... | collective-permute-start | bytes 884744 | tf_op jit(solution)/shard_map/ppermute | solution.py:380
  144.1 22.5 %collective-permute-start.10 = (bf16[1152,128]{1,0:T(8,128)(2,1)S(1)}, bf16[1152,128]{1,0:T(8,128)(2,1)S(1)}, u32[]{:S(2)}, u32[]{:S(2)}) collective-permute-start(bf16[1152,128]{1,0:T(8,128)(2,1)S(1)} %copy-done.15), channel_id=1, source_target_pairs={{0,96},{48,144},{96,0},{144,48},{1,97},{49,145},{97,1},{145,49},{2... | collective-permute-start | bytes 884744 | tf_op jit(solution)/shard_map/ppermute | solution.py:380
  147.6 21.2 %collective-permute-start.11 = (bf16[1152,128]{1,0:T(8,128)(2,1)S(1)}, bf16[1152,128]{1,0:T(8,128)(2,1)S(1)}, u32[]{:S(2)}, u32[]{:S(2)}) collective-permute-start(bf16[1152,128]{1,0:T(8,128)(2,1)S(1)} %copy-done.13), channel_id=1, source_target_pairs={{0,48},{48,96},{96,144},{144,0},{1,49},{49,97},{97,145},{145,1},{2... | collective-permute-start | bytes 884744 | tf_op jit(solution)/shard_map/ppermute | solution.py:380
  169.7 23.5 %all-to-all-start.5 = ((bf16[12,96,128]{2,1,0:T(8,128)(2,1)}), bf16[12,96,128]{2,1,0:T(8,128)(2,1)S(1)}, u32[]{:S(2)}, u32[]{:S(2)}) async-start(bf16[12,96,128]{2,1,0:T(8,128)(2,1)} %get-tuple-element.26), calls=%async_computation.5 | async-start | bytes 589824 | tf_op jit(solution)/shard_map/all_to_all | solution.py:394
  178.4 11.7 %collective-permute-start.12 = (bf16[80,128]{1,0:T(8,128)(2,1)S(1)}, bf16[80,128]{1,0:T(8,128)(2,1)S(1)}, u32[]{:S(2)}, u32[]{:S(2)}) collective-permute-start(bf16[80,128]{1,0:T(8,128)(2,1)S(1)} %get-tuple-element.28), channel_id=1, source_target_pairs={{0,144},{48,0},{96,48},{144,96},{1,145},{49,1},{97,49},{145,97},{2... | collective-permute-start | bytes 61448 | tf_op jit(solution)/shard_map/ppermute | solution.py:393
  182.7 8.5 %collective-permute-start.13 = (bf16[80,128]{1,0:T(8,128)(2,1)S(1)}, bf16[80,128]{1,0:T(8,128)(2,1)S(1)}, u32[]{:S(2)}, u32[]{:S(2)}) collective-permute-start(bf16[80,128]{1,0:T(8,128)(2,1)S(1)} %get-tuple-element.29), channel_id=1, source_target_pairs={{0,96},{48,144},{96,0},{144,48},{1,97},{49,145},{97,1},{145,49},{2... | collective-permute-start | bytes 61448 | tf_op jit(solution)/shard_map/ppermute | solution.py:393
  186.2 6.9 %collective-permute-start.14 = (bf16[80,128]{1,0:T(8,128)(2,1)S(1)}, bf16[80,128]{1,0:T(8,128)(2,1)S(1)}, u32[]{:S(2)}, u32[]{:S(2)}) collective-permute-start(bf16[80,128]{1,0:T(8,128)(2,1)S(1)} %get-tuple-element.30), channel_id=1, source_target_pairs={{0,48},{48,96},{96,144},{144,0},{1,49},{49,97},{97,145},{145,1},{2... | collective-permute-start | bytes 61448 | tf_op jit(solution)/shard_map/ppermute | solution.py:393
  (6 other events, 4.2 us)

commit v4 on v3

--- a/solution.py
+++ b/solution.py
@@ -13,8 +13,6 @@
 row_axes = ("ylo", "core")
 col_axes = ("yhi", "x", "z")
 team_axes = ("ylo", "core", "x")
-ahead_rows = 80
-back_rows = 96
 group = 4
 lanes = 128
 vmem_bytes = 12 * 1024 * 1024
@@ -25,6 +23,14 @@
 def spread_out(value, axes, count):
     copies = jnp.broadcast_to(value[None], (count,) + value.shape)
     return lax.all_to_all(copies, axes, 0, 0, tiled=True)
+
+
+def codes_kernel(here, *refs, across, top):
+    out = refs[-1]
+    for source in range(across):
+        places = refs[source][pl.ds(top, 16), :].astype(jnp.float32).astype(jnp.int32)
+        mine = (places[0:1] == here[0]) | (places[0:1] == 254)
+        out[pl.ds(source, 1), :] = jnp.where(mine, places[1:2] * 64 + places[2:3], -1)
 
 
 def pick_tiles(codes, tile_refs, chosen, picked, slots, height, dummy):
@@ -48,18 +54,12 @@
 
 
 def forward_kernel(codes, *refs, slots, height, blocks, far, across):
-    lines, columns = refs[:far], refs[far]
-    tile_refs = refs[far + 1 : far + 1 + across]
-    out, slabs, chosen, totals, picked = refs[far + 1 + across :]
-    slab_count, nodes = slabs.shape[:2]
-    near = columns.shape[0]
-    ahead = lines[0].shape[0] // near
-    rest = nodes - ahead
-    for shift in range(far):
-        for index in range(near):
-            slab = shift * near + index
-            slabs[slab, pl.ds(0, ahead), :] = lines[shift][pl.ds(index * ahead, ahead), :]
-            slabs[slab, pl.ds(ahead, rest), :] = columns[index, pl.ds(shift * rest, rest), :]
+    lines, tile_refs = refs[:far], refs[far : far + across]
+    out, slabs, chosen, totals, picked = refs[far + across :]
+    slab_count = slabs.shape[0]
+    near = slab_count // far
+    for shift, line in enumerate(lines):
+        slabs[pl.ds(shift * near, near)] = line[...]
     dummy = slab_count * 64 + blocks
     totals[...] = jnp.zeros_like(totals)
     total = pick_tiles(codes, tile_refs, chosen, picked, slots, height, dummy)
@@ -164,7 +164,7 @@
 
 def backward_kernel(codes, spreads, *refs, slots, height, blocks, nodes, share, far, across):
     tile_refs, outs = refs[:across], refs[across : across + far]
-    columns, chosen, totals, picked = refs[across + far :]
+    shares, chosen, totals, picked = refs[across + far :]
     slab_count = totals.shape[0] - 1
     halves = nodes // height
     dummy = slab_count * 64 + blocks
@@ -190,61 +190,57 @@
 
     lax.fori_loop(0, (total + group - 1) // group, body, 0)
     near = slab_count // far
-    ahead = outs[0].shape[0] // near
-    rest = nodes - ahead
-    for shift in range(far):
+    for shift, out in enumerate(outs):
         for index in range(near):
-            total = totals[shift * near + index].astype(jnp.bfloat16)
-            outs[shift][pl.ds(index * ahead, ahead), :] = total[:ahead]
-            columns[index, pl.ds(shift * rest, rest), :] = total[ahead:]
+            out[index] = totals[shift * near + index].astype(jnp.bfloat16)
     weight_sum = sum_rows(spreads, nodes, 2 * share) + sum_rows(spreads, nodes + 2 * share, 2 * share)
-    weight_sum = weight_sum.astype(jnp.bfloat16)
+    high, low = split_wide(weight_sum)
     bias_block = pack_bias(sum_bias(spreads, nodes + 4 * share))
     for index in range(near):
-        columns[index, pl.ds(far * rest, 2 * share), :] = weight_sum
-        columns[index, pl.ds(far * rest + 2 * share, 16), :] = bias_block
-
-
-def middle_kernel(arrived, *refs, share, far):
-    lines, outs, line = refs[:far], refs[far : 2 * far], refs[2 * far]
-    near, ahead = line.shape[:2]
-    rest = outs[0].shape[0] - 4 * share - 16
-    for index in range(near):
-        total = lines[0][pl.ds(index * ahead, ahead), :].astype(jnp.float32)
-        for other in lines[1:]:
-            total = total + other[pl.ds(index * ahead, ahead), :].astype(jnp.float32)
-        line[index] = total.astype(jnp.bfloat16)
-    high, low = split_wide(sum_rows(arrived, far * rest, 2 * share))
-    bias_block = pack_bias(sum_bias(arrived, far * rest + 2 * share))
-    for shift, out in enumerate(outs):
-        out[pl.ds(0, rest), :] = sum_rows(arrived, shift * rest, rest).astype(jnp.bfloat16)
-        out[pl.ds(rest, 2 * share), :] = high.astype(jnp.bfloat16)
-        out[pl.ds(rest + 2 * share, 2 * share), :] = low.astype(jnp.bfloat16)
-        out[pl.ds(rest + 4 * share, 16), :] = bias_block
-
-
-def last_kernel(place, arrived, *refs, share, far, factor):
+        shares[index, pl.ds(0, 2 * share), :] = high.astype(jnp.bfloat16)
+        shares[index, pl.ds(2 * share, 2 * share), :] = low.astype(jnp.bfloat16)
+        shares[index, pl.ds(4 * share, 16), :] = bias_block
+
+
+def share_kernel(arrived, out, bias_block, *, share):
+    total = sum_rows(arrived, 0, 2 * share) + sum_rows(arrived, 2 * share, 2 * share)
+    for index in range(out.shape[0]):
+        out[index] = total
+    bias_block[...] = pack_bias(sum_bias(arrived, 4 * share))
+
+
+def gather_kernel(shares, bias_block, out, *, share):
+    step = 16 // share if share < 16 else 1
+    rows = shares.shape[0] * share
+    for half in range(2):
+        for first in range(0, shares.shape[0], step):
+            parts = [shares[first + sub, pl.ds(half * share, share), :] for sub in range(step)]
+            part = jnp.concatenate(parts, axis=0) if step > 1 else parts[0]
+            out[pl.ds(half * rows + first * share, step * share), :] = part.astype(jnp.bfloat16)
+    out[pl.ds(2 * rows, 16), :] = bias_block[...]
+
+
+def middle_kernel(*refs, far):
+    out = refs[-1]
+    for index in range(out.shape[0]):
+        total = refs[0][index].astype(jnp.float32)
+        for line in refs[1:far]:
+            total = total + line[index].astype(jnp.float32)
+        out[index] = total.astype(jnp.bfloat16)
+
+
+def last_kernel(place, arrived, *refs, far, factor):
     pieces = refs[:far]
-    grad, weight_share, bias_grad, stack = refs[far:]
-    ahead = arrived.shape[1]
-    rest = grad.shape[0] - ahead
-    grad[pl.ds(0, ahead), :] = sum_rows(arrived, 0, ahead)
+    grad, weight_grad, bias_grad, stack = refs[far:]
+    grad[...] = sum_rows(arrived, 0, grad.shape[0])
     for shift, piece in enumerate(pieces):
         stack[lax.rem(place[0] + shift, far)] = piece[...]
-    grad[pl.ds(ahead, rest), :] = sum_rows(stack, 0, rest)
-    weight_sum = sum_rows(stack, rest, 2 * share) + sum_rows(stack, rest + 2 * share, 2 * share)
-    weight_share[...] = weight_sum * factor
-    low, high = sum_bias(stack, rest + 4 * share)
+    rows = weight_grad.shape[0]
+    weight_grad[:, pl.ds(0, lanes)] = sum_rows(stack, 0, rows) * factor
+    weight_grad[:, pl.ds(lanes, lanes)] = sum_rows(stack, rows, rows) * factor
+    low, high = sum_bias(stack, 2 * rows)
     bias_grad[:, pl.ds(0, lanes)] = low * factor
     bias_grad[:, pl.ds(lanes, lanes)] = high * factor
-
-
-def copies_kernel(*refs, count):
-    out = refs[-1]
-    rows = refs[0].shape[0]
-    for index in range(out.shape[0]):
-        for shift in range(count):
-            out[index, pl.ds(shift * rows, rows), :] = refs[shift][...]
 
 
 def in_vmem():
@@ -287,42 +283,29 @@
     def ring(size, shift):
         return [(start, (start + shift) % size) for start in range(size)]
 
-    buffers = [own, lax.ppermute(own, "x", ring(across, 1))]
-    if across > 2:
-        buffers.append(lax.ppermute(own, "x", ring(across, -1)))
-    early = buffers[1:]
-    for shift in range(2, across - 1):
-        buffers.append(lax.ppermute(buffers[1 if shift == 2 else -1], "x", ring(across, 1)))
-
-    columns = [features[ahead_rows:]]
-    for shift in range(1, far):
-        columns.append(lax.ppermute(columns[0], "yhi", ring(far, shift)))
-    lines = [spread_out(features[:ahead_rows], "z", near).reshape(near * ahead_rows, width)]
-    copies = pl.pallas_call(
-        lambda *refs: copies_kernel(*refs, count=far),
-        out_shape=jax.ShapeDtypeStruct((near, far * (nodes - ahead_rows), width), jnp.bfloat16),
-        in_specs=[in_vmem()] * far + [any_place()] * (1 + len(early)),
-        out_specs=in_vmem(),
-        compiler_params=params,
-        name="column_copies",
-    )(*columns, lines[0], *early)
+    buffers = [own]
+    for shift in range(1, across):
+        buffers.append(lax.ppermute(own, "x", ring(across, shift)))
+
+    lines = [spread_out(features, "z", near)]
     for shift in range(1, far):
         lines.append(lax.ppermute(lines[0], "yhi", ring(far, shift)))
-    columns = lax.all_to_all(copies, "z", 0, 0, tiled=True)
-
-    tables = []
-    for buffer in buffers:
-        top = buffer[slots * height :].astype(jnp.int32)
-        mine = (top[0] == here) | (top[0] == 254)
-        tables.append(jnp.where(mine, top[1] * 64 + top[2], -1))
-    codes = jnp.stack(tables)
+
+    codes = pl.pallas_call(
+        lambda *refs: codes_kernel(*refs, across=across, top=slots * height),
+        out_shape=jax.ShapeDtypeStruct((across, lanes), jnp.int32),
+        in_specs=[in_smem()] + [in_vmem()] * across + [any_place()] * (far - 1),
+        out_specs=in_vmem(),
+        compiler_params=params,
+        name="tile_codes",
+    )(here.reshape(1), *buffers, *lines[1:])
 
     scratch_tiles = pltpu.VMEM((across * slots + group, height, tile_width), jnp.bfloat16)
     scratch_list = pltpu.SMEM((across * slots + group,), jnp.int32)
     partial = pl.pallas_call(
         lambda *refs: forward_kernel(*refs, slots=slots, height=height, blocks=blocks, far=far, across=across),
         out_shape=jax.ShapeDtypeStruct((members, nodes, width), jnp.bfloat16),
-        in_specs=[in_smem()] + [in_vmem()] * (far + 1 + across),
+        in_specs=[in_smem()] + [in_vmem()] * (far + across),
         out_specs=in_vmem(),
         scratch_shapes=[
             pltpu.VMEM((far * near, nodes, width), jnp.bfloat16),
@@ -332,7 +315,7 @@
         ],
         compiler_params=params,
         name="forward_tiles",
-    )(codes, *lines, columns, *buffers)
+    )(codes, *lines, *buffers)
     partials = lax.all_to_all(partial, team_axes, 0, 0, tiled=True)
 
     share = width // members
@@ -349,8 +332,6 @@
     )(partials, weight, bias.reshape(1, hidden), cotangent)
     spreads = lax.all_to_all(message, team_axes, 0, 0, tiled=True)
 
-    rest = nodes - back_rows
-    shared_rows = 2 * share + 16
     outs = pl.pallas_call(
         lambda *refs: backward_kernel(
             *refs,
@@ -362,8 +343,8 @@
             far=far,
             across=across,
         ),
-        out_shape=(jax.ShapeDtypeStruct((near * back_rows, width), jnp.bfloat16),) * far
-        + (jax.ShapeDtypeStruct((near, far * rest + shared_rows, width), jnp.bfloat16),),
+        out_shape=(jax.ShapeDtypeStruct((near, nodes, width), jnp.bfloat16),) * far
+        + (jax.ShapeDtypeStruct((near, 4 * share + 16, width), jnp.bfloat16),),
         in_specs=[in_smem(), in_vmem()] + [in_vmem()] * across,
         out_specs=(in_vmem(),) * (far + 1),
         scratch_shapes=[
@@ -379,36 +360,53 @@
     for shift in range(1, far):
         lines.append(lax.ppermute(outs[shift], "yhi", ring(far, -shift)))
     arrived = lax.all_to_all(outs[far], "z", 0, 0, tiled=True)
-    outs = pl.pallas_call(
-        lambda *refs: middle_kernel(*refs, share=share, far=far),
-        out_shape=(jax.ShapeDtypeStruct((rest + 2 * share + shared_rows, width), jnp.bfloat16),) * far
-        + (jax.ShapeDtypeStruct((near, back_rows, width), jnp.bfloat16),),
-        in_specs=[in_vmem()] * (far + 1),
-        out_specs=(in_vmem(),) * (far + 1),
+    shares, bias_block = pl.pallas_call(
+        lambda *refs: share_kernel(*refs, share=share),
+        out_shape=(
+            jax.ShapeDtypeStruct((members, 2 * share, lanes), jnp.float32),
+            jax.ShapeDtypeStruct((16, lanes), jnp.bfloat16),
+        ),
+        in_specs=[in_vmem()],
+        out_specs=(in_vmem(), in_vmem()),
+        compiler_params=params,
+        name="share_sum",
+    )(arrived)
+    shares = lax.all_to_all(shares, team_axes, 0, 0, tiled=True)
+    gradients = pl.pallas_call(
+        lambda *refs: gather_kernel(*refs, share=share),
+        out_shape=jax.ShapeDtypeStruct((2 * width + 16, lanes), jnp.bfloat16),
+        in_specs=[in_vmem(), in_vmem()],
+        out_specs=in_vmem(),
+        compiler_params=params,
+        name="share_gather",
+    )(shares, bias_block)
+    line = pl.pallas_call(
+        lambda *refs: middle_kernel(*refs, far=far),
+        out_shape=jax.ShapeDtypeStruct((near, nodes, width), jnp.bfloat16),
+        in_specs=[in_vmem()] * far + [any_place()],
+        out_specs=in_vmem(),
         compiler_params=params,
         name="middle_sums",
-    )(arrived, *lines)
-    pieces = [outs[0]]
+    )(*lines, gradients)
+
+    pieces = [gradients]
     for shift in range(1, far):
-        pieces.append(lax.ppermute(outs[shift], "yhi", ring(far, -shift)))
-    arrived = lax.all_to_all(outs[far], "z", 0, 0, tiled=True)
+        pieces.append(lax.ppermute(gradients, "yhi", ring(far, -shift)))
+    arrived = lax.all_to_all(line, "z", 0, 0, tiled=True)
     factor = 1.0 / math.sqrt(nodes * group_rows * far * across * near)
-    features_grad, weight_share, bias_grad = pl.pallas_call(
-        lambda *refs: last_kernel(*refs, share=share, far=far, factor=factor),
+    features_grad, weight_grad, bias_grad = pl.pallas_call(
+        lambda *refs: last_kernel(*refs, far=far, factor=factor),
         out_shape=(
             jax.ShapeDtypeStruct((nodes, width), jnp.float32),
-            jax.ShapeDtypeStruct((2 * share, lanes), jnp.float32),
+            jax.ShapeDtypeStruct((width, hidden), jnp.float32),
             jax.ShapeDtypeStruct((1, hidden), jnp.float32),
         ),
         in_specs=[in_smem()] + [in_vmem()] * (far + 1),
         out_specs=(in_vmem(), in_vmem(), in_vmem()),
-        scratch_shapes=[pltpu.VMEM((far,) + pieces[0].shape, jnp.bfloat16)],
+        scratch_shapes=[pltpu.VMEM((far,) + gradients.shape, jnp.bfloat16)],
         compiler_params=params,
         name="last_sums",
     )(lax.axis_index("yhi").reshape(1), arrived, *pieces)
-    shares = spread_out(weight_share, team_axes, members)
-    weight_grad = shares.reshape(members, 2, share, lanes).transpose(0, 2, 1, 3)
-    weight_grad = weight_grad.reshape(width, hidden)
     return (hidden_out, features_grad, weight_grad, bias_grad.reshape(hidden))
 
 

time: 216 us -> 204 us (0.944)
  starting transfers between devices: 99.9 us -> 75.5 us
  blocking collectives: 54.8 us -> 72.3 us
  local copies, waits for them, and re-layouts: 10.1 us -> 4.73 us
    ppermute x3, waiting for transfers between devices: 17.7 us -> 0.01 us  [local(): lines.append(lax.ppermute(outs[shift], 'yhi', ring(far, -shift)))]
    ppermute x9 -> x6, starting transfers between devices: 34.6 us -> 18.6 us  [the longest x3 9.33 us: local(): buffers.append(lax.ppermute(own, 'x', ring(across, shift)))]
    all_to_all x2 -> x1, starting transfers between devices: 18.8 us -> 5.09 us  [local(): arrived = lax.all_to_all(outs[far], 'z', 0, 0, tiled=True)]
    all_to_all x1, blocking collectives: 20.1 us -> 31.4 us  [local(): shares = lax.all_to_all(shares, team_axes, 0, 0, tiled=True)]
    all_to_all x1, waiting for transfers between devices: 0.01 us -> 8.32 us  [spread_out(): return lax.all_to_all(copies, axes, 0, 0, tiled=True)]
    ppermute x3, waiting for transfers between devices: 0.01 us -> 8.2 us  [local(): lines.append(lax.ppermute(lines[0], 'yhi', ring(far, shift)))]
    all_to_all x1, blocking collectives: 18.9 us -> 25.2 us  [local(): partials = lax.all_to_all(partial, team_axes, 0, 0, tiled=True)]
    unnamed x37 -> x20, local copies, waits for them, and re-layouts: 9.25 us -> 2.96 us
  transfers between devices with their start and end apart: 19 -> 15, of which waited for: 7 -> 7; matrix products, arithmetic and copies ran while one was open for 0% -> 0% of each run, Pallas kernels for 0% -> 0%
where the time goes in v4:
time: 204 us; the launch traced here: 201 us
  starting transfers between devices  75.5 us (37%)
  blocking collectives  72.3 us (35%)
  waiting for transfers between devices  38.6 us (19%)
  Pallas kernels  7.97 us (4%)
  local copies, waits for them, and re-layouts  4.73 us (2%)
    all_to_all x1, blocking collectives, local(): shares = lax.all_to_all(shares, team_axes, 0, 0, tiled=True)  31.4 us
    all_to_all x1, blocking collectives, local(): partials = lax.all_to_all(partial, team_axes, 0, 0, tiled=True)  25.2 us
    all_to_all x1, blocking collectives, local(): spreads = lax.all_to_all(message, team_axes, 0, 0, tiled=True)  15.8 us
    all_to_all x1, starting transfers between devices, spread_out(): return lax.all_to_all(copies, axes, 0, 0, tiled=True)  15.7 us
    ppermute x3, starting transfers between devices, local(): lines.append(lax.ppermute(lines[0], 'yhi', ring(far, shift)))  13.6 us
    ppermute x3, starting transfers between devices, local(): lines.append(lax.ppermute(outs[shift], 'yhi', ring(far, -shift)))  13.4 us
    ppermute x3, waiting for transfers between devices, local(): buffers.append(lax.ppermute(own, 'x', ring(across, shift)))  13 us
    ppermute x3, starting transfers between devices, local(): buffers.append(lax.ppermute(own, 'x', ring(across, shift)))  9.33 us
  transfers between devices with their start and end apart: 15, of which 7 were waited for; matrix products, arithmetic and copies ran while one was open for 0% of the time, Pallas kernels for 0%

profile of v4, /device:TPU:1, one launch (start us, length us, event | category | flops | bytes accessed | tf_op | source)
XLA Modules:
  0.0 200.9 jit_solution(14458586637966508009)
XLA Ops:
  0.7 1.7 broadcast_in_dim.16
  2.3 15.7 %all-to-all-start = ((bf16[12,128,128]{2,1,0:T(8,128)(2,1)}), bf16[12,128,128]{2,1,0:T(8,128)(2,1)S(1)}, u32[]{:S(2)}, u32[]{:S(2)}) async-start(bf16[12,128,128]{2,1,0:T(8,128)(2,1)} %broadcast_in_dim.16), calls=%async_computation | async-start | bytes 786432 | tf_op jit(solution)/shard_map/all_to_all | solution.py:25
  19.1 4.4 %collective-permute-start.2 = (bf16[3088,128]{1,0:T(8,128)(2,1)S(1)}, bf16[3088,128]{1,0:T(8,128)(2,1)S(1)}, u32[]{:S(2)}, u32[]{:S(2)}) collective-permute-start(bf16[3088,128]{1,0:T(8,128)(2,1)S(1)} %pad_maximum_fusion.refs_1_.refs_5_.refs_2_), channel_id=1, source_target_pairs={{0,36},{12,0},{24,12},{36,24},{1,37},{13,1},{25,13},{37,25},{2,38}... | collective-permute-start | bytes 2371592 | tf_op jit(solution)/shard_map/ppermute | solution.py:288
  23.4 2.4 %collective-permute-start.1 = (bf16[3088,128]{1,0:T(8,128)(2,1)S(1)}, bf16[3088,128]{1,0:T(8,128)(2,1)S(1)}, u32[]{:S(2)}, u32[]{:S(2)}) collective-permute-start(bf16[3088,128]{1,0:T(8,128)(2,1)S(1)} %pad_maximum_fusion.refs_1_.refs_5_.refs_2_), channel_id=1, source_target_pairs={{0,24},{12,36},{24,0},{36,12},{1,25},{13,37},{25,1},{37,13},{2,26}... | collective-permute-start | bytes 2371592 | tf_op jit(solution)/shard_map/ppermute | solution.py:288
  25.9 2.5 %collective-permute-start = (bf16[3088,128]{1,0:T(8,128)(2,1)S(1)}, bf16[3088,128]{1,0:T(8,128)(2,1)S(1)}, u32[]{:S(2)}, u32[]{:S(2)}) collective-permute-start(bf16[3088,128]{1,0:T(8,128)(2,1)S(1)} %pad_maximum_fusion.refs_1_.refs_5_.refs_2_), channel_id=1, source_target_pairs={{0,12},{12,24},{24,36},{36,0},{1,13},{13,25},{25,37},{37,1},{2,14}... | collective-permute-start | bytes 2371592 | tf_op jit(solution)/shard_map/ppermute | solution.py:288
  28.4 8.3 %all-to-all-done.refs_1_ = bf16[12,128,128]{2,1,0:T(8,128)(2,1)S(1)} async-done(((bf16[12,128,128]{2,1,0:T(8,128)(2,1)}), bf16[12,128,128]{2,1,0:T(8,128)(2,1)S(1)}, u32[]{:S(2)}, u32[]{:S(2)}) %all-to-all-start) | async-done | bytes 393248 | tf_op jit(solution)/shard_map/all_to_all | solution.py:25
  36.7 5.9 %collective-permute-start.5 = (bf16[12,128,128]{2,1,0:T(8,128)(2,1)S(1)}, bf16[12,128,128]{2,1,0:T(8,128)(2,1)S(1)}, u32[]{:S(2)}, u32[]{:S(2)}) collective-permute-start(bf16[12,128,128]{2,1,0:T(8,128)(2,1)S(1)} %all-to-all-done.refs_1_), channel_id=1, source_target_pairs={{0,144},{48,0},{96,48},{144,96},{1,145},{49,1},{97,49},{145,97},{2... | collective-permute-start | bytes 1179656 | tf_op jit(solution)/shard_map/ppermute | solution.py:292
  42.6 3.5 %collective-permute-start.4 = (bf16[12,128,128]{2,1,0:T(8,128)(2,1)S(1)}, bf16[12,128,128]{2,1,0:T(8,128)(2,1)S(1)}, u32[]{:S(2)}, u32[]{:S(2)}) collective-permute-start(bf16[12,128,128]{2,1,0:T(8,128)(2,1)S(1)} %all-to-all-done.refs_1_), channel_id=1, source_target_pairs={{0,96},{48,144},{96,0},{144,48},{1,97},{49,145},{97,1},{145,49},{2... | collective-permute-start | bytes 1179656 | tf_op jit(solution)/shard_map/ppermute | solution.py:292
  46.2 4.2 %collective-permute-start.3 = (bf16[12,128,128]{2,1,0:T(8,128)(2,1)S(1)}, bf16[12,128,128]{2,1,0:T(8,128)(2,1)S(1)}, u32[]{:S(2)}, u32[]{:S(2)}) collective-permute-start(bf16[12,128,128]{2,1,0:T(8,128)(2,1)S(1)} %all-to-all-done.refs_1_), channel_id=1, source_target_pairs={{0,48},{48,96},{96,144},{144,0},{1,49},{49,97},{97,145},{145,1},{2... | collective-permute-start | bytes 1179656 | tf_op jit(solution)/shard_map/ppermute | solution.py:292
  50.4 12.9 %collective-permute-done.refs_2_.refs_6_.refs_3_ = bf16[3088,128]{1,0:T(8,128)(2,1)S(1)} collective-permute-done((bf16[3088,128]{1,0:T(8,128)(2,1)S(1)}, bf16[3088,128]{1,0:T(8,128)(2,1)S(1)}, u32[]{:S(2)}, u32[]{:S(2)}) %collective-permute-start) | collective-permute-done | bytes 790560 | tf_op jit(solution)/shard_map/ppermute | solution.py:288
  63.3 2.6 %collective-permute-done.5.refs_7_.refs_4_ = bf16[12,128,128]{2,1,0:T(8,128)(2,1)S(1)} collective-permute-done((bf16[12,128,128]{2,1,0:T(8,128)(2,1)S(1)}, bf16[12,128,128]{2,1,0:T(8,128)(2,1)S(1)}, u32[]{:S(2)}, u32[]{:S(2)}) %collective-permute-start.5) | collective-permute-done | bytes 393248 | tf_op jit(solution)/shard_map/ppermute | solution.py:292
  65.9 5.6 %collective-permute-done.3.refs_5_.refs_2_ = bf16[12,128,128]{2,1,0:T(8,128)(2,1)S(1)} collective-permute-done((bf16[12,128,128]{2,1,0:T(8,128)(2,1)S(1)}, bf16[12,128,128]{2,1,0:T(8,128)(2,1)S(1)}, u32[]{:S(2)}, u32[]{:S(2)}) %collective-permute-start.3) | collective-permute-done | bytes 393248 | tf_op jit(solution)/shard_map/ppermute | solution.py:292
  71.6 2.3 %forward_tiles.1 = bf16[16,128,128]{2,1,0:T(8,128)(2,1)S(1)} custom-call(s32[4,128]{1,0:T(4,128)S(1)} %tile_codes.1.refs_0_, bf16[12,128,128]{2,1,0:T(8,128)(2,1)S(1)} %all-to-all-done.refs_1_, bf16[12,128,128]{2,1,0:T(8,128)(2,1)S(1)} %collective-permute-done.3.refs_5_.refs_2_, bf16[12,128,128]{2,1,0:T(8,128)(2,1)S(1)} %collective-permute-done.4.refs_6_.refs_3_, ...), custom_call_target="tpu_custom_call" | custom-call | tf_op jit(solution)/shard_map/forward_tiles/pallas_call | solution.py:305
  73.9 25.2 %all_to_all.30.partials = bf16[16,128,128]{2,1,0:T(8,128)(2,1)S(1)} all-to-all(bf16[16,128,128]{2,1,0:T(8,128)(2,1)S(1)} %forward_tiles.1), channel_id=1, replica_groups=mesh['ylo'=2,'core'=2,'yhi'=4,'x'=4,'z'=12] {'ylo','core','x'}, dimensions={0} | all-to-all | bytes 1048576 | tf_op jit(solution)/shard_map/all_to_all | solution.py:319
  99.1 1.1 dense_layer.1
  100.2 15.8 %all_to_all.31.refs_1_ = bf16[16,176,128]{2,1,0:T(8,128)(2,1)S(1)} all-to-all(bf16[16,176,128]{2,1,0:T(8,128)(2,1)S(1)} %get-tuple-element.17), channel_id=1, replica_groups=mesh['ylo'=2,'core'=2,'yhi'=4,'x'=4,'z'=12] {'ylo','core','x'}, dimensions={0} | all-to-all | bytes 1441792 | tf_op jit(solution)/shard_map/all_to_all | solution.py:333
  116.0 2.8 %backward_tiles.1 = (bf16[12,128,128]{2,1,0:T(8,128)(2,1)S(1)}, bf16[12,128,128]{2,1,0:T(8,128)(2,1)S(1)}, bf16[12,128,128]{2,1,0:T(8,128)(2,1)S(1)}, bf16[12,12...) custom-call(s32[4,128]{1,0:T(4,128)S(1)} %tile_codes.1.refs_0_, bf16[16,176,128]{2,1,0:T(8,128)(2,1)S(1)} %all_to_all.31.refs_1_, ...), custom_call_target="tpu_custom_call" | custom-call | tf_op jit(solution)/shard_map/backward_tiles/pallas_call | solution.py:335
  120.2 0.8 copy-done.5
  121.0 0.8 copy-done.6
  121.7 5.1 %all-to-all-start.3 = ((bf16[12,48,128]{2,1,0:T(8,128)(2,1)}), bf16[12,48,128]{2,1,0:T(8,128)(2,1)S(1)}, u32[]{:S(2)}, u32[]{:S(2)}) async-start(bf16[12,48,128]{2,1,0:T(8,128)(2,1)} %copy-done), calls=%async_computation.3 | async-start | bytes 294912 | tf_op jit(solution)/shard_map/all_to_all | solution.py:362
  126.8 4.6 %collective-permute-start.6 = (bf16[12,128,128]{2,1,0:T(8,128)(2,1)}, bf16[12,128,128]{2,1,0:T(8,128)(2,1)S(1)}, u32[]{:S(2)}, u32[]{:S(2)}) collective-permute-start(bf16[12,128,128]{2,1,0:T(8,128)(2,1)} %copy-done.6), channel_id=1, source_target_pairs={{0,144},{48,0},{96,48},{144,96},{1,145},{49,1},{97,49},{145,97},{2... | collective-permute-start | bytes 1179656 | tf_op jit(solution)/shard_map/ppermute | solution.py:361
  131.5 4.5 %collective-permute-start.7 = (bf16[12,128,128]{2,1,0:T(8,128)(2,1)}, bf16[12,128,128]{2,1,0:T(8,128)(2,1)S(1)}, u32[]{:S(2)}, u32[]{:S(2)}) collective-permute-start(bf16[12,128,128]{2,1,0:T(8,128)(2,1)} %copy-done.5), channel_id=1, source_target_pairs={{0,96},{48,144},{96,0},{144,48},{1,97},{49,145},{97,1},{145,49},{2... | collective-permute-start | bytes 1179656 | tf_op jit(solution)/shard_map/ppermute | solution.py:361
  136.0 4.3 %collective-permute-start.8 = (bf16[12,128,128]{2,1,0:T(8,128)(2,1)}, bf16[12,128,128]{2,1,0:T(8,128)(2,1)S(1)}, u32[]{:S(2)}, u32[]{:S(2)}) collective-permute-start(bf16[12,128,128]{2,1,0:T(8,128)(2,1)} %copy-done.4), channel_id=1, source_target_pairs={{0,48},{48,96},{96,144},{144,0},{1,49},{49,97},{97,145},{145,1},{2... | collective-permute-start | bytes 1179656 | tf_op jit(solution)/shard_map/ppermute | solution.py:361
  140.3 31.4 %all_to_all.32.refs_0_ = f32[16,16,128]{2,1,0:T(8,128)S(1)} all-to-all(f32[16,16,128]{2,1,0:T(8,128)S(1)} %get-tuple-element.23), channel_id=1, replica_groups=mesh['ylo'=2,'core'=2,'yhi'=4,'x'=4,'z'=12] {'ylo','core','x'}, dimensions={0} | all-to-all | bytes 262144 | tf_op jit(solution)/shard_map/all_to_all | solution.py:374
  171.7 1.0 middle_sums.1
  172.7 9.0 %all-to-all-start.5 = ((bf16[12,128,128]{2,1,0:T(8,128)(2,1)}), bf16[12,128,128]{2,1,0:T(8,128)(2,1)S(1)}, u32[]{:S(2)}, u32[]{:S(2)}) async-start(bf16[12,128,128]{2,1,0:T(8,128)(2,1)} %middle_sums.1), calls=%async_computation.5 | async-start | bytes 786432 | tf_op jit(solution)/shard_map/all_to_all | solution.py:395
  181.7 1.9 collective-permute-start.11
  183.7 3.4 %collective-permute-start.10 = (bf16[272,128]{1,0:T(8,128)(2,1)S(1)}, bf16[272,128]{1,0:T(8,128)(2,1)S(1)}, u32[]{:S(2)}, u32[]{:S(2)}) collective-permute-start(bf16[272,128]{1,0:T(8,128)(2,1)S(1)} %share_gather.1.refs_4_.refs_2_), channel_id=1, source_target_pairs={{0,96},{48,144},{96,0},{144,48},{1,97},{49,145},{97,1},{145,49},{2... | collective-permute-start | bytes 208904 | tf_op jit(solution)/shard_map/ppermute | solution.py:394
  187.0 4.0 %collective-permute-start.9 = (bf16[272,128]{1,0:T(8,128)(2,1)S(1)}, bf16[272,128]{1,0:T(8,128)(2,1)S(1)}, u32[]{:S(2)}, u32[]{:S(2)}) collective-permute-start(bf16[272,128]{1,0:T(8,128)(2,1)S(1)} %share_gather.1.refs_4_.refs_2_), channel_id=1, source_target_pairs={{0,144},{48,0},{96,48},{144,96},{1,145},{49,1},{97,49},{145,97},{2... | collective-permute-start | bytes 208904 | tf_op jit(solution)/shard_map/ppermute | solution.py:394
  191.1 2.6 %collective-permute-done.10.refs_4_ = bf16[272,128]{1,0:T(8,128)(2,1)S(1)} collective-permute-done((bf16[272,128]{1,0:T(8,128)(2,1)S(1)}, bf16[272,128]{1,0:T(8,128)(2,1)S(1)}, u32[]{:S(2)}, u32[]{:S(2)}) %collective-permute-start.10) | collective-permute-done | bytes 69664 | tf_op jit(solution)/shard_map/ppermute | solution.py:394
  193.7 2.2 %collective-permute-done.9.refs_3_ = bf16[272,128]{1,0:T(8,128)(2,1)S(1)} collective-permute-done((bf16[272,128]{1,0:T(8,128)(2,1)S(1)}, bf16[272,128]{1,0:T(8,128)(2,1)S(1)}, u32[]{:S(2)}, u32[]{:S(2)}) %collective-permute-start.9) | collective-permute-done | bytes 69664 | tf_op jit(solution)/shard_map/ppermute | solution.py:394
  195.9 4.3 %all-to-all-done.5.refs_1_ = bf16[12,128,128]{2,1,0:T(8,128)(2,1)S(1)} async-done(((bf16[12,128,128]{2,1,0:T(8,128)(2,1)}), bf16[12,128,128]{2,1,0:T(8,128)(2,1)S(1)}, u32[]{:S(2)}, u32[]{:S(2)}) %all-to-all-start.5) | async-done | bytes 393248 | tf_op jit(solution)/shard_map/all_to_all | solution.py:395
  (35 shorter events, 2.6 us)
Async XLA Ops:
  0.6 18.3 %copy-start.8 = (s32[1,1,48]{2,1,0:T(1,128)S(1)}, s32[1,1,48]{2,1,0:T(1,128)}, u32[]{:S(2)}) copy-start(s32[1,1,48]{2,1,0:T(1,128)} %param.10) | copy-start | bytes 580
  0.6 18.2 %copy-start.9 = (s32[1,1,48]{2,1,0:T(1,128)S(1)}, s32[1,1,48]{2,1,0:T(1,128)}, u32[]{:S(2)}) copy-start(s32[1,1,48]{2,1,0:T(1,128)} %param.9) | copy-start | bytes 580
  0.7 18.3 %copy-start.7 = (bf16[1,1,48,64,128]{4,3,2,1,0:T(8,128)(2,1)S(1)}, bf16[1,1,48,64,128]{4,3,2,1,0:T(8,128)(2,1)}, u32[]{:S(2)}) copy-start(bf16[1,1,48,64,128]{4,3,2,1,0:T(8,128)(2,1)} %param.12) | copy-start | bytes 2359300
  2.3 34.4 %all-to-all-start = ((bf16[12,128,128]{2,1,0:T(8,128)(2,1)}), bf16[12,128,128]{2,1,0:T(8,128)(2,1)S(1)}, u32[]{:S(2)}, u32[]{:S(2)}) async-start(bf16[12,128,128]{2,1,0:T(8,128)(2,1)} %broadcast_in_dim.16), calls=%async_computation | async-start | bytes 786432 | tf_op jit(solution)/shard_map/all_to_all | solution.py:25
  19.1 27.1 %collective-permute-start.2 = (bf16[3088,128]{1,0:T(8,128)(2,1)S(1)}, bf16[3088,128]{1,0:T(8,128)(2,1)S(1)}, u32[]{:S(2)}, u32[]{:S(2)}) collective-permute-start(bf16[3088,128]{1,0:T(8,128)(2,1)S(1)} %pad_maximum_fusion.refs_1_.refs_5_.refs_2_), channel_id=1, source_target_pairs={{0,36},{12,0},{24,12},{36,24},{1,37},{13,1},{25,13},{37,25},{2,38}... | collective-permute-start | bytes 2371592 | tf_op jit(solution)/shard_map/ppermute | solution.py:288
  23.4 26.9 %collective-permute-start.1 = (bf16[3088,128]{1,0:T(8,128)(2,1)S(1)}, bf16[3088,128]{1,0:T(8,128)(2,1)S(1)}, u32[]{:S(2)}, u32[]{:S(2)}) collective-permute-start(bf16[3088,128]{1,0:T(8,128)(2,1)S(1)} %pad_maximum_fusion.refs_1_.refs_5_.refs_2_), channel_id=1, source_target_pairs={{0,24},{12,36},{24,0},{36,12},{1,25},{13,37},{25,1},{37,13},{2,26}... | collective-permute-start | bytes 2371592 | tf_op jit(solution)/shard_map/ppermute | solution.py:288
  25.9 37.5 %collective-permute-start = (bf16[3088,128]{1,0:T(8,128)(2,1)S(1)}, bf16[3088,128]{1,0:T(8,128)(2,1)S(1)}, u32[]{:S(2)}, u32[]{:S(2)}) collective-permute-start(bf16[3088,128]{1,0:T(8,128)(2,1)S(1)} %pad_maximum_fusion.refs_1_.refs_5_.refs_2_), channel_id=1, source_target_pairs={{0,12},{12,24},{24,36},{36,0},{1,13},{13,25},{25,37},{37,1},{2,14}... | collective-permute-start | bytes 2371592 | tf_op jit(solution)/shard_map/ppermute | solution.py:288
  36.7 29.2 %collective-permute-start.5 = (bf16[12,128,128]{2,1,0:T(8,128)(2,1)S(1)}, bf16[12,128,128]{2,1,0:T(8,128)(2,1)S(1)}, u32[]{:S(2)}, u32[]{:S(2)}) collective-permute-start(bf16[12,128,128]{2,1,0:T(8,128)(2,1)S(1)} %all-to-all-done.refs_1_), channel_id=1, source_target_pairs={{0,144},{48,0},{96,48},{144,96},{1,145},{49,1},{97,49},{145,97},{2... | collective-permute-start | bytes 1179656 | tf_op jit(solution)/shard_map/ppermute | solution.py:292
  42.6 23.3 %collective-permute-start.4 = (bf16[12,128,128]{2,1,0:T(8,128)(2,1)S(1)}, bf16[12,128,128]{2,1,0:T(8,128)(2,1)S(1)}, u32[]{:S(2)}, u32[]{:S(2)}) collective-permute-start(bf16[12,128,128]{2,1,0:T(8,128)(2,1)S(1)} %all-to-all-done.refs_1_), channel_id=1, source_target_pairs={{0,96},{48,144},{96,0},{144,48},{1,97},{49,145},{97,1},{145,49},{2... | collective-permute-start | bytes 1179656 | tf_op jit(solution)/shard_map/ppermute | solution.py:292
  46.2 25.4 %collective-permute-start.3 = (bf16[12,128,128]{2,1,0:T(8,128)(2,1)S(1)}, bf16[12,128,128]{2,1,0:T(8,128)(2,1)S(1)}, u32[]{:S(2)}, u32[]{:S(2)}) collective-permute-start(bf16[12,128,128]{2,1,0:T(8,128)(2,1)S(1)} %all-to-all-done.refs_1_), channel_id=1, source_target_pairs={{0,48},{48,96},{96,144},{144,0},{1,49},{49,97},{97,145},{145,1},{2... | collective-permute-start | bytes 1179656 | tf_op jit(solution)/shard_map/ppermute | solution.py:292
  73.9 25.2 %copy-start.1 = (bf16[128,256]{1,0:T(8,128)(2,1)S(1)}, bf16[128,256]{1,0:T(8,128)(2,1)}, u32[]{:S(2)}) copy-start(bf16[128,256]{1,0:T(8,128)(2,1)} %weight.1) | copy-start | bytes 196612
  73.9 25.2 %copy-start.2 = (bf16[128,256]{1,0:T(8,128)(2,1)S(1)}, bf16[128,256]{1,0:T(8,128)(2,1)}, u32[]{:S(2)}) copy-start(bf16[128,256]{1,0:T(8,128)(2,1)} %cotangent.1) | copy-start | bytes 196612
  73.9 25.2 %copy-start.3 = (f32[256]{0:T(256)S(1)}, f32[256]{0:T(256)}, u32[]{:S(2)}) copy-start(f32[256]{0:T(256)} %param.14) | copy-start | bytes 3076
  118.8 0.7 copy-start
  119.4 0.8 copy-start.4
  120.2 0.8 copy-start.5
  120.9 0.8 copy-start.6
  121.7 18.5 %all-to-all-start.3 = ((bf16[12,48,128]{2,1,0:T(8,128)(2,1)}), bf16[12,48,128]{2,1,0:T(8,128)(2,1)S(1)}, u32[]{:S(2)}, u32[]{:S(2)}) async-start(bf16[12,48,128]{2,1,0:T(8,128)(2,1)} %copy-done), calls=%async_computation.3 | async-start | bytes 294912 | tf_op jit(solution)/shard_map/all_to_all | solution.py:362
  126.8 44.9 %collective-permute-start.6 = (bf16[12,128,128]{2,1,0:T(8,128)(2,1)}, bf16[12,128,128]{2,1,0:T(8,128)(2,1)S(1)}, u32[]{:S(2)}, u32[]{:S(2)}) collective-permute-start(bf16[12,128,128]{2,1,0:T(8,128)(2,1)} %copy-done.6), channel_id=1, source_target_pairs={{0,144},{48,0},{96,48},{144,96},{1,145},{49,1},{97,49},{145,97},{2... | collective-permute-start | bytes 1179656 | tf_op jit(solution)/shard_map/ppermute | solution.py:361
  131.5 40.3 %collective-permute-start.7 = (bf16[12,128,128]{2,1,0:T(8,128)(2,1)}, bf16[12,128,128]{2,1,0:T(8,128)(2,1)S(1)}, u32[]{:S(2)}, u32[]{:S(2)}) collective-permute-start(bf16[12,128,128]{2,1,0:T(8,128)(2,1)} %copy-done.5), channel_id=1, source_target_pairs={{0,96},{48,144},{96,0},{144,48},{1,97},{49,145},{97,1},{145,49},{2... | collective-permute-start | bytes 1179656 | tf_op jit(solution)/shard_map/ppermute | solution.py:361
  136.0 35.8 %collective-permute-start.8 = (bf16[12,128,128]{2,1,0:T(8,128)(2,1)}, bf16[12,128,128]{2,1,0:T(8,128)(2,1)S(1)}, u32[]{:S(2)}, u32[]{:S(2)}) collective-permute-start(bf16[12,128,128]{2,1,0:T(8,128)(2,1)} %copy-done.4), channel_id=1, source_target_pairs={{0,48},{48,96},{96,144},{144,0},{1,49},{49,97},{97,145},{145,1},{2... | collective-permute-start | bytes 1179656 | tf_op jit(solution)/shard_map/ppermute | solution.py:361
  172.7 27.5 %all-to-all-start.5 = ((bf16[12,128,128]{2,1,0:T(8,128)(2,1)}), bf16[12,128,128]{2,1,0:T(8,128)(2,1)S(1)}, u32[]{:S(2)}, u32[]{:S(2)}) async-start(bf16[12,128,128]{2,1,0:T(8,128)(2,1)} %middle_sums.1), calls=%async_computation.5 | async-start | bytes 786432 | tf_op jit(solution)/shard_map/all_to_all | solution.py:395
  181.7 9.3 %collective-permute-start.11 = (bf16[272,128]{1,0:T(8,128)(2,1)S(1)}, bf16[272,128]{1,0:T(8,128)(2,1)S(1)}, u32[]{:S(2)}, u32[]{:S(2)}) collective-permute-start(bf16[272,128]{1,0:T(8,128)(2,1)S(1)} %share_gather.1.refs_4_.refs_2_), channel_id=1, source_target_pairs={{0,48},{48,96},{96,144},{144,0},{1,49},{49,97},{97,145},{145,1},{2... | collective-permute-start | bytes 208904 | tf_op jit(solution)/shard_map/ppermute | solution.py:394
  183.7 10.0 %collective-permute-start.10 = (bf16[272,128]{1,0:T(8,128)(2,1)S(1)}, bf16[272,128]{1,0:T(8,128)(2,1)S(1)}, u32[]{:S(2)}, u32[]{:S(2)}) collective-permute-start(bf16[272,128]{1,0:T(8,128)(2,1)S(1)} %share_gather.1.refs_4_.refs_2_), channel_id=1, source_target_pairs={{0,96},{48,144},{96,0},{144,48},{1,97},{49,145},{97,1},{145,49},{2... | collective-permute-start | bytes 208904 | tf_op jit(solution)/shard_map/ppermute | solution.py:394
  187.0 8.9 %collective-permute-start.9 = (bf16[272,128]{1,0:T(8,128)(2,1)S(1)}, bf16[272,128]{1,0:T(8,128)(2,1)S(1)}, u32[]{:S(2)}, u32[]{:S(2)}) collective-permute-start(bf16[272,128]{1,0:T(8,128)(2,1)S(1)} %share_gather.1.refs_4_.refs_2_), channel_id=1, source_target_pairs={{0,144},{48,0},{96,48},{144,96},{1,145},{49,1},{97,49},{145,97},{2... | collective-permute-start | bytes 208904 | tf_op jit(solution)/shard_map/ppermute | solution.py:394

commit v5 on v4

--- a/solution.py
+++ b/solution.py
@@ -359,27 +359,36 @@
     lines = [outs[0]]
     for shift in range(1, far):
         lines.append(lax.ppermute(outs[shift], "yhi", ring(far, -shift)))
-    arrived = lax.all_to_all(outs[far], "z", 0, 0, tiled=True)
-    shares, bias_block = pl.pallas_call(
-        lambda *refs: share_kernel(*refs, share=share),
-        out_shape=(
-            jax.ShapeDtypeStruct((members, 2 * share, lanes), jnp.float32),
-            jax.ShapeDtypeStruct((16, lanes), jnp.bfloat16),
-        ),
-        in_specs=[in_vmem()],
-        out_specs=(in_vmem(), in_vmem()),
-        compiler_params=params,
-        name="share_sum",
-    )(arrived)
-    shares = lax.all_to_all(shares, team_axes, 0, 0, tiled=True)
-    gradients = pl.pallas_call(
-        lambda *refs: gather_kernel(*refs, share=share),
-        out_shape=jax.ShapeDtypeStruct((2 * width + 16, lanes), jnp.bfloat16),
-        in_specs=[in_vmem(), in_vmem()],
-        out_specs=in_vmem(),
-        compiler_params=params,
-        name="share_gather",
-    )(shares, bias_block)
+
+    def gather_gradients(value):
+        arrived = lax.all_to_all(value, "z", 0, 0, tiled=True)
+        shares, bias_block = pl.pallas_call(
+            lambda *refs: share_kernel(*refs, share=share),
+            out_shape=(
+                jax.ShapeDtypeStruct((members, 2 * share, lanes), jnp.float32),
+                jax.ShapeDtypeStruct((16, lanes), jnp.bfloat16),
+            ),
+            in_specs=[in_vmem()],
+            out_specs=(in_vmem(), in_vmem()),
+            compiler_params=params,
+            name="share_sum",
+        )(arrived)
+        shares = lax.all_to_all(shares, team_axes, 0, 0, tiled=True)
+        return pl.pallas_call(
+            lambda *refs: gather_kernel(*refs, share=share),
+            out_shape=jax.ShapeDtypeStruct((2 * width + 16, lanes), jnp.bfloat16),
+            in_specs=[in_vmem(), in_vmem()],
+            out_specs=in_vmem(),
+            compiler_params=params,
+            name="share_gather",
+        )(shares, bias_block)
+
+    gradients = lax.cond(
+        tile_counts[0, 0] > 0,
+        gather_gradients,
+        lambda value: jnp.zeros((2 * width + 16, lanes), jnp.bfloat16),
+        outs[far],
+    )
     line = pl.pallas_call(
         lambda *refs: middle_kernel(*refs, far=far),
         out_shape=jax.ShapeDtypeStruct((near, nodes, width), jnp.bfloat16),

time: 204 us -> 193 us (0.946)
  starting transfers between devices: 75.5 us -> 70.4 us
  local copies, waits for them, and re-layouts: 4.73 us -> 1.79 us
  waiting for transfers between devices: 38.6 us -> 35.7 us
    all_to_all x1 -> x0, starting transfers between devices: 5.09 us -> none  [local(): arrived = lax.all_to_all(outs[far], 'z', 0, 0, tiled=True)]
    all_to_all x1, starting transfers between devices: 9.04 us -> 5.24 us  [local(): arrived = lax.all_to_all(line, 'z', 0, 0, tiled=True)]
    ppermute x3, starting transfers between devices: 9.31 us -> 12.3 us  [local(): pieces.append(lax.ppermute(gradients, 'yhi', ring(far, -shift)))]
    unnamed x20 -> x12, local copies, waits for them, and re-layouts: 2.96 us -> 0.03 us
    ppermute x3, waiting for transfers between devices: 4.83 us -> 2.13 us  [local(): pieces.append(lax.ppermute(gradients, 'yhi', ring(far, -shift)))]
    all_to_all x1 -> x2, blocking collectives: 31.4 us -> 31.5 us  [the longest x1 16.4 us: gather_gradients(): arrived = lax.all_to_all(value, 'z', 0, 0, tiled=True)]
  transfers between devices with their start and end apart: 15 -> 14, of which waited for: 7 -> 7; matrix products, arithmetic and copies ran while one was open for 0% -> 0% of each run, Pallas kernels for 0% -> 0%
where the time goes in v5:
time: 193 us; the launch traced here: 190 us
  blocking collectives  73.5 us (38%)
  starting transfers between devices  70.4 us (36%)
  waiting for transfers between devices  35.7 us (18%)
  Pallas kernels  6.85 us (4%)
    all_to_all x1, blocking collectives, local(): partials = lax.all_to_all(partial, team_axes, 0, 0, tiled=True)  26.3 us
    all_to_all x1, blocking collectives, gather_gradients(): arrived = lax.all_to_all(value, 'z', 0, 0, tiled=True)  16.4 us
    all_to_all x1, blocking collectives, local(): spreads = lax.all_to_all(message, team_axes, 0, 0, tiled=True)  15.8 us
    all_to_all x1, starting transfers between devices, spread_out(): return lax.all_to_all(copies, axes, 0, 0, tiled=True)  15.7 us
    all_to_all x1, blocking collectives, gather_gradients(): shares = lax.all_to_all(shares, team_axes, 0, 0, tiled=True)  15.1 us
    ppermute x3, starting transfers between devices, local(): lines.append(lax.ppermute(outs[shift], 'yhi', ring(far, -shift)))  14.3 us
    ppermute x3, starting transfers between devices, local(): lines.append(lax.ppermute(lines[0], 'yhi', ring(far, shift)))  13.6 us
    ppermute x3, waiting for transfers between devices, local(): buffers.append(lax.ppermute(own, 'x', ring(across, shift)))  13 us
  transfers between devices with their start and end apart: 14, of which 7 were waited for; matrix products, arithmetic and copies ran while one was open for 0% of the time, Pallas kernels for 0%

profile of v5, /device:TPU:1, one launch (start us, length us, event | category | flops | bytes accessed | tf_op | source)
XLA Modules:
  0.0 190.1 jit_solution(15786633330830901374)
XLA Ops:
  0.7 1.6 broadcast_in_dim.16
  2.3 15.7 %all-to-all-start.2 = ((bf16[12,128,128]{2,1,0:T(8,128)(2,1)}), bf16[12,128,128]{2,1,0:T(8,128)(2,1)S(1)}, u32[]{:S(2)}, u32[]{:S(2)}) async-start(bf16[12,128,128]{2,1,0:T(8,128)(2,1)} %broadcast_in_dim.16), calls=%async_computation.2 | async-start | bytes 786432 | tf_op jit(solution)/shard_map/all_to_all | solution.py:25
  19.0 4.4 %collective-permute-start.2 = (bf16[3088,128]{1,0:T(8,128)(2,1)S(1)}, bf16[3088,128]{1,0:T(8,128)(2,1)S(1)}, u32[]{:S(2)}, u32[]{:S(2)}) collective-permute-start(bf16[3088,128]{1,0:T(8,128)(2,1)S(1)} %pad_maximum_fusion.refs_1_.refs_5_.refs_2_), channel_id=1, source_target_pairs={{0,36},{12,0},{24,12},{36,24},{1,37},{13,1},{25,13},{37,25},{2,38}... | collective-permute-start | bytes 2371592 | tf_op jit(solution)/shard_map/ppermute | solution.py:288
  23.4 2.4 %collective-permute-start.1 = (bf16[3088,128]{1,0:T(8,128)(2,1)S(1)}, bf16[3088,128]{1,0:T(8,128)(2,1)S(1)}, u32[]{:S(2)}, u32[]{:S(2)}) collective-permute-start(bf16[3088,128]{1,0:T(8,128)(2,1)S(1)} %pad_maximum_fusion.refs_1_.refs_5_.refs_2_), channel_id=1, source_target_pairs={{0,24},{12,36},{24,0},{36,12},{1,25},{13,37},{25,1},{37,13},{2,26}... | collective-permute-start | bytes 2371592 | tf_op jit(solution)/shard_map/ppermute | solution.py:288
  25.9 2.5 %collective-permute-start = (bf16[3088,128]{1,0:T(8,128)(2,1)S(1)}, bf16[3088,128]{1,0:T(8,128)(2,1)S(1)}, u32[]{:S(2)}, u32[]{:S(2)}) collective-permute-start(bf16[3088,128]{1,0:T(8,128)(2,1)S(1)} %pad_maximum_fusion.refs_1_.refs_5_.refs_2_), channel_id=1, source_target_pairs={{0,12},{12,24},{24,36},{36,0},{1,13},{13,25},{25,37},{37,1},{2,14}... | collective-permute-start | bytes 2371592 | tf_op jit(solution)/shard_map/ppermute | solution.py:288
  28.4 8.3 %all-to-all-done.2.refs_1_ = bf16[12,128,128]{2,1,0:T(8,128)(2,1)S(1)} async-done(((bf16[12,128,128]{2,1,0:T(8,128)(2,1)}), bf16[12,128,128]{2,1,0:T(8,128)(2,1)S(1)}, u32[]{:S(2)}, u32[]{:S(2)}) %all-to-all-start.2) | async-done | bytes 393248 | tf_op jit(solution)/shard_map/all_to_all | solution.py:25
  36.7 5.9 %collective-permute-start.5 = (bf16[12,128,128]{2,1,0:T(8,128)(2,1)S(1)}, bf16[12,128,128]{2,1,0:T(8,128)(2,1)S(1)}, u32[]{:S(2)}, u32[]{:S(2)}) collective-permute-start(bf16[12,128,128]{2,1,0:T(8,128)(2,1)S(1)} %all-to-all-done.2.refs_1_), channel_id=1, source_target_pairs={{0,144},{48,0},{96,48},{144,96},{1,145},{49,1},{97,49},{145,97},{2... | collective-permute-start | bytes 1179656 | tf_op jit(solution)/shard_map/ppermute | solution.py:292
  42.6 3.5 %collective-permute-start.4 = (bf16[12,128,128]{2,1,0:T(8,128)(2,1)S(1)}, bf16[12,128,128]{2,1,0:T(8,128)(2,1)S(1)}, u32[]{:S(2)}, u32[]{:S(2)}) collective-permute-start(bf16[12,128,128]{2,1,0:T(8,128)(2,1)S(1)} %all-to-all-done.2.refs_1_), channel_id=1, source_target_pairs={{0,96},{48,144},{96,0},{144,48},{1,97},{49,145},{97,1},{145,49},{2... | collective-permute-start | bytes 1179656 | tf_op jit(solution)/shard_map/ppermute | solution.py:292
  46.1 4.2 %collective-permute-start.3 = (bf16[12,128,128]{2,1,0:T(8,128)(2,1)S(1)}, bf16[12,128,128]{2,1,0:T(8,128)(2,1)S(1)}, u32[]{:S(2)}, u32[]{:S(2)}) collective-permute-start(bf16[12,128,128]{2,1,0:T(8,128)(2,1)S(1)} %all-to-all-done.2.refs_1_), channel_id=1, source_target_pairs={{0,48},{48,96},{96,144},{144,0},{1,49},{49,97},{97,145},{145,1},{2... | collective-permute-start | bytes 1179656 | tf_op jit(solution)/shard_map/ppermute | solution.py:292
  50.4 12.9 %collective-permute-done.refs_2_.refs_6_.refs_3_ = bf16[3088,128]{1,0:T(8,128)(2,1)S(1)} collective-permute-done((bf16[3088,128]{1,0:T(8,128)(2,1)S(1)}, bf16[3088,128]{1,0:T(8,128)(2,1)S(1)}, u32[]{:S(2)}, u32[]{:S(2)}) %collective-permute-start) | collective-permute-done | bytes 790560 | tf_op jit(solution)/shard_map/ppermute | solution.py:288
  63.3 2.6 %collective-permute-done.5.refs_7_.refs_4_ = bf16[12,128,128]{2,1,0:T(8,128)(2,1)S(1)} collective-permute-done((bf16[12,128,128]{2,1,0:T(8,128)(2,1)S(1)}, bf16[12,128,128]{2,1,0:T(8,128)(2,1)S(1)}, u32[]{:S(2)}, u32[]{:S(2)}) %collective-permute-start.5) | collective-permute-done | bytes 393248 | tf_op jit(solution)/shard_map/ppermute | solution.py:292
  65.9 5.6 %collective-permute-done.3.refs_5_.refs_2_ = bf16[12,128,128]{2,1,0:T(8,128)(2,1)S(1)} collective-permute-done((bf16[12,128,128]{2,1,0:T(8,128)(2,1)S(1)}, bf16[12,128,128]{2,1,0:T(8,128)(2,1)S(1)}, u32[]{:S(2)}, u32[]{:S(2)}) %collective-permute-start.3) | collective-permute-done | bytes 393248 | tf_op jit(solution)/shard_map/ppermute | solution.py:292
  71.5 1.4 forward_tiles.1
  73.0 26.3 %all_to_all.30.partials = bf16[16,128,128]{2,1,0:T(8,128)(2,1)S(1)} all-to-all(bf16[16,128,128]{2,1,0:T(8,128)(2,1)S(1)} %forward_tiles.1), channel_id=1, replica_groups=mesh['ylo'=2,'core'=2,'yhi'=4,'x'=4,'z'=12] {'ylo','core','x'}, dimensions={0} | all-to-all | bytes 1048576 | tf_op jit(solution)/shard_map/all_to_all | solution.py:319
  99.3 1.1 dense_layer.1
  100.4 15.8 %all_to_all.31.refs_1_ = bf16[16,176,128]{2,1,0:T(8,128)(2,1)S(1)} all-to-all(bf16[16,176,128]{2,1,0:T(8,128)(2,1)S(1)} %get-tuple-element.21), channel_id=1, replica_groups=mesh['ylo'=2,'core'=2,'yhi'=4,'x'=4,'z'=12] {'ylo','core','x'}, dimensions={0} | all-to-all | bytes 1441792 | tf_op jit(solution)/shard_map/all_to_all | solution.py:333
  116.1 2.6 %backward_tiles.1 = (bf16[12,128,128]{2,1,0:T(8,128)(2,1)S(1)}, bf16[12,128,128]{2,1,0:T(8,128)(2,1)}, bf16[12,128,128]{2,1,0:T(8,128)(2,1)}, bf16[12,128,128]{2,1,0:T(8,128)(2,1)}, bf16[12,48,128]{2,1,0:T(8,128)(2,1)}) custom-call(s32[4,128]{1,0:T(4,128)S(1)} %tile_codes.1.refs_0_, bf16[16,176,128]{2,1,0:T(8,128)(2,1)S(1)} %all_to_all.31.refs_1_, ...), custom_call_target="tpu_custom_call" | custom-call | tf_op jit(solution)/shard_map/backward_tiles/pallas_call | solution.py:335
  118.8 6.3 %collective-permute-start.6 = (bf16[12,128,128]{2,1,0:T(8,128)(2,1)}, bf16[12,128,128]{2,1,0:T(8,128)(2,1)S(1)}, u32[]{:S(2)}, u32[]{:S(2)}) collective-permute-start(bf16[12,128,128]{2,1,0:T(8,128)(2,1)} %get-tuple-element.23), channel_id=1, source_target_pairs={{0,144},{48,0},{96,48},{144,96},{1,145},{49,1},{97,49},{145,97},{2... | collective-permute-start | bytes 1179656 | tf_op jit(solution)/shard_map/ppermute | solution.py:361
  125.1 3.7 %collective-permute-start.7 = (bf16[12,128,128]{2,1,0:T(8,128)(2,1)}, bf16[12,128,128]{2,1,0:T(8,128)(2,1)S(1)}, u32[]{:S(2)}, u32[]{:S(2)}) collective-permute-start(bf16[12,128,128]{2,1,0:T(8,128)(2,1)} %get-tuple-element.24), channel_id=1, source_target_pairs={{0,96},{48,144},{96,0},{144,48},{1,97},{49,145},{97,1},{145,49},{2... | collective-permute-start | bytes 1179656 | tf_op jit(solution)/shard_map/ppermute | solution.py:361
  128.8 4.3 %collective-permute-start.8 = (bf16[12,128,128]{2,1,0:T(8,128)(2,1)}, bf16[12,128,128]{2,1,0:T(8,128)(2,1)S(1)}, u32[]{:S(2)}, u32[]{:S(2)}) collective-permute-start(bf16[12,128,128]{2,1,0:T(8,128)(2,1)} %get-tuple-element.25), channel_id=1, source_target_pairs={{0,48},{48,96},{96,144},{144,0},{1,49},{49,97},{97,145},{145,1},{2... | collective-permute-start | bytes 1179656 | tf_op jit(solution)/shard_map/ppermute | solution.py:361
  133.1 31.6 %conditional.1 = (bf16[272,128]{1,0:T(8,128)(2,1)S(1)}) conditional(s32[]{:T(128)} %convert_element_type.4, () %tuple.14, bf16[12,48,128]{2,1,0:T(8,128)(2,1)} %get-tuple-element.26), branch_computations={%region_0.1_spmd, %region_1.2_spmd} | conditional | bytes 557064 | solution.py:386
  133.1 16.4 %all_to_all.28.refs_0_ = bf16[12,48,128]{2,1,0:T(8,128)(2,1)S(1)} all-to-all(bf16[12,48,128]{2,1,0:T(8,128)(2,1)} %param.1), channel_id=1, replica_groups=mesh['ylo'=2,'core'=2,'yhi'=4,'x'=4,'z'=12] {'z'}, dimensions={0} | all-to-all | bytes 294912 | tf_op jit(solution)/shard_map/cond/branch_1_fun/all_to_all | solution.py:364
  149.5 15.1 %all_to_all.29.refs_0_ = f32[16,16,128]{2,1,0:T(8,128)S(1)} all-to-all(f32[16,16,128]{2,1,0:T(8,128)S(1)} %get-tuple-element.4), channel_id=1, replica_groups=mesh['ylo'=2,'core'=2,'yhi'=4,'x'=4,'z'=12] {'ylo','core','x'}, dimensions={0} | all-to-all | bytes 262144 | tf_op jit(solution)/shard_map/cond/branch_1_fun/all_to_all | solution.py:376
  164.7 0.9 middle_sums.1
  165.6 5.2 %all-to-all-start.5 = ((bf16[12,128,128]{2,1,0:T(8,128)(2,1)}), bf16[12,128,128]{2,1,0:T(8,128)(2,1)S(1)}, u32[]{:S(2)}, u32[]{:S(2)}) async-start(bf16[12,128,128]{2,1,0:T(8,128)(2,1)} %middle_sums.1), calls=%async_computation.5 | async-start | bytes 786432 | tf_op jit(solution)/shard_map/all_to_all | solution.py:404
  170.8 3.9 %collective-permute-start.11 = (bf16[272,128]{1,0:T(8,128)(2,1)S(1)}, bf16[272,128]{1,0:T(8,128)(2,1)S(1)}, u32[]{:S(2)}, u32[]{:S(2)}) collective-permute-start(bf16[272,128]{1,0:T(8,128)(2,1)S(1)} %get-tuple-element.33.refs_4_.refs_2_), channel_id=1, source_target_pairs={{0,48},{48,96},{96,144},{144,0},{1,49},{49,97},{97,145},{145,1},{2... | collective-permute-start | bytes 208904 | tf_op jit(solution)/shard_map/ppermute | solution.py:403
  174.7 2.9 %collective-permute-start.10 = (bf16[272,128]{1,0:T(8,128)(2,1)S(1)}, bf16[272,128]{1,0:T(8,128)(2,1)S(1)}, u32[]{:S(2)}, u32[]{:S(2)}) collective-permute-start(bf16[272,128]{1,0:T(8,128)(2,1)S(1)} %get-tuple-element.33.refs_4_.refs_2_), channel_id=1, source_target_pairs={{0,96},{48,144},{96,0},{144,48},{1,97},{49,145},{97,1},{145,49},{2... | collective-permute-start | bytes 208904 | tf_op jit(solution)/shard_map/ppermute | solution.py:403
  177.7 5.5 %collective-permute-start.9 = (bf16[272,128]{1,0:T(8,128)(2,1)S(1)}, bf16[272,128]{1,0:T(8,128)(2,1)S(1)}, u32[]{:S(2)}, u32[]{:S(2)}) collective-permute-start(bf16[272,128]{1,0:T(8,128)(2,1)S(1)} %get-tuple-element.33.refs_4_.refs_2_), channel_id=1, source_target_pairs={{0,144},{48,0},{96,48},{144,96},{1,145},{49,1},{97,49},{145,97},{2... | collective-permute-start | bytes 208904 | tf_op jit(solution)/shard_map/ppermute | solution.py:403
  183.1 1.4 collective-permute-done.10.refs_4_
  184.6 0.7 collective-permute-done.9.refs_3_
  185.3 4.1 %all-to-all-done.5.refs_1_ = bf16[12,128,128]{2,1,0:T(8,128)(2,1)S(1)} async-done(((bf16[12,128,128]{2,1,0:T(8,128)(2,1)}), bf16[12,128,128]{2,1,0:T(8,128)(2,1)S(1)}, u32[]{:S(2)}, u32[]{:S(2)}) %all-to-all-start.5) | async-done | bytes 393248 | tf_op jit(solution)/shard_map/all_to_all | solution.py:404
  189.4 0.7 last_sums.1
  (27 shorter events, 0.4 us)
Async XLA Ops:
  0.6 18.2 %copy-start.4 = (s32[1,1,48]{2,1,0:T(1,128)S(1)}, s32[1,1,48]{2,1,0:T(1,128)}, u32[]{:S(2)}) copy-start(s32[1,1,48]{2,1,0:T(1,128)} %param.12) | copy-start | bytes 580
  0.6 18.2 %copy-start.5 = (s32[1,1,48]{2,1,0:T(1,128)S(1)}, s32[1,1,48]{2,1,0:T(1,128)}, u32[]{:S(2)}) copy-start(s32[1,1,48]{2,1,0:T(1,128)} %param.11) | copy-start | bytes 580
  0.7 18.3 %copy-start.3 = (bf16[1,1,48,64,128]{4,3,2,1,0:T(8,128)(2,1)S(1)}, bf16[1,1,48,64,128]{4,3,2,1,0:T(8,128)(2,1)}, u32[]{:S(2)}) copy-start(bf16[1,1,48,64,128]{4,3,2,1,0:T(8,128)(2,1)} %param.14) | copy-start | bytes 2359300
  2.3 34.4 %all-to-all-start.2 = ((bf16[12,128,128]{2,1,0:T(8,128)(2,1)}), bf16[12,128,128]{2,1,0:T(8,128)(2,1)S(1)}, u32[]{:S(2)}, u32[]{:S(2)}) async-start(bf16[12,128,128]{2,1,0:T(8,128)(2,1)} %broadcast_in_dim.16), calls=%async_computation.2 | async-start | bytes 786432 | tf_op jit(solution)/shard_map/all_to_all | solution.py:25
  19.0 27.1 %collective-permute-start.2 = (bf16[3088,128]{1,0:T(8,128)(2,1)S(1)}, bf16[3088,128]{1,0:T(8,128)(2,1)S(1)}, u32[]{:S(2)}, u32[]{:S(2)}) collective-permute-start(bf16[3088,128]{1,0:T(8,128)(2,1)S(1)} %pad_maximum_fusion.refs_1_.refs_5_.refs_2_), channel_id=1, source_target_pairs={{0,36},{12,0},{24,12},{36,24},{1,37},{13,1},{25,13},{37,25},{2,38}... | collective-permute-start | bytes 2371592 | tf_op jit(solution)/shard_map/ppermute | solution.py:288
  23.4 26.9 %collective-permute-start.1 = (bf16[3088,128]{1,0:T(8,128)(2,1)S(1)}, bf16[3088,128]{1,0:T(8,128)(2,1)S(1)}, u32[]{:S(2)}, u32[]{:S(2)}) collective-permute-start(bf16[3088,128]{1,0:T(8,128)(2,1)S(1)} %pad_maximum_fusion.refs_1_.refs_5_.refs_2_), channel_id=1, source_target_pairs={{0,24},{12,36},{24,0},{36,12},{1,25},{13,37},{25,1},{37,13},{2,26}... | collective-permute-start | bytes 2371592 | tf_op jit(solution)/shard_map/ppermute | solution.py:288
  25.9 37.5 %collective-permute-start = (bf16[3088,128]{1,0:T(8,128)(2,1)S(1)}, bf16[3088,128]{1,0:T(8,128)(2,1)S(1)}, u32[]{:S(2)}, u32[]{:S(2)}) collective-permute-start(bf16[3088,128]{1,0:T(8,128)(2,1)S(1)} %pad_maximum_fusion.refs_1_.refs_5_.refs_2_), channel_id=1, source_target_pairs={{0,12},{12,24},{24,36},{36,0},{1,13},{13,25},{25,37},{37,1},{2,14}... | collective-permute-start | bytes 2371592 | tf_op jit(solution)/shard_map/ppermute | solution.py:288
  36.7 29.2 %collective-permute-start.5 = (bf16[12,128,128]{2,1,0:T(8,128)(2,1)S(1)}, bf16[12,128,128]{2,1,0:T(8,128)(2,1)S(1)}, u32[]{:S(2)}, u32[]{:S(2)}) collective-permute-start(bf16[12,128,128]{2,1,0:T(8,128)(2,1)S(1)} %all-to-all-done.2.refs_1_), channel_id=1, source_target_pairs={{0,144},{48,0},{96,48},{144,96},{1,145},{49,1},{97,49},{145,97},{2... | collective-permute-start | bytes 1179656 | tf_op jit(solution)/shard_map/ppermute | solution.py:292
  42.6 23.3 %collective-permute-start.4 = (bf16[12,128,128]{2,1,0:T(8,128)(2,1)S(1)}, bf16[12,128,128]{2,1,0:T(8,128)(2,1)S(1)}, u32[]{:S(2)}, u32[]{:S(2)}) collective-permute-start(bf16[12,128,128]{2,1,0:T(8,128)(2,1)S(1)} %all-to-all-done.2.refs_1_), channel_id=1, source_target_pairs={{0,96},{48,144},{96,0},{144,48},{1,97},{49,145},{97,1},{145,49},{2... | collective-permute-start | bytes 1179656 | tf_op jit(solution)/shard_map/ppermute | solution.py:292
  46.1 25.4 %collective-permute-start.3 = (bf16[12,128,128]{2,1,0:T(8,128)(2,1)S(1)}, bf16[12,128,128]{2,1,0:T(8,128)(2,1)S(1)}, u32[]{:S(2)}, u32[]{:S(2)}) collective-permute-start(bf16[12,128,128]{2,1,0:T(8,128)(2,1)S(1)} %all-to-all-done.2.refs_1_), channel_id=1, source_target_pairs={{0,48},{48,96},{96,144},{144,0},{1,49},{49,97},{97,145},{145,1},{2... | collective-permute-start | bytes 1179656 | tf_op jit(solution)/shard_map/ppermute | solution.py:292
  73.0 26.3 %copy-start = (bf16[128,256]{1,0:T(8,128)(2,1)S(1)}, bf16[128,256]{1,0:T(8,128)(2,1)}, u32[]{:S(2)}) copy-start(bf16[128,256]{1,0:T(8,128)(2,1)} %weight.1) | copy-start | bytes 196612
  73.0 26.3 %copy-start.1 = (bf16[128,256]{1,0:T(8,128)(2,1)S(1)}, bf16[128,256]{1,0:T(8,128)(2,1)}, u32[]{:S(2)}) copy-start(bf16[128,256]{1,0:T(8,128)(2,1)} %cotangent.1) | copy-start | bytes 196612
  73.0 26.3 %copy-start.2 = (f32[256]{0:T(256)S(1)}, f32[256]{0:T(256)}, u32[]{:S(2)}) copy-start(f32[256]{0:T(256)} %param.16) | copy-start | bytes 3076
  118.8 45.9 %collective-permute-start.6 = (bf16[12,128,128]{2,1,0:T(8,128)(2,1)}, bf16[12,128,128]{2,1,0:T(8,128)(2,1)S(1)}, u32[]{:S(2)}, u32[]{:S(2)}) collective-permute-start(bf16[12,128,128]{2,1,0:T(8,128)(2,1)} %get-tuple-element.23), channel_id=1, source_target_pairs={{0,144},{48,0},{96,48},{144,96},{1,145},{49,1},{97,49},{145,97},{2... | collective-permute-start | bytes 1179656 | tf_op jit(solution)/shard_map/ppermute | solution.py:361
  125.1 39.5 %collective-permute-start.7 = (bf16[12,128,128]{2,1,0:T(8,128)(2,1)}, bf16[12,128,128]{2,1,0:T(8,128)(2,1)S(1)}, u32[]{:S(2)}, u32[]{:S(2)}) collective-permute-start(bf16[12,128,128]{2,1,0:T(8,128)(2,1)} %get-tuple-element.24), channel_id=1, source_target_pairs={{0,96},{48,144},{96,0},{144,48},{1,97},{49,145},{97,1},{145,49},{2... | collective-permute-start | bytes 1179656 | tf_op jit(solution)/shard_map/ppermute | solution.py:361
  128.8 35.9 %collective-permute-start.8 = (bf16[12,128,128]{2,1,0:T(8,128)(2,1)}, bf16[12,128,128]{2,1,0:T(8,128)(2,1)S(1)}, u32[]{:S(2)}, u32[]{:S(2)}) collective-permute-start(bf16[12,128,128]{2,1,0:T(8,128)(2,1)} %get-tuple-element.25), channel_id=1, source_target_pairs={{0,48},{48,96},{96,144},{144,0},{1,49},{49,97},{97,145},{145,1},{2... | collective-permute-start | bytes 1179656 | tf_op jit(solution)/shard_map/ppermute | solution.py:361
  165.6 23.8 %all-to-all-start.5 = ((bf16[12,128,128]{2,1,0:T(8,128)(2,1)}), bf16[12,128,128]{2,1,0:T(8,128)(2,1)S(1)}, u32[]{:S(2)}, u32[]{:S(2)}) async-start(bf16[12,128,128]{2,1,0:T(8,128)(2,1)} %middle_sums.1), calls=%async_computation.5 | async-start | bytes 786432 | tf_op jit(solution)/shard_map/all_to_all | solution.py:404
  170.8 12.3 %collective-permute-start.11 = (bf16[272,128]{1,0:T(8,128)(2,1)S(1)}, bf16[272,128]{1,0:T(8,128)(2,1)S(1)}, u32[]{:S(2)}, u32[]{:S(2)}) collective-permute-start(bf16[272,128]{1,0:T(8,128)(2,1)S(1)} %get-tuple-element.33.refs_4_.refs_2_), channel_id=1, source_target_pairs={{0,48},{48,96},{96,144},{144,0},{1,49},{49,97},{97,145},{145,1},{2... | collective-permute-start | bytes 208904 | tf_op jit(solution)/shard_map/ppermute | solution.py:403
  174.7 9.9 %collective-permute-start.10 = (bf16[272,128]{1,0:T(8,128)(2,1)S(1)}, bf16[272,128]{1,0:T(8,128)(2,1)S(1)}, u32[]{:S(2)}, u32[]{:S(2)}) collective-permute-start(bf16[272,128]{1,0:T(8,128)(2,1)S(1)} %get-tuple-element.33.refs_4_.refs_2_), channel_id=1, source_target_pairs={{0,96},{48,144},{96,0},{144,48},{1,97},{49,145},{97,1},{145,49},{2... | collective-permute-start | bytes 208904 | tf_op jit(solution)/shard_map/ppermute | solution.py:403
  177.7 7.6 %collective-permute-start.9 = (bf16[272,128]{1,0:T(8,128)(2,1)S(1)}, bf16[272,128]{1,0:T(8,128)(2,1)S(1)}, u32[]{:S(2)}, u32[]{:S(2)}) collective-permute-start(bf16[272,128]{1,0:T(8,128)(2,1)S(1)} %get-tuple-element.33.refs_4_.refs_2_), channel_id=1, source_target_pairs={{0,144},{48,0},{96,48},{144,96},{1,145},{49,1},{97,49},{145,97},{2... | collective-permute-start | bytes 208904 | tf_op jit(solution)/shard_map/ppermute | solution.py:403

commit v6 on v5

--- a/solution.py
+++ b/solution.py
@@ -25,12 +25,14 @@
     return lax.all_to_all(copies, axes, 0, 0, tiled=True)
 
 
-def codes_kernel(here, *refs, across, top):
+def codes_kernel(here, places, *refs):
     out = refs[-1]
+    across = places.shape[0]
     for source in range(across):
-        places = refs[source][pl.ds(top, 16), :].astype(jnp.float32).astype(jnp.int32)
-        mine = (places[0:1] == here[0]) | (places[0:1] == 254)
-        out[pl.ds(source, 1), :] = jnp.where(mine, places[1:2] * 64 + places[2:3], -1)
+        place = places[lax.rem(here[0] - source + across, across)].astype(jnp.float32)
+        place = place.astype(jnp.int32)
+        mine = (place[0:1] == here[0]) | (place[0:1] == 254)
+        out[pl.ds(source, 1), :] = jnp.where(mine, place[1:2] * 64 + place[2:3], -1)
 
 
 def pick_tiles(codes, tile_refs, chosen, picked, slots, height, dummy):
@@ -229,16 +231,12 @@
         out[index] = total.astype(jnp.bfloat16)
 
 
-def last_kernel(place, arrived, *refs, far, factor):
-    pieces = refs[:far]
-    grad, weight_grad, bias_grad, stack = refs[far:]
+def last_kernel(arrived, pieces, grad, weight_grad, bias_grad, *, factor):
     grad[...] = sum_rows(arrived, 0, grad.shape[0])
-    for shift, piece in enumerate(pieces):
-        stack[lax.rem(place[0] + shift, far)] = piece[...]
     rows = weight_grad.shape[0]
-    weight_grad[:, pl.ds(0, lanes)] = sum_rows(stack, 0, rows) * factor
-    weight_grad[:, pl.ds(lanes, lanes)] = sum_rows(stack, rows, rows) * factor
-    low, high = sum_bias(stack, 2 * rows)
+    weight_grad[:, pl.ds(0, lanes)] = sum_rows(pieces, 0, rows) * factor
+    weight_grad[:, pl.ds(lanes, lanes)] = sum_rows(pieces, rows, rows) * factor
+    low, high = sum_bias(pieces, 2 * rows)
     bias_grad[:, pl.ds(0, lanes)] = low * factor
     bias_grad[:, pl.ds(lanes, lanes)] = high * factor
 
@@ -278,27 +276,30 @@
     ends = jnp.stack([jnp.int32(254), jnp.int32(0), tile_counts[0, 0]])[:, None]
     places = jnp.concatenate([places, ends], axis=1)
     places = jnp.pad(places, ((0, 13), (0, lanes - slots - 1))).astype(jnp.bfloat16)
-    own = jnp.concatenate([tile_values[0, 0].reshape(slots * height, tile_width), places], axis=0)
+    places = lax.all_gather(places, "x", axis=0)
 
     def ring(size, shift):
         return [(start, (start + shift) % size) for start in range(size)]
 
-    buffers = [own]
-    for shift in range(1, across):
-        buffers.append(lax.ppermute(own, "x", ring(across, shift)))
+    own = tile_values[0, 0].reshape(slots * height, tile_width)
+    buffers = [own, lax.ppermute(own, "x", ring(across, 1))]
+    for shift in range(2, across - 1):
+        buffers.append(lax.ppermute(buffers[-1], "x", ring(across, 1)))
+    if across > 2:
+        buffers.append(lax.ppermute(own, "x", ring(across, -1)))
 
     lines = [spread_out(features, "z", near)]
     for shift in range(1, far):
         lines.append(lax.ppermute(lines[0], "yhi", ring(far, shift)))
 
     codes = pl.pallas_call(
-        lambda *refs: codes_kernel(*refs, across=across, top=slots * height),
+        codes_kernel,
         out_shape=jax.ShapeDtypeStruct((across, lanes), jnp.int32),
-        in_specs=[in_smem()] + [in_vmem()] * across + [any_place()] * (far - 1),
+        in_specs=[in_smem(), in_vmem()] + [any_place()] * (far - 1),
         out_specs=in_vmem(),
         compiler_params=params,
         name="tile_codes",
-    )(here.reshape(1), *buffers, *lines[1:])
+    )(here.reshape(1), places, *lines[1:])
 
     scratch_tiles = pltpu.VMEM((across * slots + group, height, tile_width), jnp.bfloat16)
     scratch_list = pltpu.SMEM((across * slots + group,), jnp.int32)
@@ -398,24 +399,21 @@
         name="middle_sums",
     )(*lines, gradients)
 
-    pieces = [gradients]
-    for shift in range(1, far):
-        pieces.append(lax.ppermute(gradients, "yhi", ring(far, -shift)))
+    pieces = lax.all_gather(gradients, "yhi", axis=0)
     arrived = lax.all_to_all(line, "z", 0, 0, tiled=True)
     factor = 1.0 / math.sqrt(nodes * group_rows * far * across * near)
     features_grad, weight_grad, bias_grad = pl.pallas_call(
-        lambda *refs: last_kernel(*refs, far=far, factor=factor),
+        lambda *refs: last_kernel(*refs, factor=factor),
         out_shape=(
             jax.ShapeDtypeStruct((nodes, width), jnp.float32),
             jax.ShapeDtypeStruct((width, hidden), jnp.float32),
             jax.ShapeDtypeStruct((1, hidden), jnp.float32),
         ),
-        in_specs=[in_smem()] + [in_vmem()] * (far + 1),
+        in_specs=[in_vmem(), in_vmem()],
         out_specs=(in_vmem(), in_vmem(), in_vmem()),
-        scratch_shapes=[pltpu.VMEM((far,) + gradients.shape, jnp.bfloat16)],
         compiler_params=params,
         name="last_sums",
-    )(lax.axis_index("yhi").reshape(1), arrived, *pieces)
+    )(arrived, pieces)
     return (hidden_out, features_grad, weight_grad, bias_grad.reshape(hidden))
 
 

time: 193 us -> 197 us (1.021)
  blocking collectives: 73.5 us -> 94 us
  starting transfers between devices: 70.4 us -> 55.1 us
  waiting for transfers between devices: 35.7 us -> 29.9 us
  Pallas kernels: 6.85 us -> 9.55 us
    all_gather x0 -> x2, blocking collectives: none -> 21.7 us  [the longest x1 11.7 us: local(): pieces = lax.all_gather(gradients, 'yhi', axis=0)]
    ppermute x6 -> x3, waiting for transfers between devices: 15.1 us -> 0.01 us  [the longest x1 0.01 us: local(): buffers.append(lax.ppermute(own, 'x', ring(across, -1)))]
    ppermute x6 -> x3, starting transfers between devices: 21.6 us -> 9.37 us  [the longest x1 4.08 us: local(): buffers = [own, lax.ppermute(own, 'x', ring(across, 1))]]
    all_to_all x1, waiting for transfers between devices: 8.32 us -> 12.6 us  [spread_out(): return lax.all_to_all(copies, axes, 0, 0, tiled=True)]
    all_to_all x1, waiting for transfers between devices: 4.1 us -> 6.76 us  [local(): arrived = lax.all_to_all(line, 'z', 0, 0, tiled=True)]
    all_to_all x1, blocking collectives: 16.4 us -> 13.9 us  [gather_gradients(): arrived = lax.all_to_all(value, 'z', 0, 0, tiled=True)]
    ppermute x3, waiting for transfers between devices: 8.2 us -> 10.5 us  [local(): lines.append(lax.ppermute(lines[0], 'yhi', ring(far, shift)))]
    all_to_all x1, blocking collectives: 15.1 us -> 17.3 us  [gather_gradients(): shares = lax.all_to_all(shares, team_axes, 0, 0, tiled=True)]
  transfers between devices with their start and end apart: 14 -> 11, of which waited for: 7 -> 4; matrix products, arithmetic and copies ran while one was open for 0% -> 1% of each run, Pallas kernels for 0% -> 0%
where the time goes in v6:
time: 197 us; the launch traced here: 193 us
  blocking collectives  94 us (48%)
  starting transfers between devices  55.1 us (28%)
  waiting for transfers between devices  29.9 us (15%)
  Pallas kernels  9.55 us (5%)
  local copies, waits for them, and re-layouts  3.05 us (2%)
    all_to_all x1, blocking collectives, local(): partials = lax.all_to_all(partial, team_axes, 0, 0, tiled=True)  25.4 us
    all_to_all x1, blocking collectives, gather_gradients(): shares = lax.all_to_all(shares, team_axes, 0, 0, tiled=True)  17.3 us
    all_to_all x1, blocking collectives, local(): spreads = lax.all_to_all(message, team_axes, 0, 0, tiled=True)  15.8 us
    all_to_all x1, starting transfers between devices, spread_out(): return lax.all_to_all(copies, axes, 0, 0, tiled=True)  14.9 us
    all_to_all x1, blocking collectives, gather_gradients(): arrived = lax.all_to_all(value, 'z', 0, 0, tiled=True)  13.9 us
    ppermute x3, starting transfers between devices, local(): lines.append(lax.ppermute(lines[0], 'yhi', ring(far, shift)))  13.6 us
    ppermute x3, starting transfers between devices, local(): lines.append(lax.ppermute(outs[shift], 'yhi', ring(far, -shift)))  13 us
    all_to_all x1, waiting for transfers between devices, spread_out(): return lax.all_to_all(copies, axes, 0, 0, tiled=True)  12.6 us
  transfers between devices with their start and end apart: 11, of which 4 were waited for; matrix products, arithmetic and copies ran while one was open for 1% of the time, Pallas kernels for 0%

profile of v6, /device:TPU:1, one launch (start us, length us, event | category | flops | bytes accessed | tf_op | source)
XLA Modules:
  0.0 193.4 jit_solution(16931179636948205226)
XLA Ops:
  0.6 4.1 %collective-permute-start.3 = (bf16[3072,128]{1,0:T(8,128)(2,1)}, bf16[3072,128]{1,0:T(8,128)(2,1)S(1)}, u32[]{:S(2)}, u32[]{:S(2)}) collective-permute-start(bf16[3072,128]{1,0:T(8,128)(2,1)} %bitcast.63), channel_id=1, source_target_pairs={{0,12},{12,24},{24,36},{36,0},{1,13},{13,25},{25,37},{37,1},{2,14}... | collective-permute-start | bytes 2359304 | tf_op jit(solution)/shard_map/ppermute | solution.py:285
  4.7 1.6 broadcast_in_dim.16
  6.3 14.9 %all-to-all-start.2 = ((bf16[12,128,128]{2,1,0:T(8,128)(2,1)}), bf16[12,128,128]{2,1,0:T(8,128)(2,1)S(1)}, u32[]{:S(2)}, u32[]{:S(2)}) async-start(bf16[12,128,128]{2,1,0:T(8,128)(2,1)} %broadcast_in_dim.16), calls=%async_computation.2 | async-start | bytes 786432 | tf_op jit(solution)/shard_map/all_to_all | solution.py:25
  21.2 3.4 %collective-permute-start.5 = (bf16[3072,128]{1,0:T(8,128)(2,1)S(1)}, bf16[3072,128]{1,0:T(8,128)(2,1)S(1)}, u32[]{:S(2)}, u32[]{:S(2)}) collective-permute-start(bf16[3072,128]{1,0:T(8,128)(2,1)S(1)} %bitcast.64), channel_id=1, source_target_pairs={{0,36},{12,0},{24,12},{36,24},{1,37},{13,1},{25,13},{37,25},{2,38}... | collective-permute-start | bytes 2359304 | tf_op jit(solution)/shard_map/ppermute | solution.py:289
  24.6 1.9 collective-permute-start.4
  27.2 12.6 %all-to-all-done.2.refs_1_ = bf16[12,128,128]{2,1,0:T(8,128)(2,1)S(1)} async-done(((bf16[12,128,128]{2,1,0:T(8,128)(2,1)}), bf16[12,128,128]{2,1,0:T(8,128)(2,1)S(1)}, u32[]{:S(2)}, u32[]{:S(2)}) %all-to-all-start.2) | async-done | bytes 393248 | tf_op jit(solution)/shard_map/all_to_all | solution.py:25
  39.8 5.9 %collective-permute-start.2 = (bf16[12,128,128]{2,1,0:T(8,128)(2,1)S(1)}, bf16[12,128,128]{2,1,0:T(8,128)(2,1)}, u32[]{:S(2)}, u32[]{:S(2)}) collective-permute-start(bf16[12,128,128]{2,1,0:T(8,128)(2,1)S(1)} %all-to-all-done.2.refs_1_), channel_id=1, source_target_pairs={{0,144},{48,0},{96,48},{144,96},{1,145},{49,1},{97,49},{145,97},{2... | collective-permute-start | bytes 1179656 | tf_op jit(solution)/shard_map/ppermute | solution.py:293
  45.7 3.5 %collective-permute-start.1 = (bf16[12,128,128]{2,1,0:T(8,128)(2,1)S(1)}, bf16[12,128,128]{2,1,0:T(8,128)(2,1)}, u32[]{:S(2)}, u32[]{:S(2)}) collective-permute-start(bf16[12,128,128]{2,1,0:T(8,128)(2,1)S(1)} %all-to-all-done.2.refs_1_), channel_id=1, source_target_pairs={{0,96},{48,144},{96,0},{144,48},{1,97},{49,145},{97,1},{145,49},{2... | collective-permute-start | bytes 1179656 | tf_op jit(solution)/shard_map/ppermute | solution.py:293
  49.2 4.2 %collective-permute-start = (bf16[12,128,128]{2,1,0:T(8,128)(2,1)S(1)}, bf16[12,128,128]{2,1,0:T(8,128)(2,1)}, u32[]{:S(2)}, u32[]{:S(2)}) collective-permute-start(bf16[12,128,128]{2,1,0:T(8,128)(2,1)S(1)} %all-to-all-done.2.refs_1_), channel_id=1, source_target_pairs={{0,48},{48,96},{96,144},{144,0},{1,49},{49,97},{97,145},{145,1},{2... | collective-permute-start | bytes 1179656 | tf_op jit(solution)/shard_map/ppermute | solution.py:293
  53.5 0.1 copy.12
  53.6 0.7 copy-done.4
  54.3 0.1 fusion.8
  54.4 10.0 %all-gather = bf16[64,128]{1,0:T(8,128)(2,1)S(1)} all-gather(bf16[16,128]{1,0:T(8,128)(2,1)S(1)} %fusion.8), channel_id=2, replica_groups=mesh['ylo'=2,'core'=2,'yhi'=4,'x'=4,'z'=12] {'x'}, dimensions={0}, use_global_device_ids=true | all-gather | bytes 20480 | tf_op jit(solution)/shard_map/all_gather | solution.py:279
  64.5 4.6 %collective-permute-done.2.refs_2_.refs_4_ = bf16[12,128,128]{2,1,0:T(8,128)(2,1)} collective-permute-done((bf16[12,128,128]{2,1,0:T(8,128)(2,1)S(1)}, bf16[12,128,128]{2,1,0:T(8,128)(2,1)}, u32[]{:S(2)}, u32[]{:S(2)}) %collective-permute-start.2) | collective-permute-done | bytes 393248 | tf_op jit(solution)/shard_map/ppermute | solution.py:293
  69.1 5.9 %collective-permute-done.refs_0_.refs_2_ = bf16[12,128,128]{2,1,0:T(8,128)(2,1)} collective-permute-done((bf16[12,128,128]{2,1,0:T(8,128)(2,1)S(1)}, bf16[12,128,128]{2,1,0:T(8,128)(2,1)}, u32[]{:S(2)}, u32[]{:S(2)}) %collective-permute-start) | collective-permute-done | bytes 393248 | tf_op jit(solution)/shard_map/ppermute | solution.py:293
  75.0 3.0 %forward_tiles.1 = bf16[16,128,128]{2,1,0:T(8,128)(2,1)S(1)} custom-call(s32[4,128]{1,0:T(4,128)S(1)} %tile_codes.1.refs_0_, bf16[12,128,128]{2,1,0:T(8,128)(2,1)S(1)} %all-to-all-done.2.refs_1_, bf16[12,128,128]{2,1,0:T(8,128)(2,1)} %collective-permute-done.refs_0_.refs_2_, bf16[12,128,128]{2,1,0:T(8,128)(2,1)} %collective-permute-done.1.refs_1_.refs_3_, ...), custom_call_target="tpu_custom_call" | custom-call | tf_op jit(solution)/shard_map/forward_tiles/pallas_call | solution.py:306
  78.1 25.4 %all_to_all.30.partials = bf16[16,128,128]{2,1,0:T(8,128)(2,1)S(1)} all-to-all(bf16[16,128,128]{2,1,0:T(8,128)(2,1)S(1)} %forward_tiles.1), channel_id=1, replica_groups=mesh['ylo'=2,'core'=2,'yhi'=4,'x'=4,'z'=12] {'ylo','core','x'}, dimensions={0} | all-to-all | bytes 1048576 | tf_op jit(solution)/shard_map/all_to_all | solution.py:320
  103.5 0.7 copy-done.3
  104.1 1.1 dense_layer.1
  105.2 15.8 %all_to_all.31.refs_1_ = bf16[16,176,128]{2,1,0:T(8,128)(2,1)S(1)} all-to-all(bf16[16,176,128]{2,1,0:T(8,128)(2,1)S(1)} %get-tuple-element.21), channel_id=1, replica_groups=mesh['ylo'=2,'core'=2,'yhi'=4,'x'=4,'z'=12] {'ylo','core','x'}, dimensions={0} | all-to-all | bytes 1441792 | tf_op jit(solution)/shard_map/all_to_all | solution.py:334
  121.0 3.7 %backward_tiles.1 = (bf16[12,128,128]{2,1,0:T(8,128)(2,1)S(1)}, bf16[12,128,128]{2,1,0:T(8,128)(2,1)}, bf16[12,128,128]{2,1,0:T(8,128)(2,1)}, bf16[12,128,128]{2,1,0:T(8,128)(2,1)}, bf16[12,48,128]{2,1,0:T(8,128)(2,1)}) custom-call(s32[4,128]{1,0:T(4,128)S(1)} %tile_codes.1.refs_0_, bf16[16,176,128]{2,1,0:T(8,128)(2,1)S(1)} %all_to_all.31.refs_1_, ...), custom_call_target="tpu_custom_call" | custom-call | tf_op jit(solution)/shard_map/backward_tiles/pallas_call | solution.py:336
  124.7 4.7 %collective-permute-start.6 = (bf16[12,128,128]{2,1,0:T(8,128)(2,1)}, bf16[12,128,128]{2,1,0:T(8,128)(2,1)S(1)}, u32[]{:S(2)}, u32[]{:S(2)}) collective-permute-start(bf16[12,128,128]{2,1,0:T(8,128)(2,1)} %get-tuple-element.23), channel_id=1, source_target_pairs={{0,144},{48,0},{96,48},{144,96},{1,145},{49,1},{97,49},{145,97},{2... | collective-permute-start | bytes 1179656 | tf_op jit(solution)/shard_map/ppermute | solution.py:362
  129.4 4.1 %collective-permute-start.7 = (bf16[12,128,128]{2,1,0:T(8,128)(2,1)}, bf16[12,128,128]{2,1,0:T(8,128)(2,1)S(1)}, u32[]{:S(2)}, u32[]{:S(2)}) collective-permute-start(bf16[12,128,128]{2,1,0:T(8,128)(2,1)} %get-tuple-element.24), channel_id=1, source_target_pairs={{0,96},{48,144},{96,0},{144,48},{1,97},{49,145},{97,1},{145,49},{2... | collective-permute-start | bytes 1179656 | tf_op jit(solution)/shard_map/ppermute | solution.py:362
  133.5 4.3 %collective-permute-start.8 = (bf16[12,128,128]{2,1,0:T(8,128)(2,1)}, bf16[12,128,128]{2,1,0:T(8,128)(2,1)S(1)}, u32[]{:S(2)}, u32[]{:S(2)}) collective-permute-start(bf16[12,128,128]{2,1,0:T(8,128)(2,1)} %get-tuple-element.25), channel_id=1, source_target_pairs={{0,48},{48,96},{96,144},{144,0},{1,49},{49,97},{97,145},{145,1},{2... | collective-permute-start | bytes 1179656 | tf_op jit(solution)/shard_map/ppermute | solution.py:362
  137.7 31.3 %conditional.1 = (bf16[272,128]{1,0:T(8,128)(2,1)S(1)}) conditional(s32[]{:T(128)} %convert_element_type.4, () %tuple.14, bf16[12,48,128]{2,1,0:T(8,128)(2,1)} %get-tuple-element.26), branch_computations={%region_0.1_spmd, %region_1.2_spmd} | conditional | bytes 557064 | solution.py:387
  137.8 13.9 %all_to_all.28.refs_0_ = bf16[12,48,128]{2,1,0:T(8,128)(2,1)S(1)} all-to-all(bf16[12,48,128]{2,1,0:T(8,128)(2,1)} %param.1), channel_id=1, replica_groups=mesh['ylo'=2,'core'=2,'yhi'=4,'x'=4,'z'=12] {'z'}, dimensions={0} | all-to-all | bytes 294912 | tf_op jit(solution)/shard_map/cond/branch_1_fun/all_to_all | solution.py:365
  151.7 17.3 %all_to_all.29.refs_0_ = f32[16,16,128]{2,1,0:T(8,128)S(1)} all-to-all(f32[16,16,128]{2,1,0:T(8,128)S(1)} %get-tuple-element.4), channel_id=1, replica_groups=mesh['ylo'=2,'core'=2,'yhi'=4,'x'=4,'z'=12] {'ylo','core','x'}, dimensions={0} | all-to-all | bytes 262144 | tf_op jit(solution)/shard_map/cond/branch_1_fun/all_to_all | solution.py:377
  169.0 0.9 middle_sums.1
  170.0 4.2 %all-to-all-start.5 = ((bf16[12,128,128]{2,1,0:T(8,128)(2,1)}), bf16[12,128,128]{2,1,0:T(8,128)(2,1)S(1)}, u32[]{:S(2)}, u32[]{:S(2)}) async-start(bf16[12,128,128]{2,1,0:T(8,128)(2,1)} %middle_sums.1), calls=%async_computation.5 | async-start | bytes 786432 | tf_op jit(solution)/shard_map/all_to_all | solution.py:403
  174.2 11.7 %all-gather.1 = bf16[1088,128]{1,0:T(8,128)(2,1)S(1)} all-gather(bf16[272,128]{1,0:T(8,128)(2,1)S(1)} %get-tuple-element.33.refs_4_), channel_id=3, replica_groups=mesh['ylo'=2,'core'=2,'yhi'=4,'x'=4,'z'=12] {'yhi'}, dimensions={0}, use_global_device_ids=true | all-gather | bytes 348160 | tf_op jit(solution)/shard_map/all_gather | solution.py:402
  185.9 6.8 %all-to-all-done.5.refs_0_ = bf16[12,128,128]{2,1,0:T(8,128)(2,1)S(1)} async-done(((bf16[12,128,128]{2,1,0:T(8,128)(2,1)}), bf16[12,128,128]{2,1,0:T(8,128)(2,1)S(1)}, u32[]{:S(2)}, u32[]{:S(2)}) %all-to-all-start.5) | async-done | bytes 393248 | tf_op jit(solution)/shard_map/all_to_all | solution.py:403
  192.6 0.7 last_sums.1
  (22 shorter events, 0.2 us)
Async XLA Ops:
  0.6 20.6 %copy-start = (bf16[1,1,48,64,128]{4,3,2,1,0:T(8,128)(2,1)S(1)}, bf16[1,1,48,64,128]{4,3,2,1,0:T(8,128)(2,1)}, u32[]{:S(2)}) copy-start(bf16[1,1,48,64,128]{4,3,2,1,0:T(8,128)(2,1)} %param.14) | copy-start | bytes 2359300
  0.6 23.9 %collective-permute-start.3 = (bf16[3072,128]{1,0:T(8,128)(2,1)}, bf16[3072,128]{1,0:T(8,128)(2,1)S(1)}, u32[]{:S(2)}, u32[]{:S(2)}) collective-permute-start(bf16[3072,128]{1,0:T(8,128)(2,1)} %bitcast.63), channel_id=1, source_target_pairs={{0,12},{12,24},{24,36},{36,0},{1,13},{13,25},{25,37},{37,1},{2,14}... | collective-permute-start | bytes 2359304 | tf_op jit(solution)/shard_map/ppermute | solution.py:285
  6.3 33.5 %all-to-all-start.2 = ((bf16[12,128,128]{2,1,0:T(8,128)(2,1)}), bf16[12,128,128]{2,1,0:T(8,128)(2,1)S(1)}, u32[]{:S(2)}, u32[]{:S(2)}) async-start(bf16[12,128,128]{2,1,0:T(8,128)(2,1)} %broadcast_in_dim.16), calls=%async_computation.2 | async-start | bytes 786432 | tf_op jit(solution)/shard_map/all_to_all | solution.py:25
  21.2 53.8 %collective-permute-start.5 = (bf16[3072,128]{1,0:T(8,128)(2,1)S(1)}, bf16[3072,128]{1,0:T(8,128)(2,1)S(1)}, u32[]{:S(2)}, u32[]{:S(2)}) collective-permute-start(bf16[3072,128]{1,0:T(8,128)(2,1)S(1)} %bitcast.64), channel_id=1, source_target_pairs={{0,36},{12,0},{24,12},{36,24},{1,37},{13,1},{25,13},{37,25},{2,38}... | collective-permute-start | bytes 2359304 | tf_op jit(solution)/shard_map/ppermute | solution.py:289
  24.6 50.4 %collective-permute-start.4 = (bf16[3072,128]{1,0:T(8,128)(2,1)S(1)}, bf16[3072,128]{1,0:T(8,128)(2,1)S(1)}, u32[]{:S(2)}, u32[]{:S(2)}) collective-permute-start(bf16[3072,128]{1,0:T(8,128)(2,1)S(1)} %collective-permute-done.3.refs_6_.refs_3_), channel_id=1, source_target_pairs={{0,12},{12,24},{24,36},{36,0},{1,13},{13,25},{25,37},{37,1},{2,14}... | collective-permute-start | bytes 2359304 | tf_op jit(solution)/shard_map/ppermute | solution.py:287
  39.8 29.3 %collective-permute-start.2 = (bf16[12,128,128]{2,1,0:T(8,128)(2,1)S(1)}, bf16[12,128,128]{2,1,0:T(8,128)(2,1)}, u32[]{:S(2)}, u32[]{:S(2)}) collective-permute-start(bf16[12,128,128]{2,1,0:T(8,128)(2,1)S(1)} %all-to-all-done.2.refs_1_), channel_id=1, source_target_pairs={{0,144},{48,0},{96,48},{144,96},{1,145},{49,1},{97,49},{145,97},{2... | collective-permute-start | bytes 1179656 | tf_op jit(solution)/shard_map/ppermute | solution.py:293
  45.7 23.4 %collective-permute-start.1 = (bf16[12,128,128]{2,1,0:T(8,128)(2,1)S(1)}, bf16[12,128,128]{2,1,0:T(8,128)(2,1)}, u32[]{:S(2)}, u32[]{:S(2)}) collective-permute-start(bf16[12,128,128]{2,1,0:T(8,128)(2,1)S(1)} %all-to-all-done.2.refs_1_), channel_id=1, source_target_pairs={{0,96},{48,144},{96,0},{144,48},{1,97},{49,145},{97,1},{145,49},{2... | collective-permute-start | bytes 1179656 | tf_op jit(solution)/shard_map/ppermute | solution.py:293
  49.2 25.8 %collective-permute-start = (bf16[12,128,128]{2,1,0:T(8,128)(2,1)S(1)}, bf16[12,128,128]{2,1,0:T(8,128)(2,1)}, u32[]{:S(2)}, u32[]{:S(2)}) collective-permute-start(bf16[12,128,128]{2,1,0:T(8,128)(2,1)S(1)} %all-to-all-done.2.refs_1_), channel_id=1, source_target_pairs={{0,48},{48,96},{96,144},{144,0},{1,49},{49,97},{97,145},{145,1},{2... | collective-permute-start | bytes 1179656 | tf_op jit(solution)/shard_map/ppermute | solution.py:293
  53.6 0.7 copy-start.4
  53.6 0.7 copy-start.5
  78.0 25.4 %copy-start.1 = (bf16[128,256]{1,0:T(8,128)(2,1)S(1)}, bf16[128,256]{1,0:T(8,128)(2,1)}, u32[]{:S(2)}) copy-start(bf16[128,256]{1,0:T(8,128)(2,1)} %weight.1) | copy-start | bytes 196612
  78.1 25.4 %copy-start.2 = (bf16[128,256]{1,0:T(8,128)(2,1)S(1)}, bf16[128,256]{1,0:T(8,128)(2,1)}, u32[]{:S(2)}) copy-start(bf16[128,256]{1,0:T(8,128)(2,1)} %cotangent.1) | copy-start | bytes 196612
  103.4 0.7 copy-start.3
  124.7 44.3 %collective-permute-start.6 = (bf16[12,128,128]{2,1,0:T(8,128)(2,1)}, bf16[12,128,128]{2,1,0:T(8,128)(2,1)S(1)}, u32[]{:S(2)}, u32[]{:S(2)}) collective-permute-start(bf16[12,128,128]{2,1,0:T(8,128)(2,1)} %get-tuple-element.23), channel_id=1, source_target_pairs={{0,144},{48,0},{96,48},{144,96},{1,145},{49,1},{97,49},{145,97},{2... | collective-permute-start | bytes 1179656 | tf_op jit(solution)/shard_map/ppermute | solution.py:362
  129.4 39.6 %collective-permute-start.7 = (bf16[12,128,128]{2,1,0:T(8,128)(2,1)}, bf16[12,128,128]{2,1,0:T(8,128)(2,1)S(1)}, u32[]{:S(2)}, u32[]{:S(2)}) collective-permute-start(bf16[12,128,128]{2,1,0:T(8,128)(2,1)} %get-tuple-element.24), channel_id=1, source_target_pairs={{0,96},{48,144},{96,0},{144,48},{1,97},{49,145},{97,1},{145,49},{2... | collective-permute-start | bytes 1179656 | tf_op jit(solution)/shard_map/ppermute | solution.py:362
  133.5 35.6 %collective-permute-start.8 = (bf16[12,128,128]{2,1,0:T(8,128)(2,1)}, bf16[12,128,128]{2,1,0:T(8,128)(2,1)S(1)}, u32[]{:S(2)}, u32[]{:S(2)}) collective-permute-start(bf16[12,128,128]{2,1,0:T(8,128)(2,1)} %get-tuple-element.25), channel_id=1, source_target_pairs={{0,48},{48,96},{96,144},{144,0},{1,49},{49,97},{97,145},{145,1},{2... | collective-permute-start | bytes 1179656 | tf_op jit(solution)/shard_map/ppermute | solution.py:362
  170.0 22.7 %all-to-all-start.5 = ((bf16[12,128,128]{2,1,0:T(8,128)(2,1)}), bf16[12,128,128]{2,1,0:T(8,128)(2,1)S(1)}, u32[]{:S(2)}, u32[]{:S(2)}) async-start(bf16[12,128,128]{2,1,0:T(8,128)(2,1)} %middle_sums.1), calls=%async_computation.5 | async-start | bytes 786432 | tf_op jit(solution)/shard_map/all_to_all | solution.py:403

commit v7 on v6

--- a/solution.py
+++ b/solution.py
@@ -13,6 +13,7 @@
 row_axes = ("ylo", "core")
 col_axes = ("yhi", "x", "z")
 team_axes = ("ylo", "core", "x")
+back_rows = 112
 group = 4
 lanes = 128
 vmem_bytes = 12 * 1024 * 1024
@@ -55,12 +56,13 @@
     return total
 
 
-def forward_kernel(codes, *refs, slots, height, blocks, far, across):
+def forward_kernel(codes, *refs, slots, height, blocks, line_order, across):
+    far = len(line_order)
     lines, tile_refs = refs[:far], refs[far : far + across]
     out, slabs, chosen, totals, picked = refs[far + across :]
     slab_count = slabs.shape[0]
     near = slab_count // far
-    for shift, line in enumerate(lines):
+    for shift, line in zip(line_order, lines):
         slabs[pl.ds(shift * near, near)] = line[...]
     dummy = slab_count * 64 + blocks
     totals[...] = jnp.zeros_like(totals)
@@ -192,9 +194,13 @@
 
     lax.fori_loop(0, (total + group - 1) // group, body, 0)
     near = slab_count // far
+    ahead = outs[0].shape[1]
+    rest = nodes - ahead
     for shift, out in enumerate(outs):
         for index in range(near):
-            out[index] = totals[shift * near + index].astype(jnp.bfloat16)
+            total = totals[shift * near + index].astype(jnp.bfloat16)
+            out[index] = total[:ahead]
+            shares[index, pl.ds(4 * share + 16 + shift * rest, rest), :] = total[ahead:]
     weight_sum = sum_rows(spreads, nodes, 2 * share) + sum_rows(spreads, nodes + 2 * share, 2 * share)
     high, low = split_wide(weight_sum)
     bias_block = pack_bias(sum_bias(spreads, nodes + 4 * share))
@@ -204,22 +210,27 @@
         shares[index, pl.ds(4 * share, 16), :] = bias_block
 
 
-def share_kernel(arrived, out, bias_block, *, share):
+def share_kernel(arrived, out, bias_block, rest_sums, *, share):
     total = sum_rows(arrived, 0, 2 * share) + sum_rows(arrived, 2 * share, 2 * share)
     for index in range(out.shape[0]):
         out[index] = total
     bias_block[...] = pack_bias(sum_bias(arrived, 4 * share))
-
-
-def gather_kernel(shares, bias_block, out, *, share):
+    rest_sums[...] = sum_rows(arrived, 4 * share + 16, rest_sums.shape[0]).astype(jnp.bfloat16)
+
+
+def gather_kernel(shares, bias_block, rest_sums, *outs, share):
     step = 16 // share if share < 16 else 1
     rows = shares.shape[0] * share
+    rest = rest_sums.shape[0] // len(outs)
     for half in range(2):
         for first in range(0, shares.shape[0], step):
             parts = [shares[first + sub, pl.ds(half * share, share), :] for sub in range(step)]
             part = jnp.concatenate(parts, axis=0) if step > 1 else parts[0]
-            out[pl.ds(half * rows + first * share, step * share), :] = part.astype(jnp.bfloat16)
-    out[pl.ds(2 * rows, 16), :] = bias_block[...]
+            for out in outs:
+                out[pl.ds(half * rows + first * share, step * share), :] = part.astype(jnp.bfloat16)
+    for shift, out in enumerate(outs):
+        out[pl.ds(2 * rows, 16), :] = bias_block[...]
+        out[pl.ds(2 * rows + 16, rest), :] = rest_sums[pl.ds(shift * rest, rest), :]
 
 
 def middle_kernel(*refs, far):
@@ -231,14 +242,20 @@
         out[index] = total.astype(jnp.bfloat16)
 
 
-def last_kernel(arrived, pieces, grad, weight_grad, bias_grad, *, factor):
-    grad[...] = sum_rows(arrived, 0, grad.shape[0])
+def last_kernel(place, arrived, *refs, far, factor):
+    grad, weight_grad, bias_grad, stack = refs[far:]
+    ahead = arrived.shape[1]
+    rest = grad.shape[0] - ahead
+    for shift, piece in enumerate(refs[:far]):
+        stack[lax.rem(place[0] + shift, far)] = piece[...]
     rows = weight_grad.shape[0]
-    weight_grad[:, pl.ds(0, lanes)] = sum_rows(pieces, 0, rows) * factor
-    weight_grad[:, pl.ds(lanes, lanes)] = sum_rows(pieces, rows, rows) * factor
-    low, high = sum_bias(pieces, 2 * rows)
+    weight_grad[:, pl.ds(0, lanes)] = sum_rows(stack, 0, rows) * factor
+    weight_grad[:, pl.ds(lanes, lanes)] = sum_rows(stack, rows, rows) * factor
+    low, high = sum_bias(stack, 2 * rows)
     bias_grad[:, pl.ds(0, lanes)] = low * factor
     bias_grad[:, pl.ds(lanes, lanes)] = high * factor
+    grad[pl.ds(0, ahead), :] = sum_rows(arrived, 0, ahead)
+    grad[pl.ds(ahead, rest), :] = sum_rows(stack, 2 * rows + 16, rest)
 
 
 def in_vmem():
@@ -281,6 +298,8 @@
     def ring(size, shift):
         return [(start, (start + shift) % size) for start in range(size)]
 
+    longest_first = sorted(range(1, far), key=lambda shift: -min(shift, far - shift))
+
     own = tile_values[0, 0].reshape(slots * height, tile_width)
     buffers = [own, lax.ppermute(own, "x", ring(across, 1))]
     for shift in range(2, across - 1):
@@ -289,7 +308,8 @@
         buffers.append(lax.ppermute(own, "x", ring(across, -1)))
 
     lines = [spread_out(features, "z", near)]
-    for shift in range(1, far):
+    line_order = [0] + longest_first[::-1]
+    for shift in line_order[1:]:
         lines.append(lax.ppermute(lines[0], "yhi", ring(far, shift)))
 
     codes = pl.pallas_call(
@@ -304,7 +324,14 @@
     scratch_tiles = pltpu.VMEM((across * slots + group, height, tile_width), jnp.bfloat16)
     scratch_list = pltpu.SMEM((across * slots + group,), jnp.int32)
     partial = pl.pallas_call(
-        lambda *refs: forward_kernel(*refs, slots=slots, height=height, blocks=blocks, far=far, across=across),
+        lambda *refs: forward_kernel(
+            *refs,
+            slots=slots,
+            height=height,
+            blocks=blocks,
+            line_order=line_order,
+            across=across,
+        ),
         out_shape=jax.ShapeDtypeStruct((members, nodes, width), jnp.bfloat16),
         in_specs=[in_smem()] + [in_vmem()] * (far + across),
         out_specs=in_vmem(),
@@ -333,6 +360,7 @@
     )(partials, weight, bias.reshape(1, hidden), cotangent)
     spreads = lax.all_to_all(message, team_axes, 0, 0, tiled=True)
 
+    rest = nodes - back_rows
     outs = pl.pallas_call(
         lambda *refs: backward_kernel(
             *refs,
@@ -344,8 +372,8 @@
             far=far,
             across=across,
         ),
-        out_shape=(jax.ShapeDtypeStruct((near, nodes, width), jnp.bfloat16),) * far
-        + (jax.ShapeDtypeStruct((near, 4 * share + 16, width), jnp.bfloat16),),
+        out_shape=(jax.ShapeDtypeStruct((near, back_rows, width), jnp.bfloat16),) * far
+        + (jax.ShapeDtypeStruct((near, 4 * share + 16 + far * rest, width), jnp.bfloat16),),
         in_specs=[in_smem(), in_vmem()] + [in_vmem()] * across,
         out_specs=(in_vmem(),) * (far + 1),
         scratch_shapes=[
@@ -358,62 +386,68 @@
     )(codes, spreads, *buffers)
 
     lines = [outs[0]]
-    for shift in range(1, far):
+    for shift in longest_first:
         lines.append(lax.ppermute(outs[shift], "yhi", ring(far, -shift)))
+
+    gradients_shape = (2 * width + 16 + rest, lanes)
 
     def gather_gradients(value):
         arrived = lax.all_to_all(value, "z", 0, 0, tiled=True)
-        shares, bias_block = pl.pallas_call(
+        shares, bias_block, rest_sums = pl.pallas_call(
             lambda *refs: share_kernel(*refs, share=share),
             out_shape=(
                 jax.ShapeDtypeStruct((members, 2 * share, lanes), jnp.float32),
                 jax.ShapeDtypeStruct((16, lanes), jnp.bfloat16),
+                jax.ShapeDtypeStruct((far * rest, width), jnp.bfloat16),
             ),
             in_specs=[in_vmem()],
-            out_specs=(in_vmem(), in_vmem()),
+            out_specs=(in_vmem(), in_vmem(), in_vmem()),
             compiler_params=params,
             name="share_sum",
         )(arrived)
         shares = lax.all_to_all(shares, team_axes, 0, 0, tiled=True)
         return pl.pallas_call(
             lambda *refs: gather_kernel(*refs, share=share),
-            out_shape=jax.ShapeDtypeStruct((2 * width + 16, lanes), jnp.bfloat16),
-            in_specs=[in_vmem(), in_vmem()],
-            out_specs=in_vmem(),
+            out_shape=(jax.ShapeDtypeStruct(gradients_shape, jnp.bfloat16),) * far,
+            in_specs=[in_vmem()] * 3,
+            out_specs=(in_vmem(),) * far,
             compiler_params=params,
             name="share_gather",
-        )(shares, bias_block)
+        )(shares, bias_block, rest_sums)
 
     gradients = lax.cond(
         tile_counts[0, 0] > 0,
         gather_gradients,
-        lambda value: jnp.zeros((2 * width + 16, lanes), jnp.bfloat16),
+        lambda value: (jnp.zeros(gradients_shape, jnp.bfloat16),) * far,
         outs[far],
     )
     line = pl.pallas_call(
         lambda *refs: middle_kernel(*refs, far=far),
-        out_shape=jax.ShapeDtypeStruct((near, nodes, width), jnp.bfloat16),
+        out_shape=jax.ShapeDtypeStruct((near, back_rows, width), jnp.bfloat16),
         in_specs=[in_vmem()] * far + [any_place()],
         out_specs=in_vmem(),
         compiler_params=params,
         name="middle_sums",
-    )(*lines, gradients)
-
-    pieces = lax.all_gather(gradients, "yhi", axis=0)
+    )(*lines, gradients[0])
+
+    pieces = [gradients[0]]
+    for shift in range(1, far):
+        pieces.append(lax.ppermute(gradients[shift], "yhi", ring(far, -shift)))
     arrived = lax.all_to_all(line, "z", 0, 0, tiled=True)
     factor = 1.0 / math.sqrt(nodes * group_rows * far * across * near)
     features_grad, weight_grad, bias_grad = pl.pallas_call(
-        lambda *refs: last_kernel(*refs, factor=factor),
+        lambda *refs: last_kernel(*refs, far=far, factor=factor),
         out_shape=(
             jax.ShapeDtypeStruct((nodes, width), jnp.float32),
             jax.ShapeDtypeStruct((width, hidden), jnp.float32),
             jax.ShapeDtypeStruct((1, hidden), jnp.float32),
         ),
-        in_specs=[in_vmem(), in_vmem()],
+        in_specs=[in_smem()] + [in_vmem()] * (far + 1),
         out_specs=(in_vmem(), in_vmem(), in_vmem()),
+        scratch_shapes=[pltpu.VMEM((far,) + gradients_shape, jnp.bfloat16)],
         compiler_params=params,
         name="last_sums",
-    )(arrived, pieces)
+    )(lax.axis_index("yhi").reshape(1), arrived, *pieces)
     return (hidden_out, features_grad, weight_grad, bias_grad.reshape(hidden))
 
 

time: 197 us -> 192 us (0.975)
  blocking collectives: 94 us -> 75.5 us
  starting transfers between devices: 55.1 us -> 65.3 us
  waiting for transfers between devices: 29.9 us -> 36.2 us
    all_gather x1 -> x0, blocking collectives: 11.7 us -> none  [local(): pieces = lax.all_gather(gradients, 'yhi', axis=0)]
    ppermute x0 -> x3, starting transfers between devices: none -> 10.9 us  [local(): pieces.append(lax.ppermute(gradients[shift], 'yhi', ring(far, -shift)))]
    all_to_all x1, blocking collectives: 25.4 us -> 15.6 us  [local(): partials = lax.all_to_all(partial, team_axes, 0, 0, tiled=True)]
    all_to_all x1, blocking collectives: 13.9 us -> 22.8 us  [gather_gradients(): arrived = lax.all_to_all(value, 'z', 0, 0, tiled=True)]
    ppermute x3, waiting for transfers between devices: 10.5 us -> 17.3 us  [local(): lines.append(lax.ppermute(lines[0], 'yhi', ring(far, shift)))]
    all_to_all x1, waiting for transfers between devices: 6.76 us -> 0.35 us  [local(): arrived = lax.all_to_all(line, 'z', 0, 0, tiled=True)]
    all_to_all x1, blocking collectives: 17.3 us -> 11.3 us  [gather_gradients(): shares = lax.all_to_all(shares, team_axes, 0, 0, tiled=True)]
    ppermute x0 -> x3, waiting for transfers between devices: none -> 5.92 us  [local(): pieces.append(lax.ppermute(gradients[shift], 'yhi', ring(far, -shift)))]
  transfers between devices with their start and end apart: 11 -> 14, of which waited for: 4 -> 6; matrix products, arithmetic and copies ran while one was open for 1% -> 1% of each run, Pallas kernels for 0% -> 0%
where the time goes in v7:
time: 192 us; the launch traced here: 190 us
  blocking collectives  75.5 us (39%)
  starting transfers between devices  65.3 us (34%)
  waiting for transfers between devices  36.2 us (19%)
  Pallas kernels  8.16 us (4%)
  local copies, waits for them, and re-layouts  3.05 us (2%)
    all_to_all x1, blocking collectives, gather_gradients(): arrived = lax.all_to_all(value, 'z', 0, 0, tiled=True)  22.8 us
    ppermute x3, waiting for transfers between devices, local(): lines.append(lax.ppermute(lines[0], 'yhi', ring(far, shift)))  17.3 us
    all_to_all x1, blocking collectives, local(): spreads = lax.all_to_all(message, team_axes, 0, 0, tiled=True)  15.8 us
    all_to_all x1, blocking collectives, local(): partials = lax.all_to_all(partial, team_axes, 0, 0, tiled=True)  15.6 us
    all_to_all x1, starting transfers between devices, spread_out(): return lax.all_to_all(copies, axes, 0, 0, tiled=True)  14.9 us
    ppermute x3, starting transfers between devices, local(): lines.append(lax.ppermute(lines[0], 'yhi', ring(far, shift)))  14.8 us
    all_to_all x1, waiting for transfers between devices, spread_out(): return lax.all_to_all(copies, axes, 0, 0, tiled=True)  12.6 us
    ppermute x3, starting transfers between devices, local(): lines.append(lax.ppermute(outs[shift], 'yhi', ring(far, -shift)))  11.4 us
  transfers between devices with their start and end apart: 14, of which 6 were waited for; matrix products, arithmetic and copies ran while one was open for 1% of the time, Pallas kernels for 0%

profile of v7, /device:TPU:1, one launch (start us, length us, event | category | flops | bytes accessed | tf_op | source)
XLA Modules:
  0.0 189.9 jit_solution(5015224282428284984)
XLA Ops:
  0.6 4.1 %collective-permute-start.3 = (bf16[3072,128]{1,0:T(8,128)(2,1)}, bf16[3072,128]{1,0:T(8,128)(2,1)S(1)}, u32[]{:S(2)}, u32[]{:S(2)}) collective-permute-start(bf16[3072,128]{1,0:T(8,128)(2,1)} %bitcast.63), channel_id=1, source_target_pairs={{0,12},{12,24},{24,36},{36,0},{1,13},{13,25},{25,37},{37,1},{2,14}... | collective-permute-start | bytes 2359304 | tf_op jit(solution)/shard_map/ppermute | solution.py:304
  4.7 1.6 broadcast_in_dim.16
  6.3 14.9 %all-to-all-start.2 = ((bf16[12,128,128]{2,1,0:T(8,128)(2,1)}), bf16[12,128,128]{2,1,0:T(8,128)(2,1)S(1)}, u32[]{:S(2)}, u32[]{:S(2)}) async-start(bf16[12,128,128]{2,1,0:T(8,128)(2,1)} %broadcast_in_dim.16), calls=%async_computation.2 | async-start | bytes 786432 | tf_op jit(solution)/shard_map/all_to_all | solution.py:26
  21.2 3.4 %collective-permute-start.5 = (bf16[3072,128]{1,0:T(8,128)(2,1)S(1)}, bf16[3072,128]{1,0:T(8,128)(2,1)S(1)}, u32[]{:S(2)}, u32[]{:S(2)}) collective-permute-start(bf16[3072,128]{1,0:T(8,128)(2,1)S(1)} %bitcast.64), channel_id=1, source_target_pairs={{0,36},{12,0},{24,12},{36,24},{1,37},{13,1},{25,13},{37,25},{2,38}... | collective-permute-start | bytes 2359304 | tf_op jit(solution)/shard_map/ppermute | solution.py:308
  24.6 1.9 %collective-permute-start.4 = (bf16[3072,128]{1,0:T(8,128)(2,1)S(1)}, bf16[3072,128]{1,0:T(8,128)(2,1)S(1)}, u32[]{:S(2)}, u32[]{:S(2)}) collective-permute-start(bf16[3072,128]{1,0:T(8,128)(2,1)S(1)} %collective-permute-done.3.refs_6_.refs_3_), channel_id=1, source_target_pairs={{0,12},{12,24},{24,36},{36,0},{1,13},{13,25},{25,37},{37,1},{2,14}... | collective-permute-start | bytes 2359304 | tf_op jit(solution)/shard_map/ppermute | solution.py:306
  27.2 12.6 %all-to-all-done.2.refs_1_ = bf16[12,128,128]{2,1,0:T(8,128)(2,1)S(1)} async-done(((bf16[12,128,128]{2,1,0:T(8,128)(2,1)}), bf16[12,128,128]{2,1,0:T(8,128)(2,1)S(1)}, u32[]{:S(2)}, u32[]{:S(2)}) %all-to-all-start.2) | async-done | bytes 393248 | tf_op jit(solution)/shard_map/all_to_all | solution.py:26
  39.8 7.4 %collective-permute-start.2 = (bf16[12,128,128]{2,1,0:T(8,128)(2,1)S(1)}, bf16[12,128,128]{2,1,0:T(8,128)(2,1)}, u32[]{:S(2)}, u32[]{:S(2)}) collective-permute-start(bf16[12,128,128]{2,1,0:T(8,128)(2,1)S(1)} %all-to-all-done.2.refs_1_), channel_id=1, source_target_pairs={{0,96},{48,144},{96,0},{144,48},{1,97},{49,145},{97,1},{145,49},{2... | collective-permute-start | bytes 1179656 | tf_op jit(solution)/shard_map/ppermute | solution.py:313
  47.3 2.4 %collective-permute-start.1 = (bf16[12,128,128]{2,1,0:T(8,128)(2,1)S(1)}, bf16[12,128,128]{2,1,0:T(8,128)(2,1)}, u32[]{:S(2)}, u32[]{:S(2)}) collective-permute-start(bf16[12,128,128]{2,1,0:T(8,128)(2,1)S(1)} %all-to-all-done.2.refs_1_), channel_id=1, source_target_pairs={{0,48},{48,96},{96,144},{144,0},{1,49},{49,97},{97,145},{145,1},{2... | collective-permute-start | bytes 1179656 | tf_op jit(solution)/shard_map/ppermute | solution.py:313
  49.7 5.0 %collective-permute-start = (bf16[12,128,128]{2,1,0:T(8,128)(2,1)S(1)}, bf16[12,128,128]{2,1,0:T(8,128)(2,1)}, u32[]{:S(2)}, u32[]{:S(2)}) collective-permute-start(bf16[12,128,128]{2,1,0:T(8,128)(2,1)S(1)} %all-to-all-done.2.refs_1_), channel_id=1, source_target_pairs={{0,144},{48,0},{96,48},{144,96},{1,145},{49,1},{97,49},{145,97},{2... | collective-permute-start | bytes 1179656 | tf_op jit(solution)/shard_map/ppermute | solution.py:313
  55.6 10.0 %all-gather = bf16[64,128]{1,0:T(8,128)(2,1)S(1)} all-gather(bf16[16,128]{1,0:T(8,128)(2,1)S(1)} %fusion.8), channel_id=2, replica_groups=mesh['ylo'=2,'core'=2,'yhi'=4,'x'=4,'z'=12] {'x'}, dimensions={0}, use_global_device_ids=true | all-gather | bytes 20480 | tf_op jit(solution)/shard_map/all_gather | solution.py:296
  65.7 8.2 %collective-permute-done.1.refs_1_.refs_3_ = bf16[12,128,128]{2,1,0:T(8,128)(2,1)} collective-permute-done((bf16[12,128,128]{2,1,0:T(8,128)(2,1)S(1)}, bf16[12,128,128]{2,1,0:T(8,128)(2,1)}, u32[]{:S(2)}, u32[]{:S(2)}) %collective-permute-start.1) | collective-permute-done | bytes 393248 | tf_op jit(solution)/shard_map/ppermute | solution.py:313
  73.9 9.0 %collective-permute-done.refs_0_.refs_2_ = bf16[12,128,128]{2,1,0:T(8,128)(2,1)} collective-permute-done((bf16[12,128,128]{2,1,0:T(8,128)(2,1)S(1)}, bf16[12,128,128]{2,1,0:T(8,128)(2,1)}, u32[]{:S(2)}, u32[]{:S(2)}) %collective-permute-start) | collective-permute-done | bytes 393248 | tf_op jit(solution)/shard_map/ppermute | solution.py:313
  83.0 2.4 %forward_tiles.1 = bf16[16,128,128]{2,1,0:T(8,128)(2,1)S(1)} custom-call(s32[4,128]{1,0:T(4,128)S(1)} %tile_codes.1.refs_0_, bf16[12,128,128]{2,1,0:T(8,128)(2,1)S(1)} %all-to-all-done.2.refs_1_, bf16[12,128,128]{2,1,0:T(8,128)(2,1)} %collective-permute-done.refs_0_.refs_2_, bf16[12,128,128]{2,1,0:T(8,128)(2,1)} %collective-permute-done.1.refs_1_.refs_3_, ...), custom_call_target="tpu_custom_call" | custom-call | tf_op jit(solution)/shard_map/forward_tiles/pallas_call | solution.py:326
  85.4 15.6 %all_to_all.30.partials = bf16[16,128,128]{2,1,0:T(8,128)(2,1)S(1)} all-to-all(bf16[16,128,128]{2,1,0:T(8,128)(2,1)S(1)} %forward_tiles.1), channel_id=1, replica_groups=mesh['ylo'=2,'core'=2,'yhi'=4,'x'=4,'z'=12] {'ylo','core','x'}, dimensions={0} | all-to-all | bytes 1048576 | tf_op jit(solution)/shard_map/all_to_all | solution.py:347
  101.0 0.7 copy-done.3
  101.6 1.1 dense_layer.1
  102.7 15.8 %all_to_all.31.refs_1_ = bf16[16,176,128]{2,1,0:T(8,128)(2,1)S(1)} all-to-all(bf16[16,176,128]{2,1,0:T(8,128)(2,1)S(1)} %get-tuple-element.23), channel_id=1, replica_groups=mesh['ylo'=2,'core'=2,'yhi'=4,'x'=4,'z'=12] {'ylo','core','x'}, dimensions={0} | all-to-all | bytes 1441792 | tf_op jit(solution)/shard_map/all_to_all | solution.py:361
  118.5 3.0 %backward_tiles.1 = (bf16[12,112,128]{2,1,0:T(8,128)(2,1)S(1)}, bf16[12,112,128]{2,1,0:T(8,128)(2,1)}, bf16[12,112,128]{2,1,0:T(8,128)(2,1)}, bf16[12,112,128]{2,1,0:T(8,128)(2,1)}, bf16[12,112,128]{2,1,0:T(8,128)(2,1)}) custom-call(s32[4,128]{1,0:T(4,128)S(1)} %tile_codes.1.refs_0_, bf16[16,176,128]{2,1,0:T(8,128)(2,1)S(1)} %all_to_all.31.refs_1_, ...), custom_call_target="tpu_custom_call" | custom-call | tf_op jit(solution)/shard_map/backward_tiles/pallas_call | solution.py:364
  121.5 5.0 %collective-permute-start.6 = (bf16[12,112,128]{2,1,0:T(8,128)(2,1)}, bf16[12,112,128]{2,1,0:T(8,128)(2,1)S(1)}, u32[]{:S(2)}, u32[]{:S(2)}) collective-permute-start(bf16[12,112,128]{2,1,0:T(8,128)(2,1)} %get-tuple-element.25), channel_id=1, source_target_pairs={{0,96},{48,144},{96,0},{144,48},{1,97},{49,145},{97,1},{145,49},{2... | collective-permute-start | bytes 1032200 | tf_op jit(solution)/shard_map/ppermute | solution.py:390
  126.5 4.5 %collective-permute-start.7 = (bf16[12,112,128]{2,1,0:T(8,128)(2,1)}, bf16[12,112,128]{2,1,0:T(8,128)(2,1)S(1)}, u32[]{:S(2)}, u32[]{:S(2)}) collective-permute-start(bf16[12,112,128]{2,1,0:T(8,128)(2,1)} %get-tuple-element.26), channel_id=1, source_target_pairs={{0,144},{48,0},{96,48},{144,96},{1,145},{49,1},{97,49},{145,97},{2... | collective-permute-start | bytes 1032200 | tf_op jit(solution)/shard_map/ppermute | solution.py:390
  131.0 1.9 %collective-permute-start.8 = (bf16[12,112,128]{2,1,0:T(8,128)(2,1)}, bf16[12,112,128]{2,1,0:T(8,128)(2,1)S(1)}, u32[]{:S(2)}, u32[]{:S(2)}) collective-permute-start(bf16[12,112,128]{2,1,0:T(8,128)(2,1)} %get-tuple-element.27), channel_id=1, source_target_pairs={{0,48},{48,96},{96,144},{144,0},{1,49},{49,97},{97,145},{145,1},{2... | collective-permute-start | bytes 1032200 | tf_op jit(solution)/shard_map/ppermute | solution.py:390
  132.9 34.2 %conditional.1 = ((bf16[288,128]{1,0:T(8,128)(2,1)S(1)}, bf16[288,128]{1,0:T(8,128)(2,1)S(1)}, bf16[288,128]{1,0:T(8,128)(2,1)S(1)}, bf16[288,128]{1,0:T(8,128)(2,1)S(1)})) conditional(s32[]{:T(128)} %convert_element_type.4, () %tuple.15, bf16[12,112,128]{2,1,0:T(8,128)(2,1)} %get-tuple-element.28), branch_computations={%region_0.1_spmd, %region_1.2_spmd} | conditional | bytes 950280 | solution.py:418
  132.9 22.8 %all_to_all.28.refs_0_ = bf16[12,112,128]{2,1,0:T(8,128)(2,1)S(1)} all-to-all(bf16[12,112,128]{2,1,0:T(8,128)(2,1)} %param.1), channel_id=1, replica_groups=mesh['ylo'=2,'core'=2,'yhi'=4,'x'=4,'z'=12] {'z'}, dimensions={0} | all-to-all | bytes 688128 | tf_op jit(solution)/shard_map/cond/branch_1_fun/all_to_all | solution.py:395
  155.8 11.3 %all_to_all.29.refs_0_ = f32[16,16,128]{2,1,0:T(8,128)S(1)} all-to-all(f32[16,16,128]{2,1,0:T(8,128)S(1)} %get-tuple-element.1), channel_id=1, replica_groups=mesh['ylo'=2,'core'=2,'yhi'=4,'x'=4,'z'=12] {'ylo','core','x'}, dimensions={0} | all-to-all | bytes 262144 | tf_op jit(solution)/shard_map/cond/branch_1_fun/all_to_all | solution.py:408
  167.1 0.9 middle_sums.1
  168.0 3.8 %all-to-all-start.5 = ((bf16[12,112,128]{2,1,0:T(8,128)(2,1)}), bf16[12,112,128]{2,1,0:T(8,128)(2,1)S(1)}, u32[]{:S(2)}, u32[]{:S(2)}) async-start(bf16[12,112,128]{2,1,0:T(8,128)(2,1)} %middle_sums.1), calls=%async_computation.5 | async-start | bytes 688128 | tf_op jit(solution)/shard_map/all_to_all | solution.py:436
  171.9 4.5 %collective-permute-start.9 = (bf16[288,128]{1,0:T(8,128)(2,1)S(1)}, bf16[288,128]{1,0:T(8,128)(2,1)S(1)}, u32[]{:S(2)}, u32[]{:S(2)}) collective-permute-start(bf16[288,128]{1,0:T(8,128)(2,1)S(1)} %get-tuple-element.30), channel_id=1, source_target_pairs={{0,144},{48,0},{96,48},{144,96},{1,145},{49,1},{97,49},{145,97},{2... | collective-permute-start | bytes 221192 | tf_op jit(solution)/shard_map/ppermute | solution.py:435
  176.4 4.5 %collective-permute-start.10 = (bf16[288,128]{1,0:T(8,128)(2,1)S(1)}, bf16[288,128]{1,0:T(8,128)(2,1)S(1)}, u32[]{:S(2)}, u32[]{:S(2)}) collective-permute-start(bf16[288,128]{1,0:T(8,128)(2,1)S(1)} %get-tuple-element.31), channel_id=1, source_target_pairs={{0,96},{48,144},{96,0},{144,48},{1,97},{49,145},{97,1},{145,49},{2... | collective-permute-start | bytes 221192 | tf_op jit(solution)/shard_map/ppermute | solution.py:435
  180.9 1.9 %collective-permute-start.11 = (bf16[288,128]{1,0:T(8,128)(2,1)S(1)}, bf16[288,128]{1,0:T(8,128)(2,1)S(1)}, u32[]{:S(2)}, u32[]{:S(2)}) collective-permute-start(bf16[288,128]{1,0:T(8,128)(2,1)S(1)} %get-tuple-element.32), channel_id=1, source_target_pairs={{0,48},{48,96},{96,144},{144,0},{1,49},{49,97},{97,145},{145,1},{2... | collective-permute-start | bytes 221192 | tf_op jit(solution)/shard_map/ppermute | solution.py:435
  182.9 4.4 %collective-permute-done.10.refs_4_ = bf16[288,128]{1,0:T(8,128)(2,1)S(1)} collective-permute-done((bf16[288,128]{1,0:T(8,128)(2,1)S(1)}, bf16[288,128]{1,0:T(8,128)(2,1)S(1)}, u32[]{:S(2)}, u32[]{:S(2)}) %collective-permute-start.10) | collective-permute-done | bytes 73760 | tf_op jit(solution)/shard_map/ppermute | solution.py:435
  187.3 1.5 collective-permute-done.11.refs_5_
  189.1 0.7 last_sums.1
  (27 shorter events, 1.4 us)
Async XLA Ops:
  0.6 20.6 %copy-start = (bf16[1,1,48,64,128]{4,3,2,1,0:T(8,128)(2,1)S(1)}, bf16[1,1,48,64,128]{4,3,2,1,0:T(8,128)(2,1)}, u32[]{:S(2)}) copy-start(bf16[1,1,48,64,128]{4,3,2,1,0:T(8,128)(2,1)} %param.14) | copy-start | bytes 2359300
  0.6 23.9 %collective-permute-start.3 = (bf16[3072,128]{1,0:T(8,128)(2,1)}, bf16[3072,128]{1,0:T(8,128)(2,1)S(1)}, u32[]{:S(2)}, u32[]{:S(2)}) collective-permute-start(bf16[3072,128]{1,0:T(8,128)(2,1)} %bitcast.63), channel_id=1, source_target_pairs={{0,12},{12,24},{24,36},{36,0},{1,13},{13,25},{25,37},{37,1},{2,14}... | collective-permute-start | bytes 2359304 | tf_op jit(solution)/shard_map/ppermute | solution.py:304
  6.3 33.5 %all-to-all-start.2 = ((bf16[12,128,128]{2,1,0:T(8,128)(2,1)}), bf16[12,128,128]{2,1,0:T(8,128)(2,1)S(1)}, u32[]{:S(2)}, u32[]{:S(2)}) async-start(bf16[12,128,128]{2,1,0:T(8,128)(2,1)} %broadcast_in_dim.16), calls=%async_computation.2 | async-start | bytes 786432 | tf_op jit(solution)/shard_map/all_to_all | solution.py:26
  21.2 61.8 %collective-permute-start.5 = (bf16[3072,128]{1,0:T(8,128)(2,1)S(1)}, bf16[3072,128]{1,0:T(8,128)(2,1)S(1)}, u32[]{:S(2)}, u32[]{:S(2)}) collective-permute-start(bf16[3072,128]{1,0:T(8,128)(2,1)S(1)} %bitcast.64), channel_id=1, source_target_pairs={{0,36},{12,0},{24,12},{36,24},{1,37},{13,1},{25,13},{37,25},{2,38}... | collective-permute-start | bytes 2359304 | tf_op jit(solution)/shard_map/ppermute | solution.py:308
  24.6 58.4 %collective-permute-start.4 = (bf16[3072,128]{1,0:T(8,128)(2,1)S(1)}, bf16[3072,128]{1,0:T(8,128)(2,1)S(1)}, u32[]{:S(2)}, u32[]{:S(2)}) collective-permute-start(bf16[3072,128]{1,0:T(8,128)(2,1)S(1)} %collective-permute-done.3.refs_6_.refs_3_), channel_id=1, source_target_pairs={{0,12},{12,24},{24,36},{36,0},{1,13},{13,25},{25,37},{37,1},{2,14}... | collective-permute-start | bytes 2359304 | tf_op jit(solution)/shard_map/ppermute | solution.py:306
  39.8 25.9 %collective-permute-start.2 = (bf16[12,128,128]{2,1,0:T(8,128)(2,1)S(1)}, bf16[12,128,128]{2,1,0:T(8,128)(2,1)}, u32[]{:S(2)}, u32[]{:S(2)}) collective-permute-start(bf16[12,128,128]{2,1,0:T(8,128)(2,1)S(1)} %all-to-all-done.2.refs_1_), channel_id=1, source_target_pairs={{0,96},{48,144},{96,0},{144,48},{1,97},{49,145},{97,1},{145,49},{2... | collective-permute-start | bytes 1179656 | tf_op jit(solution)/shard_map/ppermute | solution.py:313
  47.3 26.6 %collective-permute-start.1 = (bf16[12,128,128]{2,1,0:T(8,128)(2,1)S(1)}, bf16[12,128,128]{2,1,0:T(8,128)(2,1)}, u32[]{:S(2)}, u32[]{:S(2)}) collective-permute-start(bf16[12,128,128]{2,1,0:T(8,128)(2,1)S(1)} %all-to-all-done.2.refs_1_), channel_id=1, source_target_pairs={{0,48},{48,96},{96,144},{144,0},{1,49},{49,97},{97,145},{145,1},{2... | collective-permute-start | bytes 1179656 | tf_op jit(solution)/shard_map/ppermute | solution.py:313
  49.7 33.2 %collective-permute-start = (bf16[12,128,128]{2,1,0:T(8,128)(2,1)S(1)}, bf16[12,128,128]{2,1,0:T(8,128)(2,1)}, u32[]{:S(2)}, u32[]{:S(2)}) collective-permute-start(bf16[12,128,128]{2,1,0:T(8,128)(2,1)S(1)} %all-to-all-done.2.refs_1_), channel_id=1, source_target_pairs={{0,144},{48,0},{96,48},{144,96},{1,145},{49,1},{97,49},{145,97},{2... | collective-permute-start | bytes 1179656 | tf_op jit(solution)/shard_map/ppermute | solution.py:313
  54.9 0.7 copy-start.4
  54.9 0.7 copy-start.5
  85.3 15.6 %copy-start.1 = (bf16[128,256]{1,0:T(8,128)(2,1)S(1)}, bf16[128,256]{1,0:T(8,128)(2,1)}, u32[]{:S(2)}) copy-start(bf16[128,256]{1,0:T(8,128)(2,1)} %weight.1) | copy-start | bytes 196612
  85.4 15.6 %copy-start.2 = (bf16[128,256]{1,0:T(8,128)(2,1)S(1)}, bf16[128,256]{1,0:T(8,128)(2,1)}, u32[]{:S(2)}) copy-start(bf16[128,256]{1,0:T(8,128)(2,1)} %cotangent.1) | copy-start | bytes 196612
  101.0 0.7 copy-start.3
  121.5 45.6 %collective-permute-start.6 = (bf16[12,112,128]{2,1,0:T(8,128)(2,1)}, bf16[12,112,128]{2,1,0:T(8,128)(2,1)S(1)}, u32[]{:S(2)}, u32[]{:S(2)}) collective-permute-start(bf16[12,112,128]{2,1,0:T(8,128)(2,1)} %get-tuple-element.25), channel_id=1, source_target_pairs={{0,96},{48,144},{96,0},{144,48},{1,97},{49,145},{97,1},{145,49},{2... | collective-permute-start | bytes 1032200 | tf_op jit(solution)/shard_map/ppermute | solution.py:390
  126.5 40.6 %collective-permute-start.7 = (bf16[12,112,128]{2,1,0:T(8,128)(2,1)}, bf16[12,112,128]{2,1,0:T(8,128)(2,1)S(1)}, u32[]{:S(2)}, u32[]{:S(2)}) collective-permute-start(bf16[12,112,128]{2,1,0:T(8,128)(2,1)} %get-tuple-element.26), channel_id=1, source_target_pairs={{0,144},{48,0},{96,48},{144,96},{1,145},{49,1},{97,49},{145,97},{2... | collective-permute-start | bytes 1032200 | tf_op jit(solution)/shard_map/ppermute | solution.py:390
  131.0 36.2 %collective-permute-start.8 = (bf16[12,112,128]{2,1,0:T(8,128)(2,1)}, bf16[12,112,128]{2,1,0:T(8,128)(2,1)S(1)}, u32[]{:S(2)}, u32[]{:S(2)}) collective-permute-start(bf16[12,112,128]{2,1,0:T(8,128)(2,1)} %get-tuple-element.27), channel_id=1, source_target_pairs={{0,48},{48,96},{96,144},{144,0},{1,49},{49,97},{97,145},{145,1},{2... | collective-permute-start | bytes 1032200 | tf_op jit(solution)/shard_map/ppermute | solution.py:390
  168.0 21.1 %all-to-all-start.5 = ((bf16[12,112,128]{2,1,0:T(8,128)(2,1)}), bf16[12,112,128]{2,1,0:T(8,128)(2,1)S(1)}, u32[]{:S(2)}, u32[]{:S(2)}) async-start(bf16[12,112,128]{2,1,0:T(8,128)(2,1)} %middle_sums.1), calls=%async_computation.5 | async-start | bytes 688128 | tf_op jit(solution)/shard_map/all_to_all | solution.py:436
  171.9 11.0 %collective-permute-start.9 = (bf16[288,128]{1,0:T(8,128)(2,1)S(1)}, bf16[288,128]{1,0:T(8,128)(2,1)S(1)}, u32[]{:S(2)}, u32[]{:S(2)}) collective-permute-start(bf16[288,128]{1,0:T(8,128)(2,1)S(1)} %get-tuple-element.30), channel_id=1, source_target_pairs={{0,144},{48,0},{96,48},{144,96},{1,145},{49,1},{97,49},{145,97},{2... | collective-permute-start | bytes 221192 | tf_op jit(solution)/shard_map/ppermute | solution.py:435
  176.4 10.9 %collective-permute-start.10 = (bf16[288,128]{1,0:T(8,128)(2,1)S(1)}, bf16[288,128]{1,0:T(8,128)(2,1)S(1)}, u32[]{:S(2)}, u32[]{:S(2)}) collective-permute-start(bf16[288,128]{1,0:T(8,128)(2,1)S(1)} %get-tuple-element.31), channel_id=1, source_target_pairs={{0,96},{48,144},{96,0},{144,48},{1,97},{49,145},{97,1},{145,49},{2... | collective-permute-start | bytes 221192 | tf_op jit(solution)/shard_map/ppermute | solution.py:435
  180.9 7.9 %collective-permute-start.11 = (bf16[288,128]{1,0:T(8,128)(2,1)S(1)}, bf16[288,128]{1,0:T(8,128)(2,1)S(1)}, u32[]{:S(2)}, u32[]{:S(2)}) collective-permute-start(bf16[288,128]{1,0:T(8,128)(2,1)S(1)} %get-tuple-element.32), channel_id=1, source_target_pairs={{0,48},{48,96},{96,144},{144,0},{1,49},{49,97},{97,145},{145,1},{2... | collective-permute-start | bytes 221192 | tf_op jit(solution)/shard_map/ppermute | solution.py:435

commit v8 on v6

--- a/solution.py
+++ b/solution.py
@@ -55,12 +55,13 @@
     return total
 
 
-def forward_kernel(codes, *refs, slots, height, blocks, far, across):
+def forward_kernel(codes, *refs, slots, height, blocks, line_order, across):
+    far = len(line_order)
     lines, tile_refs = refs[:far], refs[far : far + across]
     out, slabs, chosen, totals, picked = refs[far + across :]
     slab_count = slabs.shape[0]
     near = slab_count // far
-    for shift, line in enumerate(lines):
+    for shift, line in zip(line_order, lines):
         slabs[pl.ds(shift * near, near)] = line[...]
     dummy = slab_count * 64 + blocks
     totals[...] = jnp.zeros_like(totals)
@@ -281,6 +282,8 @@
     def ring(size, shift):
         return [(start, (start + shift) % size) for start in range(size)]
 
+    longest_first = sorted(range(1, far), key=lambda shift: -min(shift, far - shift))
+
     own = tile_values[0, 0].reshape(slots * height, tile_width)
     buffers = [own, lax.ppermute(own, "x", ring(across, 1))]
     for shift in range(2, across - 1):
@@ -289,7 +292,8 @@
         buffers.append(lax.ppermute(own, "x", ring(across, -1)))
 
     lines = [spread_out(features, "z", near)]
-    for shift in range(1, far):
+    line_order = [0] + longest_first[::-1]
+    for shift in line_order[1:]:
         lines.append(lax.ppermute(lines[0], "yhi", ring(far, shift)))
 
     codes = pl.pallas_call(
@@ -304,7 +308,14 @@
     scratch_tiles = pltpu.VMEM((across * slots + group, height, tile_width), jnp.bfloat16)
     scratch_list = pltpu.SMEM((across * slots + group,), jnp.int32)
     partial = pl.pallas_call(
-        lambda *refs: forward_kernel(*refs, slots=slots, height=height, blocks=blocks, far=far, across=across),
+        lambda *refs: forward_kernel(
+            *refs,
+            slots=slots,
+            height=height,
+            blocks=blocks,
+            line_order=line_order,
+            across=across,
+        ),
         out_shape=jax.ShapeDtypeStruct((members, nodes, width), jnp.bfloat16),
         in_specs=[in_smem()] + [in_vmem()] * (far + across),
         out_specs=in_vmem(),
@@ -358,7 +369,7 @@
     )(codes, spreads, *buffers)
 
     lines = [outs[0]]
-    for shift in range(1, far):
+    for shift in longest_first:
         lines.append(lax.ppermute(outs[shift], "yhi", ring(far, -shift)))
 
     def gather_gradients(value):

time: 197 us -> 192 us (0.975); the launches traced: 193 us -> 191 us
  blocking collectives: 94 us -> 83.5 us
  waiting for transfers between devices: 29.9 us -> 36.5 us
    all_to_all x1, blocking collectives: 25.4 us -> 14.9 us  [local(): partials = lax.all_to_all(partial, team_axes, 0, 0, tiled=True)]
    ppermute x3, waiting for transfers between devices: 10.5 us -> 17.3 us  [local(): lines.append(lax.ppermute(lines[0], 'yhi', ring(far, shift)))]
where the time goes in v8:
time: 192 us; the launch traced here: 191 us
  blocking collectives  83.5 us (43%)
  starting transfers between devices  57 us (30%)
  waiting for transfers between devices  36.5 us (19%)
  Pallas kernels  8.81 us (5%)
  local copies, waits for them, and re-layouts  3.05 us (2%)
    ppermute x3, waiting for transfers between devices, local(): lines.append(lax.ppermute(lines[0], 'yhi', ring(far, shift)))  17.3 us
    all_to_all x1, blocking collectives, gather_gradients(): shares = lax.all_to_all(shares, team_axes, 0, 0, tiled=True)  16.8 us
    all_to_all x1, blocking collectives, local(): spreads = lax.all_to_all(message, team_axes, 0, 0, tiled=True)  15.8 us
    all_to_all x1, starting transfers between devices, spread_out(): return lax.all_to_all(copies, axes, 0, 0, tiled=True)  14.9 us
    all_to_all x1, blocking collectives, local(): partials = lax.all_to_all(partial, team_axes, 0, 0, tiled=True)  14.9 us
    ppermute x3, starting transfers between devices, local(): lines.append(lax.ppermute(lines[0], 'yhi', ring(far, shift)))  14.8 us
    all_to_all x1, blocking collectives, gather_gradients(): arrived = lax.all_to_all(value, 'z', 0, 0, tiled=True)  13.9 us
    ppermute x3, starting transfers between devices, local(): lines.append(lax.ppermute(outs[shift], 'yhi', ring(far, -shift)))  13.1 us
  transfers between devices with their start and end apart: 11, of which 4 were waited for; matrix products, arithmetic and copies ran while one was open for 1% of the time, Pallas kernels for 0%

profile of v8, /device:TPU:1, one launch (start us, length us, event | category | flops | bytes accessed | tf_op | source)
XLA Modules:
  0.0 190.6 jit_solution(10212052939824102899)
XLA Ops:
  0.6 4.1 %collective-permute-start.3 = (bf16[3072,128]{1,0:T(8,128)(2,1)}, bf16[3072,128]{1,0:T(8,128)(2,1)S(1)}, u32[]{:S(2)}, u32[]{:S(2)}) collective-permute-start(bf16[3072,128]{1,0:T(8,128)(2,1)} %bitcast.63), channel_id=1, source_target_pairs={{0,12},{12,24},{24,36},{36,0},{1,13},{13,25},{25,37},{37,1},{2,14}... | collective-permute-start | bytes 2359304 | tf_op jit(solution)/shard_map/ppermute | solution.py:288
  4.7 1.6 broadcast_in_dim.16
  6.3 14.9 %all-to-all-start.2 = ((bf16[12,128,128]{2,1,0:T(8,128)(2,1)}), bf16[12,128,128]{2,1,0:T(8,128)(2,1)S(1)}, u32[]{:S(2)}, u32[]{:S(2)}) async-start(bf16[12,128,128]{2,1,0:T(8,128)(2,1)} %broadcast_in_dim.16), calls=%async_computation.2 | async-start | bytes 786432 | tf_op jit(solution)/shard_map/all_to_all | solution.py:25
  21.2 3.4 %collective-permute-start.5 = (bf16[3072,128]{1,0:T(8,128)(2,1)S(1)}, bf16[3072,128]{1,0:T(8,128)(2,1)S(1)}, u32[]{:S(2)}, u32[]{:S(2)}) collective-permute-start(bf16[3072,128]{1,0:T(8,128)(2,1)S(1)} %bitcast.64), channel_id=1, source_target_pairs={{0,36},{12,0},{24,12},{36,24},{1,37},{13,1},{25,13},{37,25},{2,38}... | collective-permute-start | bytes 2359304 | tf_op jit(solution)/shard_map/ppermute | solution.py:292
  24.6 1.9 %collective-permute-start.4 = (bf16[3072,128]{1,0:T(8,128)(2,1)S(1)}, bf16[3072,128]{1,0:T(8,128)(2,1)S(1)}, u32[]{:S(2)}, u32[]{:S(2)}) collective-permute-start(bf16[3072,128]{1,0:T(8,128)(2,1)S(1)} %collective-permute-done.3.refs_6_.refs_3_), channel_id=1, source_target_pairs={{0,12},{12,24},{24,36},{36,0},{1,13},{13,25},{25,37},{37,1},{2,14}... | collective-permute-start | bytes 2359304 | tf_op jit(solution)/shard_map/ppermute | solution.py:290
  27.2 12.6 %all-to-all-done.2.refs_1_ = bf16[12,128,128]{2,1,0:T(8,128)(2,1)S(1)} async-done(((bf16[12,128,128]{2,1,0:T(8,128)(2,1)}), bf16[12,128,128]{2,1,0:T(8,128)(2,1)S(1)}, u32[]{:S(2)}, u32[]{:S(2)}) %all-to-all-start.2) | async-done | bytes 393248 | tf_op jit(solution)/shard_map/all_to_all | solution.py:25
  39.8 7.4 %collective-permute-start.2 = (bf16[12,128,128]{2,1,0:T(8,128)(2,1)S(1)}, bf16[12,128,128]{2,1,0:T(8,128)(2,1)}, u32[]{:S(2)}, u32[]{:S(2)}) collective-permute-start(bf16[12,128,128]{2,1,0:T(8,128)(2,1)S(1)} %all-to-all-done.2.refs_1_), channel_id=1, source_target_pairs={{0,96},{48,144},{96,0},{144,48},{1,97},{49,145},{97,1},{145,49},{2... | collective-permute-start | bytes 1179656 | tf_op jit(solution)/shard_map/ppermute | solution.py:297
  47.3 2.4 %collective-permute-start.1 = (bf16[12,128,128]{2,1,0:T(8,128)(2,1)S(1)}, bf16[12,128,128]{2,1,0:T(8,128)(2,1)}, u32[]{:S(2)}, u32[]{:S(2)}) collective-permute-start(bf16[12,128,128]{2,1,0:T(8,128)(2,1)S(1)} %all-to-all-done.2.refs_1_), channel_id=1, source_target_pairs={{0,48},{48,96},{96,144},{144,0},{1,49},{49,97},{97,145},{145,1},{2... | collective-permute-start | bytes 1179656 | tf_op jit(solution)/shard_map/ppermute | solution.py:297
  49.7 5.0 %collective-permute-start = (bf16[12,128,128]{2,1,0:T(8,128)(2,1)S(1)}, bf16[12,128,128]{2,1,0:T(8,128)(2,1)}, u32[]{:S(2)}, u32[]{:S(2)}) collective-permute-start(bf16[12,128,128]{2,1,0:T(8,128)(2,1)S(1)} %all-to-all-done.2.refs_1_), channel_id=1, source_target_pairs={{0,144},{48,0},{96,48},{144,96},{1,145},{49,1},{97,49},{145,97},{2... | collective-permute-start | bytes 1179656 | tf_op jit(solution)/shard_map/ppermute | solution.py:297
  54.7 0.1 copy.12
  54.9 0.7 copy-done.4
  55.6 0.1 fusion.8
  55.6 10.0 %all-gather = bf16[64,128]{1,0:T(8,128)(2,1)S(1)} all-gather(bf16[16,128]{1,0:T(8,128)(2,1)S(1)} %fusion.8), channel_id=2, replica_groups=mesh['ylo'=2,'core'=2,'yhi'=4,'x'=4,'z'=12] {'x'}, dimensions={0}, use_global_device_ids=true | all-gather | bytes 20480 | tf_op jit(solution)/shard_map/all_gather | solution.py:280
  65.7 8.2 %collective-permute-done.1.refs_1_.refs_3_ = bf16[12,128,128]{2,1,0:T(8,128)(2,1)} collective-permute-done((bf16[12,128,128]{2,1,0:T(8,128)(2,1)S(1)}, bf16[12,128,128]{2,1,0:T(8,128)(2,1)}, u32[]{:S(2)}, u32[]{:S(2)}) %collective-permute-start.1) | collective-permute-done | bytes 393248 | tf_op jit(solution)/shard_map/ppermute | solution.py:297
  73.9 9.0 %collective-permute-done.refs_0_.refs_2_ = bf16[12,128,128]{2,1,0:T(8,128)(2,1)} collective-permute-done((bf16[12,128,128]{2,1,0:T(8,128)(2,1)S(1)}, bf16[12,128,128]{2,1,0:T(8,128)(2,1)}, u32[]{:S(2)}, u32[]{:S(2)}) %collective-permute-start) | collective-permute-done | bytes 393248 | tf_op jit(solution)/shard_map/ppermute | solution.py:297
  83.0 2.7 %forward_tiles.1 = bf16[16,128,128]{2,1,0:T(8,128)(2,1)S(1)} custom-call(s32[4,128]{1,0:T(4,128)S(1)} %tile_codes.1.refs_0_, bf16[12,128,128]{2,1,0:T(8,128)(2,1)S(1)} %all-to-all-done.2.refs_1_, bf16[12,128,128]{2,1,0:T(8,128)(2,1)} %collective-permute-done.refs_0_.refs_2_, bf16[12,128,128]{2,1,0:T(8,128)(2,1)} %collective-permute-done.1.refs_1_.refs_3_, ...), custom_call_target="tpu_custom_call" | custom-call | tf_op jit(solution)/shard_map/forward_tiles/pallas_call | solution.py:310
  85.7 14.9 %all_to_all.30.partials = bf16[16,128,128]{2,1,0:T(8,128)(2,1)S(1)} all-to-all(bf16[16,128,128]{2,1,0:T(8,128)(2,1)S(1)} %forward_tiles.1), channel_id=1, replica_groups=mesh['ylo'=2,'core'=2,'yhi'=4,'x'=4,'z'=12] {'ylo','core','x'}, dimensions={0} | all-to-all | bytes 1048576 | tf_op jit(solution)/shard_map/all_to_all | solution.py:331
  100.6 0.7 copy-done.3
  101.2 1.1 dense_layer.1
  102.3 15.8 %all_to_all.31.refs_1_ = bf16[16,176,128]{2,1,0:T(8,128)(2,1)S(1)} all-to-all(bf16[16,176,128]{2,1,0:T(8,128)(2,1)S(1)} %get-tuple-element.21), channel_id=1, replica_groups=mesh['ylo'=2,'core'=2,'yhi'=4,'x'=4,'z'=12] {'ylo','core','x'}, dimensions={0} | all-to-all | bytes 1441792 | tf_op jit(solution)/shard_map/all_to_all | solution.py:345
  118.1 3.3 %backward_tiles.1 = (bf16[12,128,128]{2,1,0:T(8,128)(2,1)S(1)}, bf16[12,128,128]{2,1,0:T(8,128)(2,1)}, bf16[12,128,128]{2,1,0:T(8,128)(2,1)}, bf16[12,128,128]{2,1,0:T(8,128)(2,1)}, bf16[12,48,128]{2,1,0:T(8,128)(2,1)}) custom-call(s32[4,128]{1,0:T(4,128)S(1)} %tile_codes.1.refs_0_, bf16[16,176,128]{2,1,0:T(8,128)(2,1)S(1)} %all_to_all.31.refs_1_, ...), custom_call_target="tpu_custom_call" | custom-call | tf_op jit(solution)/shard_map/backward_tiles/pallas_call | solution.py:347
  121.4 6.9 %collective-permute-start.6 = (bf16[12,128,128]{2,1,0:T(8,128)(2,1)}, bf16[12,128,128]{2,1,0:T(8,128)(2,1)S(1)}, u32[]{:S(2)}, u32[]{:S(2)}) collective-permute-start(bf16[12,128,128]{2,1,0:T(8,128)(2,1)} %get-tuple-element.23), channel_id=1, source_target_pairs={{0,96},{48,144},{96,0},{144,48},{1,97},{49,145},{97,1},{145,49},{2... | collective-permute-start | bytes 1179656 | tf_op jit(solution)/shard_map/ppermute | solution.py:373
  128.3 1.9 %collective-permute-start.7 = (bf16[12,128,128]{2,1,0:T(8,128)(2,1)}, bf16[12,128,128]{2,1,0:T(8,128)(2,1)S(1)}, u32[]{:S(2)}, u32[]{:S(2)}) collective-permute-start(bf16[12,128,128]{2,1,0:T(8,128)(2,1)} %get-tuple-element.24), channel_id=1, source_target_pairs={{0,144},{48,0},{96,48},{144,96},{1,145},{49,1},{97,49},{145,97},{2... | collective-permute-start | bytes 1179656 | tf_op jit(solution)/shard_map/ppermute | solution.py:373
  130.2 4.3 %collective-permute-start.8 = (bf16[12,128,128]{2,1,0:T(8,128)(2,1)}, bf16[12,128,128]{2,1,0:T(8,128)(2,1)S(1)}, u32[]{:S(2)}, u32[]{:S(2)}) collective-permute-start(bf16[12,128,128]{2,1,0:T(8,128)(2,1)} %get-tuple-element.25), channel_id=1, source_target_pairs={{0,48},{48,96},{96,144},{144,0},{1,49},{49,97},{97,145},{145,1},{2... | collective-permute-start | bytes 1179656 | tf_op jit(solution)/shard_map/ppermute | solution.py:373
  134.5 30.8 %conditional.1 = (bf16[272,128]{1,0:T(8,128)(2,1)S(1)}) conditional(s32[]{:T(128)} %convert_element_type.4, () %tuple.14, bf16[12,48,128]{2,1,0:T(8,128)(2,1)} %get-tuple-element.26), branch_computations={%region_0.1_spmd, %region_1.2_spmd} | conditional | bytes 557064 | solution.py:398
  134.5 13.9 %all_to_all.28.refs_0_ = bf16[12,48,128]{2,1,0:T(8,128)(2,1)S(1)} all-to-all(bf16[12,48,128]{2,1,0:T(8,128)(2,1)} %param.1), channel_id=1, replica_groups=mesh['ylo'=2,'core'=2,'yhi'=4,'x'=4,'z'=12] {'z'}, dimensions={0} | all-to-all | bytes 294912 | tf_op jit(solution)/shard_map/cond/branch_1_fun/all_to_all | solution.py:376
  148.4 16.8 %all_to_all.29.refs_0_ = f32[16,16,128]{2,1,0:T(8,128)S(1)} all-to-all(f32[16,16,128]{2,1,0:T(8,128)S(1)} %get-tuple-element.4), channel_id=1, replica_groups=mesh['ylo'=2,'core'=2,'yhi'=4,'x'=4,'z'=12] {'ylo','core','x'}, dimensions={0} | all-to-all | bytes 262144 | tf_op jit(solution)/shard_map/cond/branch_1_fun/all_to_all | solution.py:388
  165.3 0.9 middle_sums.1
  166.2 4.9 %all-to-all-start.5 = ((bf16[12,128,128]{2,1,0:T(8,128)(2,1)}), bf16[12,128,128]{2,1,0:T(8,128)(2,1)S(1)}, u32[]{:S(2)}, u32[]{:S(2)}) async-start(bf16[12,128,128]{2,1,0:T(8,128)(2,1)} %middle_sums.1), calls=%async_computation.5 | async-start | bytes 786432 | tf_op jit(solution)/shard_map/all_to_all | solution.py:414
  171.1 12.2 %all-gather.1 = bf16[1088,128]{1,0:T(8,128)(2,1)S(1)} all-gather(bf16[272,128]{1,0:T(8,128)(2,1)S(1)} %get-tuple-element.33.refs_4_), channel_id=3, replica_groups=mesh['ylo'=2,'core'=2,'yhi'=4,'x'=4,'z'=12] {'yhi'}, dimensions={0}, use_global_device_ids=true | all-gather | bytes 348160 | tf_op jit(solution)/shard_map/all_gather | solution.py:413
  183.3 6.6 %all-to-all-done.5.refs_0_ = bf16[12,128,128]{2,1,0:T(8,128)(2,1)S(1)} async-done(((bf16[12,128,128]{2,1,0:T(8,128)(2,1)}), bf16[12,128,128]{2,1,0:T(8,128)(2,1)S(1)}, u32[]{:S(2)}, u32[]{:S(2)}) %all-to-all-start.5) | async-done | bytes 393248 | tf_op jit(solution)/shard_map/all_to_all | solution.py:414
  189.9 0.7 last_sums.1
  (22 shorter events, 0.2 us)
Async XLA Ops:
  0.6 20.6 %copy-start = (bf16[1,1,48,64,128]{4,3,2,1,0:T(8,128)(2,1)S(1)}, bf16[1,1,48,64,128]{4,3,2,1,0:T(8,128)(2,1)}, u32[]{:S(2)}) copy-start(bf16[1,1,48,64,128]{4,3,2,1,0:T(8,128)(2,1)} %param.14) | copy-start | bytes 2359300
  0.6 23.9 %collective-permute-start.3 = (bf16[3072,128]{1,0:T(8,128)(2,1)}, bf16[3072,128]{1,0:T(8,128)(2,1)S(1)}, u32[]{:S(2)}, u32[]{:S(2)}) collective-permute-start(bf16[3072,128]{1,0:T(8,128)(2,1)} %bitcast.63), channel_id=1, source_target_pairs={{0,12},{12,24},{24,36},{36,0},{1,13},{13,25},{25,37},{37,1},{2,14}... | collective-permute-start | bytes 2359304 | tf_op jit(solution)/shard_map/ppermute | solution.py:288
  6.3 33.5 %all-to-all-start.2 = ((bf16[12,128,128]{2,1,0:T(8,128)(2,1)}), bf16[12,128,128]{2,1,0:T(8,128)(2,1)S(1)}, u32[]{:S(2)}, u32[]{:S(2)}) async-start(bf16[12,128,128]{2,1,0:T(8,128)(2,1)} %broadcast_in_dim.16), calls=%async_computation.2 | async-start | bytes 786432 | tf_op jit(solution)/shard_map/all_to_all | solution.py:25
  21.2 61.8 %collective-permute-start.5 = (bf16[3072,128]{1,0:T(8,128)(2,1)S(1)}, bf16[3072,128]{1,0:T(8,128)(2,1)S(1)}, u32[]{:S(2)}, u32[]{:S(2)}) collective-permute-start(bf16[3072,128]{1,0:T(8,128)(2,1)S(1)} %bitcast.64), channel_id=1, source_target_pairs={{0,36},{12,0},{24,12},{36,24},{1,37},{13,1},{25,13},{37,25},{2,38}... | collective-permute-start | bytes 2359304 | tf_op jit(solution)/shard_map/ppermute | solution.py:292
  24.6 58.4 %collective-permute-start.4 = (bf16[3072,128]{1,0:T(8,128)(2,1)S(1)}, bf16[3072,128]{1,0:T(8,128)(2,1)S(1)}, u32[]{:S(2)}, u32[]{:S(2)}) collective-permute-start(bf16[3072,128]{1,0:T(8,128)(2,1)S(1)} %collective-permute-done.3.refs_6_.refs_3_), channel_id=1, source_target_pairs={{0,12},{12,24},{24,36},{36,0},{1,13},{13,25},{25,37},{37,1},{2,14}... | collective-permute-start | bytes 2359304 | tf_op jit(solution)/shard_map/ppermute | solution.py:290
  39.8 25.9 %collective-permute-start.2 = (bf16[12,128,128]{2,1,0:T(8,128)(2,1)S(1)}, bf16[12,128,128]{2,1,0:T(8,128)(2,1)}, u32[]{:S(2)}, u32[]{:S(2)}) collective-permute-start(bf16[12,128,128]{2,1,0:T(8,128)(2,1)S(1)} %all-to-all-done.2.refs_1_), channel_id=1, source_target_pairs={{0,96},{48,144},{96,0},{144,48},{1,97},{49,145},{97,1},{145,49},{2... | collective-permute-start | bytes 1179656 | tf_op jit(solution)/shard_map/ppermute | solution.py:297
  47.3 26.6 %collective-permute-start.1 = (bf16[12,128,128]{2,1,0:T(8,128)(2,1)S(1)}, bf16[12,128,128]{2,1,0:T(8,128)(2,1)}, u32[]{:S(2)}, u32[]{:S(2)}) collective-permute-start(bf16[12,128,128]{2,1,0:T(8,128)(2,1)S(1)} %all-to-all-done.2.refs_1_), channel_id=1, source_target_pairs={{0,48},{48,96},{96,144},{144,0},{1,49},{49,97},{97,145},{145,1},{2... | collective-permute-start | bytes 1179656 | tf_op jit(solution)/shard_map/ppermute | solution.py:297
  49.7 33.2 %collective-permute-start = (bf16[12,128,128]{2,1,0:T(8,128)(2,1)S(1)}, bf16[12,128,128]{2,1,0:T(8,128)(2,1)}, u32[]{:S(2)}, u32[]{:S(2)}) collective-permute-start(bf16[12,128,128]{2,1,0:T(8,128)(2,1)S(1)} %all-to-all-done.2.refs_1_), channel_id=1, source_target_pairs={{0,144},{48,0},{96,48},{144,96},{1,145},{49,1},{97,49},{145,97},{2... | collective-permute-start | bytes 1179656 | tf_op jit(solution)/shard_map/ppermute | solution.py:297
  54.9 0.7 copy-start.4
  54.9 0.7 copy-start.5
  85.7 14.9 %copy-start.1 = (bf16[128,256]{1,0:T(8,128)(2,1)S(1)}, bf16[128,256]{1,0:T(8,128)(2,1)}, u32[]{:S(2)}) copy-start(bf16[128,256]{1,0:T(8,128)(2,1)} %weight.1) | copy-start | bytes 196612
  85.7 14.9 %copy-start.2 = (bf16[128,256]{1,0:T(8,128)(2,1)S(1)}, bf16[128,256]{1,0:T(8,128)(2,1)}, u32[]{:S(2)}) copy-start(bf16[128,256]{1,0:T(8,128)(2,1)} %cotangent.1) | copy-start | bytes 196612
  100.6 0.7 copy-start.3
  121.4 43.9 %collective-permute-start.6 = (bf16[12,128,128]{2,1,0:T(8,128)(2,1)}, bf16[12,128,128]{2,1,0:T(8,128)(2,1)S(1)}, u32[]{:S(2)}, u32[]{:S(2)}) collective-permute-start(bf16[12,128,128]{2,1,0:T(8,128)(2,1)} %get-tuple-element.23), channel_id=1, source_target_pairs={{0,96},{48,144},{96,0},{144,48},{1,97},{49,145},{97,1},{145,49},{2... | collective-permute-start | bytes 1179656 | tf_op jit(solution)/shard_map/ppermute | solution.py:373
  128.3 37.0 %collective-permute-start.7 = (bf16[12,128,128]{2,1,0:T(8,128)(2,1)}, bf16[12,128,128]{2,1,0:T(8,128)(2,1)S(1)}, u32[]{:S(2)}, u32[]{:S(2)}) collective-permute-start(bf16[12,128,128]{2,1,0:T(8,128)(2,1)} %get-tuple-element.24), channel_id=1, source_target_pairs={{0,144},{48,0},{96,48},{144,96},{1,145},{49,1},{97,49},{145,97},{2... | collective-permute-start | bytes 1179656 | tf_op jit(solution)/shard_map/ppermute | solution.py:373
  130.2 35.1 %collective-permute-start.8 = (bf16[12,128,128]{2,1,0:T(8,128)(2,1)}, bf16[12,128,128]{2,1,0:T(8,128)(2,1)S(1)}, u32[]{:S(2)}, u32[]{:S(2)}) collective-permute-start(bf16[12,128,128]{2,1,0:T(8,128)(2,1)} %get-tuple-element.25), channel_id=1, source_target_pairs={{0,48},{48,96},{96,144},{144,0},{1,49},{49,97},{97,145},{145,1},{2... | collective-permute-start | bytes 1179656 | tf_op jit(solution)/shard_map/ppermute | solution.py:373
  166.2 23.7 %all-to-all-start.5 = ((bf16[12,128,128]{2,1,0:T(8,128)(2,1)}), bf16[12,128,128]{2,1,0:T(8,128)(2,1)S(1)}, u32[]{:S(2)}, u32[]{:S(2)}) async-start(bf16[12,128,128]{2,1,0:T(8,128)(2,1)} %middle_sums.1), calls=%async_computation.5 | async-start | bytes 786432 | tf_op jit(solution)/shard_map/all_to_all | solution.py:414

commit v9 on v8

--- a/solution.py
+++ b/solution.py
@@ -25,14 +25,12 @@
     return lax.all_to_all(copies, axes, 0, 0, tiled=True)
 
 
-def codes_kernel(here, places, *refs):
+def codes_kernel(here, *refs, across, top):
     out = refs[-1]
-    across = places.shape[0]
     for source in range(across):
-        place = places[lax.rem(here[0] - source + across, across)].astype(jnp.float32)
-        place = place.astype(jnp.int32)
-        mine = (place[0:1] == here[0]) | (place[0:1] == 254)
-        out[pl.ds(source, 1), :] = jnp.where(mine, place[1:2] * 64 + place[2:3], -1)
+        places = refs[source][pl.ds(top, 16), :].astype(jnp.float32).astype(jnp.int32)
+        mine = (places[0:1] == here[0]) | (places[0:1] == 254)
+        out[pl.ds(source, 1), :] = jnp.where(mine, places[1:2] * 64 + places[2:3], -1)
 
 
 def pick_tiles(codes, tile_refs, chosen, picked, slots, height, dummy):
@@ -277,19 +275,16 @@
     ends = jnp.stack([jnp.int32(254), jnp.int32(0), tile_counts[0, 0]])[:, None]
     places = jnp.concatenate([places, ends], axis=1)
     places = jnp.pad(places, ((0, 13), (0, lanes - slots - 1))).astype(jnp.bfloat16)
-    places = lax.all_gather(places, "x", axis=0)
+    own = jnp.concatenate([tile_values[0, 0].reshape(slots * height, tile_width), places], axis=0)
 
     def ring(size, shift):
         return [(start, (start + shift) % size) for start in range(size)]
 
     longest_first = sorted(range(1, far), key=lambda shift: -min(shift, far - shift))
 
-    own = tile_values[0, 0].reshape(slots * height, tile_width)
-    buffers = [own, lax.ppermute(own, "x", ring(across, 1))]
-    for shift in range(2, across - 1):
-        buffers.append(lax.ppermute(buffers[-1], "x", ring(across, 1)))
-    if across > 2:
-        buffers.append(lax.ppermute(own, "x", ring(across, -1)))
+    buffers = [own]
+    for shift in sorted(range(1, across), key=lambda shift: -min(shift, across - shift)):
+        buffers.append(lax.ppermute(own, "x", ring(across, shift)))
 
     lines = [spread_out(features, "z", near)]
     line_order = [0] + longest_first[::-1]
@@ -297,13 +292,13 @@
         lines.append(lax.ppermute(lines[0], "yhi", ring(far, shift)))
 
     codes = pl.pallas_call(
-        codes_kernel,
+        lambda *refs: codes_kernel(*refs, across=across, top=slots * height),
         out_shape=jax.ShapeDtypeStruct((across, lanes), jnp.int32),
-        in_specs=[in_smem(), in_vmem()] + [any_place()] * (far - 1),
+        in_specs=[in_smem()] + [in_vmem()] * across + [any_place()] * (far - 1),
         out_specs=in_vmem(),
         compiler_params=params,
         name="tile_codes",
-    )(here.reshape(1), places, *lines[1:])
+    )(here.reshape(1), *buffers, *lines[1:])
 
     scratch_tiles = pltpu.VMEM((across * slots + group, height, tile_width), jnp.bfloat16)
     scratch_list = pltpu.SMEM((across * slots + group,), jnp.int32)

time: 192 us -> 187 us (0.974)
  blocking collectives: 83.5 us -> 75.2 us
  waiting for transfers between devices: 36.5 us -> 39.8 us
    all_gather x1 -> x0, blocking collectives: 10 us -> none  [local(): places = lax.all_gather(places, 'x', axis=0)]
    ppermute x3, waiting for transfers between devices: 0.01 us -> 8.88 us  [local(): buffers.append(lax.ppermute(own, 'x', ring(across, shift)))]
    all_to_all x1, waiting for transfers between devices: 12.6 us -> 7.71 us  [spread_out(): return lax.all_to_all(copies, axes, 0, 0, tiled=True)]
    all_to_all x1, waiting for transfers between devices: 6.62 us -> 3.92 us  [local(): arrived = lax.all_to_all(line, 'z', 0, 0, tiled=True)]
    all_to_all x1, blocking collectives: 13.9 us -> 15.9 us  [gather_gradients(): arrived = lax.all_to_all(value, 'z', 0, 0, tiled=True)]
    ppermute x3, waiting for transfers between devices: 17.3 us -> 19.3 us  [local(): lines.append(lax.ppermute(lines[0], 'yhi', ring(far, shift)))]
  transfers between devices with their start and end apart: 11 -> 11, of which waited for: 4 -> 5; matrix products, arithmetic and copies ran while one was open for 1% -> 0% of each run, Pallas kernels for 0% -> 0%
where the time goes in v9:
time: 187 us; the launch traced here: 184 us
  blocking collectives  75.2 us (40%)
  starting transfers between devices  58.1 us (31%)
  waiting for transfers between devices  39.8 us (21%)
  Pallas kernels  7.16 us (4%)
    ppermute x3, waiting for transfers between devices, local(): lines.append(lax.ppermute(lines[0], 'yhi', ring(far, shift)))  19.3 us
    all_to_all x1, blocking collectives, gather_gradients(): arrived = lax.all_to_all(value, 'z', 0, 0, tiled=True)  15.9 us
    all_to_all x1, blocking collectives, local(): spreads = lax.all_to_all(message, team_axes, 0, 0, tiled=True)  15.8 us
    all_to_all x1, starting transfers between devices, spread_out(): return lax.all_to_all(copies, axes, 0, 0, tiled=True)  15.7 us
    all_to_all x1, blocking collectives, local(): partials = lax.all_to_all(partial, team_axes, 0, 0, tiled=True)  15.6 us
    all_to_all x1, blocking collectives, gather_gradients(): shares = lax.all_to_all(shares, team_axes, 0, 0, tiled=True)  15.1 us
    ppermute x3, starting transfers between devices, local(): lines.append(lax.ppermute(lines[0], 'yhi', ring(far, shift)))  14.8 us
    ppermute x3, starting transfers between devices, local(): lines.append(lax.ppermute(outs[shift], 'yhi', ring(far, -shift)))  13.1 us
  transfers between devices with their start and end apart: 11, of which 5 were waited for; matrix products, arithmetic and copies ran while one was open for 0% of the time, Pallas kernels for 0%

profile of v9, /device:TPU:1, one launch (start us, length us, event | category | flops | bytes accessed | tf_op | source)
XLA Modules:
  0.0 183.8 jit_solution(5065904996814946942)
XLA Ops:
  0.7 1.7 broadcast_in_dim.16
  2.3 15.7 %all-to-all-start.2 = ((bf16[12,128,128]{2,1,0:T(8,128)(2,1)}), bf16[12,128,128]{2,1,0:T(8,128)(2,1)S(1)}, u32[]{:S(2)}, u32[]{:S(2)}) async-start(bf16[12,128,128]{2,1,0:T(8,128)(2,1)} %broadcast_in_dim.16), calls=%async_computation.2 | async-start | bytes 786432 | tf_op jit(solution)/shard_map/all_to_all | solution.py:25
  18.7 0.1 maximum_bitcast_fusion
  18.8 0.1 copy.12
  18.9 0.1 fusion.8
  19.0 0.1 pad_maximum_fusion.refs_1_.refs_5_.refs_2_
  19.0 4.4 %collective-permute-start.2 = (bf16[3088,128]{1,0:T(8,128)(2,1)S(1)}, bf16[3088,128]{1,0:T(8,128)(2,1)S(1)}, u32[]{:S(2)}, u32[]{:S(2)}) collective-permute-start(bf16[3088,128]{1,0:T(8,128)(2,1)S(1)} %pad_maximum_fusion.refs_1_.refs_5_.refs_2_), channel_id=1, source_target_pairs={{0,36},{12,0},{24,12},{36,24},{1,37},{13,1},{25,13},{37,25},{2,38}... | collective-permute-start | bytes 2371592 | tf_op jit(solution)/shard_map/ppermute | solution.py:287
  23.4 1.9 %collective-permute-start.1 = (bf16[3088,128]{1,0:T(8,128)(2,1)S(1)}, bf16[3088,128]{1,0:T(8,128)(2,1)S(1)}, u32[]{:S(2)}, u32[]{:S(2)}) collective-permute-start(bf16[3088,128]{1,0:T(8,128)(2,1)S(1)} %pad_maximum_fusion.refs_1_.refs_5_.refs_2_), channel_id=1, source_target_pairs={{0,12},{12,24},{24,36},{36,0},{1,13},{13,25},{25,37},{37,1},{2,14}... | collective-permute-start | bytes 2371592 | tf_op jit(solution)/shard_map/ppermute | solution.py:287
  25.4 3.6 %collective-permute-start = (bf16[3088,128]{1,0:T(8,128)(2,1)S(1)}, bf16[3088,128]{1,0:T(8,128)(2,1)S(1)}, u32[]{:S(2)}, u32[]{:S(2)}) collective-permute-start(bf16[3088,128]{1,0:T(8,128)(2,1)S(1)} %pad_maximum_fusion.refs_1_.refs_5_.refs_2_), channel_id=1, source_target_pairs={{0,24},{12,36},{24,0},{36,12},{1,25},{13,37},{25,1},{37,13},{2,26}... | collective-permute-start | bytes 2371592 | tf_op jit(solution)/shard_map/ppermute | solution.py:287
  29.0 7.7 %all-to-all-done.2.refs_1_ = bf16[12,128,128]{2,1,0:T(8,128)(2,1)S(1)} async-done(((bf16[12,128,128]{2,1,0:T(8,128)(2,1)}), bf16[12,128,128]{2,1,0:T(8,128)(2,1)S(1)}, u32[]{:S(2)}, u32[]{:S(2)}) %all-to-all-start.2) | async-done | bytes 393248 | tf_op jit(solution)/shard_map/all_to_all | solution.py:25
  36.7 7.4 %collective-permute-start.5 = (bf16[12,128,128]{2,1,0:T(8,128)(2,1)S(1)}, bf16[12,128,128]{2,1,0:T(8,128)(2,1)S(1)}, u32[]{:S(2)}, u32[]{:S(2)}) collective-permute-start(bf16[12,128,128]{2,1,0:T(8,128)(2,1)S(1)} %all-to-all-done.2.refs_1_), channel_id=1, source_target_pairs={{0,96},{48,144},{96,0},{144,48},{1,97},{49,145},{97,1},{145,49},{2... | collective-permute-start | bytes 1179656 | tf_op jit(solution)/shard_map/ppermute | solution.py:292
  44.2 2.4 %collective-permute-start.4 = (bf16[12,128,128]{2,1,0:T(8,128)(2,1)S(1)}, bf16[12,128,128]{2,1,0:T(8,128)(2,1)S(1)}, u32[]{:S(2)}, u32[]{:S(2)}) collective-permute-start(bf16[12,128,128]{2,1,0:T(8,128)(2,1)S(1)} %all-to-all-done.2.refs_1_), channel_id=1, source_target_pairs={{0,48},{48,96},{96,144},{144,0},{1,49},{49,97},{97,145},{145,1},{2... | collective-permute-start | bytes 1179656 | tf_op jit(solution)/shard_map/ppermute | solution.py:292
  46.6 5.0 %collective-permute-start.3 = (bf16[12,128,128]{2,1,0:T(8,128)(2,1)S(1)}, bf16[12,128,128]{2,1,0:T(8,128)(2,1)S(1)}, u32[]{:S(2)}, u32[]{:S(2)}) collective-permute-start(bf16[12,128,128]{2,1,0:T(8,128)(2,1)S(1)} %all-to-all-done.2.refs_1_), channel_id=1, source_target_pairs={{0,144},{48,0},{96,48},{144,96},{1,145},{49,1},{97,49},{145,97},{2... | collective-permute-start | bytes 1179656 | tf_op jit(solution)/shard_map/ppermute | solution.py:292
  51.6 8.9 %collective-permute-done.refs_2_.refs_6_.refs_3_ = bf16[3088,128]{1,0:T(8,128)(2,1)S(1)} collective-permute-done((bf16[3088,128]{1,0:T(8,128)(2,1)S(1)}, bf16[3088,128]{1,0:T(8,128)(2,1)S(1)}, u32[]{:S(2)}, u32[]{:S(2)}) %collective-permute-start) | collective-permute-done | bytes 790560 | tf_op jit(solution)/shard_map/ppermute | solution.py:287
  60.5 10.2 %collective-permute-done.4.refs_6_.refs_3_ = bf16[12,128,128]{2,1,0:T(8,128)(2,1)S(1)} collective-permute-done((bf16[12,128,128]{2,1,0:T(8,128)(2,1)S(1)}, bf16[12,128,128]{2,1,0:T(8,128)(2,1)S(1)}, u32[]{:S(2)}, u32[]{:S(2)}) %collective-permute-start.4) | collective-permute-done | bytes 393248 | tf_op jit(solution)/shard_map/ppermute | solution.py:292
  70.7 9.1 %collective-permute-done.3.refs_5_.refs_2_ = bf16[12,128,128]{2,1,0:T(8,128)(2,1)S(1)} collective-permute-done((bf16[12,128,128]{2,1,0:T(8,128)(2,1)S(1)}, bf16[12,128,128]{2,1,0:T(8,128)(2,1)S(1)}, u32[]{:S(2)}, u32[]{:S(2)}) %collective-permute-start.3) | collective-permute-done | bytes 393248 | tf_op jit(solution)/shard_map/ppermute | solution.py:292
  79.8 1.6 forward_tiles.1
  81.4 15.6 %all_to_all.30.partials = bf16[16,128,128]{2,1,0:T(8,128)(2,1)S(1)} all-to-all(bf16[16,128,128]{2,1,0:T(8,128)(2,1)S(1)} %forward_tiles.1), channel_id=1, replica_groups=mesh['ylo'=2,'core'=2,'yhi'=4,'x'=4,'z'=12] {'ylo','core','x'}, dimensions={0} | all-to-all | bytes 1048576 | tf_op jit(solution)/shard_map/all_to_all | solution.py:326
  97.0 1.1 dense_layer.1
  98.1 15.8 %all_to_all.31.refs_1_ = bf16[16,176,128]{2,1,0:T(8,128)(2,1)S(1)} all-to-all(bf16[16,176,128]{2,1,0:T(8,128)(2,1)S(1)} %get-tuple-element.21), channel_id=1, replica_groups=mesh['ylo'=2,'core'=2,'yhi'=4,'x'=4,'z'=12] {'ylo','core','x'}, dimensions={0} | all-to-all | bytes 1441792 | tf_op jit(solution)/shard_map/all_to_all | solution.py:340
  113.9 2.8 %backward_tiles.1 = (bf16[12,128,128]{2,1,0:T(8,128)(2,1)S(1)}, bf16[12,128,128]{2,1,0:T(8,128)(2,1)}, bf16[12,128,128]{2,1,0:T(8,128)(2,1)}, bf16[12,128,128]{2,1,0:T(8,128)(2,1)}, bf16[12,48,128]{2,1,0:T(8,128)(2,1)}) custom-call(s32[4,128]{1,0:T(4,128)S(1)} %tile_codes.1.refs_0_, bf16[16,176,128]{2,1,0:T(8,128)(2,1)S(1)} %all_to_all.31.refs_1_, ...), custom_call_target="tpu_custom_call" | custom-call | tf_op jit(solution)/shard_map/backward_tiles/pallas_call | solution.py:342
  116.7 6.9 %collective-permute-start.6 = (bf16[12,128,128]{2,1,0:T(8,128)(2,1)}, bf16[12,128,128]{2,1,0:T(8,128)(2,1)S(1)}, u32[]{:S(2)}, u32[]{:S(2)}) collective-permute-start(bf16[12,128,128]{2,1,0:T(8,128)(2,1)} %get-tuple-element.23), channel_id=1, source_target_pairs={{0,96},{48,144},{96,0},{144,48},{1,97},{49,145},{97,1},{145,49},{2... | collective-permute-start | bytes 1179656 | tf_op jit(solution)/shard_map/ppermute | solution.py:368
  123.5 2.5 %collective-permute-start.7 = (bf16[12,128,128]{2,1,0:T(8,128)(2,1)}, bf16[12,128,128]{2,1,0:T(8,128)(2,1)S(1)}, u32[]{:S(2)}, u32[]{:S(2)}) collective-permute-start(bf16[12,128,128]{2,1,0:T(8,128)(2,1)} %get-tuple-element.24), channel_id=1, source_target_pairs={{0,144},{48,0},{96,48},{144,96},{1,145},{49,1},{97,49},{145,97},{2... | collective-permute-start | bytes 1179656 | tf_op jit(solution)/shard_map/ppermute | solution.py:368
  126.0 3.7 %collective-permute-start.8 = (bf16[12,128,128]{2,1,0:T(8,128)(2,1)}, bf16[12,128,128]{2,1,0:T(8,128)(2,1)S(1)}, u32[]{:S(2)}, u32[]{:S(2)}) collective-permute-start(bf16[12,128,128]{2,1,0:T(8,128)(2,1)} %get-tuple-element.25), channel_id=1, source_target_pairs={{0,48},{48,96},{96,144},{144,0},{1,49},{49,97},{97,145},{145,1},{2... | collective-permute-start | bytes 1179656 | tf_op jit(solution)/shard_map/ppermute | solution.py:368
  129.7 31.0 %conditional.1 = (bf16[272,128]{1,0:T(8,128)(2,1)S(1)}) conditional(s32[]{:T(128)} %convert_element_type.4, () %tuple.14, bf16[12,48,128]{2,1,0:T(8,128)(2,1)} %get-tuple-element.26), branch_computations={%region_0.1_spmd, %region_1.2_spmd} | conditional | bytes 557064 | solution.py:393
  129.8 15.9 %all_to_all.28.refs_0_ = bf16[12,48,128]{2,1,0:T(8,128)(2,1)S(1)} all-to-all(bf16[12,48,128]{2,1,0:T(8,128)(2,1)} %param.1), channel_id=1, replica_groups=mesh['ylo'=2,'core'=2,'yhi'=4,'x'=4,'z'=12] {'z'}, dimensions={0} | all-to-all | bytes 294912 | tf_op jit(solution)/shard_map/cond/branch_1_fun/all_to_all | solution.py:371
  145.7 15.1 %all_to_all.29.refs_0_ = f32[16,16,128]{2,1,0:T(8,128)S(1)} all-to-all(f32[16,16,128]{2,1,0:T(8,128)S(1)} %get-tuple-element.4), channel_id=1, replica_groups=mesh['ylo'=2,'core'=2,'yhi'=4,'x'=4,'z'=12] {'ylo','core','x'}, dimensions={0} | all-to-all | bytes 262144 | tf_op jit(solution)/shard_map/cond/branch_1_fun/all_to_all | solution.py:383
  160.8 0.9 middle_sums.1
  161.7 4.6 %all-to-all-start.5 = ((bf16[12,128,128]{2,1,0:T(8,128)(2,1)}), bf16[12,128,128]{2,1,0:T(8,128)(2,1)S(1)}, u32[]{:S(2)}, u32[]{:S(2)}) async-start(bf16[12,128,128]{2,1,0:T(8,128)(2,1)} %middle_sums.1), calls=%async_computation.5 | async-start | bytes 786432 | tf_op jit(solution)/shard_map/all_to_all | solution.py:409
  166.4 12.9 %all-gather = bf16[1088,128]{1,0:T(8,128)(2,1)S(1)} all-gather(bf16[272,128]{1,0:T(8,128)(2,1)S(1)} %get-tuple-element.33.refs_4_), channel_id=2, replica_groups=mesh['ylo'=2,'core'=2,'yhi'=4,'x'=4,'z'=12] {'yhi'}, dimensions={0}, use_global_device_ids=true | all-gather | bytes 348160 | tf_op jit(solution)/shard_map/all_gather | solution.py:408
  179.2 3.9 %all-to-all-done.5.refs_0_ = bf16[12,128,128]{2,1,0:T(8,128)(2,1)S(1)} async-done(((bf16[12,128,128]{2,1,0:T(8,128)(2,1)}), bf16[12,128,128]{2,1,0:T(8,128)(2,1)S(1)}, u32[]{:S(2)}, u32[]{:S(2)}) %all-to-all-start.5) | async-done | bytes 393248 | tf_op jit(solution)/shard_map/all_to_all | solution.py:409
  183.1 0.7 last_sums.1
  (22 shorter events, 0.1 us)
Async XLA Ops:
  0.6 18.2 %copy-start.4 = (s32[1,1,48]{2,1,0:T(1,128)S(1)}, s32[1,1,48]{2,1,0:T(1,128)}, u32[]{:S(2)}) copy-start(s32[1,1,48]{2,1,0:T(1,128)} %param.12) | copy-start | bytes 580
  0.6 18.2 %copy-start.5 = (s32[1,1,48]{2,1,0:T(1,128)S(1)}, s32[1,1,48]{2,1,0:T(1,128)}, u32[]{:S(2)}) copy-start(s32[1,1,48]{2,1,0:T(1,128)} %param.11) | copy-start | bytes 580
  0.7 18.3 %copy-start.3 = (bf16[1,1,48,64,128]{4,3,2,1,0:T(8,128)(2,1)S(1)}, bf16[1,1,48,64,128]{4,3,2,1,0:T(8,128)(2,1)}, u32[]{:S(2)}) copy-start(bf16[1,1,48,64,128]{4,3,2,1,0:T(8,128)(2,1)} %param.14) | copy-start | bytes 2359300
  2.3 34.4 %all-to-all-start.2 = ((bf16[12,128,128]{2,1,0:T(8,128)(2,1)}), bf16[12,128,128]{2,1,0:T(8,128)(2,1)S(1)}, u32[]{:S(2)}, u32[]{:S(2)}) async-start(bf16[12,128,128]{2,1,0:T(8,128)(2,1)} %broadcast_in_dim.16), calls=%async_computation.2 | async-start | bytes 786432 | tf_op jit(solution)/shard_map/all_to_all | solution.py:25
  19.0 27.5 %collective-permute-start.2 = (bf16[3088,128]{1,0:T(8,128)(2,1)S(1)}, bf16[3088,128]{1,0:T(8,128)(2,1)S(1)}, u32[]{:S(2)}, u32[]{:S(2)}) collective-permute-start(bf16[3088,128]{1,0:T(8,128)(2,1)S(1)} %pad_maximum_fusion.refs_1_.refs_5_.refs_2_), channel_id=1, source_target_pairs={{0,36},{12,0},{24,12},{36,24},{1,37},{13,1},{25,13},{37,25},{2,38}... | collective-permute-start | bytes 2371592 | tf_op jit(solution)/shard_map/ppermute | solution.py:287
  23.4 28.1 %collective-permute-start.1 = (bf16[3088,128]{1,0:T(8,128)(2,1)S(1)}, bf16[3088,128]{1,0:T(8,128)(2,1)S(1)}, u32[]{:S(2)}, u32[]{:S(2)}) collective-permute-start(bf16[3088,128]{1,0:T(8,128)(2,1)S(1)} %pad_maximum_fusion.refs_1_.refs_5_.refs_2_), channel_id=1, source_target_pairs={{0,12},{12,24},{24,36},{36,0},{1,13},{13,25},{25,37},{37,1},{2,14}... | collective-permute-start | bytes 2371592 | tf_op jit(solution)/shard_map/ppermute | solution.py:287
  25.4 35.1 %collective-permute-start = (bf16[3088,128]{1,0:T(8,128)(2,1)S(1)}, bf16[3088,128]{1,0:T(8,128)(2,1)S(1)}, u32[]{:S(2)}, u32[]{:S(2)}) collective-permute-start(bf16[3088,128]{1,0:T(8,128)(2,1)S(1)} %pad_maximum_fusion.refs_1_.refs_5_.refs_2_), channel_id=1, source_target_pairs={{0,24},{12,36},{24,0},{36,12},{1,25},{13,37},{25,1},{37,13},{2,26}... | collective-permute-start | bytes 2371592 | tf_op jit(solution)/shard_map/ppermute | solution.py:287
  36.7 23.8 %collective-permute-start.5 = (bf16[12,128,128]{2,1,0:T(8,128)(2,1)S(1)}, bf16[12,128,128]{2,1,0:T(8,128)(2,1)S(1)}, u32[]{:S(2)}, u32[]{:S(2)}) collective-permute-start(bf16[12,128,128]{2,1,0:T(8,128)(2,1)S(1)} %all-to-all-done.2.refs_1_), channel_id=1, source_target_pairs={{0,96},{48,144},{96,0},{144,48},{1,97},{49,145},{97,1},{145,49},{2... | collective-permute-start | bytes 1179656 | tf_op jit(solution)/shard_map/ppermute | solution.py:292
  44.2 26.5 %collective-permute-start.4 = (bf16[12,128,128]{2,1,0:T(8,128)(2,1)S(1)}, bf16[12,128,128]{2,1,0:T(8,128)(2,1)S(1)}, u32[]{:S(2)}, u32[]{:S(2)}) collective-permute-start(bf16[12,128,128]{2,1,0:T(8,128)(2,1)S(1)} %all-to-all-done.2.refs_1_), channel_id=1, source_target_pairs={{0,48},{48,96},{96,144},{144,0},{1,49},{49,97},{97,145},{145,1},{2... | collective-permute-start | bytes 1179656 | tf_op jit(solution)/shard_map/ppermute | solution.py:292
  46.6 33.1 %collective-permute-start.3 = (bf16[12,128,128]{2,1,0:T(8,128)(2,1)S(1)}, bf16[12,128,128]{2,1,0:T(8,128)(2,1)S(1)}, u32[]{:S(2)}, u32[]{:S(2)}) collective-permute-start(bf16[12,128,128]{2,1,0:T(8,128)(2,1)S(1)} %all-to-all-done.2.refs_1_), channel_id=1, source_target_pairs={{0,144},{48,0},{96,48},{144,96},{1,145},{49,1},{97,49},{145,97},{2... | collective-permute-start | bytes 1179656 | tf_op jit(solution)/shard_map/ppermute | solution.py:292
  81.3 15.7 %copy-start = (bf16[128,256]{1,0:T(8,128)(2,1)S(1)}, bf16[128,256]{1,0:T(8,128)(2,1)}, u32[]{:S(2)}) copy-start(bf16[128,256]{1,0:T(8,128)(2,1)} %weight.1) | copy-start | bytes 196612
  81.3 15.7 %copy-start.1 = (bf16[128,256]{1,0:T(8,128)(2,1)S(1)}, bf16[128,256]{1,0:T(8,128)(2,1)}, u32[]{:S(2)}) copy-start(bf16[128,256]{1,0:T(8,128)(2,1)} %cotangent.1) | copy-start | bytes 196612
  81.4 15.6 %copy-start.2 = (f32[256]{0:T(256)S(1)}, f32[256]{0:T(256)}, u32[]{:S(2)}) copy-start(f32[256]{0:T(256)} %param.16) | copy-start | bytes 3076
  116.7 44.1 %collective-permute-start.6 = (bf16[12,128,128]{2,1,0:T(8,128)(2,1)}, bf16[12,128,128]{2,1,0:T(8,128)(2,1)S(1)}, u32[]{:S(2)}, u32[]{:S(2)}) collective-permute-start(bf16[12,128,128]{2,1,0:T(8,128)(2,1)} %get-tuple-element.23), channel_id=1, source_target_pairs={{0,96},{48,144},{96,0},{144,48},{1,97},{49,145},{97,1},{145,49},{2... | collective-permute-start | bytes 1179656 | tf_op jit(solution)/shard_map/ppermute | solution.py:368
  123.5 37.2 %collective-permute-start.7 = (bf16[12,128,128]{2,1,0:T(8,128)(2,1)}, bf16[12,128,128]{2,1,0:T(8,128)(2,1)S(1)}, u32[]{:S(2)}, u32[]{:S(2)}) collective-permute-start(bf16[12,128,128]{2,1,0:T(8,128)(2,1)} %get-tuple-element.24), channel_id=1, source_target_pairs={{0,144},{48,0},{96,48},{144,96},{1,145},{49,1},{97,49},{145,97},{2... | collective-permute-start | bytes 1179656 | tf_op jit(solution)/shard_map/ppermute | solution.py:368
  126.0 34.8 %collective-permute-start.8 = (bf16[12,128,128]{2,1,0:T(8,128)(2,1)}, bf16[12,128,128]{2,1,0:T(8,128)(2,1)S(1)}, u32[]{:S(2)}, u32[]{:S(2)}) collective-permute-start(bf16[12,128,128]{2,1,0:T(8,128)(2,1)} %get-tuple-element.25), channel_id=1, source_target_pairs={{0,48},{48,96},{96,144},{144,0},{1,49},{49,97},{97,145},{145,1},{2... | collective-permute-start | bytes 1179656 | tf_op jit(solution)/shard_map/ppermute | solution.py:368
  161.7 21.4 %all-to-all-start.5 = ((bf16[12,128,128]{2,1,0:T(8,128)(2,1)}), bf16[12,128,128]{2,1,0:T(8,128)(2,1)S(1)}, u32[]{:S(2)}, u32[]{:S(2)}) async-start(bf16[12,128,128]{2,1,0:T(8,128)(2,1)} %middle_sums.1), calls=%async_computation.5 | async-start | bytes 786432 | tf_op jit(solution)/shard_map/all_to_all | solution.py:409

commit v10 on v9

--- a/solution.py
+++ b/solution.py
@@ -13,6 +13,7 @@
 row_axes = ("ylo", "core")
 col_axes = ("yhi", "x", "z")
 team_axes = ("ylo", "core", "x")
+share_axes = ("core", "x")
 group = 4
 lanes = 128
 vmem_bytes = 12 * 1024 * 1024
@@ -106,7 +107,7 @@
     return value
 
 
-def dense_kernel(partials, weight, bias, cotangent, hidden, message):
+def dense_kernel(partials, weight, bias, cotangent, hidden, message, *, share):
     members = partials.shape[0]
     nodes = partials.shape[1]
     aggregate = sum_rows(partials, 0, nodes)
@@ -142,15 +143,13 @@
     high, low = split_wide(bias_part)
     bias_block = bias_rows([high[:, :lanes], high[:, lanes:], low[:, :lanes], low[:, lanes:]])
     bias_block = bias_block.astype(jnp.bfloat16)
-    share = weight_part.shape[0] // members
     for member in range(members):
         message[member, pl.ds(0, nodes), :] = spread
-        part = weight_part[member * share : (member + 1) * share]
+        first = member * share % weight_part.shape[0]
+        part = weight_part[first : first + share]
         part = jnp.concatenate([part[:, :lanes], part[:, lanes:]], axis=0)
-        high, low = split_wide(part)
-        message[member, pl.ds(nodes, 2 * share), :] = high.astype(jnp.bfloat16)
-        message[member, pl.ds(nodes + 2 * share, 2 * share), :] = low.astype(jnp.bfloat16)
-        message[member, pl.ds(nodes + 4 * share, 16), :] = bias_block
+        message[member, pl.ds(nodes, 2 * share), :] = part.astype(jnp.bfloat16)
+        message[member, pl.ds(nodes + 2 * share, 16), :] = bias_block
 
 
 def sum_bias(ref, start):
@@ -194,30 +193,26 @@
     for shift, out in enumerate(outs):
         for index in range(near):
             out[index] = totals[shift * near + index].astype(jnp.bfloat16)
-    weight_sum = sum_rows(spreads, nodes, 2 * share) + sum_rows(spreads, nodes + 2 * share, 2 * share)
-    high, low = split_wide(weight_sum)
-    bias_block = pack_bias(sum_bias(spreads, nodes + 4 * share))
+    weight_sum = sum_rows(spreads, nodes, 2 * share).astype(jnp.bfloat16)
+    bias_block = pack_bias(sum_bias(spreads, nodes + 2 * share))
     for index in range(near):
-        shares[index, pl.ds(0, 2 * share), :] = high.astype(jnp.bfloat16)
-        shares[index, pl.ds(2 * share, 2 * share), :] = low.astype(jnp.bfloat16)
-        shares[index, pl.ds(4 * share, 16), :] = bias_block
+        shares[index, pl.ds(0, 2 * share), :] = weight_sum
+        shares[index, pl.ds(2 * share, 16), :] = bias_block
 
 
 def share_kernel(arrived, out, bias_block, *, share):
-    total = sum_rows(arrived, 0, 2 * share) + sum_rows(arrived, 2 * share, 2 * share)
+    total = sum_rows(arrived, 0, 2 * share).astype(jnp.bfloat16)
     for index in range(out.shape[0]):
         out[index] = total
-    bias_block[...] = pack_bias(sum_bias(arrived, 4 * share))
+    bias_block[...] = pack_bias(sum_bias(arrived, 2 * share))
 
 
 def gather_kernel(shares, bias_block, out, *, share):
-    step = 16 // share if share < 16 else 1
     rows = shares.shape[0] * share
-    for half in range(2):
-        for first in range(0, shares.shape[0], step):
-            parts = [shares[first + sub, pl.ds(half * share, share), :] for sub in range(step)]
-            part = jnp.concatenate(parts, axis=0) if step > 1 else parts[0]
-            out[pl.ds(half * rows + first * share, step * share), :] = part.astype(jnp.bfloat16)
+    for index in range(shares.shape[0]):
+        for half in range(2):
+            part = shares[index, pl.ds(half * share, share), :]
+            out[pl.ds(half * rows + index * share, share), :] = part
     out[pl.ds(2 * rows, 16), :] = bias_block[...]
 
 
@@ -325,12 +320,13 @@
     )(codes, *lines, *buffers)
     partials = lax.all_to_all(partial, team_axes, 0, 0, tiled=True)
 
-    share = width // members
+    holders = lax.axis_size(share_axes)
+    share = width // holders
     hidden_out, message = pl.pallas_call(
-        dense_kernel,
+        lambda *refs: dense_kernel(*refs, share=share),
         out_shape=(
             jax.ShapeDtypeStruct((nodes, hidden), jnp.bfloat16),
-            jax.ShapeDtypeStruct((members, nodes + 4 * share + 16, width), jnp.bfloat16),
+            jax.ShapeDtypeStruct((members, nodes + 2 * share + 16, width), jnp.bfloat16),
         ),
         in_specs=[in_vmem()] * 4,
         out_specs=(in_vmem(), in_vmem()),
@@ -351,7 +347,7 @@
             across=across,
         ),
         out_shape=(jax.ShapeDtypeStruct((near, nodes, width), jnp.bfloat16),) * far
-        + (jax.ShapeDtypeStruct((near, 4 * share + 16, width), jnp.bfloat16),),
+        + (jax.ShapeDtypeStruct((near, 2 * share + 16, width), jnp.bfloat16),),
         in_specs=[in_smem(), in_vmem()] + [in_vmem()] * across,
         out_specs=(in_vmem(),) * (far + 1),
         scratch_shapes=[
@@ -372,7 +368,7 @@
         shares, bias_block = pl.pallas_call(
             lambda *refs: share_kernel(*refs, share=share),
             out_shape=(
-                jax.ShapeDtypeStruct((members, 2 * share, lanes), jnp.float32),
+                jax.ShapeDtypeStruct((holders, 2 * share, lanes), jnp.bfloat16),
                 jax.ShapeDtypeStruct((16, lanes), jnp.bfloat16),
             ),
             in_specs=[in_vmem()],
@@ -380,7 +376,7 @@
             compiler_params=params,
             name="share_sum",
         )(arrived)
-        shares = lax.all_to_all(shares, team_axes, 0, 0, tiled=True)
+        shares = lax.all_to_all(shares, share_axes, 0, 0, tiled=True)
         return pl.pallas_call(
             lambda *refs: gather_kernel(*refs, share=share),
             out_shape=jax.ShapeDtypeStruct((2 * width + 16, lanes), jnp.bfloat16),

time: 187 us -> 186 us (level)
  waiting for transfers between devices: 39.8 us -> 46.4 us
  blocking collectives: 75.2 us -> 69.8 us
  starting transfers between devices: 58.1 us -> 55.9 us
    all_to_all x1, blocking collectives: 15.1 us -> 10.5 us  [gather_gradients(): shares = lax.all_to_all(shares, share_axes, 0, 0, tiled=True)]
    ppermute x3, waiting for transfers between devices: 0.01 us -> 3.94 us  [local(): lines.append(lax.ppermute(outs[shift], 'yhi', ring(far, -shift)))]
    all_to_all x1, waiting for transfers between devices: 3.92 us -> 6.58 us  [local(): arrived = lax.all_to_all(line, 'z', 0, 0, tiled=True)]
  transfers between devices with their start and end apart: 11 -> 11, of which waited for: 5 -> 6; matrix products, arithmetic and copies ran while one was open for 0% -> 0% of each run, Pallas kernels for 0% -> 0%
where the time goes in v10:
time: 186 us; the launch traced here: 184 us
  blocking collectives  69.8 us (38%)
  starting transfers between devices  55.9 us (30%)
  waiting for transfers between devices  46.4 us (25%)
  Pallas kernels  8.54 us (5%)
    ppermute x3, waiting for transfers between devices, local(): lines.append(lax.ppermute(lines[0], 'yhi', ring(far, shift)))  19.3 us
    all_to_all x1, blocking collectives, gather_gradients(): arrived = lax.all_to_all(value, 'z', 0, 0, tiled=True)  16.2 us
    all_to_all x1, blocking collectives, local(): spreads = lax.all_to_all(message, team_axes, 0, 0, tiled=True)  15.8 us
    all_to_all x1, starting transfers between devices, spread_out(): return lax.all_to_all(copies, axes, 0, 0, tiled=True)  15.7 us
    all_to_all x1, blocking collectives, local(): partials = lax.all_to_all(partial, team_axes, 0, 0, tiled=True)  15.2 us
    ppermute x3, starting transfers between devices, local(): lines.append(lax.ppermute(lines[0], 'yhi', ring(far, shift)))  14.8 us
    all_gather x1, blocking collectives, local(): pieces = lax.all_gather(gradients, 'yhi', axis=0)  12.1 us
    ppermute x3, starting transfers between devices, local(): lines.append(lax.ppermute(outs[shift], 'yhi', ring(far, -shift)))  11.3 us
  transfers between devices with their start and end apart: 11, of which 6 were waited for; matrix products, arithmetic and copies ran while one was open for 0% of the time, Pallas kernels for 0%

profile of v10, /device:TPU:1, one launch (start us, length us, event | category | flops | bytes accessed | tf_op | source)
XLA Modules:
  0.0 184.1 jit_solution(16955789016500934995)
XLA Ops:
  0.7 1.7 broadcast_in_dim.16
  2.3 15.7 %all-to-all-start.2 = ((bf16[12,128,128]{2,1,0:T(8,128)(2,1)}), bf16[12,128,128]{2,1,0:T(8,128)(2,1)S(1)}, u32[]{:S(2)}, u32[]{:S(2)}) async-start(bf16[12,128,128]{2,1,0:T(8,128)(2,1)} %broadcast_in_dim.16), calls=%async_computation.2 | async-start | bytes 786432 | tf_op jit(solution)/shard_map/all_to_all | solution.py:26
  18.7 0.1 maximum_bitcast_fusion
  18.8 0.1 copy.12
  18.9 0.1 fusion.8
  19.0 4.4 %collective-permute-start.2 = (bf16[3088,128]{1,0:T(8,128)(2,1)S(1)}, bf16[3088,128]{1,0:T(8,128)(2,1)S(1)}, u32[]{:S(2)}, u32[]{:S(2)}) collective-permute-start(bf16[3088,128]{1,0:T(8,128)(2,1)S(1)} %pad_maximum_fusion.refs_1_.refs_5_.refs_2_), channel_id=1, source_target_pairs={{0,36},{12,0},{24,12},{36,24},{1,37},{13,1},{25,13},{37,25},{2,38}... | collective-permute-start | bytes 2371592 | tf_op jit(solution)/shard_map/ppermute | solution.py:282
  23.4 1.9 %collective-permute-start.1 = (bf16[3088,128]{1,0:T(8,128)(2,1)S(1)}, bf16[3088,128]{1,0:T(8,128)(2,1)S(1)}, u32[]{:S(2)}, u32[]{:S(2)}) collective-permute-start(bf16[3088,128]{1,0:T(8,128)(2,1)S(1)} %pad_maximum_fusion.refs_1_.refs_5_.refs_2_), channel_id=1, source_target_pairs={{0,12},{12,24},{24,36},{36,0},{1,13},{13,25},{25,37},{37,1},{2,14}... | collective-permute-start | bytes 2371592 | tf_op jit(solution)/shard_map/ppermute | solution.py:282
  25.4 3.6 %collective-permute-start = (bf16[3088,128]{1,0:T(8,128)(2,1)S(1)}, bf16[3088,128]{1,0:T(8,128)(2,1)S(1)}, u32[]{:S(2)}, u32[]{:S(2)}) collective-permute-start(bf16[3088,128]{1,0:T(8,128)(2,1)S(1)} %pad_maximum_fusion.refs_1_.refs_5_.refs_2_), channel_id=1, source_target_pairs={{0,24},{12,36},{24,0},{36,12},{1,25},{13,37},{25,1},{37,13},{2,26}... | collective-permute-start | bytes 2371592 | tf_op jit(solution)/shard_map/ppermute | solution.py:282
  29.0 7.7 %all-to-all-done.2.refs_1_ = bf16[12,128,128]{2,1,0:T(8,128)(2,1)S(1)} async-done(((bf16[12,128,128]{2,1,0:T(8,128)(2,1)}), bf16[12,128,128]{2,1,0:T(8,128)(2,1)S(1)}, u32[]{:S(2)}, u32[]{:S(2)}) %all-to-all-start.2) | async-done | bytes 393248 | tf_op jit(solution)/shard_map/all_to_all | solution.py:26
  36.7 7.4 %collective-permute-start.5 = (bf16[12,128,128]{2,1,0:T(8,128)(2,1)S(1)}, bf16[12,128,128]{2,1,0:T(8,128)(2,1)S(1)}, u32[]{:S(2)}, u32[]{:S(2)}) collective-permute-start(bf16[12,128,128]{2,1,0:T(8,128)(2,1)S(1)} %all-to-all-done.2.refs_1_), channel_id=1, source_target_pairs={{0,96},{48,144},{96,0},{144,48},{1,97},{49,145},{97,1},{145,49},{2... | collective-permute-start | bytes 1179656 | tf_op jit(solution)/shard_map/ppermute | solution.py:287
  44.2 2.4 %collective-permute-start.4 = (bf16[12,128,128]{2,1,0:T(8,128)(2,1)S(1)}, bf16[12,128,128]{2,1,0:T(8,128)(2,1)S(1)}, u32[]{:S(2)}, u32[]{:S(2)}) collective-permute-start(bf16[12,128,128]{2,1,0:T(8,128)(2,1)S(1)} %all-to-all-done.2.refs_1_), channel_id=1, source_target_pairs={{0,48},{48,96},{96,144},{144,0},{1,49},{49,97},{97,145},{145,1},{2... | collective-permute-start | bytes 1179656 | tf_op jit(solution)/shard_map/ppermute | solution.py:287
  46.6 5.0 %collective-permute-start.3 = (bf16[12,128,128]{2,1,0:T(8,128)(2,1)S(1)}, bf16[12,128,128]{2,1,0:T(8,128)(2,1)S(1)}, u32[]{:S(2)}, u32[]{:S(2)}) collective-permute-start(bf16[12,128,128]{2,1,0:T(8,128)(2,1)S(1)} %all-to-all-done.2.refs_1_), channel_id=1, source_target_pairs={{0,144},{48,0},{96,48},{144,96},{1,145},{49,1},{97,49},{145,97},{2... | collective-permute-start | bytes 1179656 | tf_op jit(solution)/shard_map/ppermute | solution.py:287
  51.6 8.9 %collective-permute-done.refs_2_.refs_6_.refs_3_ = bf16[3088,128]{1,0:T(8,128)(2,1)S(1)} collective-permute-done((bf16[3088,128]{1,0:T(8,128)(2,1)S(1)}, bf16[3088,128]{1,0:T(8,128)(2,1)S(1)}, u32[]{:S(2)}, u32[]{:S(2)}) %collective-permute-start) | collective-permute-done | bytes 790560 | tf_op jit(solution)/shard_map/ppermute | solution.py:282
  60.5 10.2 %collective-permute-done.4.refs_6_.refs_3_ = bf16[12,128,128]{2,1,0:T(8,128)(2,1)S(1)} collective-permute-done((bf16[12,128,128]{2,1,0:T(8,128)(2,1)S(1)}, bf16[12,128,128]{2,1,0:T(8,128)(2,1)S(1)}, u32[]{:S(2)}, u32[]{:S(2)}) %collective-permute-start.4) | collective-permute-done | bytes 393248 | tf_op jit(solution)/shard_map/ppermute | solution.py:287
  70.7 9.1 %collective-permute-done.3.refs_5_.refs_2_ = bf16[12,128,128]{2,1,0:T(8,128)(2,1)S(1)} collective-permute-done((bf16[12,128,128]{2,1,0:T(8,128)(2,1)S(1)}, bf16[12,128,128]{2,1,0:T(8,128)(2,1)S(1)}, u32[]{:S(2)}, u32[]{:S(2)}) %collective-permute-start.3) | collective-permute-done | bytes 393248 | tf_op jit(solution)/shard_map/ppermute | solution.py:287
  79.8 2.2 %forward_tiles.1 = bf16[16,128,128]{2,1,0:T(8,128)(2,1)S(1)} custom-call(s32[4,128]{1,0:T(4,128)S(1)} %tile_codes.1.refs_0_, bf16[12,128,128]{2,1,0:T(8,128)(2,1)S(1)} %all-to-all-done.2.refs_1_, bf16[12,128,128]{2,1,0:T(8,128)(2,1)S(1)} %collective-permute-done.3.refs_5_.refs_2_, bf16[12,128,128]{2,1,0:T(8,128)(2,1)S(1)} %collective-permute-done.4.refs_6_.refs_3_, ...), custom_call_target="tpu_custom_call" | custom-call | tf_op jit(solution)/shard_map/forward_tiles/pallas_call | solution.py:300
  82.0 15.2 %all_to_all.30.refs_0_ = bf16[16,128,128]{2,1,0:T(8,128)(2,1)S(1)} all-to-all(bf16[16,128,128]{2,1,0:T(8,128)(2,1)S(1)} %forward_tiles.1), channel_id=1, replica_groups=mesh['ylo'=2,'core'=2,'yhi'=4,'x'=4,'z'=12] {'ylo','core','x'}, dimensions={0} | all-to-all | bytes 1048576 | tf_op jit(solution)/shard_map/all_to_all | solution.py:321
  97.2 1.1 dense_layer.1
  98.3 15.8 %all_to_all.31.refs_1_ = bf16[16,176,128]{2,1,0:T(8,128)(2,1)S(1)} all-to-all(bf16[16,176,128]{2,1,0:T(8,128)(2,1)S(1)} %get-tuple-element.21), channel_id=1, replica_groups=mesh['ylo'=2,'core'=2,'yhi'=4,'x'=4,'z'=12] {'ylo','core','x'}, dimensions={0} | all-to-all | bytes 1441792 | tf_op jit(solution)/shard_map/all_to_all | solution.py:336
  114.1 3.5 %backward_tiles.1 = (bf16[12,128,128]{2,1,0:T(8,128)(2,1)S(1)}, bf16[12,128,128]{2,1,0:T(8,128)(2,1)}, bf16[12,128,128]{2,1,0:T(8,128)(2,1)}, bf16[12,128,128]{2,1,0:T(8,128)(2,1)}, bf16[12,48,128]{2,1,0:T(8,128)(2,1)}) custom-call(s32[4,128]{1,0:T(4,128)S(1)} %tile_codes.1.refs_0_, bf16[16,176,128]{2,1,0:T(8,128)(2,1)S(1)} %all_to_all.31.refs_1_, ...), custom_call_target="tpu_custom_call" | custom-call | tf_op jit(solution)/shard_map/backward_tiles/pallas_call | solution.py:338
  117.6 5.2 %collective-permute-start.6 = (bf16[12,128,128]{2,1,0:T(8,128)(2,1)}, bf16[12,128,128]{2,1,0:T(8,128)(2,1)S(1)}, u32[]{:S(2)}, u32[]{:S(2)}) collective-permute-start(bf16[12,128,128]{2,1,0:T(8,128)(2,1)} %get-tuple-element.23), channel_id=1, source_target_pairs={{0,96},{48,144},{96,0},{144,48},{1,97},{49,145},{97,1},{145,49},{2... | collective-permute-start | bytes 1179656 | tf_op jit(solution)/shard_map/ppermute | solution.py:364
  122.8 4.1 %collective-permute-start.7 = (bf16[12,128,128]{2,1,0:T(8,128)(2,1)}, bf16[12,128,128]{2,1,0:T(8,128)(2,1)S(1)}, u32[]{:S(2)}, u32[]{:S(2)}) collective-permute-start(bf16[12,128,128]{2,1,0:T(8,128)(2,1)} %get-tuple-element.24), channel_id=1, source_target_pairs={{0,144},{48,0},{96,48},{144,96},{1,145},{49,1},{97,49},{145,97},{2... | collective-permute-start | bytes 1179656 | tf_op jit(solution)/shard_map/ppermute | solution.py:364
  126.8 2.1 %collective-permute-start.8 = (bf16[12,128,128]{2,1,0:T(8,128)(2,1)}, bf16[12,128,128]{2,1,0:T(8,128)(2,1)S(1)}, u32[]{:S(2)}, u32[]{:S(2)}) collective-permute-start(bf16[12,128,128]{2,1,0:T(8,128)(2,1)} %get-tuple-element.25), channel_id=1, source_target_pairs={{0,48},{48,96},{96,144},{144,0},{1,49},{49,97},{97,145},{145,1},{2... | collective-permute-start | bytes 1179656 | tf_op jit(solution)/shard_map/ppermute | solution.py:364
  129.0 26.8 %conditional.1 = (bf16[272,128]{1,0:T(8,128)(2,1)S(1)}) conditional(s32[]{:T(128)} %convert_element_type.4, () %tuple.14, bf16[12,48,128]{2,1,0:T(8,128)(2,1)} %get-tuple-element.26), branch_computations={%region_0.1_spmd, %region_1.2_spmd} | conditional | bytes 425992 | solution.py:389
  129.0 16.2 %all_to_all.28.refs_0_ = bf16[12,48,128]{2,1,0:T(8,128)(2,1)S(1)} all-to-all(bf16[12,48,128]{2,1,0:T(8,128)(2,1)} %param.1), channel_id=1, replica_groups=mesh['ylo'=2,'core'=2,'yhi'=4,'x'=4,'z'=12] {'z'}, dimensions={0} | all-to-all | bytes 294912 | tf_op jit(solution)/shard_map/cond/branch_1_fun/all_to_all | solution.py:367
  145.2 10.5 %all_to_all.29.refs_0_ = bf16[8,32,128]{2,1,0:T(8,128)(2,1)S(1)} all-to-all(bf16[8,32,128]{2,1,0:T(8,128)(2,1)S(1)} %get-tuple-element.4), channel_id=1, replica_groups=mesh['ylo'=2,'core'=2,'yhi'=4,'x'=4,'z'=12] {'core','x'}, dimensions={0} | all-to-all | bytes 131072 | tf_op jit(solution)/shard_map/cond/branch_1_fun/all_to_all | solution.py:379
  155.7 3.9 %collective-permute-done.7.refs_2_ = bf16[12,128,128]{2,1,0:T(8,128)(2,1)S(1)} collective-permute-done((bf16[12,128,128]{2,1,0:T(8,128)(2,1)}, bf16[12,128,128]{2,1,0:T(8,128)(2,1)S(1)}, u32[]{:S(2)}, u32[]{:S(2)}) %collective-permute-start.7) | collective-permute-done | bytes 393248 | tf_op jit(solution)/shard_map/ppermute | solution.py:364
  159.7 0.9 middle_sums.1
  160.6 4.1 %all-to-all-start.5 = ((bf16[12,128,128]{2,1,0:T(8,128)(2,1)}), bf16[12,128,128]{2,1,0:T(8,128)(2,1)S(1)}, u32[]{:S(2)}, u32[]{:S(2)}) async-start(bf16[12,128,128]{2,1,0:T(8,128)(2,1)} %middle_sums.1), calls=%async_computation.5 | async-start | bytes 786432 | tf_op jit(solution)/shard_map/all_to_all | solution.py:405
  164.7 12.1 %all-gather = bf16[1088,128]{1,0:T(8,128)(2,1)S(1)} all-gather(bf16[272,128]{1,0:T(8,128)(2,1)S(1)} %get-tuple-element.33.refs_4_), channel_id=2, replica_groups=mesh['ylo'=2,'core'=2,'yhi'=4,'x'=4,'z'=12] {'yhi'}, dimensions={0}, use_global_device_ids=true | all-gather | bytes 348160 | tf_op jit(solution)/shard_map/all_gather | solution.py:404
  176.8 6.6 %all-to-all-done.5.refs_0_ = bf16[12,128,128]{2,1,0:T(8,128)(2,1)S(1)} async-done(((bf16[12,128,128]{2,1,0:T(8,128)(2,1)}), bf16[12,128,128]{2,1,0:T(8,128)(2,1)S(1)}, u32[]{:S(2)}, u32[]{:S(2)}) %all-to-all-start.5) | async-done | bytes 393248 | tf_op jit(solution)/shard_map/all_to_all | solution.py:405
  183.4 0.7 last_sums.1
  (22 shorter events, 0.2 us)
Async XLA Ops:
  0.6 18.2 %copy-start.4 = (s32[1,1,48]{2,1,0:T(1,128)S(1)}, s32[1,1,48]{2,1,0:T(1,128)}, u32[]{:S(2)}) copy-start(s32[1,1,48]{2,1,0:T(1,128)} %param.12) | copy-start | bytes 580
  0.6 18.2 %copy-start.5 = (s32[1,1,48]{2,1,0:T(1,128)S(1)}, s32[1,1,48]{2,1,0:T(1,128)}, u32[]{:S(2)}) copy-start(s32[1,1,48]{2,1,0:T(1,128)} %param.11) | copy-start | bytes 580
  0.7 18.3 %copy-start.3 = (bf16[1,1,48,64,128]{4,3,2,1,0:T(8,128)(2,1)S(1)}, bf16[1,1,48,64,128]{4,3,2,1,0:T(8,128)(2,1)}, u32[]{:S(2)}) copy-start(bf16[1,1,48,64,128]{4,3,2,1,0:T(8,128)(2,1)} %param.14) | copy-start | bytes 2359300
  2.3 34.4 %all-to-all-start.2 = ((bf16[12,128,128]{2,1,0:T(8,128)(2,1)}), bf16[12,128,128]{2,1,0:T(8,128)(2,1)S(1)}, u32[]{:S(2)}, u32[]{:S(2)}) async-start(bf16[12,128,128]{2,1,0:T(8,128)(2,1)} %broadcast_in_dim.16), calls=%async_computation.2 | async-start | bytes 786432 | tf_op jit(solution)/shard_map/all_to_all | solution.py:26
  19.0 27.5 %collective-permute-start.2 = (bf16[3088,128]{1,0:T(8,128)(2,1)S(1)}, bf16[3088,128]{1,0:T(8,128)(2,1)S(1)}, u32[]{:S(2)}, u32[]{:S(2)}) collective-permute-start(bf16[3088,128]{1,0:T(8,128)(2,1)S(1)} %pad_maximum_fusion.refs_1_.refs_5_.refs_2_), channel_id=1, source_target_pairs={{0,36},{12,0},{24,12},{36,24},{1,37},{13,1},{25,13},{37,25},{2,38}... | collective-permute-start | bytes 2371592 | tf_op jit(solution)/shard_map/ppermute | solution.py:282
  23.4 28.1 %collective-permute-start.1 = (bf16[3088,128]{1,0:T(8,128)(2,1)S(1)}, bf16[3088,128]{1,0:T(8,128)(2,1)S(1)}, u32[]{:S(2)}, u32[]{:S(2)}) collective-permute-start(bf16[3088,128]{1,0:T(8,128)(2,1)S(1)} %pad_maximum_fusion.refs_1_.refs_5_.refs_2_), channel_id=1, source_target_pairs={{0,12},{12,24},{24,36},{36,0},{1,13},{13,25},{25,37},{37,1},{2,14}... | collective-permute-start | bytes 2371592 | tf_op jit(solution)/shard_map/ppermute | solution.py:282
  25.4 35.1 %collective-permute-start = (bf16[3088,128]{1,0:T(8,128)(2,1)S(1)}, bf16[3088,128]{1,0:T(8,128)(2,1)S(1)}, u32[]{:S(2)}, u32[]{:S(2)}) collective-permute-start(bf16[3088,128]{1,0:T(8,128)(2,1)S(1)} %pad_maximum_fusion.refs_1_.refs_5_.refs_2_), channel_id=1, source_target_pairs={{0,24},{12,36},{24,0},{36,12},{1,25},{13,37},{25,1},{37,13},{2,26}... | collective-permute-start | bytes 2371592 | tf_op jit(solution)/shard_map/ppermute | solution.py:282
  36.7 23.8 %collective-permute-start.5 = (bf16[12,128,128]{2,1,0:T(8,128)(2,1)S(1)}, bf16[12,128,128]{2,1,0:T(8,128)(2,1)S(1)}, u32[]{:S(2)}, u32[]{:S(2)}) collective-permute-start(bf16[12,128,128]{2,1,0:T(8,128)(2,1)S(1)} %all-to-all-done.2.refs_1_), channel_id=1, source_target_pairs={{0,96},{48,144},{96,0},{144,48},{1,97},{49,145},{97,1},{145,49},{2... | collective-permute-start | bytes 1179656 | tf_op jit(solution)/shard_map/ppermute | solution.py:287
  44.2 26.5 %collective-permute-start.4 = (bf16[12,128,128]{2,1,0:T(8,128)(2,1)S(1)}, bf16[12,128,128]{2,1,0:T(8,128)(2,1)S(1)}, u32[]{:S(2)}, u32[]{:S(2)}) collective-permute-start(bf16[12,128,128]{2,1,0:T(8,128)(2,1)S(1)} %all-to-all-done.2.refs_1_), channel_id=1, source_target_pairs={{0,48},{48,96},{96,144},{144,0},{1,49},{49,97},{97,145},{145,1},{2... | collective-permute-start | bytes 1179656 | tf_op jit(solution)/shard_map/ppermute | solution.py:287
  46.6 33.1 %collective-permute-start.3 = (bf16[12,128,128]{2,1,0:T(8,128)(2,1)S(1)}, bf16[12,128,128]{2,1,0:T(8,128)(2,1)S(1)}, u32[]{:S(2)}, u32[]{:S(2)}) collective-permute-start(bf16[12,128,128]{2,1,0:T(8,128)(2,1)S(1)} %all-to-all-done.2.refs_1_), channel_id=1, source_target_pairs={{0,144},{48,0},{96,48},{144,96},{1,145},{49,1},{97,49},{145,97},{2... | collective-permute-start | bytes 1179656 | tf_op jit(solution)/shard_map/ppermute | solution.py:287
  82.0 15.2 %copy-start = (bf16[128,256]{1,0:T(8,128)(2,1)S(1)}, bf16[128,256]{1,0:T(8,128)(2,1)}, u32[]{:S(2)}) copy-start(bf16[128,256]{1,0:T(8,128)(2,1)} %refs_1_.1) | copy-start | bytes 196612
  82.0 15.2 %copy-start.1 = (bf16[128,256]{1,0:T(8,128)(2,1)S(1)}, bf16[128,256]{1,0:T(8,128)(2,1)}, u32[]{:S(2)}) copy-start(bf16[128,256]{1,0:T(8,128)(2,1)} %refs_3_.1) | copy-start | bytes 196612
  82.0 15.2 %copy-start.2 = (f32[256]{0:T(256)S(1)}, f32[256]{0:T(256)}, u32[]{:S(2)}) copy-start(f32[256]{0:T(256)} %param.16) | copy-start | bytes 3076
  117.6 38.1 %collective-permute-start.6 = (bf16[12,128,128]{2,1,0:T(8,128)(2,1)}, bf16[12,128,128]{2,1,0:T(8,128)(2,1)S(1)}, u32[]{:S(2)}, u32[]{:S(2)}) collective-permute-start(bf16[12,128,128]{2,1,0:T(8,128)(2,1)} %get-tuple-element.23), channel_id=1, source_target_pairs={{0,96},{48,144},{96,0},{144,48},{1,97},{49,145},{97,1},{145,49},{2... | collective-permute-start | bytes 1179656 | tf_op jit(solution)/shard_map/ppermute | solution.py:364
  122.8 36.9 %collective-permute-start.7 = (bf16[12,128,128]{2,1,0:T(8,128)(2,1)}, bf16[12,128,128]{2,1,0:T(8,128)(2,1)S(1)}, u32[]{:S(2)}, u32[]{:S(2)}) collective-permute-start(bf16[12,128,128]{2,1,0:T(8,128)(2,1)} %get-tuple-element.24), channel_id=1, source_target_pairs={{0,144},{48,0},{96,48},{144,96},{1,145},{49,1},{97,49},{145,97},{2... | collective-permute-start | bytes 1179656 | tf_op jit(solution)/shard_map/ppermute | solution.py:364
  126.8 32.8 %collective-permute-start.8 = (bf16[12,128,128]{2,1,0:T(8,128)(2,1)}, bf16[12,128,128]{2,1,0:T(8,128)(2,1)S(1)}, u32[]{:S(2)}, u32[]{:S(2)}) collective-permute-start(bf16[12,128,128]{2,1,0:T(8,128)(2,1)} %get-tuple-element.25), channel_id=1, source_target_pairs={{0,48},{48,96},{96,144},{144,0},{1,49},{49,97},{97,145},{145,1},{2... | collective-permute-start | bytes 1179656 | tf_op jit(solution)/shard_map/ppermute | solution.py:364
  160.6 22.8 %all-to-all-start.5 = ((bf16[12,128,128]{2,1,0:T(8,128)(2,1)}), bf16[12,128,128]{2,1,0:T(8,128)(2,1)S(1)}, u32[]{:S(2)}, u32[]{:S(2)}) async-start(bf16[12,128,128]{2,1,0:T(8,128)(2,1)} %middle_sums.1), calls=%async_computation.5 | async-start | bytes 786432 | tf_op jit(solution)/shard_map/all_to_all | solution.py:405

commit v11 on v10

--- a/solution.py
+++ b/solution.py
@@ -14,6 +14,7 @@
 col_axes = ("yhi", "x", "z")
 team_axes = ("ylo", "core", "x")
 share_axes = ("core", "x")
+tail_rows = 64
 group = 4
 lanes = 128
 vmem_bytes = 12 * 1024 * 1024
@@ -56,12 +57,15 @@
 
 def forward_kernel(codes, *refs, slots, height, blocks, line_order, across):
     far = len(line_order)
-    lines, tile_refs = refs[:far], refs[far : far + across]
-    out, slabs, chosen, totals, picked = refs[far + across :]
+    lines, tails, tile_refs = refs[:far], refs[far], refs[far + 1 : far + 1 + across]
+    out, slabs, chosen, totals, picked = refs[far + 1 + across :]
     slab_count = slabs.shape[0]
     near = slab_count // far
     for shift, line in zip(line_order, lines):
-        slabs[pl.ds(shift * near, near)] = line[...]
+        lead = line.shape[1]
+        slabs[pl.ds(shift * near, near), pl.ds(0, lead), :] = line[...]
+        if lead < slabs.shape[1]:
+            slabs[pl.ds(shift * near, near), pl.ds(lead, tails.shape[1]), :] = tails[...]
     dummy = slab_count * 64 + blocks
     totals[...] = jnp.zeros_like(totals)
     total = pick_tiles(codes, tile_refs, chosen, picked, slots, height, dummy)
@@ -281,10 +285,20 @@
     for shift in sorted(range(1, across), key=lambda shift: -min(shift, across - shift)):
         buffers.append(lax.ppermute(own, "x", ring(across, shift)))
 
+    opposite = far // 2
+    tail = lax.ppermute(features[nodes - tail_rows :], "yhi", ring(far, opposite))
     lines = [spread_out(features, "z", near)]
     line_order = [0] + longest_first[::-1]
     for shift in line_order[1:]:
-        lines.append(lax.ppermute(lines[0], "yhi", ring(far, shift)))
+        line = lines[0][:, : nodes - tail_rows] if shift == opposite else lines[0]
+        lines.append(lax.ppermute(line, "yhi", ring(far, shift)))
+    some = tile_counts[0, 0] > 0
+    tails = lax.cond(
+        some,
+        lambda value: spread_out(value, "z", near),
+        lambda value: jnp.zeros((near,) + value.shape, value.dtype),
+        tail,
+    )
 
     codes = pl.pallas_call(
         lambda *refs: codes_kernel(*refs, across=across, top=slots * height),
@@ -307,7 +321,7 @@
             across=across,
         ),
         out_shape=jax.ShapeDtypeStruct((members, nodes, width), jnp.bfloat16),
-        in_specs=[in_smem()] + [in_vmem()] * (far + across),
+        in_specs=[in_smem()] + [in_vmem()] * (far + 1 + across),
         out_specs=in_vmem(),
         scratch_shapes=[
             pltpu.VMEM((far * near, nodes, width), jnp.bfloat16),
@@ -317,7 +331,7 @@
         ],
         compiler_params=params,
         name="forward_tiles",
-    )(codes, *lines, *buffers)
+    )(codes, *lines, tails, *buffers)
     partials = lax.all_to_all(partial, team_axes, 0, 0, tiled=True)
 
     holders = lax.axis_size(share_axes)
@@ -387,7 +401,7 @@
         )(shares, bias_block)
 
     gradients = lax.cond(
-        tile_counts[0, 0] > 0,
+        some,
         gather_gradients,
         lambda value: jnp.zeros((2 * width + 16, lanes), jnp.bfloat16),
         outs[far],

time: 186 us -> 195 us (1.048)
  waiting for transfers between devices: 46.4 us -> 10.9 us
  blocking collectives: 69.8 us -> 104 us
  starting transfers between devices: 55.9 us -> 62.8 us
  local copies, waits for them, and re-layouts: 1.79 us -> 4.75 us
    all_to_all x1, blocking collectives: 15.2 us -> 35 us  [local(): partials = lax.all_to_all(partial, team_axes, 0, 0, tiled=True)]
    ppermute x3 -> x4, waiting for transfers between devices: 19.3 us -> 0.01 us  [the longest x3 0.01 us: local(): lines.append(lax.ppermute(line, 'yhi', ring(far, shift)))]
    all_to_all x0 -> x1, blocking collectives: none -> 16.3 us  [spread_out(): return lax.all_to_all(copies, axes, 0, 0, tiled=True)]
    ppermute x3, waiting for transfers between devices: 8.88 us -> 0.01 us  [local(): buffers.append(lax.ppermute(own, 'x', ring(across, shift)))]
    all_to_all x1, waiting for transfers between devices: 7.71 us -> 0.01 us  [spread_out(): return lax.all_to_all(copies, axes, 0, 0, tiled=True)]
    ppermute x3 -> x4, starting transfers between devices: 14.8 us -> 21.9 us  [the longest x3 14.5 us: local(): lines.append(lax.ppermute(line, 'yhi', ring(far, shift)))]
  transfers between devices with their start and end apart: 11 -> 12, of which waited for: 6 -> 2; matrix products, arithmetic and copies ran while one was open for 0% -> 1% of each run, Pallas kernels for 0% -> 0%
where the time goes in v11:
time: 195 us; the launch traced here: 192 us
  blocking collectives  104 us (53%)
  starting transfers between devices  62.8 us (32%)
  waiting for transfers between devices  10.9 us (6%)
  Pallas kernels  7.58 us (4%)
  local copies, waits for them, and re-layouts  4.75 us (2%)
    all_to_all x1, blocking collectives, local(): partials = lax.all_to_all(partial, team_axes, 0, 0, tiled=True)  35 us
    all_to_all x1, blocking collectives, spread_out(): return lax.all_to_all(copies, axes, 0, 0, tiled=True)  16.3 us
    all_to_all x1, blocking collectives, local(): spreads = lax.all_to_all(message, team_axes, 0, 0, tiled=True)  15.8 us
    all_to_all x1, starting transfers between devices, spread_out(): return lax.all_to_all(copies, axes, 0, 0, tiled=True)  15.7 us
    all_to_all x1, blocking collectives, gather_gradients(): arrived = lax.all_to_all(value, 'z', 0, 0, tiled=True)  15 us
    ppermute x3, starting transfers between devices, local(): lines.append(lax.ppermute(line, 'yhi', ring(far, shift)))  14.5 us
    all_gather x1, blocking collectives, local(): pieces = lax.all_gather(gradients, 'yhi', axis=0)  12.2 us
    ppermute x3, starting transfers between devices, local(): lines.append(lax.ppermute(outs[shift], 'yhi', ring(far, -shift)))  11.7 us
  transfers between devices with their start and end apart: 12, of which 2 were waited for; matrix products, arithmetic and copies ran while one was open for 1% of the time, Pallas kernels for 0%

profile of v11, /device:TPU:1, one launch (start us, length us, event | category | flops | bytes accessed | tf_op | source)
XLA Modules:
  0.0 191.8 jit_solution(7940072959777200744)
XLA Ops:
  0.7 1.7 broadcast_in_dim.22
  2.3 15.7 %all-to-all-start.3 = ((bf16[12,128,128]{2,1,0:T(8,128)(2,1)}), bf16[12,128,128]{2,1,0:T(8,128)(2,1)S(1)}, u32[]{:S(2)}, u32[]{:S(2)}) async-start(bf16[12,128,128]{2,1,0:T(8,128)(2,1)} %broadcast_in_dim.22), calls=%async_computation.3 | async-start | bytes 786432 | tf_op jit(solution)/shard_map/all_to_all | solution.py:27
  19.1 4.4 %collective-permute-start.2 = (bf16[3088,128]{1,0:T(8,128)(2,1)S(1)}, bf16[3088,128]{1,0:T(8,128)(2,1)S(1)}, u32[]{:S(2)}, u32[]{:S(2)}) collective-permute-start(bf16[3088,128]{1,0:T(8,128)(2,1)S(1)} %pad_maximum_fusion.refs_1_.refs_6_.refs_2_), channel_id=1, source_target_pairs={{0,36},{12,0},{24,12},{36,24},{1,37},{13,1},{25,13},{37,25},{2,38}... | collective-permute-start | bytes 2371592 | tf_op jit(solution)/shard_map/ppermute | solution.py:286
  23.5 1.9 %collective-permute-start.1 = (bf16[3088,128]{1,0:T(8,128)(2,1)S(1)}, bf16[3088,128]{1,0:T(8,128)(2,1)S(1)}, u32[]{:S(2)}, u32[]{:S(2)}) collective-permute-start(bf16[3088,128]{1,0:T(8,128)(2,1)S(1)} %pad_maximum_fusion.refs_1_.refs_6_.refs_2_), channel_id=1, source_target_pairs={{0,12},{12,24},{24,36},{36,0},{1,13},{13,25},{25,37},{37,1},{2,14}... | collective-permute-start | bytes 2371592 | tf_op jit(solution)/shard_map/ppermute | solution.py:286
  25.4 3.6 %collective-permute-start = (bf16[3088,128]{1,0:T(8,128)(2,1)S(1)}, bf16[3088,128]{1,0:T(8,128)(2,1)S(1)}, u32[]{:S(2)}, u32[]{:S(2)}) collective-permute-start(bf16[3088,128]{1,0:T(8,128)(2,1)S(1)} %pad_maximum_fusion.refs_1_.refs_6_.refs_2_), channel_id=1, source_target_pairs={{0,24},{12,36},{24,0},{36,12},{1,25},{13,37},{25,1},{37,13},{2,26}... | collective-permute-start | bytes 2371592 | tf_op jit(solution)/shard_map/ppermute | solution.py:286
  29.0 0.6 slice.7
  29.6 7.4 %collective-permute-start.6 = (bf16[64,128]{1,0:T(8,128)(2,1)}, bf16[64,128]{1,0:T(8,128)(2,1)}, u32[]{:S(2)}, u32[]{:S(2)}) collective-permute-start(bf16[64,128]{1,0:T(8,128)(2,1)} %slice.7), channel_id=1, source_target_pairs={{0,96},{48,144},{96,0},{144,48},{1,97},{49,145},{97,1},{145,49},{2... | collective-permute-start | bytes 49160 | tf_op jit(solution)/shard_map/ppermute | solution.py:289
  37.1 3.8 %collective-permute-start.4 = (bf16[12,128,128]{2,1,0:T(8,128)(2,1)S(1)}, bf16[12,128,128]{2,1,0:T(8,128)(2,1)}, u32[]{:S(2)}, u32[]{:S(2)}) collective-permute-start(bf16[12,128,128]{2,1,0:T(8,128)(2,1)S(1)} %all-to-all-done.3.refs_1_), channel_id=1, source_target_pairs={{0,48},{48,96},{96,144},{144,0},{1,49},{49,97},{97,145},{145,1},{2... | collective-permute-start | bytes 1179656 | tf_op jit(solution)/shard_map/ppermute | solution.py:294
  40.9 3.6 %collective-permute-start.3 = (bf16[12,128,128]{2,1,0:T(8,128)(2,1)S(1)}, bf16[12,128,128]{2,1,0:T(8,128)(2,1)}, u32[]{:S(2)}, u32[]{:S(2)}) collective-permute-start(bf16[12,128,128]{2,1,0:T(8,128)(2,1)S(1)} %all-to-all-done.3.refs_1_), channel_id=1, source_target_pairs={{0,144},{48,0},{96,48},{144,96},{1,145},{49,1},{97,49},{145,97},{2... | collective-permute-start | bytes 1179656 | tf_op jit(solution)/shard_map/ppermute | solution.py:294
  44.5 0.7 slice.8
  45.2 7.0 %collective-permute-start.5 = (bf16[12,64,128]{2,1,0:T(8,128)(2,1)}, bf16[12,64,128]{2,1,0:T(8,128)(2,1)}, u32[]{:S(2)}, u32[]{:S(2)}) collective-permute-start(bf16[12,64,128]{2,1,0:T(8,128)(2,1)} %slice.8), channel_id=1, source_target_pairs={{0,96},{48,144},{96,0},{144,48},{1,97},{49,145},{97,1},{145,49},{2... | collective-permute-start | bytes 589832 | tf_op jit(solution)/shard_map/ppermute | solution.py:294
  52.3 17.1 %conditional.2 = (bf16[12,64,128]{2,1,0:T(8,128)(2,1)}) conditional(s32[]{:T(128)} %convert_element_type.2, () %tuple.20, bf16[64,128]{1,0:T(8,128)(2,1)} %collective-permute-done.6), branch_computations={%region_0.1_spmd, %region_1.2_spmd} | conditional | bytes 606216 | solution.py:296
  52.3 0.7 broadcast_in_dim.3
  53.1 16.3 %all_to_all.32 = bf16[12,64,128]{2,1,0:T(8,128)(2,1)} all-to-all(bf16[12,64,128]{2,1,0:T(8,128)(2,1)S(1)} %broadcast_in_dim.3), channel_id=1, replica_groups=mesh['ylo'=2,'core'=2,'yhi'=4,'x'=4,'z'=12] {'z'}, dimensions={0} | all-to-all | bytes 393216 | tf_op jit(solution)/shard_map/cond/branch_1_fun/all_to_all | solution.py:27
  69.4 0.9 copy-done.3
  70.3 2.1 %forward_tiles.1 = bf16[16,128,128]{2,1,0:T(8,128)(2,1)S(1)} custom-call(s32[4,128]{1,0:T(4,128)S(1)} %tile_codes.1.refs_0_, bf16[12,128,128]{2,1,0:T(8,128)(2,1)S(1)} %all-to-all-done.3.refs_1_, bf16[12,128,128]{2,1,0:T(8,128)(2,1)} %collective-permute-done.3.refs_5_.refs_2_, bf16[12,128,128]{2,1,0:T(8,128)(2,1)} %collective-permute-done.4.refs_6_.refs_3_, ...), custom_call_target="tpu_custom_call" | custom-call | tf_op jit(solution)/shard_map/forward_tiles/pallas_call | solution.py:314
  72.5 35.0 %all_to_all.35.refs_0_ = bf16[16,128,128]{2,1,0:T(8,128)(2,1)S(1)} all-to-all(bf16[16,128,128]{2,1,0:T(8,128)(2,1)S(1)} %forward_tiles.1), channel_id=1, replica_groups=mesh['ylo'=2,'core'=2,'yhi'=4,'x'=4,'z'=12] {'ylo','core','x'}, dimensions={0} | all-to-all | bytes 1048576 | tf_op jit(solution)/shard_map/all_to_all | solution.py:335
  107.5 1.1 dense_layer.1
  108.6 15.8 %all_to_all.36.refs_1_ = bf16[16,176,128]{2,1,0:T(8,128)(2,1)S(1)} all-to-all(bf16[16,176,128]{2,1,0:T(8,128)(2,1)S(1)} %get-tuple-element.25), channel_id=1, replica_groups=mesh['ylo'=2,'core'=2,'yhi'=4,'x'=4,'z'=12] {'ylo','core','x'}, dimensions={0} | all-to-all | bytes 1441792 | tf_op jit(solution)/shard_map/all_to_all | solution.py:350
  124.4 2.7 %backward_tiles.1 = (bf16[12,128,128]{2,1,0:T(8,128)(2,1)S(1)}, bf16[12,128,128]{2,1,0:T(8,128)(2,1)}, bf16[12,128,128]{2,1,0:T(8,128)(2,1)}, bf16[12,128,128]{2,1,0:T(8,128)(2,1)}, bf16[12,48,128]{2,1,0:T(8,128)(2,1)}) custom-call(s32[4,128]{1,0:T(4,128)S(1)} %tile_codes.1.refs_0_, bf16[16,176,128]{2,1,0:T(8,128)(2,1)S(1)} %all_to_all.36.refs_1_, ...), custom_call_target="tpu_custom_call" | custom-call | tf_op jit(solution)/shard_map/backward_tiles/pallas_call | solution.py:352
  127.1 5.5 %collective-permute-start.7 = (bf16[12,128,128]{2,1,0:T(8,128)(2,1)}, bf16[12,128,128]{2,1,0:T(8,128)(2,1)S(1)}, u32[]{:S(2)}, u32[]{:S(2)}) collective-permute-start(bf16[12,128,128]{2,1,0:T(8,128)(2,1)} %get-tuple-element.27), channel_id=1, source_target_pairs={{0,96},{48,144},{96,0},{144,48},{1,97},{49,145},{97,1},{145,49},{2... | collective-permute-start | bytes 1179656 | tf_op jit(solution)/shard_map/ppermute | solution.py:378
  132.6 2.1 %collective-permute-start.8 = (bf16[12,128,128]{2,1,0:T(8,128)(2,1)}, bf16[12,128,128]{2,1,0:T(8,128)(2,1)S(1)}, u32[]{:S(2)}, u32[]{:S(2)}) collective-permute-start(bf16[12,128,128]{2,1,0:T(8,128)(2,1)} %get-tuple-element.28), channel_id=1, source_target_pairs={{0,144},{48,0},{96,48},{144,96},{1,145},{49,1},{97,49},{145,97},{2... | collective-permute-start | bytes 1179656 | tf_op jit(solution)/shard_map/ppermute | solution.py:378
  134.7 4.1 %collective-permute-start.9 = (bf16[12,128,128]{2,1,0:T(8,128)(2,1)}, bf16[12,128,128]{2,1,0:T(8,128)(2,1)S(1)}, u32[]{:S(2)}, u32[]{:S(2)}) collective-permute-start(bf16[12,128,128]{2,1,0:T(8,128)(2,1)} %get-tuple-element.29), channel_id=1, source_target_pairs={{0,48},{48,96},{96,144},{144,0},{1,49},{49,97},{97,145},{145,1},{2... | collective-permute-start | bytes 1179656 | tf_op jit(solution)/shard_map/ppermute | solution.py:378
  138.8 24.7 %conditional.3 = (bf16[272,128]{1,0:T(8,128)(2,1)S(1)}) conditional(s32[]{:T(128)} %convert_element_type.2, () %tuple.21, bf16[12,48,128]{2,1,0:T(8,128)(2,1)} %get-tuple-element.30), branch_computations={%region_2.3_spmd, %region_3.4_spmd} | conditional | bytes 425992 | solution.py:403
  138.8 15.0 %all_to_all.33.refs_0_ = bf16[12,48,128]{2,1,0:T(8,128)(2,1)S(1)} all-to-all(bf16[12,48,128]{2,1,0:T(8,128)(2,1)} %param.3), channel_id=1, replica_groups=mesh['ylo'=2,'core'=2,'yhi'=4,'x'=4,'z'=12] {'z'}, dimensions={0} | all-to-all | bytes 294912 | tf_op jit(solution)/shard_map/cond/branch_1_fun/all_to_all | solution.py:381
  153.9 9.6 %all_to_all.34.refs_0_ = bf16[8,32,128]{2,1,0:T(8,128)(2,1)S(1)} all-to-all(bf16[8,32,128]{2,1,0:T(8,128)(2,1)S(1)} %get-tuple-element.8), channel_id=1, replica_groups=mesh['ylo'=2,'core'=2,'yhi'=4,'x'=4,'z'=12] {'core','x'}, dimensions={0} | all-to-all | bytes 131072 | tf_op jit(solution)/shard_map/cond/branch_1_fun/all_to_all | solution.py:393
  163.5 4.7 %collective-permute-done.8.refs_2_ = bf16[12,128,128]{2,1,0:T(8,128)(2,1)S(1)} collective-permute-done((bf16[12,128,128]{2,1,0:T(8,128)(2,1)}, bf16[12,128,128]{2,1,0:T(8,128)(2,1)S(1)}, u32[]{:S(2)}, u32[]{:S(2)}) %collective-permute-start.8) | collective-permute-done | bytes 393248 | tf_op jit(solution)/shard_map/ppermute | solution.py:378
  168.2 0.9 middle_sums.1
  169.2 3.6 %all-to-all-start.6 = ((bf16[12,128,128]{2,1,0:T(8,128)(2,1)}), bf16[12,128,128]{2,1,0:T(8,128)(2,1)S(1)}, u32[]{:S(2)}, u32[]{:S(2)}) async-start(bf16[12,128,128]{2,1,0:T(8,128)(2,1)} %middle_sums.1), calls=%async_computation.6 | async-start | bytes 786432 | tf_op jit(solution)/shard_map/all_to_all | solution.py:419
  172.7 12.2 %all-gather = bf16[1088,128]{1,0:T(8,128)(2,1)S(1)} all-gather(bf16[272,128]{1,0:T(8,128)(2,1)S(1)} %get-tuple-element.38.refs_4_), channel_id=2, replica_groups=mesh['ylo'=2,'core'=2,'yhi'=4,'x'=4,'z'=12] {'yhi'}, dimensions={0}, use_global_device_ids=true | all-gather | bytes 348160 | tf_op jit(solution)/shard_map/all_gather | solution.py:418
  185.0 6.1 %all-to-all-done.6.refs_0_ = bf16[12,128,128]{2,1,0:T(8,128)(2,1)S(1)} async-done(((bf16[12,128,128]{2,1,0:T(8,128)(2,1)}), bf16[12,128,128]{2,1,0:T(8,128)(2,1)S(1)}, u32[]{:S(2)}, u32[]{:S(2)}) %all-to-all-start.6) | async-done | bytes 393248 | tf_op jit(solution)/shard_map/all_to_all | solution.py:419
  191.1 0.7 last_sums.1
  (33 shorter events, 0.5 us)
Async XLA Ops:
  0.6 18.3 %copy-start.6 = (s32[1,1,48]{2,1,0:T(1,128)S(1)}, s32[1,1,48]{2,1,0:T(1,128)}, u32[]{:S(2)}) copy-start(s32[1,1,48]{2,1,0:T(1,128)} %param.14) | copy-start | bytes 580
  0.6 18.2 %copy-start.7 = (s32[1,1,48]{2,1,0:T(1,128)S(1)}, s32[1,1,48]{2,1,0:T(1,128)}, u32[]{:S(2)}) copy-start(s32[1,1,48]{2,1,0:T(1,128)} %param.13) | copy-start | bytes 580
  0.7 18.3 %copy-start.4 = (bf16[1,1,48,64,128]{4,3,2,1,0:T(8,128)(2,1)S(1)}, bf16[1,1,48,64,128]{4,3,2,1,0:T(8,128)(2,1)}, u32[]{:S(2)}) copy-start(bf16[1,1,48,64,128]{4,3,2,1,0:T(8,128)(2,1)} %param.16) | copy-start | bytes 2359300
  2.3 34.8 %all-to-all-start.3 = ((bf16[12,128,128]{2,1,0:T(8,128)(2,1)}), bf16[12,128,128]{2,1,0:T(8,128)(2,1)S(1)}, u32[]{:S(2)}, u32[]{:S(2)}) async-start(bf16[12,128,128]{2,1,0:T(8,128)(2,1)} %broadcast_in_dim.22), calls=%async_computation.3 | async-start | bytes 786432 | tf_op jit(solution)/shard_map/all_to_all | solution.py:27
  19.0 10.0 %copy-start.5 = (bf16[128,128]{1,0:T(8,128)(2,1)S(1)}, bf16[128,128]{1,0:T(8,128)(2,1)}, u32[]{:S(2)}) copy-start(bf16[128,128]{1,0:T(8,128)(2,1)} %param.12) | copy-start | bytes 98308
  19.1 26.2 %collective-permute-start.2 = (bf16[3088,128]{1,0:T(8,128)(2,1)S(1)}, bf16[3088,128]{1,0:T(8,128)(2,1)S(1)}, u32[]{:S(2)}, u32[]{:S(2)}) collective-permute-start(bf16[3088,128]{1,0:T(8,128)(2,1)S(1)} %pad_maximum_fusion.refs_1_.refs_6_.refs_2_), channel_id=1, source_target_pairs={{0,36},{12,0},{24,12},{36,24},{1,37},{13,1},{25,13},{37,25},{2,38}... | collective-permute-start | bytes 2371592 | tf_op jit(solution)/shard_map/ppermute | solution.py:286
  23.5 45.9 %collective-permute-start.1 = (bf16[3088,128]{1,0:T(8,128)(2,1)S(1)}, bf16[3088,128]{1,0:T(8,128)(2,1)S(1)}, u32[]{:S(2)}, u32[]{:S(2)}) collective-permute-start(bf16[3088,128]{1,0:T(8,128)(2,1)S(1)} %pad_maximum_fusion.refs_1_.refs_6_.refs_2_), channel_id=1, source_target_pairs={{0,12},{12,24},{24,36},{36,0},{1,13},{13,25},{25,37},{37,1},{2,14}... | collective-permute-start | bytes 2371592 | tf_op jit(solution)/shard_map/ppermute | solution.py:286
  25.4 44.0 %collective-permute-start = (bf16[3088,128]{1,0:T(8,128)(2,1)S(1)}, bf16[3088,128]{1,0:T(8,128)(2,1)S(1)}, u32[]{:S(2)}, u32[]{:S(2)}) collective-permute-start(bf16[3088,128]{1,0:T(8,128)(2,1)S(1)} %pad_maximum_fusion.refs_1_.refs_6_.refs_2_), channel_id=1, source_target_pairs={{0,24},{12,36},{24,0},{36,12},{1,25},{13,37},{25,1},{37,13},{2,26}... | collective-permute-start | bytes 2371592 | tf_op jit(solution)/shard_map/ppermute | solution.py:286
  29.6 11.3 %collective-permute-start.6 = (bf16[64,128]{1,0:T(8,128)(2,1)}, bf16[64,128]{1,0:T(8,128)(2,1)}, u32[]{:S(2)}, u32[]{:S(2)}) collective-permute-start(bf16[64,128]{1,0:T(8,128)(2,1)} %slice.7), channel_id=1, source_target_pairs={{0,96},{48,144},{96,0},{144,48},{1,97},{49,145},{97,1},{145,49},{2... | collective-permute-start | bytes 49160 | tf_op jit(solution)/shard_map/ppermute | solution.py:289
  37.1 32.3 %collective-permute-start.4 = (bf16[12,128,128]{2,1,0:T(8,128)(2,1)S(1)}, bf16[12,128,128]{2,1,0:T(8,128)(2,1)}, u32[]{:S(2)}, u32[]{:S(2)}) collective-permute-start(bf16[12,128,128]{2,1,0:T(8,128)(2,1)S(1)} %all-to-all-done.3.refs_1_), channel_id=1, source_target_pairs={{0,48},{48,96},{96,144},{144,0},{1,49},{49,97},{97,145},{145,1},{2... | collective-permute-start | bytes 1179656 | tf_op jit(solution)/shard_map/ppermute | solution.py:294
  40.9 28.5 %collective-permute-start.3 = (bf16[12,128,128]{2,1,0:T(8,128)(2,1)S(1)}, bf16[12,128,128]{2,1,0:T(8,128)(2,1)}, u32[]{:S(2)}, u32[]{:S(2)}) collective-permute-start(bf16[12,128,128]{2,1,0:T(8,128)(2,1)S(1)} %all-to-all-done.3.refs_1_), channel_id=1, source_target_pairs={{0,144},{48,0},{96,48},{144,96},{1,145},{49,1},{97,49},{145,97},{2... | collective-permute-start | bytes 1179656 | tf_op jit(solution)/shard_map/ppermute | solution.py:294
  45.2 24.1 %collective-permute-start.5 = (bf16[12,64,128]{2,1,0:T(8,128)(2,1)}, bf16[12,64,128]{2,1,0:T(8,128)(2,1)}, u32[]{:S(2)}, u32[]{:S(2)}) collective-permute-start(bf16[12,64,128]{2,1,0:T(8,128)(2,1)} %slice.8), channel_id=1, source_target_pairs={{0,96},{48,144},{96,0},{144,48},{1,97},{49,145},{97,1},{145,49},{2... | collective-permute-start | bytes 589832 | tf_op jit(solution)/shard_map/ppermute | solution.py:294
  69.4 0.9 copy-start.3
  72.4 35.1 %copy-start = (bf16[128,256]{1,0:T(8,128)(2,1)S(1)}, bf16[128,256]{1,0:T(8,128)(2,1)}, u32[]{:S(2)}) copy-start(bf16[128,256]{1,0:T(8,128)(2,1)} %refs_1_.1) | copy-start | bytes 196612
  72.4 35.1 %copy-start.1 = (bf16[128,256]{1,0:T(8,128)(2,1)S(1)}, bf16[128,256]{1,0:T(8,128)(2,1)}, u32[]{:S(2)}) copy-start(bf16[128,256]{1,0:T(8,128)(2,1)} %refs_3_.1) | copy-start | bytes 196612
  72.5 35.1 %copy-start.2 = (f32[256]{0:T(256)S(1)}, f32[256]{0:T(256)}, u32[]{:S(2)}) copy-start(f32[256]{0:T(256)} %param.18) | copy-start | bytes 3076
  127.1 36.4 %collective-permute-start.7 = (bf16[12,128,128]{2,1,0:T(8,128)(2,1)}, bf16[12,128,128]{2,1,0:T(8,128)(2,1)S(1)}, u32[]{:S(2)}, u32[]{:S(2)}) collective-permute-start(bf16[12,128,128]{2,1,0:T(8,128)(2,1)} %get-tuple-element.27), channel_id=1, source_target_pairs={{0,96},{48,144},{96,0},{144,48},{1,97},{49,145},{97,1},{145,49},{2... | collective-permute-start | bytes 1179656 | tf_op jit(solution)/shard_map/ppermute | solution.py:378
  132.6 35.6 %collective-permute-start.8 = (bf16[12,128,128]{2,1,0:T(8,128)(2,1)}, bf16[12,128,128]{2,1,0:T(8,128)(2,1)S(1)}, u32[]{:S(2)}, u32[]{:S(2)}) collective-permute-start(bf16[12,128,128]{2,1,0:T(8,128)(2,1)} %get-tuple-element.28), channel_id=1, source_target_pairs={{0,144},{48,0},{96,48},{144,96},{1,145},{49,1},{97,49},{145,97},{2... | collective-permute-start | bytes 1179656 | tf_op jit(solution)/shard_map/ppermute | solution.py:378
  134.7 33.6 %collective-permute-start.9 = (bf16[12,128,128]{2,1,0:T(8,128)(2,1)}, bf16[12,128,128]{2,1,0:T(8,128)(2,1)S(1)}, u32[]{:S(2)}, u32[]{:S(2)}) collective-permute-start(bf16[12,128,128]{2,1,0:T(8,128)(2,1)} %get-tuple-element.29), channel_id=1, source_target_pairs={{0,48},{48,96},{96,144},{144,0},{1,49},{49,97},{97,145},{145,1},{2... | collective-permute-start | bytes 1179656 | tf_op jit(solution)/shard_map/ppermute | solution.py:378
  169.2 21.9 %all-to-all-start.6 = ((bf16[12,128,128]{2,1,0:T(8,128)(2,1)}), bf16[12,128,128]{2,1,0:T(8,128)(2,1)S(1)}, u32[]{:S(2)}, u32[]{:S(2)}) async-start(bf16[12,128,128]{2,1,0:T(8,128)(2,1)} %middle_sums.1), calls=%async_computation.6 | async-start | bytes 786432 | tf_op jit(solution)/shard_map/all_to_all | solution.py:419

commit v12 on v10

--- a/solution.py
+++ b/solution.py
@@ -278,10 +278,13 @@
     longest_first = sorted(range(1, far), key=lambda shift: -min(shift, far - shift))
 
     buffers = [own]
-    for shift in sorted(range(1, across), key=lambda shift: -min(shift, across - shift)):
-        buffers.append(lax.ppermute(own, "x", ring(across, shift)))
+    for shift in range(1, across):
+        if shift != across // 2:
+            buffers.append(lax.ppermute(own, "x", ring(across, shift)))
 
     lines = [spread_out(features, "z", near)]
+    own, lines[0] = lax.optimization_barrier((own, lines[0]))
+    buffers.append(lax.ppermute(own, "x", ring(across, across // 2)))
     line_order = [0] + longest_first[::-1]
     for shift in line_order[1:]:
         lines.append(lax.ppermute(lines[0], "yhi", ring(far, shift)))

time: 186 us -> 189 us (1.016)
  waiting for transfers between devices: 46.4 us -> 49.2 us
  starting transfers between devices: 55.9 us -> 58.5 us
    ppermute x3 -> x2, waiting for transfers between devices: 8.88 us -> 0.01 us  [local(): buffers.append(lax.ppermute(own, 'x', ring(across, shift)))]
    ppermute x3, waiting for transfers between devices: 19.3 us -> 28.1 us  [local(): lines.append(lax.ppermute(lines[0], 'yhi', ring(far, shift)))]
    ppermute x0 -> x1, starting transfers between devices: none -> 4.64 us  [local(): buffers.append(lax.ppermute(own, 'x', ring(across, across // 2)))]
    ppermute x3 -> x2, starting transfers between devices: 9.93 us -> 6.31 us  [local(): buffers.append(lax.ppermute(own, 'x', ring(across, shift)))]
    all_to_all x1, waiting for transfers between devices: 7.71 us -> 11.3 us  [spread_out(): return lax.all_to_all(copies, axes, 0, 0, tiled=True)]
where the time goes in v12:
time: 189 us; the launch traced here: 187 us
  blocking collectives  69.3 us (37%)
  starting transfers between devices  58.5 us (31%)
  waiting for transfers between devices  49.2 us (26%)
  Pallas kernels  6.7 us (4%)
    ppermute x3, waiting for transfers between devices, local(): lines.append(lax.ppermute(lines[0], 'yhi', ring(far, shift)))  28.1 us
    all_to_all x1, blocking collectives, gather_gradients(): arrived = lax.all_to_all(value, 'z', 0, 0, tiled=True)  17.9 us
    all_to_all x1, blocking collectives, local(): spreads = lax.all_to_all(message, team_axes, 0, 0, tiled=True)  15.8 us
    all_to_all x1, starting transfers between devices, spread_out(): return lax.all_to_all(copies, axes, 0, 0, tiled=True)  15.7 us
    ppermute x3, starting transfers between devices, local(): lines.append(lax.ppermute(lines[0], 'yhi', ring(far, shift)))  14.8 us
    all_to_all x1, blocking collectives, local(): partials = lax.all_to_all(partial, team_axes, 0, 0, tiled=True)  14.2 us
    all_gather x1, blocking collectives, local(): pieces = lax.all_gather(gradients, 'yhi', axis=0)  12.2 us
    ppermute x3, starting transfers between devices, local(): lines.append(lax.ppermute(outs[shift], 'yhi', ring(far, -shift)))  11.9 us
  transfers between devices with their start and end apart: 11, of which 6 were waited for; matrix products, arithmetic and copies ran while one was open for 0% of the time, Pallas kernels for 0%

profile of v12, /device:TPU:1, one launch (start us, length us, event | category | flops | bytes accessed | tf_op | source)
XLA Modules:
  0.0 187.4 jit_solution(7815172543318770241)
XLA Ops:
  0.7 1.7 broadcast_in_dim.16
  2.3 15.7 %all-to-all-start.2 = ((bf16[12,128,128]{2,1,0:T(8,128)(2,1)}), bf16[12,128,128]{2,1,0:T(8,128)(2,1)S(1)}, u32[]{:S(2)}, u32[]{:S(2)}) async-start(bf16[12,128,128]{2,1,0:T(8,128)(2,1)} %broadcast_in_dim.16), calls=%async_computation.2 | async-start | bytes 786432 | tf_op jit(solution)/shard_map/all_to_all | solution.py:26
  18.7 0.1 maximum_bitcast_fusion
  18.8 0.1 copy.12
  18.9 0.1 fusion.8
  19.1 4.4 %collective-permute-start.1 = (bf16[3088,128]{1,0:T(8,128)(2,1)S(1)}, bf16[3088,128]{1,0:T(8,128)(2,1)S(1)}, u32[]{:S(2)}, u32[]{:S(2)}) collective-permute-start(bf16[3088,128]{1,0:T(8,128)(2,1)S(1)} %pad_maximum_fusion.refs_1_.refs_5_.refs_2_), channel_id=1, source_target_pairs={{0,36},{12,0},{24,12},{36,24},{1,37},{13,1},{25,13},{37,25},{2,38}... | collective-permute-start | bytes 2371592 | tf_op jit(solution)/shard_map/ppermute | solution.py:283
  23.5 1.9 %collective-permute-start = (bf16[3088,128]{1,0:T(8,128)(2,1)S(1)}, bf16[3088,128]{1,0:T(8,128)(2,1)S(1)}, u32[]{:S(2)}, u32[]{:S(2)}) collective-permute-start(bf16[3088,128]{1,0:T(8,128)(2,1)S(1)} %pad_maximum_fusion.refs_1_.refs_5_.refs_2_), channel_id=1, source_target_pairs={{0,12},{12,24},{24,36},{36,0},{1,13},{13,25},{25,37},{37,1},{2,14}... | collective-permute-start | bytes 2371592 | tf_op jit(solution)/shard_map/ppermute | solution.py:283
  25.4 11.3 %all-to-all-done.2.refs_1_ = bf16[12,128,128]{2,1,0:T(8,128)(2,1)S(1)} async-done(((bf16[12,128,128]{2,1,0:T(8,128)(2,1)}), bf16[12,128,128]{2,1,0:T(8,128)(2,1)S(1)}, u32[]{:S(2)}, u32[]{:S(2)}) %all-to-all-start.2) | async-done | bytes 393248 | tf_op jit(solution)/shard_map/all_to_all | solution.py:26
  36.7 4.6 %collective-permute-start.2 = (bf16[3088,128]{1,0:T(8,128)(2,1)S(1)}, bf16[3088,128]{1,0:T(8,128)(2,1)S(1)}, u32[]{:S(2)}, u32[]{:S(2)}) collective-permute-start(bf16[3088,128]{1,0:T(8,128)(2,1)S(1)} %pad_maximum_fusion.refs_1_.refs_5_.refs_2_), channel_id=1, source_target_pairs={{0,24},{12,36},{24,0},{36,12},{1,25},{13,37},{25,1},{37,13},{2,26}... | collective-permute-start | bytes 2371592 | tf_op jit(solution)/shard_map/ppermute | solution.py:287
  41.4 7.5 %collective-permute-start.5 = (bf16[12,128,128]{2,1,0:T(8,128)(2,1)S(1)}, bf16[12,128,128]{2,1,0:T(8,128)(2,1)S(1)}, u32[]{:S(2)}, u32[]{:S(2)}) collective-permute-start(bf16[12,128,128]{2,1,0:T(8,128)(2,1)S(1)} %all-to-all-done.2.refs_1_), channel_id=1, source_target_pairs={{0,96},{48,144},{96,0},{144,48},{1,97},{49,145},{97,1},{145,49},{2... | collective-permute-start | bytes 1179656 | tf_op jit(solution)/shard_map/ppermute | solution.py:290
  48.8 2.4 %collective-permute-start.4 = (bf16[12,128,128]{2,1,0:T(8,128)(2,1)S(1)}, bf16[12,128,128]{2,1,0:T(8,128)(2,1)S(1)}, u32[]{:S(2)}, u32[]{:S(2)}) collective-permute-start(bf16[12,128,128]{2,1,0:T(8,128)(2,1)S(1)} %all-to-all-done.2.refs_1_), channel_id=1, source_target_pairs={{0,48},{48,96},{96,144},{144,0},{1,49},{49,97},{97,145},{145,1},{2... | collective-permute-start | bytes 1179656 | tf_op jit(solution)/shard_map/ppermute | solution.py:290
  51.3 5.0 %collective-permute-start.3 = (bf16[12,128,128]{2,1,0:T(8,128)(2,1)S(1)}, bf16[12,128,128]{2,1,0:T(8,128)(2,1)S(1)}, u32[]{:S(2)}, u32[]{:S(2)}) collective-permute-start(bf16[12,128,128]{2,1,0:T(8,128)(2,1)S(1)} %all-to-all-done.2.refs_1_), channel_id=1, source_target_pairs={{0,144},{48,0},{96,48},{144,96},{1,145},{49,1},{97,49},{145,97},{2... | collective-permute-start | bytes 1179656 | tf_op jit(solution)/shard_map/ppermute | solution.py:290
  56.3 1.4 collective-permute-done.5.refs_7_.refs_4_
  57.6 17.7 %collective-permute-done.4.refs_6_.refs_3_ = bf16[12,128,128]{2,1,0:T(8,128)(2,1)S(1)} collective-permute-done((bf16[12,128,128]{2,1,0:T(8,128)(2,1)S(1)}, bf16[12,128,128]{2,1,0:T(8,128)(2,1)S(1)}, u32[]{:S(2)}, u32[]{:S(2)}) %collective-permute-start.4) | collective-permute-done | bytes 393248 | tf_op jit(solution)/shard_map/ppermute | solution.py:290
  75.3 9.0 %collective-permute-done.3.refs_5_.refs_2_ = bf16[12,128,128]{2,1,0:T(8,128)(2,1)S(1)} collective-permute-done((bf16[12,128,128]{2,1,0:T(8,128)(2,1)S(1)}, bf16[12,128,128]{2,1,0:T(8,128)(2,1)S(1)}, u32[]{:S(2)}, u32[]{:S(2)}) %collective-permute-start.3) | collective-permute-done | bytes 393248 | tf_op jit(solution)/shard_map/ppermute | solution.py:290
  84.4 1.4 forward_tiles.1
  85.9 14.2 %all_to_all.30.refs_0_ = bf16[16,128,128]{2,1,0:T(8,128)(2,1)S(1)} all-to-all(bf16[16,128,128]{2,1,0:T(8,128)(2,1)S(1)} %forward_tiles.1), channel_id=1, replica_groups=mesh['ylo'=2,'core'=2,'yhi'=4,'x'=4,'z'=12] {'ylo','core','x'}, dimensions={0} | all-to-all | bytes 1048576 | tf_op jit(solution)/shard_map/all_to_all | solution.py:324
  100.1 1.1 dense_layer.1
  101.2 15.8 %all_to_all.31.refs_1_ = bf16[16,176,128]{2,1,0:T(8,128)(2,1)S(1)} all-to-all(bf16[16,176,128]{2,1,0:T(8,128)(2,1)S(1)} %get-tuple-element.25), channel_id=1, replica_groups=mesh['ylo'=2,'core'=2,'yhi'=4,'x'=4,'z'=12] {'ylo','core','x'}, dimensions={0} | all-to-all | bytes 1441792 | tf_op jit(solution)/shard_map/all_to_all | solution.py:339
  117.0 2.4 %backward_tiles.1 = (bf16[12,128,128]{2,1,0:T(8,128)(2,1)S(1)}, bf16[12,128,128]{2,1,0:T(8,128)(2,1)S(1)}, bf16[12,128,128]{2,1,0:T(8,128)(2,1)}, bf16[12,128,128]{2,1,0:T(8,128)(2,1)S(1)}, bf16[12,48,128]{2,1,0:T(8,128)(2,1)}) custom-call(s32[4,128]{1,0:T(4,128)S(1)} %tile_codes.1.refs_0_, bf16[16,176,128]{2,1,0:T(8,128)(2,1)S(1)} %all_to_all.31.refs_1_, ...), custom_call_target="tpu_custom_call" | custom-call | tf_op jit(solution)/shard_map/backward_tiles/pallas_call | solution.py:341
  119.4 5.1 %collective-permute-start.6 = (bf16[12,128,128]{2,1,0:T(8,128)(2,1)}, bf16[12,128,128]{2,1,0:T(8,128)(2,1)S(1)}, u32[]{:S(2)}, u32[]{:S(2)}) collective-permute-start(bf16[12,128,128]{2,1,0:T(8,128)(2,1)} %get-tuple-element.27), channel_id=1, source_target_pairs={{0,96},{48,144},{96,0},{144,48},{1,97},{49,145},{97,1},{145,49},{2... | collective-permute-start | bytes 1179656 | tf_op jit(solution)/shard_map/ppermute | solution.py:367
  124.5 4.9 %collective-permute-start.7 = (bf16[12,128,128]{2,1,0:T(8,128)(2,1)S(1)}, bf16[12,128,128]{2,1,0:T(8,128)(2,1)S(1)}, u32[]{:S(2)}, u32[]{:S(2)}) collective-permute-start(bf16[12,128,128]{2,1,0:T(8,128)(2,1)S(1)} %get-tuple-element.28), channel_id=1, source_target_pairs={{0,144},{48,0},{96,48},{144,96},{1,145},{49,1},{97,49},{145,97},{2... | collective-permute-start | bytes 1179656 | tf_op jit(solution)/shard_map/ppermute | solution.py:367
  129.4 1.9 %collective-permute-start.8 = (bf16[12,128,128]{2,1,0:T(8,128)(2,1)S(1)}, bf16[12,128,128]{2,1,0:T(8,128)(2,1)S(1)}, u32[]{:S(2)}, u32[]{:S(2)}) collective-permute-start(bf16[12,128,128]{2,1,0:T(8,128)(2,1)S(1)} %get-tuple-element.29), channel_id=1, source_target_pairs={{0,48},{48,96},{96,144},{144,0},{1,49},{49,97},{97,145},{145,1},{2... | collective-permute-start | bytes 1179656 | tf_op jit(solution)/shard_map/ppermute | solution.py:367
  131.4 27.2 %conditional.1 = (bf16[272,128]{1,0:T(8,128)(2,1)S(1)}) conditional(s32[]{:T(128)} %convert_element_type.4, () %tuple.16, bf16[12,48,128]{2,1,0:T(8,128)(2,1)} %get-tuple-element.30), branch_computations={%region_0.1_spmd, %region_1.2_spmd} | conditional | bytes 425992 | solution.py:392
  131.4 17.9 %all_to_all.28.refs_0_ = bf16[12,48,128]{2,1,0:T(8,128)(2,1)S(1)} all-to-all(bf16[12,48,128]{2,1,0:T(8,128)(2,1)} %param.1), channel_id=1, replica_groups=mesh['ylo'=2,'core'=2,'yhi'=4,'x'=4,'z'=12] {'z'}, dimensions={0} | all-to-all | bytes 294912 | tf_op jit(solution)/shard_map/cond/branch_1_fun/all_to_all | solution.py:370
  149.3 9.3 %all_to_all.29.refs_0_ = bf16[8,32,128]{2,1,0:T(8,128)(2,1)S(1)} all-to-all(bf16[8,32,128]{2,1,0:T(8,128)(2,1)S(1)} %get-tuple-element.4), channel_id=1, replica_groups=mesh['ylo'=2,'core'=2,'yhi'=4,'x'=4,'z'=12] {'core','x'}, dimensions={0} | all-to-all | bytes 131072 | tf_op jit(solution)/shard_map/cond/branch_1_fun/all_to_all | solution.py:382
  158.6 3.4 %collective-permute-done.7.refs_2_ = bf16[12,128,128]{2,1,0:T(8,128)(2,1)S(1)} collective-permute-done((bf16[12,128,128]{2,1,0:T(8,128)(2,1)S(1)}, bf16[12,128,128]{2,1,0:T(8,128)(2,1)S(1)}, u32[]{:S(2)}, u32[]{:S(2)}) %collective-permute-start.7) | collective-permute-done | bytes 393248 | tf_op jit(solution)/shard_map/ppermute | solution.py:367
  162.0 1.0 middle_sums.1
  162.9 5.1 %all-to-all-start.5 = ((bf16[12,128,128]{2,1,0:T(8,128)(2,1)}), bf16[12,128,128]{2,1,0:T(8,128)(2,1)S(1)}, u32[]{:S(2)}, u32[]{:S(2)}) async-start(bf16[12,128,128]{2,1,0:T(8,128)(2,1)} %middle_sums.1), calls=%async_computation.5 | async-start | bytes 786432 | tf_op jit(solution)/shard_map/all_to_all | solution.py:408
  168.1 12.2 %all-gather = bf16[1088,128]{1,0:T(8,128)(2,1)S(1)} all-gather(bf16[272,128]{1,0:T(8,128)(2,1)S(1)} %get-tuple-element.37.refs_4_), channel_id=2, replica_groups=mesh['ylo'=2,'core'=2,'yhi'=4,'x'=4,'z'=12] {'yhi'}, dimensions={0}, use_global_device_ids=true | all-gather | bytes 348160 | tf_op jit(solution)/shard_map/all_gather | solution.py:407
  180.3 6.4 %all-to-all-done.5.refs_0_ = bf16[12,128,128]{2,1,0:T(8,128)(2,1)S(1)} async-done(((bf16[12,128,128]{2,1,0:T(8,128)(2,1)}), bf16[12,128,128]{2,1,0:T(8,128)(2,1)S(1)}, u32[]{:S(2)}, u32[]{:S(2)}) %all-to-all-start.5) | async-done | bytes 393248 | tf_op jit(solution)/shard_map/all_to_all | solution.py:408
  186.6 0.7 last_sums.1
  (22 shorter events, 0.2 us)
Async XLA Ops:
  0.6 18.1 %copy-start.4 = (s32[1,1,48]{2,1,0:T(1,128)S(1)}, s32[1,1,48]{2,1,0:T(1,128)}, u32[]{:S(2)}) copy-start(s32[1,1,48]{2,1,0:T(1,128)} %param.12) | copy-start | bytes 580
  0.6 18.1 %copy-start.5 = (s32[1,1,48]{2,1,0:T(1,128)S(1)}, s32[1,1,48]{2,1,0:T(1,128)}, u32[]{:S(2)}) copy-start(s32[1,1,48]{2,1,0:T(1,128)} %param.11) | copy-start | bytes 580
  0.7 18.4 %copy-start.3 = (bf16[1,1,48,64,128]{4,3,2,1,0:T(8,128)(2,1)S(1)}, bf16[1,1,48,64,128]{4,3,2,1,0:T(8,128)(2,1)}, u32[]{:S(2)}) copy-start(bf16[1,1,48,64,128]{4,3,2,1,0:T(8,128)(2,1)} %param.14) | copy-start | bytes 2359300
  2.3 34.4 %all-to-all-start.2 = ((bf16[12,128,128]{2,1,0:T(8,128)(2,1)}), bf16[12,128,128]{2,1,0:T(8,128)(2,1)S(1)}, u32[]{:S(2)}, u32[]{:S(2)}) async-start(bf16[12,128,128]{2,1,0:T(8,128)(2,1)} %broadcast_in_dim.16), calls=%async_computation.2 | async-start | bytes 786432 | tf_op jit(solution)/shard_map/all_to_all | solution.py:26
  19.1 32.2 %collective-permute-start.1 = (bf16[3088,128]{1,0:T(8,128)(2,1)S(1)}, bf16[3088,128]{1,0:T(8,128)(2,1)S(1)}, u32[]{:S(2)}, u32[]{:S(2)}) collective-permute-start(bf16[3088,128]{1,0:T(8,128)(2,1)S(1)} %pad_maximum_fusion.refs_1_.refs_5_.refs_2_), channel_id=1, source_target_pairs={{0,36},{12,0},{24,12},{36,24},{1,37},{13,1},{25,13},{37,25},{2,38}... | collective-permute-start | bytes 2371592 | tf_op jit(solution)/shard_map/ppermute | solution.py:283
  23.5 32.8 %collective-permute-start = (bf16[3088,128]{1,0:T(8,128)(2,1)S(1)}, bf16[3088,128]{1,0:T(8,128)(2,1)S(1)}, u32[]{:S(2)}, u32[]{:S(2)}) collective-permute-start(bf16[3088,128]{1,0:T(8,128)(2,1)S(1)} %pad_maximum_fusion.refs_1_.refs_5_.refs_2_), channel_id=1, source_target_pairs={{0,12},{12,24},{24,36},{36,0},{1,13},{13,25},{25,37},{37,1},{2,14}... | collective-permute-start | bytes 2371592 | tf_op jit(solution)/shard_map/ppermute | solution.py:283
  36.7 47.7 %collective-permute-start.2 = (bf16[3088,128]{1,0:T(8,128)(2,1)S(1)}, bf16[3088,128]{1,0:T(8,128)(2,1)S(1)}, u32[]{:S(2)}, u32[]{:S(2)}) collective-permute-start(bf16[3088,128]{1,0:T(8,128)(2,1)S(1)} %pad_maximum_fusion.refs_1_.refs_5_.refs_2_), channel_id=1, source_target_pairs={{0,24},{12,36},{24,0},{36,12},{1,25},{13,37},{25,1},{37,13},{2,26}... | collective-permute-start | bytes 2371592 | tf_op jit(solution)/shard_map/ppermute | solution.py:287
  41.4 16.3 %collective-permute-start.5 = (bf16[12,128,128]{2,1,0:T(8,128)(2,1)S(1)}, bf16[12,128,128]{2,1,0:T(8,128)(2,1)S(1)}, u32[]{:S(2)}, u32[]{:S(2)}) collective-permute-start(bf16[12,128,128]{2,1,0:T(8,128)(2,1)S(1)} %all-to-all-done.2.refs_1_), channel_id=1, source_target_pairs={{0,96},{48,144},{96,0},{144,48},{1,97},{49,145},{97,1},{145,49},{2... | collective-permute-start | bytes 1179656 | tf_op jit(solution)/shard_map/ppermute | solution.py:290
  48.8 26.5 %collective-permute-start.4 = (bf16[12,128,128]{2,1,0:T(8,128)(2,1)S(1)}, bf16[12,128,128]{2,1,0:T(8,128)(2,1)S(1)}, u32[]{:S(2)}, u32[]{:S(2)}) collective-permute-start(bf16[12,128,128]{2,1,0:T(8,128)(2,1)S(1)} %all-to-all-done.2.refs_1_), channel_id=1, source_target_pairs={{0,48},{48,96},{96,144},{144,0},{1,49},{49,97},{97,145},{145,1},{2... | collective-permute-start | bytes 1179656 | tf_op jit(solution)/shard_map/ppermute | solution.py:290
  51.3 33.1 %collective-permute-start.3 = (bf16[12,128,128]{2,1,0:T(8,128)(2,1)S(1)}, bf16[12,128,128]{2,1,0:T(8,128)(2,1)S(1)}, u32[]{:S(2)}, u32[]{:S(2)}) collective-permute-start(bf16[12,128,128]{2,1,0:T(8,128)(2,1)S(1)} %all-to-all-done.2.refs_1_), channel_id=1, source_target_pairs={{0,144},{48,0},{96,48},{144,96},{1,145},{49,1},{97,49},{145,97},{2... | collective-permute-start | bytes 1179656 | tf_op jit(solution)/shard_map/ppermute | solution.py:290
  85.9 14.3 %copy-start = (bf16[128,256]{1,0:T(8,128)(2,1)S(1)}, bf16[128,256]{1,0:T(8,128)(2,1)}, u32[]{:S(2)}) copy-start(bf16[128,256]{1,0:T(8,128)(2,1)} %refs_1_.1) | copy-start | bytes 196612
  85.9 14.3 %copy-start.1 = (bf16[128,256]{1,0:T(8,128)(2,1)S(1)}, bf16[128,256]{1,0:T(8,128)(2,1)}, u32[]{:S(2)}) copy-start(bf16[128,256]{1,0:T(8,128)(2,1)} %refs_3_.1) | copy-start | bytes 196612
  85.9 14.2 %copy-start.2 = (f32[256]{0:T(256)S(1)}, f32[256]{0:T(256)}, u32[]{:S(2)}) copy-start(f32[256]{0:T(256)} %param.16) | copy-start | bytes 3076
  119.4 39.2 %collective-permute-start.6 = (bf16[12,128,128]{2,1,0:T(8,128)(2,1)}, bf16[12,128,128]{2,1,0:T(8,128)(2,1)S(1)}, u32[]{:S(2)}, u32[]{:S(2)}) collective-permute-start(bf16[12,128,128]{2,1,0:T(8,128)(2,1)} %get-tuple-element.27), channel_id=1, source_target_pairs={{0,96},{48,144},{96,0},{144,48},{1,97},{49,145},{97,1},{145,49},{2... | collective-permute-start | bytes 1179656 | tf_op jit(solution)/shard_map/ppermute | solution.py:367
  124.5 37.4 %collective-permute-start.7 = (bf16[12,128,128]{2,1,0:T(8,128)(2,1)S(1)}, bf16[12,128,128]{2,1,0:T(8,128)(2,1)S(1)}, u32[]{:S(2)}, u32[]{:S(2)}) collective-permute-start(bf16[12,128,128]{2,1,0:T(8,128)(2,1)S(1)} %get-tuple-element.28), channel_id=1, source_target_pairs={{0,144},{48,0},{96,48},{144,96},{1,145},{49,1},{97,49},{145,97},{2... | collective-permute-start | bytes 1179656 | tf_op jit(solution)/shard_map/ppermute | solution.py:367
  129.4 32.5 %collective-permute-start.8 = (bf16[12,128,128]{2,1,0:T(8,128)(2,1)S(1)}, bf16[12,128,128]{2,1,0:T(8,128)(2,1)S(1)}, u32[]{:S(2)}, u32[]{:S(2)}) collective-permute-start(bf16[12,128,128]{2,1,0:T(8,128)(2,1)S(1)} %get-tuple-element.29), channel_id=1, source_target_pairs={{0,48},{48,96},{96,144},{144,0},{1,49},{49,97},{97,145},{145,1},{2... | collective-permute-start | bytes 1179656 | tf_op jit(solution)/shard_map/ppermute | solution.py:367
  162.9 23.7 %all-to-all-start.5 = ((bf16[12,128,128]{2,1,0:T(8,128)(2,1)}), bf16[12,128,128]{2,1,0:T(8,128)(2,1)S(1)}, u32[]{:S(2)}, u32[]{:S(2)}) async-start(bf16[12,128,128]{2,1,0:T(8,128)(2,1)} %middle_sums.1), calls=%async_computation.5 | async-start | bytes 786432 | tf_op jit(solution)/shard_map/all_to_all | solution.py:408

commit v13 on v10

--- a/solution.py
+++ b/solution.py
@@ -8,10 +8,11 @@
 from jax.sharding import Mesh, PartitionSpec as P
 
 row_split = (2, 2)
-col_split = (4, 4, 12)
-axis_names = ("ylo", "core", "yhi", "x", "z")
+col_split = (2, 2, 4, 12)
+axis_names = ("ylo", "core", "yfar", "ynear", "x", "z")
 row_axes = ("ylo", "core")
-col_axes = ("yhi", "x", "z")
+y_axes = ("yfar", "ynear")
+col_axes = y_axes + ("x", "z")
 team_axes = ("ylo", "core", "x")
 share_axes = ("core", "x")
 group = 4
@@ -54,14 +55,15 @@
     return total
 
 
-def forward_kernel(codes, *refs, slots, height, blocks, line_order, across):
+def forward_kernel(codes, partner, *refs, slots, height, blocks, line_order, across):
     far = len(line_order)
-    lines, tile_refs = refs[:far], refs[far : far + across]
-    out, slabs, chosen, totals, picked = refs[far + across :]
+    lines, pair, tile_refs = refs[:far], refs[far], refs[far + 1 : far + 1 + across]
+    out, slabs, chosen, totals, picked = refs[far + 1 + across :]
     slab_count = slabs.shape[0]
-    near = slab_count // far
+    near = slab_count // (far + 1)
     for shift, line in zip(line_order, lines):
         slabs[pl.ds(shift * near, near)] = line[...]
+    slabs[pl.ds((far + 1) // 2 * near, near)] = pair[partner[0]]
     dummy = slab_count * 64 + blocks
     totals[...] = jnp.zeros_like(totals)
     total = pick_tiles(codes, tile_refs, chosen, picked, slots, height, dummy)
@@ -247,7 +249,7 @@
     nodes, width = features.shape
     slots, height, tile_width = tile_values.shape[2:]
     hidden = weight.shape[1]
-    far = lax.axis_size("yhi")
+    far = lax.axis_size(y_axes)
     across = lax.axis_size("x")
     near = lax.axis_size("z")
     members = lax.axis_size(team_axes)
@@ -263,7 +265,7 @@
     live = jnp.arange(slots, dtype=jnp.int32) < tile_counts[0, 0]
     columns, rows = tile_cols[0, 0], tile_rows[0, 0]
     owner = jnp.where(live, (columns // near) % across, 255)
-    distance = (lax.axis_index("yhi") - columns // (across * near)) % far
+    distance = (lax.axis_index(y_axes) - columns // (across * near)) % far
     slab = distance * near + columns % near
     block = ((rows // halves) * across + here) * halves + rows % halves
     places = jnp.stack([owner, slab, block])
@@ -282,9 +284,11 @@
         buffers.append(lax.ppermute(own, "x", ring(across, shift)))
 
     lines = [spread_out(features, "z", near)]
-    line_order = [0] + longest_first[::-1]
+    line_order = [0] + [shift for shift in range(1, far) if shift != far // 2]
+    pair = spread_out(lines[0], "yfar", 2)
     for shift in line_order[1:]:
-        lines.append(lax.ppermute(lines[0], "yhi", ring(far, shift)))
+        lines.append(lax.ppermute(lines[0], y_axes, ring(far, shift)))
+    partner = (1 - lax.axis_index("yfar")).reshape(1)
 
     codes = pl.pallas_call(
         lambda *refs: codes_kernel(*refs, across=across, top=slots * height),
@@ -293,7 +297,7 @@
         out_specs=in_vmem(),
         compiler_params=params,
         name="tile_codes",
-    )(here.reshape(1), *buffers, *lines[1:])
+    )(here.reshape(1), *buffers, *lines[1:], pair)
 
     scratch_tiles = pltpu.VMEM((across * slots + group, height, tile_width), jnp.bfloat16)
     scratch_list = pltpu.SMEM((across * slots + group,), jnp.int32)
@@ -307,7 +311,7 @@
             across=across,
         ),
         out_shape=jax.ShapeDtypeStruct((members, nodes, width), jnp.bfloat16),
-        in_specs=[in_smem()] + [in_vmem()] * (far + across),
+        in_specs=[in_smem(), in_smem()] + [in_vmem()] * (far + across),
         out_specs=in_vmem(),
         scratch_shapes=[
             pltpu.VMEM((far * near, nodes, width), jnp.bfloat16),
@@ -317,7 +321,7 @@
         ],
         compiler_params=params,
         name="forward_tiles",
-    )(codes, *lines, *buffers)
+    )(codes, partner, *lines, pair, *buffers)
     partials = lax.all_to_all(partial, team_axes, 0, 0, tiled=True)
 
     holders = lax.axis_size(share_axes)
@@ -361,7 +365,7 @@
 
     lines = [outs[0]]
     for shift in longest_first:
-        lines.append(lax.ppermute(outs[shift], "yhi", ring(far, -shift)))
+        lines.append(lax.ppermute(outs[shift], y_axes, ring(far, -shift)))
 
     def gather_gradients(value):
         arrived = lax.all_to_all(value, "z", 0, 0, tiled=True)
@@ -401,7 +405,7 @@
         name="middle_sums",
     )(*lines, gradients)
 
-    pieces = lax.all_gather(gradients, "yhi", axis=0)
+    pieces = lax.all_gather(gradients, y_axes, axis=0)
     arrived = lax.all_to_all(line, "z", 0, 0, tiled=True)
     factor = 1.0 / math.sqrt(nodes * group_rows * far * across * near)
     features_grad, weight_grad, bias_grad = pl.pallas_call(

time: 186 us -> 191 us (1.027)
  blocking collectives: 69.8 us -> 74.3 us
  waiting for transfers between devices: 46.4 us -> 43.8 us
    ppermute x6 -> x5, starting transfers between devices: 26.2 us -> 17.1 us  [the longest x3 9.47 us: local(): lines.append(lax.ppermute(outs[shift], y_axes, ring(far, -shift)))]
    all_to_all x1 -> x2, starting transfers between devices: 15.7 us -> 22.5 us  [spread_out(): return lax.all_to_all(copies, axes, 0, 0, tiled=True)]
    all_to_all x1, blocking collectives: 15.2 us -> 18.9 us  [local(): partials = lax.all_to_all(partial, team_axes, 0, 0, tiled=True)]
    ppermute x6 -> x5, waiting for transfers between devices: 23.2 us -> 21.9 us  [the longest x2 20.1 us: local(): lines.append(lax.ppermute(lines[0], y_axes, ring(far, shift)))]
    all_to_all x1 -> x2, waiting for transfers between devices: 7.71 us -> 7.71 us  [spread_out(): return lax.all_to_all(copies, axes, 0, 0, tiled=True)]
  transfers between devices with their start and end apart: 11 -> 11, of which waited for: 6 -> 5; matrix products, arithmetic and copies ran while one was open for 0% -> 1% of each run, Pallas kernels for 0% -> 0%
where the time goes in v13:
time: 191 us; the launch traced here: 188 us
  blocking collectives  74.3 us (39%)
  starting transfers between devices  55.4 us (29%)
  waiting for transfers between devices  43.8 us (23%)
  Pallas kernels  9.66 us (5%)
  local copies, waits for them, and re-layouts  2.88 us (2%)
    all_to_all x2, starting transfers between devices, spread_out(): return lax.all_to_all(copies, axes, 0, 0, tiled=True)  22.5 us
    ppermute x2, waiting for transfers between devices, local(): lines.append(lax.ppermute(lines[0], y_axes, ring(far, shift)))  20.1 us
    all_to_all x1, blocking collectives, local(): partials = lax.all_to_all(partial, team_axes, 0, 0, tiled=True)  18.9 us
    all_to_all x1, blocking collectives, gather_gradients(): arrived = lax.all_to_all(value, 'z', 0, 0, tiled=True)  17.5 us
    all_to_all x1, blocking collectives, local(): spreads = lax.all_to_all(message, team_axes, 0, 0, tiled=True)  15.8 us
    all_gather x1, blocking collectives, local(): pieces = lax.all_gather(gradients, y_axes, axis=0)  12.4 us
    ppermute x3, starting transfers between devices, local(): buffers.append(lax.ppermute(own, 'x', ring(across, shift)))  9.93 us
    all_to_all x1, blocking collectives, gather_gradients(): shares = lax.all_to_all(shares, share_axes, 0, 0, tiled=True)  9.78 us
  transfers between devices with their start and end apart: 11, of which 5 were waited for; matrix products, arithmetic and copies ran while one was open for 1% of the time, Pallas kernels for 0%

profile of v13, /device:TPU:1, one launch (start us, length us, event | category | flops | bytes accessed | tf_op | source)
XLA Modules:
  0.0 187.7 jit_solution(14185651991623284490)
XLA Ops:
  0.7 1.6 broadcast_in_dim.22
  2.3 15.7 %all-to-all-start.2 = ((bf16[12,128,128]{2,1,0:T(8,128)(2,1)}), bf16[12,128,128]{2,1,0:T(8,128)(2,1)S(1)}, u32[]{:S(2)}, u32[]{:S(2)}) async-start(bf16[12,128,128]{2,1,0:T(8,128)(2,1)} %broadcast_in_dim.22), calls=%async_computation.2 | async-start | bytes 786432 | tf_op jit(solution)/shard_map/all_to_all | solution.py:27
  18.7 0.1 maximum_bitcast_fusion
  18.8 0.1 copy.12
  18.9 0.1 fusion.8
  19.0 4.4 %collective-permute-start.2 = (bf16[3088,128]{1,0:T(8,128)(2,1)S(1)}, bf16[3088,128]{1,0:T(8,128)(2,1)S(1)}, u32[]{:S(2)}, u32[]{:S(2)}) collective-permute-start(bf16[3088,128]{1,0:T(8,128)(2,1)S(1)} %pad_maximum_fusion.refs_1_.refs_6_.refs_2_), channel_id=1, source_target_pairs={{0,36},{12,0},{24,12},{36,24},{1,37},{13,1},{25,13},{37,25},{2,38}... | collective-permute-start | bytes 2371592 | tf_op jit(solution)/shard_map/ppermute | solution.py:284
  23.4 1.9 %collective-permute-start.1 = (bf16[3088,128]{1,0:T(8,128)(2,1)S(1)}, bf16[3088,128]{1,0:T(8,128)(2,1)S(1)}, u32[]{:S(2)}, u32[]{:S(2)}) collective-permute-start(bf16[3088,128]{1,0:T(8,128)(2,1)S(1)} %pad_maximum_fusion.refs_1_.refs_6_.refs_2_), channel_id=1, source_target_pairs={{0,12},{12,24},{24,36},{36,0},{1,13},{13,25},{25,37},{37,1},{2,14}... | collective-permute-start | bytes 2371592 | tf_op jit(solution)/shard_map/ppermute | solution.py:284
  25.4 3.6 %collective-permute-start = (bf16[3088,128]{1,0:T(8,128)(2,1)S(1)}, bf16[3088,128]{1,0:T(8,128)(2,1)S(1)}, u32[]{:S(2)}, u32[]{:S(2)}) collective-permute-start(bf16[3088,128]{1,0:T(8,128)(2,1)S(1)} %pad_maximum_fusion.refs_1_.refs_6_.refs_2_), channel_id=1, source_target_pairs={{0,24},{12,36},{24,0},{36,12},{1,25},{13,37},{25,1},{37,13},{2,26}... | collective-permute-start | bytes 2371592 | tf_op jit(solution)/shard_map/ppermute | solution.py:284
  29.0 7.7 %all-to-all-done.2.refs_2_ = bf16[12,128,128]{2,1,0:T(8,128)(2,1)S(1)} async-done(((bf16[12,128,128]{2,1,0:T(8,128)(2,1)}), bf16[12,128,128]{2,1,0:T(8,128)(2,1)S(1)}, u32[]{:S(2)}, u32[]{:S(2)}) %all-to-all-start.2) | async-done | bytes 393248 | tf_op jit(solution)/shard_map/all_to_all | solution.py:27
  36.7 1.1 broadcast_in_dim.23
  37.8 6.8 %all-to-all-start.3 = ((bf16[2,12,128,128]{3,2,1,0:T(8,128)(2,1)}), bf16[2,12,128,128]{3,2,1,0:T(8,128)(2,1)}, u32[]{:S(2)}, u32[]{:S(2)}) async-start(bf16[2,12,128,128]{3,2,1,0:T(8,128)(2,1)} %broadcast_in_dim.23), calls=%async_computation.3 | async-start | bytes 1572864 | tf_op jit(solution)/shard_map/all_to_all | solution.py:27
  44.6 5.7 %collective-permute-start.4 = (bf16[12,128,128]{2,1,0:T(8,128)(2,1)S(1)}, bf16[12,128,128]{2,1,0:T(8,128)(2,1)}, u32[]{:S(2)}, u32[]{:S(2)}) collective-permute-start(bf16[12,128,128]{2,1,0:T(8,128)(2,1)S(1)} %all-to-all-done.2.refs_2_), channel_id=1, source_target_pairs={{0,144},{48,0},{96,48},{144,96},{1,145},{49,1},{97,49},{145,97},{2... | collective-permute-start | bytes 1179656 | tf_op jit(solution)/shard_map/ppermute | solution.py:290
  50.3 1.9 %collective-permute-start.3 = (bf16[12,128,128]{2,1,0:T(8,128)(2,1)S(1)}, bf16[12,128,128]{2,1,0:T(8,128)(2,1)}, u32[]{:S(2)}, u32[]{:S(2)}) collective-permute-start(bf16[12,128,128]{2,1,0:T(8,128)(2,1)S(1)} %all-to-all-done.2.refs_2_), channel_id=1, source_target_pairs={{0,48},{48,96},{96,144},{144,0},{1,49},{49,97},{97,145},{145,1},{2... | collective-permute-start | bytes 1179656 | tf_op jit(solution)/shard_map/ppermute | solution.py:290
  52.3 8.3 %collective-permute-done.refs_2_.refs_7_.refs_3_ = bf16[3088,128]{1,0:T(8,128)(2,1)S(1)} collective-permute-done((bf16[3088,128]{1,0:T(8,128)(2,1)S(1)}, bf16[3088,128]{1,0:T(8,128)(2,1)S(1)}, u32[]{:S(2)}, u32[]{:S(2)}) %collective-permute-start) | collective-permute-done | bytes 790560 | tf_op jit(solution)/shard_map/ppermute | solution.py:284
  60.6 20.1 %collective-permute-done.4.refs_6_.refs_4_ = bf16[12,128,128]{2,1,0:T(8,128)(2,1)} collective-permute-done((bf16[12,128,128]{2,1,0:T(8,128)(2,1)S(1)}, bf16[12,128,128]{2,1,0:T(8,128)(2,1)}, u32[]{:S(2)}, u32[]{:S(2)}) %collective-permute-start.4) | collective-permute-done | bytes 393248 | tf_op jit(solution)/shard_map/ppermute | solution.py:290
  80.7 3.1 %forward_tiles.1 = bf16[16,128,128]{2,1,0:T(8,128)(2,1)S(1)} custom-call(s32[4,128]{1,0:T(4,128)S(1)} %tile_codes.1.refs_0_, s32[1]{0:T(128)} %bitcast.11.refs_1_, bf16[12,128,128]{2,1,0:T(8,128)(2,1)S(1)} %all-to-all-done.2.refs_2_, bf16[12,128,128]{2,1,0:T(8,128)(2,1)} %collective-permute-done.3.refs_5_.refs_3_, ...), custom_call_target="tpu_custom_call" | custom-call | tf_op jit(solution)/shard_map/forward_tiles/pallas_call | solution.py:304
  83.8 18.9 %all_to_all.35.refs_0_ = bf16[16,128,128]{2,1,0:T(8,128)(2,1)S(1)} all-to-all(bf16[16,128,128]{2,1,0:T(8,128)(2,1)S(1)} %forward_tiles.1), channel_id=1, replica_groups=mesh['ylo'=2,'core'=2,'yfar'=2,'ynear'=2,'x'=4,'z'=12] {'ylo','core','x'}, dimensions={0} | all-to-all | bytes 1048576 | tf_op jit(solution)/shard_map/all_to_all | solution.py:325
  102.7 1.1 dense_layer.1
  103.8 15.8 %all_to_all.36.refs_1_ = bf16[16,176,128]{2,1,0:T(8,128)(2,1)S(1)} all-to-all(bf16[16,176,128]{2,1,0:T(8,128)(2,1)S(1)} %get-tuple-element.21), channel_id=1, replica_groups=mesh['ylo'=2,'core'=2,'yfar'=2,'ynear'=2,'x'=4,'z'=12] {'ylo','core','x'}, dimensions={0} | all-to-all | bytes 1441792 | tf_op jit(solution)/shard_map/all_to_all | solution.py:340
  119.6 3.7 %backward_tiles.1 = (bf16[12,128,128]{2,1,0:T(8,128)(2,1)S(1)}, bf16[12,128,128]{2,1,0:T(8,128)(2,1)}, bf16[12,128,128]{2,1,0:T(8,128)(2,1)}, bf16[12,128,128]{2,1,0:T(8,128)(2,1)}, bf16[12,48,128]{2,1,0:T(8,128)(2,1)}) custom-call(s32[4,128]{1,0:T(4,128)S(1)} %tile_codes.1.refs_0_, bf16[16,176,128]{2,1,0:T(8,128)(2,1)S(1)} %all_to_all.36.refs_1_, ...), custom_call_target="tpu_custom_call" | custom-call | tf_op jit(solution)/shard_map/backward_tiles/pallas_call | solution.py:342
  123.3 2.6 %collective-permute-start.5 = (bf16[12,128,128]{2,1,0:T(8,128)(2,1)}, bf16[12,128,128]{2,1,0:T(8,128)(2,1)S(1)}, u32[]{:S(2)}, u32[]{:S(2)}) collective-permute-start(bf16[12,128,128]{2,1,0:T(8,128)(2,1)} %get-tuple-element.23), channel_id=1, source_target_pairs={{0,96},{48,144},{96,0},{144,48},{1,97},{49,145},{97,1},{145,49},{2... | collective-permute-start | bytes 1179656 | tf_op jit(solution)/shard_map/ppermute | solution.py:368
  126.0 4.9 %collective-permute-start.6 = (bf16[12,128,128]{2,1,0:T(8,128)(2,1)}, bf16[12,128,128]{2,1,0:T(8,128)(2,1)S(1)}, u32[]{:S(2)}, u32[]{:S(2)}) collective-permute-start(bf16[12,128,128]{2,1,0:T(8,128)(2,1)} %get-tuple-element.24), channel_id=1, source_target_pairs={{0,144},{48,0},{96,48},{144,96},{1,145},{49,1},{97,49},{145,97},{2... | collective-permute-start | bytes 1179656 | tf_op jit(solution)/shard_map/ppermute | solution.py:368
  130.9 1.9 %collective-permute-start.7 = (bf16[12,128,128]{2,1,0:T(8,128)(2,1)}, bf16[12,128,128]{2,1,0:T(8,128)(2,1)S(1)}, u32[]{:S(2)}, u32[]{:S(2)}) collective-permute-start(bf16[12,128,128]{2,1,0:T(8,128)(2,1)} %get-tuple-element.25), channel_id=1, source_target_pairs={{0,48},{48,96},{96,144},{144,0},{1,49},{49,97},{97,145},{145,1},{2... | collective-permute-start | bytes 1179656 | tf_op jit(solution)/shard_map/ppermute | solution.py:368
  132.8 27.3 %conditional.1 = (bf16[272,128]{1,0:T(8,128)(2,1)S(1)}) conditional(s32[]{:T(128)} %convert_element_type.4, () %tuple.14, bf16[12,48,128]{2,1,0:T(8,128)(2,1)} %get-tuple-element.26), branch_computations={%region_0.1_spmd, %region_1.2_spmd} | conditional | bytes 425992 | solution.py:393
  132.8 17.5 %all_to_all.33.refs_0_ = bf16[12,48,128]{2,1,0:T(8,128)(2,1)S(1)} all-to-all(bf16[12,48,128]{2,1,0:T(8,128)(2,1)} %param.1), channel_id=1, replica_groups=mesh['ylo'=2,'core'=2,'yfar'=2,'ynear'=2,'x'=4,'z'=12] {'z'}, dimensions={0} | all-to-all | bytes 294912 | tf_op jit(solution)/shard_map/cond/branch_1_fun/all_to_all | solution.py:371
  150.3 9.8 %all_to_all.34.refs_0_ = bf16[8,32,128]{2,1,0:T(8,128)(2,1)S(1)} all-to-all(bf16[8,32,128]{2,1,0:T(8,128)(2,1)S(1)} %get-tuple-element.4), channel_id=1, replica_groups=mesh['ylo'=2,'core'=2,'yfar'=2,'ynear'=2,'x'=4,'z'=12] {'core','x'}, dimensions={0} | all-to-all | bytes 131072 | tf_op jit(solution)/shard_map/cond/branch_1_fun/all_to_all | solution.py:383
  160.1 1.8 collective-permute-done.6.refs_2_
  161.9 0.9 middle_sums.1
  162.9 5.9 %all-to-all-start.6 = ((bf16[12,128,128]{2,1,0:T(8,128)(2,1)}), bf16[12,128,128]{2,1,0:T(8,128)(2,1)S(1)}, u32[]{:S(2)}, u32[]{:S(2)}) async-start(bf16[12,128,128]{2,1,0:T(8,128)(2,1)} %middle_sums.1), calls=%async_computation.6 | async-start | bytes 786432 | tf_op jit(solution)/shard_map/all_to_all | solution.py:409
  168.8 12.4 %all-gather = bf16[1088,128]{1,0:T(8,128)(2,1)S(1)} all-gather(bf16[272,128]{1,0:T(8,128)(2,1)S(1)} %get-tuple-element.33.refs_4_), channel_id=2, replica_groups=mesh['ylo'=2,'core'=2,'yfar'=2,'ynear'=2,'x'=4,'z'=12] {'yfar','ynear'}, dimensions={0}, use_global_device_ids=true | all-gather | bytes 348160 | tf_op jit(solution)/shard_map/all_gather | solution.py:408
  181.1 5.9 %all-to-all-done.6.refs_0_ = bf16[12,128,128]{2,1,0:T(8,128)(2,1)S(1)} async-done(((bf16[12,128,128]{2,1,0:T(8,128)(2,1)}), bf16[12,128,128]{2,1,0:T(8,128)(2,1)S(1)}, u32[]{:S(2)}, u32[]{:S(2)}) %all-to-all-start.6) | async-done | bytes 393248 | tf_op jit(solution)/shard_map/all_to_all | solution.py:409
  187.0 0.7 last_sums.1
  (23 shorter events, 0.2 us)
Async XLA Ops:
  0.6 18.2 %copy-start.4 = (s32[1,1,48]{2,1,0:T(1,128)S(1)}, s32[1,1,48]{2,1,0:T(1,128)}, u32[]{:S(2)}) copy-start(s32[1,1,48]{2,1,0:T(1,128)} %param.12) | copy-start | bytes 580
  0.6 18.2 %copy-start.5 = (s32[1,1,48]{2,1,0:T(1,128)S(1)}, s32[1,1,48]{2,1,0:T(1,128)}, u32[]{:S(2)}) copy-start(s32[1,1,48]{2,1,0:T(1,128)} %param.11) | copy-start | bytes 580
  0.7 18.3 %copy-start.3 = (bf16[1,1,48,64,128]{4,3,2,1,0:T(8,128)(2,1)S(1)}, bf16[1,1,48,64,128]{4,3,2,1,0:T(8,128)(2,1)}, u32[]{:S(2)}) copy-start(bf16[1,1,48,64,128]{4,3,2,1,0:T(8,128)(2,1)} %param.14) | copy-start | bytes 2359300
  2.3 34.4 %all-to-all-start.2 = ((bf16[12,128,128]{2,1,0:T(8,128)(2,1)}), bf16[12,128,128]{2,1,0:T(8,128)(2,1)S(1)}, u32[]{:S(2)}, u32[]{:S(2)}) async-start(bf16[12,128,128]{2,1,0:T(8,128)(2,1)} %broadcast_in_dim.22), calls=%async_computation.2 | async-start | bytes 786432 | tf_op jit(solution)/shard_map/all_to_all | solution.py:27
  19.0 33.2 %collective-permute-start.2 = (bf16[3088,128]{1,0:T(8,128)(2,1)S(1)}, bf16[3088,128]{1,0:T(8,128)(2,1)S(1)}, u32[]{:S(2)}, u32[]{:S(2)}) collective-permute-start(bf16[3088,128]{1,0:T(8,128)(2,1)S(1)} %pad_maximum_fusion.refs_1_.refs_6_.refs_2_), channel_id=1, source_target_pairs={{0,36},{12,0},{24,12},{36,24},{1,37},{13,1},{25,13},{37,25},{2,38}... | collective-permute-start | bytes 2371592 | tf_op jit(solution)/shard_map/ppermute | solution.py:284
  23.4 28.8 %collective-permute-start.1 = (bf16[3088,128]{1,0:T(8,128)(2,1)S(1)}, bf16[3088,128]{1,0:T(8,128)(2,1)S(1)}, u32[]{:S(2)}, u32[]{:S(2)}) collective-permute-start(bf16[3088,128]{1,0:T(8,128)(2,1)S(1)} %pad_maximum_fusion.refs_1_.refs_6_.refs_2_), channel_id=1, source_target_pairs={{0,12},{12,24},{24,36},{36,0},{1,13},{13,25},{25,37},{37,1},{2,14}... | collective-permute-start | bytes 2371592 | tf_op jit(solution)/shard_map/ppermute | solution.py:284
  25.4 35.2 %collective-permute-start = (bf16[3088,128]{1,0:T(8,128)(2,1)S(1)}, bf16[3088,128]{1,0:T(8,128)(2,1)S(1)}, u32[]{:S(2)}, u32[]{:S(2)}) collective-permute-start(bf16[3088,128]{1,0:T(8,128)(2,1)S(1)} %pad_maximum_fusion.refs_1_.refs_6_.refs_2_), channel_id=1, source_target_pairs={{0,24},{12,36},{24,0},{36,12},{1,25},{13,37},{25,1},{37,13},{2,26}... | collective-permute-start | bytes 2371592 | tf_op jit(solution)/shard_map/ppermute | solution.py:284
  37.8 42.8 %all-to-all-start.3 = ((bf16[2,12,128,128]{3,2,1,0:T(8,128)(2,1)}), bf16[2,12,128,128]{3,2,1,0:T(8,128)(2,1)}, u32[]{:S(2)}, u32[]{:S(2)}) async-start(bf16[2,12,128,128]{3,2,1,0:T(8,128)(2,1)} %broadcast_in_dim.23), calls=%async_computation.3 | async-start | bytes 1572864 | tf_op jit(solution)/shard_map/all_to_all | solution.py:27
  44.6 36.0 %collective-permute-start.4 = (bf16[12,128,128]{2,1,0:T(8,128)(2,1)S(1)}, bf16[12,128,128]{2,1,0:T(8,128)(2,1)}, u32[]{:S(2)}, u32[]{:S(2)}) collective-permute-start(bf16[12,128,128]{2,1,0:T(8,128)(2,1)S(1)} %all-to-all-done.2.refs_2_), channel_id=1, source_target_pairs={{0,144},{48,0},{96,48},{144,96},{1,145},{49,1},{97,49},{145,97},{2... | collective-permute-start | bytes 1179656 | tf_op jit(solution)/shard_map/ppermute | solution.py:290
  50.3 30.3 %collective-permute-start.3 = (bf16[12,128,128]{2,1,0:T(8,128)(2,1)S(1)}, bf16[12,128,128]{2,1,0:T(8,128)(2,1)}, u32[]{:S(2)}, u32[]{:S(2)}) collective-permute-start(bf16[12,128,128]{2,1,0:T(8,128)(2,1)S(1)} %all-to-all-done.2.refs_2_), channel_id=1, source_target_pairs={{0,48},{48,96},{96,144},{144,0},{1,49},{49,97},{97,145},{145,1},{2... | collective-permute-start | bytes 1179656 | tf_op jit(solution)/shard_map/ppermute | solution.py:290
  83.8 18.9 %copy-start = (bf16[128,256]{1,0:T(8,128)(2,1)S(1)}, bf16[128,256]{1,0:T(8,128)(2,1)}, u32[]{:S(2)}) copy-start(bf16[128,256]{1,0:T(8,128)(2,1)} %refs_1_.1) | copy-start | bytes 196612
  83.8 18.9 %copy-start.1 = (bf16[128,256]{1,0:T(8,128)(2,1)S(1)}, bf16[128,256]{1,0:T(8,128)(2,1)}, u32[]{:S(2)}) copy-start(bf16[128,256]{1,0:T(8,128)(2,1)} %refs_3_.1) | copy-start | bytes 196612
  83.8 18.9 %copy-start.2 = (f32[256]{0:T(256)S(1)}, f32[256]{0:T(256)}, u32[]{:S(2)}) copy-start(f32[256]{0:T(256)} %param.16) | copy-start | bytes 3076
  123.3 36.8 %collective-permute-start.5 = (bf16[12,128,128]{2,1,0:T(8,128)(2,1)}, bf16[12,128,128]{2,1,0:T(8,128)(2,1)S(1)}, u32[]{:S(2)}, u32[]{:S(2)}) collective-permute-start(bf16[12,128,128]{2,1,0:T(8,128)(2,1)} %get-tuple-element.23), channel_id=1, source_target_pairs={{0,96},{48,144},{96,0},{144,48},{1,97},{49,145},{97,1},{145,49},{2... | collective-permute-start | bytes 1179656 | tf_op jit(solution)/shard_map/ppermute | solution.py:368
  126.0 36.0 %collective-permute-start.6 = (bf16[12,128,128]{2,1,0:T(8,128)(2,1)}, bf16[12,128,128]{2,1,0:T(8,128)(2,1)S(1)}, u32[]{:S(2)}, u32[]{:S(2)}) collective-permute-start(bf16[12,128,128]{2,1,0:T(8,128)(2,1)} %get-tuple-element.24), channel_id=1, source_target_pairs={{0,144},{48,0},{96,48},{144,96},{1,145},{49,1},{97,49},{145,97},{2... | collective-permute-start | bytes 1179656 | tf_op jit(solution)/shard_map/ppermute | solution.py:368
  130.9 31.1 %collective-permute-start.7 = (bf16[12,128,128]{2,1,0:T(8,128)(2,1)}, bf16[12,128,128]{2,1,0:T(8,128)(2,1)S(1)}, u32[]{:S(2)}, u32[]{:S(2)}) collective-permute-start(bf16[12,128,128]{2,1,0:T(8,128)(2,1)} %get-tuple-element.25), channel_id=1, source_target_pairs={{0,48},{48,96},{96,144},{144,0},{1,49},{49,97},{97,145},{145,1},{2... | collective-permute-start | bytes 1179656 | tf_op jit(solution)/shard_map/ppermute | solution.py:368
  162.9 24.1 %all-to-all-start.6 = ((bf16[12,128,128]{2,1,0:T(8,128)(2,1)}), bf16[12,128,128]{2,1,0:T(8,128)(2,1)S(1)}, u32[]{:S(2)}, u32[]{:S(2)}) async-start(bf16[12,128,128]{2,1,0:T(8,128)(2,1)} %middle_sums.1), calls=%async_computation.6 | async-start | bytes 786432 | tf_op jit(solution)/shard_map/all_to_all | solution.py:409

commit v14 on v10

--- a/solution.py
+++ b/solution.py
@@ -14,6 +14,7 @@
 col_axes = ("yhi", "x", "z")
 team_axes = ("ylo", "core", "x")
 share_axes = ("core", "x")
+tail_rows = 64
 group = 4
 lanes = 128
 vmem_bytes = 12 * 1024 * 1024
@@ -191,8 +192,12 @@
     lax.fori_loop(0, (total + group - 1) // group, body, 0)
     near = slab_count // far
     for shift, out in enumerate(outs):
+        rows = out.shape[1]
         for index in range(near):
-            out[index] = totals[shift * near + index].astype(jnp.bfloat16)
+            total = totals[shift * near + index].astype(jnp.bfloat16)
+            out[index] = total[:rows]
+            if rows < nodes:
+                shares[index, pl.ds(2 * share + 16, nodes - rows), :] = total[rows:]
     weight_sum = sum_rows(spreads, nodes, 2 * share).astype(jnp.bfloat16)
     bias_block = pack_bias(sum_bias(spreads, nodes + 2 * share))
     for index in range(near):
@@ -200,37 +205,45 @@
         shares[index, pl.ds(2 * share, 16), :] = bias_block
 
 
-def share_kernel(arrived, out, bias_block, *, share):
-    total = sum_rows(arrived, 0, 2 * share).astype(jnp.bfloat16)
+def share_kernel(arrived, out):
+    rows = out.shape[0]
+    share_rows = rows - 16 - tail_rows
+    out[pl.ds(0, share_rows), :] = sum_rows(arrived, 0, share_rows).astype(jnp.bfloat16)
+    out[pl.ds(share_rows, 16), :] = pack_bias(sum_bias(arrived, share_rows))
+    out[pl.ds(share_rows + 16, tail_rows), :] = sum_rows(
+        arrived, share_rows + 16, tail_rows
+    ).astype(jnp.bfloat16)
+
+
+def share_sum_kernel(pieces, out):
+    out[...] = sum_rows(pieces, 0, out.shape[0])
+
+
+def middle_kernel(*refs, far):
+    lines, out = refs[:far], refs[-1]
+    nodes = out.shape[1]
+    rows = min(line.shape[1] for line in lines)
     for index in range(out.shape[0]):
-        out[index] = total
-    bias_block[...] = pack_bias(sum_bias(arrived, 2 * share))
-
-
-def gather_kernel(shares, bias_block, out, *, share):
-    rows = shares.shape[0] * share
+        for top, size in ((0, rows), (rows, nodes - rows)):
+            total = jnp.zeros((size, lanes), jnp.float32)
+            for line in lines:
+                if top < line.shape[1]:
+                    total = total + line[index, pl.ds(top, size), :].astype(jnp.float32)
+            out[index, pl.ds(top, size), :] = total.astype(jnp.bfloat16)
+
+
+def last_kernel(opposite, arrived, pieces, shares, grad, weight_grad, bias_grad, *, factor):
+    share_rows = shares.shape[1]
+    share = share_rows // 2
+    lead = grad.shape[0] - tail_rows
+    grad[pl.ds(0, lead), :] = sum_rows(arrived, 0, lead)
+    late = pieces[opposite[0], pl.ds(share_rows + 16, tail_rows), :].astype(jnp.float32)
+    grad[pl.ds(lead, tail_rows), :] = sum_rows(arrived, lead, tail_rows) + late
     for index in range(shares.shape[0]):
         for half in range(2):
-            part = shares[index, pl.ds(half * share, share), :]
-            out[pl.ds(half * rows + index * share, share), :] = part
-    out[pl.ds(2 * rows, 16), :] = bias_block[...]
-
-
-def middle_kernel(*refs, far):
-    out = refs[-1]
-    for index in range(out.shape[0]):
-        total = refs[0][index].astype(jnp.float32)
-        for line in refs[1:far]:
-            total = total + line[index].astype(jnp.float32)
-        out[index] = total.astype(jnp.bfloat16)
-
-
-def last_kernel(arrived, pieces, grad, weight_grad, bias_grad, *, factor):
-    grad[...] = sum_rows(arrived, 0, grad.shape[0])
-    rows = weight_grad.shape[0]
-    weight_grad[:, pl.ds(0, lanes)] = sum_rows(pieces, 0, rows) * factor
-    weight_grad[:, pl.ds(lanes, lanes)] = sum_rows(pieces, rows, rows) * factor
-    low, high = sum_bias(pieces, 2 * rows)
+            part = shares[index, pl.ds(half * share, share), :] * factor
+            weight_grad[pl.ds(index * share, share), pl.ds(half * lanes, lanes)] = part
+    low, high = sum_bias(pieces, share_rows)
     bias_grad[:, pl.ds(0, lanes)] = low * factor
     bias_grad[:, pl.ds(lanes, lanes)] = high * factor
 
@@ -335,6 +348,7 @@
     )(partials, weight, bias.reshape(1, hidden), cotangent)
     spreads = lax.all_to_all(message, team_axes, 0, 0, tiled=True)
 
+    opposite = far // 2
     outs = pl.pallas_call(
         lambda *refs: backward_kernel(
             *refs,
@@ -346,8 +360,13 @@
             far=far,
             across=across,
         ),
-        out_shape=(jax.ShapeDtypeStruct((near, nodes, width), jnp.bfloat16),) * far
-        + (jax.ShapeDtypeStruct((near, 2 * share + 16, width), jnp.bfloat16),),
+        out_shape=tuple(
+            jax.ShapeDtypeStruct(
+                (near, nodes - (tail_rows if shift == opposite else 0), width), jnp.bfloat16
+            )
+            for shift in range(far)
+        )
+        + (jax.ShapeDtypeStruct((near, 2 * share + 16 + tail_rows, width), jnp.bfloat16),),
         in_specs=[in_smem(), in_vmem()] + [in_vmem()] * across,
         out_specs=(in_vmem(),) * (far + 1),
         scratch_shapes=[
@@ -363,33 +382,23 @@
     for shift in longest_first:
         lines.append(lax.ppermute(outs[shift], "yhi", ring(far, -shift)))
 
+    small_shape = (2 * share + 16 + tail_rows, lanes)
+
     def gather_gradients(value):
         arrived = lax.all_to_all(value, "z", 0, 0, tiled=True)
-        shares, bias_block = pl.pallas_call(
-            lambda *refs: share_kernel(*refs, share=share),
-            out_shape=(
-                jax.ShapeDtypeStruct((holders, 2 * share, lanes), jnp.bfloat16),
-                jax.ShapeDtypeStruct((16, lanes), jnp.bfloat16),
-            ),
+        return pl.pallas_call(
+            share_kernel,
+            out_shape=jax.ShapeDtypeStruct(small_shape, jnp.bfloat16),
             in_specs=[in_vmem()],
-            out_specs=(in_vmem(), in_vmem()),
+            out_specs=in_vmem(),
             compiler_params=params,
             name="share_sum",
         )(arrived)
-        shares = lax.all_to_all(shares, share_axes, 0, 0, tiled=True)
-        return pl.pallas_call(
-            lambda *refs: gather_kernel(*refs, share=share),
-            out_shape=jax.ShapeDtypeStruct((2 * width + 16, lanes), jnp.bfloat16),
-            in_specs=[in_vmem(), in_vmem()],
-            out_specs=in_vmem(),
-            compiler_params=params,
-            name="share_gather",
-        )(shares, bias_block)
 
     gradients = lax.cond(
         tile_counts[0, 0] > 0,
         gather_gradients,
-        lambda value: jnp.zeros((2 * width + 16, lanes), jnp.bfloat16),
+        lambda value: jnp.zeros(small_shape, jnp.bfloat16),
         outs[far],
     )
     line = pl.pallas_call(
@@ -402,6 +411,15 @@
     )(*lines, gradients)
 
     pieces = lax.all_gather(gradients, "yhi", axis=0)
+    shares = pl.pallas_call(
+        share_sum_kernel,
+        out_shape=jax.ShapeDtypeStruct((2 * share, lanes), jnp.float32),
+        in_specs=[in_vmem()],
+        out_specs=in_vmem(),
+        compiler_params=params,
+        name="share_sum_far",
+    )(pieces)
+    shares = lax.all_gather(shares, share_axes, axis=0)
     arrived = lax.all_to_all(line, "z", 0, 0, tiled=True)
     factor = 1.0 / math.sqrt(nodes * group_rows * far * across * near)
     features_grad, weight_grad, bias_grad = pl.pallas_call(
@@ -411,11 +429,11 @@
             jax.ShapeDtypeStruct((width, hidden), jnp.float32),
             jax.ShapeDtypeStruct((1, hidden), jnp.float32),
         ),
-        in_specs=[in_vmem(), in_vmem()],
+        in_specs=[in_smem()] + [in_vmem()] * 3,
         out_specs=(in_vmem(), in_vmem(), in_vmem()),
         compiler_params=params,
         name="last_sums",
-    )(arrived, pieces)
+    )(((lax.axis_index("yhi") + opposite) % far).reshape(1), arrived, pieces, shares)
     return (hidden_out, features_grad, weight_grad, bias_grad.reshape(hidden))
 
 

time: 186 us -> 196 us (1.054)
  blocking collectives: 69.8 us -> 86.6 us
  waiting for transfers between devices: 46.4 us -> 35.9 us
  starting transfers between devices: 55.9 us -> 60.4 us
    all_gather x0 -> x1, blocking collectives: none -> 24.6 us  [local(): shares = lax.all_gather(shares, share_axes, axis=0)]
    all_to_all x1 -> x0, blocking collectives: 10.5 us -> none  [gather_gradients(): shares = lax.all_to_all(shares, share_axes, 0, 0, tiled=True)]
    all_to_all x1, waiting for transfers between devices: 6.58 us -> 0.01 us  [local(): arrived = lax.all_to_all(line, 'z', 0, 0, tiled=True)]
    ppermute x3, waiting for transfers between devices: 3.94 us -> 0.01 us  [local(): lines.append(lax.ppermute(outs[shift], 'yhi', ring(far, -shift)))]
    all_to_all x1, starting transfers between devices: 4.05 us -> 6.92 us  [local(): arrived = lax.all_to_all(line, 'z', 0, 0, tiled=True)]
    all_to_all x1, blocking collectives: 16.2 us -> 18.4 us  [gather_gradients(): arrived = lax.all_to_all(value, 'z', 0, 0, tiled=True)]
  transfers between devices with their start and end apart: 11 -> 11, of which waited for: 6 -> 4; matrix products, arithmetic and copies ran while one was open for 0% -> 0% of each run, Pallas kernels for 0% -> 0%
where the time goes in v14:
time: 196 us; the launch traced here: 195 us
  blocking collectives  86.6 us (44%)
  starting transfers between devices  60.4 us (31%)
  waiting for transfers between devices  35.9 us (18%)
  Pallas kernels  8.38 us (4%)
    all_gather x1, blocking collectives, local(): shares = lax.all_gather(shares, share_axes, axis=0)  24.6 us
    ppermute x3, waiting for transfers between devices, local(): lines.append(lax.ppermute(lines[0], 'yhi', ring(far, shift)))  19.3 us
    all_to_all x1, blocking collectives, gather_gradients(): arrived = lax.all_to_all(value, 'z', 0, 0, tiled=True)  18.4 us
    all_to_all x1, blocking collectives, local(): spreads = lax.all_to_all(message, team_axes, 0, 0, tiled=True)  15.8 us
    all_to_all x1, starting transfers between devices, spread_out(): return lax.all_to_all(copies, axes, 0, 0, tiled=True)  15.7 us
    all_to_all x1, blocking collectives, local(): partials = lax.all_to_all(partial, team_axes, 0, 0, tiled=True)  15.1 us
    ppermute x3, starting transfers between devices, local(): lines.append(lax.ppermute(lines[0], 'yhi', ring(far, shift)))  14.8 us
    ppermute x3, starting transfers between devices, local(): lines.append(lax.ppermute(outs[shift], 'yhi', ring(far, -shift)))  13 us
  transfers between devices with their start and end apart: 11, of which 4 were waited for; matrix products, arithmetic and copies ran while one was open for 0% of the time, Pallas kernels for 0%

profile of v14, /device:TPU:1, one launch (start us, length us, event | category | flops | bytes accessed | tf_op | source)
XLA Modules:
  0.0 194.8 jit_solution(18021764162641413881)
XLA Ops:
  0.7 1.6 broadcast_in_dim.16
  2.3 15.7 %all-to-all-start.1 = ((bf16[12,128,128]{2,1,0:T(8,128)(2,1)}), bf16[12,128,128]{2,1,0:T(8,128)(2,1)S(1)}, u32[]{:S(2)}, u32[]{:S(2)}) async-start(bf16[12,128,128]{2,1,0:T(8,128)(2,1)} %broadcast_in_dim.16), calls=%async_computation.1 | async-start | bytes 786432 | tf_op jit(solution)/shard_map/all_to_all | solution.py:27
  18.7 0.1 maximum_bitcast_fusion
  18.8 0.1 copy.12
  18.9 0.1 fusion.8
  19.0 0.1 pad_maximum_fusion.refs_1_.refs_5_.refs_2_
  19.0 4.4 %collective-permute-start.2 = (bf16[3088,128]{1,0:T(8,128)(2,1)S(1)}, bf16[3088,128]{1,0:T(8,128)(2,1)S(1)}, u32[]{:S(2)}, u32[]{:S(2)}) collective-permute-start(bf16[3088,128]{1,0:T(8,128)(2,1)S(1)} %pad_maximum_fusion.refs_1_.refs_5_.refs_2_), channel_id=1, source_target_pairs={{0,36},{12,0},{24,12},{36,24},{1,37},{13,1},{25,13},{37,25},{2,38}... | collective-permute-start | bytes 2371592 | tf_op jit(solution)/shard_map/ppermute | solution.py:295
  23.4 1.9 collective-permute-start.1
  25.4 3.6 %collective-permute-start = (bf16[3088,128]{1,0:T(8,128)(2,1)S(1)}, bf16[3088,128]{1,0:T(8,128)(2,1)S(1)}, u32[]{:S(2)}, u32[]{:S(2)}) collective-permute-start(bf16[3088,128]{1,0:T(8,128)(2,1)S(1)} %pad_maximum_fusion.refs_1_.refs_5_.refs_2_), channel_id=1, source_target_pairs={{0,24},{12,36},{24,0},{36,12},{1,25},{13,37},{25,1},{37,13},{2,26}... | collective-permute-start | bytes 2371592 | tf_op jit(solution)/shard_map/ppermute | solution.py:295
  29.0 7.7 %all-to-all-done.1.refs_1_ = bf16[12,128,128]{2,1,0:T(8,128)(2,1)S(1)} async-done(((bf16[12,128,128]{2,1,0:T(8,128)(2,1)}), bf16[12,128,128]{2,1,0:T(8,128)(2,1)S(1)}, u32[]{:S(2)}, u32[]{:S(2)}) %all-to-all-start.1) | async-done | bytes 393248 | tf_op jit(solution)/shard_map/all_to_all | solution.py:27
  36.7 7.4 %collective-permute-start.5 = (bf16[12,128,128]{2,1,0:T(8,128)(2,1)S(1)}, bf16[12,128,128]{2,1,0:T(8,128)(2,1)S(1)}, u32[]{:S(2)}, u32[]{:S(2)}) collective-permute-start(bf16[12,128,128]{2,1,0:T(8,128)(2,1)S(1)} %all-to-all-done.1.refs_1_), channel_id=1, source_target_pairs={{0,96},{48,144},{96,0},{144,48},{1,97},{49,145},{97,1},{145,49},{2... | collective-permute-start | bytes 1179656 | tf_op jit(solution)/shard_map/ppermute | solution.py:300
  44.2 2.4 %collective-permute-start.4 = (bf16[12,128,128]{2,1,0:T(8,128)(2,1)S(1)}, bf16[12,128,128]{2,1,0:T(8,128)(2,1)S(1)}, u32[]{:S(2)}, u32[]{:S(2)}) collective-permute-start(bf16[12,128,128]{2,1,0:T(8,128)(2,1)S(1)} %all-to-all-done.1.refs_1_), channel_id=1, source_target_pairs={{0,48},{48,96},{96,144},{144,0},{1,49},{49,97},{97,145},{145,1},{2... | collective-permute-start | bytes 1179656 | tf_op jit(solution)/shard_map/ppermute | solution.py:300
  46.6 5.0 %collective-permute-start.3 = (bf16[12,128,128]{2,1,0:T(8,128)(2,1)S(1)}, bf16[12,128,128]{2,1,0:T(8,128)(2,1)S(1)}, u32[]{:S(2)}, u32[]{:S(2)}) collective-permute-start(bf16[12,128,128]{2,1,0:T(8,128)(2,1)S(1)} %all-to-all-done.1.refs_1_), channel_id=1, source_target_pairs={{0,144},{48,0},{96,48},{144,96},{1,145},{49,1},{97,49},{145,97},{2... | collective-permute-start | bytes 1179656 | tf_op jit(solution)/shard_map/ppermute | solution.py:300
  51.6 8.9 %collective-permute-done.refs_2_.refs_6_.refs_3_ = bf16[3088,128]{1,0:T(8,128)(2,1)S(1)} collective-permute-done((bf16[3088,128]{1,0:T(8,128)(2,1)S(1)}, bf16[3088,128]{1,0:T(8,128)(2,1)S(1)}, u32[]{:S(2)}, u32[]{:S(2)}) %collective-permute-start) | collective-permute-done | bytes 790560 | tf_op jit(solution)/shard_map/ppermute | solution.py:295
  60.5 10.2 %collective-permute-done.4.refs_6_.refs_3_ = bf16[12,128,128]{2,1,0:T(8,128)(2,1)S(1)} collective-permute-done((bf16[12,128,128]{2,1,0:T(8,128)(2,1)S(1)}, bf16[12,128,128]{2,1,0:T(8,128)(2,1)S(1)}, u32[]{:S(2)}, u32[]{:S(2)}) %collective-permute-start.4) | collective-permute-done | bytes 393248 | tf_op jit(solution)/shard_map/ppermute | solution.py:300
  70.7 9.1 %collective-permute-done.3.refs_5_.refs_2_ = bf16[12,128,128]{2,1,0:T(8,128)(2,1)S(1)} collective-permute-done((bf16[12,128,128]{2,1,0:T(8,128)(2,1)S(1)}, bf16[12,128,128]{2,1,0:T(8,128)(2,1)S(1)}, u32[]{:S(2)}, u32[]{:S(2)}) %collective-permute-start.3) | collective-permute-done | bytes 393248 | tf_op jit(solution)/shard_map/ppermute | solution.py:300
  79.8 2.1 %forward_tiles.1 = bf16[16,128,128]{2,1,0:T(8,128)(2,1)S(1)} custom-call(s32[4,128]{1,0:T(4,128)S(1)} %tile_codes.1.refs_0_, bf16[12,128,128]{2,1,0:T(8,128)(2,1)S(1)} %all-to-all-done.1.refs_1_, bf16[12,128,128]{2,1,0:T(8,128)(2,1)S(1)} %collective-permute-done.3.refs_5_.refs_2_, bf16[12,128,128]{2,1,0:T(8,128)(2,1)S(1)} %collective-permute-done.4.refs_6_.refs_3_, ...), custom_call_target="tpu_custom_call" | custom-call | tf_op jit(solution)/shard_map/forward_tiles/pallas_call | solution.py:313
  81.9 15.1 %all_to_all.25.refs_0_ = bf16[16,128,128]{2,1,0:T(8,128)(2,1)S(1)} all-to-all(bf16[16,128,128]{2,1,0:T(8,128)(2,1)S(1)} %forward_tiles.1), channel_id=1, replica_groups=mesh['ylo'=2,'core'=2,'yhi'=4,'x'=4,'z'=12] {'ylo','core','x'}, dimensions={0} | all-to-all | bytes 1048576 | tf_op jit(solution)/shard_map/all_to_all | solution.py:334
  97.0 1.1 dense_layer.1
  98.1 15.8 %all_to_all.26.refs_1_ = bf16[16,176,128]{2,1,0:T(8,128)(2,1)S(1)} all-to-all(bf16[16,176,128]{2,1,0:T(8,128)(2,1)S(1)} %get-tuple-element.19), channel_id=1, replica_groups=mesh['ylo'=2,'core'=2,'yhi'=4,'x'=4,'z'=12] {'ylo','core','x'}, dimensions={0} | all-to-all | bytes 1441792 | tf_op jit(solution)/shard_map/all_to_all | solution.py:349
  113.9 3.5 %backward_tiles.1 = (bf16[12,128,128]{2,1,0:T(8,128)(2,1)S(1)}, bf16[12,128,128]{2,1,0:T(8,128)(2,1)}, bf16[12,64,128]{2,1,0:T(8,128)(2,1)}, bf16[12,128,128]{2,1,0:T(8,128)(2,1)}, bf16[12,112,128]{2,1,0:T(8,128)(2,1)}) custom-call(s32[4,128]{1,0:T(4,128)S(1)} %tile_codes.1.refs_0_, bf16[16,176,128]{2,1,0:T(8,128)(2,1)S(1)} %all_to_all.26.refs_1_, ...), custom_call_target="tpu_custom_call" | custom-call | tf_op jit(solution)/shard_map/backward_tiles/pallas_call | solution.py:352
  117.4 5.0 %collective-permute-start.7 = (bf16[12,128,128]{2,1,0:T(8,128)(2,1)}, bf16[12,128,128]{2,1,0:T(8,128)(2,1)S(1)}, u32[]{:S(2)}, u32[]{:S(2)}) collective-permute-start(bf16[12,128,128]{2,1,0:T(8,128)(2,1)} %get-tuple-element.22), channel_id=1, source_target_pairs={{0,144},{48,0},{96,48},{144,96},{1,145},{49,1},{97,49},{145,97},{2... | collective-permute-start | bytes 1179656 | tf_op jit(solution)/shard_map/ppermute | solution.py:383
  122.3 1.9 collective-permute-start.8
  124.3 6.1 %collective-permute-start.6 = (bf16[12,64,128]{2,1,0:T(8,128)(2,1)}, bf16[12,64,128]{2,1,0:T(8,128)(2,1)S(1)}, u32[]{:S(2)}, u32[]{:S(2)}) collective-permute-start(bf16[12,64,128]{2,1,0:T(8,128)(2,1)} %get-tuple-element.21), channel_id=1, source_target_pairs={{0,96},{48,144},{96,0},{144,48},{1,97},{49,145},{97,1},{145,49},{2... | collective-permute-start | bytes 589832 | tf_op jit(solution)/shard_map/ppermute | solution.py:383
  130.4 18.5 %conditional.1 = (bf16[112,128]{1,0:T(8,128)(2,1)S(1)}) conditional(s32[]{:T(128)} %convert_element_type.4, () %tuple.14, bf16[12,112,128]{2,1,0:T(8,128)(2,1)} %get-tuple-element.24), branch_computations={%region_0.1_spmd, %region_1.2_spmd} | conditional | bytes 688136 | solution.py:398
  130.4 18.4 %all_to_all.24.arrived = bf16[12,112,128]{2,1,0:T(8,128)(2,1)S(1)} all-to-all(bf16[12,112,128]{2,1,0:T(8,128)(2,1)} %param.1), channel_id=1, replica_groups=mesh['ylo'=2,'core'=2,'yhi'=4,'x'=4,'z'=12] {'z'}, dimensions={0} | all-to-all | bytes 688128 | tf_op jit(solution)/shard_map/cond/branch_1_fun/all_to_all | solution.py:388
  148.8 0.1 share_sum.1
  148.9 0.9 middle_sums.1
  149.8 6.9 %all-to-all-start.4 = ((bf16[12,128,128]{2,1,0:T(8,128)(2,1)}), bf16[12,128,128]{2,1,0:T(8,128)(2,1)S(1)}, u32[]{:S(2)}, u32[]{:S(2)}) async-start(bf16[12,128,128]{2,1,0:T(8,128)(2,1)} %middle_sums.1), calls=%async_computation.4 | async-start | bytes 786432 | tf_op jit(solution)/shard_map/all_to_all | solution.py:423
  156.8 12.7 %all-gather = bf16[448,128]{1,0:T(8,128)(2,1)S(1)} all-gather(bf16[112,128]{1,0:T(8,128)(2,1)S(1)} %get-tuple-element.31.refs_4_), channel_id=2, replica_groups=mesh['ylo'=2,'core'=2,'yhi'=4,'x'=4,'z'=12] {'yhi'}, dimensions={0}, use_global_device_ids=true | all-gather | bytes 143360 | tf_op jit(solution)/shard_map/all_gather | solution.py:413
  169.5 24.6 %all-gather.1 = f32[256,128]{1,0:T(8,128)S(1)} all-gather(f32[32,128]{1,0:T(8,128)S(1)} %share_sum_far.1), channel_id=3, replica_groups=mesh['ylo'=2,'core'=2,'yhi'=4,'x'=4,'z'=12] {'core','x'}, dimensions={0}, use_global_device_ids=true | all-gather | bytes 147456 | tf_op jit(solution)/shard_map/all_gather | solution.py:422
  194.1 0.7 last_sums.1
  (22 shorter events, 0.1 us)
Async XLA Ops:
  0.6 18.2 %copy-start.4 = (s32[1,1,48]{2,1,0:T(1,128)S(1)}, s32[1,1,48]{2,1,0:T(1,128)}, u32[]{:S(2)}) copy-start(s32[1,1,48]{2,1,0:T(1,128)} %param.12) | copy-start | bytes 580
  0.6 18.2 %copy-start.5 = (s32[1,1,48]{2,1,0:T(1,128)S(1)}, s32[1,1,48]{2,1,0:T(1,128)}, u32[]{:S(2)}) copy-start(s32[1,1,48]{2,1,0:T(1,128)} %param.11) | copy-start | bytes 580
  0.7 18.3 %copy-start.3 = (bf16[1,1,48,64,128]{4,3,2,1,0:T(8,128)(2,1)S(1)}, bf16[1,1,48,64,128]{4,3,2,1,0:T(8,128)(2,1)}, u32[]{:S(2)}) copy-start(bf16[1,1,48,64,128]{4,3,2,1,0:T(8,128)(2,1)} %param.14) | copy-start | bytes 2359300
  2.3 34.4 %all-to-all-start.1 = ((bf16[12,128,128]{2,1,0:T(8,128)(2,1)}), bf16[12,128,128]{2,1,0:T(8,128)(2,1)S(1)}, u32[]{:S(2)}, u32[]{:S(2)}) async-start(bf16[12,128,128]{2,1,0:T(8,128)(2,1)} %broadcast_in_dim.16), calls=%async_computation.1 | async-start | bytes 786432 | tf_op jit(solution)/shard_map/all_to_all | solution.py:27
  19.0 27.5 %collective-permute-start.2 = (bf16[3088,128]{1,0:T(8,128)(2,1)S(1)}, bf16[3088,128]{1,0:T(8,128)(2,1)S(1)}, u32[]{:S(2)}, u32[]{:S(2)}) collective-permute-start(bf16[3088,128]{1,0:T(8,128)(2,1)S(1)} %pad_maximum_fusion.refs_1_.refs_5_.refs_2_), channel_id=1, source_target_pairs={{0,36},{12,0},{24,12},{36,24},{1,37},{13,1},{25,13},{37,25},{2,38}... | collective-permute-start | bytes 2371592 | tf_op jit(solution)/shard_map/ppermute | solution.py:295
  23.4 28.1 %collective-permute-start.1 = (bf16[3088,128]{1,0:T(8,128)(2,1)S(1)}, bf16[3088,128]{1,0:T(8,128)(2,1)S(1)}, u32[]{:S(2)}, u32[]{:S(2)}) collective-permute-start(bf16[3088,128]{1,0:T(8,128)(2,1)S(1)} %pad_maximum_fusion.refs_1_.refs_5_.refs_2_), channel_id=1, source_target_pairs={{0,12},{12,24},{24,36},{36,0},{1,13},{13,25},{25,37},{37,1},{2,14}... | collective-permute-start | bytes 2371592 | tf_op jit(solution)/shard_map/ppermute | solution.py:295
  25.4 35.1 %collective-permute-start = (bf16[3088,128]{1,0:T(8,128)(2,1)S(1)}, bf16[3088,128]{1,0:T(8,128)(2,1)S(1)}, u32[]{:S(2)}, u32[]{:S(2)}) collective-permute-start(bf16[3088,128]{1,0:T(8,128)(2,1)S(1)} %pad_maximum_fusion.refs_1_.refs_5_.refs_2_), channel_id=1, source_target_pairs={{0,24},{12,36},{24,0},{36,12},{1,25},{13,37},{25,1},{37,13},{2,26}... | collective-permute-start | bytes 2371592 | tf_op jit(solution)/shard_map/ppermute | solution.py:295
  36.7 23.8 %collective-permute-start.5 = (bf16[12,128,128]{2,1,0:T(8,128)(2,1)S(1)}, bf16[12,128,128]{2,1,0:T(8,128)(2,1)S(1)}, u32[]{:S(2)}, u32[]{:S(2)}) collective-permute-start(bf16[12,128,128]{2,1,0:T(8,128)(2,1)S(1)} %all-to-all-done.1.refs_1_), channel_id=1, source_target_pairs={{0,96},{48,144},{96,0},{144,48},{1,97},{49,145},{97,1},{145,49},{2... | collective-permute-start | bytes 1179656 | tf_op jit(solution)/shard_map/ppermute | solution.py:300
  44.2 26.5 %collective-permute-start.4 = (bf16[12,128,128]{2,1,0:T(8,128)(2,1)S(1)}, bf16[12,128,128]{2,1,0:T(8,128)(2,1)S(1)}, u32[]{:S(2)}, u32[]{:S(2)}) collective-permute-start(bf16[12,128,128]{2,1,0:T(8,128)(2,1)S(1)} %all-to-all-done.1.refs_1_), channel_id=1, source_target_pairs={{0,48},{48,96},{96,144},{144,0},{1,49},{49,97},{97,145},{145,1},{2... | collective-permute-start | bytes 1179656 | tf_op jit(solution)/shard_map/ppermute | solution.py:300
  46.6 33.1 %collective-permute-start.3 = (bf16[12,128,128]{2,1,0:T(8,128)(2,1)S(1)}, bf16[12,128,128]{2,1,0:T(8,128)(2,1)S(1)}, u32[]{:S(2)}, u32[]{:S(2)}) collective-permute-start(bf16[12,128,128]{2,1,0:T(8,128)(2,1)S(1)} %all-to-all-done.1.refs_1_), channel_id=1, source_target_pairs={{0,144},{48,0},{96,48},{144,96},{1,145},{49,1},{97,49},{145,97},{2... | collective-permute-start | bytes 1179656 | tf_op jit(solution)/shard_map/ppermute | solution.py:300
  81.9 15.1 %copy-start = (bf16[128,256]{1,0:T(8,128)(2,1)S(1)}, bf16[128,256]{1,0:T(8,128)(2,1)}, u32[]{:S(2)}) copy-start(bf16[128,256]{1,0:T(8,128)(2,1)} %refs_1_.1) | copy-start | bytes 196612
  81.9 15.1 %copy-start.1 = (bf16[128,256]{1,0:T(8,128)(2,1)S(1)}, bf16[128,256]{1,0:T(8,128)(2,1)}, u32[]{:S(2)}) copy-start(bf16[128,256]{1,0:T(8,128)(2,1)} %refs_3_.1) | copy-start | bytes 196612
  81.9 15.1 %copy-start.2 = (f32[256]{0:T(256)S(1)}, f32[256]{0:T(256)}, u32[]{:S(2)}) copy-start(f32[256]{0:T(256)} %param.16) | copy-start | bytes 3076
  117.4 31.5 %collective-permute-start.7 = (bf16[12,128,128]{2,1,0:T(8,128)(2,1)}, bf16[12,128,128]{2,1,0:T(8,128)(2,1)S(1)}, u32[]{:S(2)}, u32[]{:S(2)}) collective-permute-start(bf16[12,128,128]{2,1,0:T(8,128)(2,1)} %get-tuple-element.22), channel_id=1, source_target_pairs={{0,144},{48,0},{96,48},{144,96},{1,145},{49,1},{97,49},{145,97},{2... | collective-permute-start | bytes 1179656 | tf_op jit(solution)/shard_map/ppermute | solution.py:383
  122.3 26.6 %collective-permute-start.8 = (bf16[12,128,128]{2,1,0:T(8,128)(2,1)}, bf16[12,128,128]{2,1,0:T(8,128)(2,1)S(1)}, u32[]{:S(2)}, u32[]{:S(2)}) collective-permute-start(bf16[12,128,128]{2,1,0:T(8,128)(2,1)} %get-tuple-element.23), channel_id=1, source_target_pairs={{0,48},{48,96},{96,144},{144,0},{1,49},{49,97},{97,145},{145,1},{2... | collective-permute-start | bytes 1179656 | tf_op jit(solution)/shard_map/ppermute | solution.py:383
  124.3 24.6 %collective-permute-start.6 = (bf16[12,64,128]{2,1,0:T(8,128)(2,1)}, bf16[12,64,128]{2,1,0:T(8,128)(2,1)S(1)}, u32[]{:S(2)}, u32[]{:S(2)}) collective-permute-start(bf16[12,64,128]{2,1,0:T(8,128)(2,1)} %get-tuple-element.21), channel_id=1, source_target_pairs={{0,96},{48,144},{96,0},{144,48},{1,97},{49,145},{97,1},{145,49},{2... | collective-permute-start | bytes 589832 | tf_op jit(solution)/shard_map/ppermute | solution.py:383
  149.8 44.2 %all-to-all-start.4 = ((bf16[12,128,128]{2,1,0:T(8,128)(2,1)}), bf16[12,128,128]{2,1,0:T(8,128)(2,1)S(1)}, u32[]{:S(2)}, u32[]{:S(2)}) async-start(bf16[12,128,128]{2,1,0:T(8,128)(2,1)} %middle_sums.1), calls=%async_computation.4 | async-start | bytes 786432 | tf_op jit(solution)/shard_map/all_to_all | solution.py:423

commit v15 on v10

--- a/solution.py
+++ b/solution.py
@@ -14,6 +14,7 @@
 col_axes = ("yhi", "x", "z")
 team_axes = ("ylo", "core", "x")
 share_axes = ("core", "x")
+tail_rows = 16
 group = 4
 lanes = 128
 vmem_bytes = 12 * 1024 * 1024
@@ -191,8 +192,12 @@
     lax.fori_loop(0, (total + group - 1) // group, body, 0)
     near = slab_count // far
     for shift, out in enumerate(outs):
+        rows = out.shape[1]
         for index in range(near):
-            out[index] = totals[shift * near + index].astype(jnp.bfloat16)
+            total = totals[shift * near + index].astype(jnp.bfloat16)
+            out[index] = total[:rows]
+            if rows < nodes:
+                shares[index, pl.ds(2 * share + 16, nodes - rows), :] = total[rows:]
     weight_sum = sum_rows(spreads, nodes, 2 * share).astype(jnp.bfloat16)
     bias_block = pack_bias(sum_bias(spreads, nodes + 2 * share))
     for index in range(near):
@@ -200,34 +205,44 @@
         shares[index, pl.ds(2 * share, 16), :] = bias_block
 
 
-def share_kernel(arrived, out, bias_block, *, share):
+def share_kernel(arrived, out, bias_block, tail, *, share):
     total = sum_rows(arrived, 0, 2 * share).astype(jnp.bfloat16)
     for index in range(out.shape[0]):
         out[index] = total
     bias_block[...] = pack_bias(sum_bias(arrived, 2 * share))
-
-
-def gather_kernel(shares, bias_block, out, *, share):
+    tail[...] = sum_rows(arrived, 2 * share + 16, tail.shape[0]).astype(jnp.bfloat16)
+
+
+def gather_kernel(shares, bias_block, tail, out, *, share):
     rows = shares.shape[0] * share
     for index in range(shares.shape[0]):
         for half in range(2):
             part = shares[index, pl.ds(half * share, share), :]
             out[pl.ds(half * rows + index * share, share), :] = part
     out[pl.ds(2 * rows, 16), :] = bias_block[...]
+    out[pl.ds(2 * rows + 16, tail.shape[0]), :] = tail[...]
 
 
 def middle_kernel(*refs, far):
-    out = refs[-1]
+    lines, out = refs[:far], refs[-1]
+    nodes = out.shape[1]
+    rows = min(line.shape[1] for line in lines)
     for index in range(out.shape[0]):
-        total = refs[0][index].astype(jnp.float32)
-        for line in refs[1:far]:
-            total = total + line[index].astype(jnp.float32)
-        out[index] = total.astype(jnp.bfloat16)
-
-
-def last_kernel(arrived, pieces, grad, weight_grad, bias_grad, *, factor):
-    grad[...] = sum_rows(arrived, 0, grad.shape[0])
+        for top, size in ((0, rows), (rows, nodes - rows)):
+            total = jnp.zeros((size, lanes), jnp.float32)
+            for line in lines:
+                if top < line.shape[1]:
+                    total = total + line[index, pl.ds(top, size), :].astype(jnp.float32)
+            out[index, pl.ds(top, size), :] = total.astype(jnp.bfloat16)
+
+
+def last_kernel(opposite, arrived, pieces, grad, weight_grad, bias_grad, *, factor):
     rows = weight_grad.shape[0]
+    tail = pieces.shape[1] - 2 * rows - 16
+    lead = grad.shape[0] - tail
+    grad[pl.ds(0, lead), :] = sum_rows(arrived, 0, lead)
+    late = pieces[opposite[0], pl.ds(2 * rows + 16, tail), :].astype(jnp.float32)
+    grad[pl.ds(lead, tail), :] = sum_rows(arrived, lead, tail) + late
     weight_grad[:, pl.ds(0, lanes)] = sum_rows(pieces, 0, rows) * factor
     weight_grad[:, pl.ds(lanes, lanes)] = sum_rows(pieces, rows, rows) * factor
     low, high = sum_bias(pieces, 2 * rows)
@@ -335,6 +350,7 @@
     )(partials, weight, bias.reshape(1, hidden), cotangent)
     spreads = lax.all_to_all(message, team_axes, 0, 0, tiled=True)
 
+    opposite = far // 2
     outs = pl.pallas_call(
         lambda *refs: backward_kernel(
             *refs,
@@ -346,8 +362,13 @@
             far=far,
             across=across,
         ),
-        out_shape=(jax.ShapeDtypeStruct((near, nodes, width), jnp.bfloat16),) * far
-        + (jax.ShapeDtypeStruct((near, 2 * share + 16, width), jnp.bfloat16),),
+        out_shape=tuple(
+            jax.ShapeDtypeStruct(
+                (near, nodes - (tail_rows if shift == opposite else 0), width), jnp.bfloat16
+            )
+            for shift in range(far)
+        )
+        + (jax.ShapeDtypeStruct((near, 2 * share + 16 + tail_rows, width), jnp.bfloat16),),
         in_specs=[in_smem(), in_vmem()] + [in_vmem()] * across,
         out_specs=(in_vmem(),) * (far + 1),
         scratch_shapes=[
@@ -365,31 +386,32 @@
 
     def gather_gradients(value):
         arrived = lax.all_to_all(value, "z", 0, 0, tiled=True)
-        shares, bias_block = pl.pallas_call(
+        shares, bias_block, tail = pl.pallas_call(
             lambda *refs: share_kernel(*refs, share=share),
             out_shape=(
                 jax.ShapeDtypeStruct((holders, 2 * share, lanes), jnp.bfloat16),
                 jax.ShapeDtypeStruct((16, lanes), jnp.bfloat16),
+                jax.ShapeDtypeStruct((tail_rows, width), jnp.bfloat16),
             ),
             in_specs=[in_vmem()],
-            out_specs=(in_vmem(), in_vmem()),
+            out_specs=(in_vmem(), in_vmem(), in_vmem()),
             compiler_params=params,
             name="share_sum",
         )(arrived)
         shares = lax.all_to_all(shares, share_axes, 0, 0, tiled=True)
         return pl.pallas_call(
             lambda *refs: gather_kernel(*refs, share=share),
-            out_shape=jax.ShapeDtypeStruct((2 * width + 16, lanes), jnp.bfloat16),
-            in_specs=[in_vmem(), in_vmem()],
+            out_shape=jax.ShapeDtypeStruct((2 * width + 16 + tail_rows, lanes), jnp.bfloat16),
+            in_specs=[in_vmem()] * 3,
             out_specs=in_vmem(),
             compiler_params=params,
             name="share_gather",
-        )(shares, bias_block)
+        )(shares, bias_block, tail)
 
     gradients = lax.cond(
         tile_counts[0, 0] > 0,
         gather_gradients,
-        lambda value: jnp.zeros((2 * width + 16, lanes), jnp.bfloat16),
+        lambda value: jnp.zeros((2 * width + 16 + tail_rows, lanes), jnp.bfloat16),
         outs[far],
     )
     line = pl.pallas_call(
@@ -411,11 +433,11 @@
             jax.ShapeDtypeStruct((width, hidden), jnp.float32),
             jax.ShapeDtypeStruct((1, hidden), jnp.float32),
         ),
-        in_specs=[in_vmem(), in_vmem()],
+        in_specs=[in_smem(), in_vmem(), in_vmem()],
         out_specs=(in_vmem(), in_vmem(), in_vmem()),
         compiler_params=params,
         name="last_sums",
-    )(arrived, pieces)
+    )(((lax.axis_index("yhi") + opposite) % far).reshape(1), arrived, pieces)
     return (hidden_out, features_grad, weight_grad, bias_grad.reshape(hidden))
 
 

time: 186 us -> 186 us (level)
  the two profiles are of different devices: /device:TPU:1 before, /device:TPU:6 now
where the time goes in v15:
time: 186 us; the launch traced here: 185 us
  blocking collectives  71.3 us (38%)
  starting transfers between devices  61.6 us (33%)
  waiting for transfers between devices  39.7 us (21%)
  Pallas kernels  8.54 us (5%)
    all_to_all x1, blocking collectives, gather_gradients(): arrived = lax.all_to_all(value, 'z', 0, 0, tiled=True)  20 us
    ppermute x3, starting transfers between devices, local(): lines.append(lax.ppermute(lines[0], 'yhi', ring(far, shift)))  16.6 us
    all_to_all x1, blocking collectives, local(): spreads = lax.all_to_all(message, team_axes, 0, 0, tiled=True)  16.1 us
    all_to_all x1, starting transfers between devices, spread_out(): return lax.all_to_all(copies, axes, 0, 0, tiled=True)  15.2 us
    ppermute x3, waiting for transfers between devices, local(): lines.append(lax.ppermute(lines[0], 'yhi', ring(far, shift)))  15 us
    all_gather x1, blocking collectives, local(): pieces = lax.all_gather(gradients, 'yhi', axis=0)  14.5 us
    all_to_all x1, blocking collectives, local(): partials = lax.all_to_all(partial, team_axes, 0, 0, tiled=True)  12.8 us
    ppermute x3, starting transfers between devices, local(): lines.append(lax.ppermute(outs[shift], 'yhi', ring(far, -shift)))  11.7 us
  transfers between devices with their start and end apart: 11, of which 5 were waited for; matrix products, arithmetic and copies ran while one was open for 0% of the time, Pallas kernels for 0%

profile of v15, /device:TPU:6, one launch (start us, length us, event | category | flops | bytes accessed | tf_op | source)
XLA Modules:
  0.0 184.7 jit_solution(18185848379985333731)
XLA Ops:
  0.7 1.7 broadcast_in_dim.16
  2.3 15.2 %all-to-all-start.2 = ((bf16[12,128,128]{2,1,0:T(8,128)(2,1)}), bf16[12,128,128]{2,1,0:T(8,128)(2,1)S(1)}, u32[]{:S(2)}, u32[]{:S(2)}) async-start(bf16[12,128,128]{2,1,0:T(8,128)(2,1)} %broadcast_in_dim.16), calls=%async_computation.2 | async-start | bytes 786432 | tf_op jit(solution)/shard_map/all_to_all | solution.py:27
  18.1 0.1 maximum_bitcast_fusion
  18.2 0.1 copy.12
  18.4 0.1 fusion.8
  18.4 0.1 pad_maximum_fusion.refs_1_.refs_5_.refs_2_
  18.5 2.7 %collective-permute-start.2 = (bf16[3088,128]{1,0:T(8,128)(2,1)S(1)}, bf16[3088,128]{1,0:T(8,128)(2,1)S(1)}, u32[]{:S(2)}, u32[]{:S(2)}) collective-permute-start(bf16[3088,128]{1,0:T(8,128)(2,1)S(1)} %pad_maximum_fusion.refs_1_.refs_5_.refs_2_), channel_id=1, source_target_pairs={{0,36},{12,0},{24,12},{36,24},{1,37},{13,1},{25,13},{37,25},{2,38}... | collective-permute-start | bytes 2371592 | tf_op jit(solution)/shard_map/ppermute | solution.py:297
  21.2 4.3 %collective-permute-start.1 = (bf16[3088,128]{1,0:T(8,128)(2,1)S(1)}, bf16[3088,128]{1,0:T(8,128)(2,1)S(1)}, u32[]{:S(2)}, u32[]{:S(2)}) collective-permute-start(bf16[3088,128]{1,0:T(8,128)(2,1)S(1)} %pad_maximum_fusion.refs_1_.refs_5_.refs_2_), channel_id=1, source_target_pairs={{0,12},{12,24},{24,36},{36,0},{1,13},{13,25},{25,37},{37,1},{2,14}... | collective-permute-start | bytes 2371592 | tf_op jit(solution)/shard_map/ppermute | solution.py:297
  25.6 2.1 %collective-permute-start = (bf16[3088,128]{1,0:T(8,128)(2,1)S(1)}, bf16[3088,128]{1,0:T(8,128)(2,1)S(1)}, u32[]{:S(2)}, u32[]{:S(2)}) collective-permute-start(bf16[3088,128]{1,0:T(8,128)(2,1)S(1)} %pad_maximum_fusion.refs_1_.refs_5_.refs_2_), channel_id=1, source_target_pairs={{0,24},{12,36},{24,0},{36,12},{1,25},{13,37},{25,1},{37,13},{2,26}... | collective-permute-start | bytes 2371592 | tf_op jit(solution)/shard_map/ppermute | solution.py:297
  27.7 9.6 %all-to-all-done.2.refs_1_ = bf16[12,128,128]{2,1,0:T(8,128)(2,1)S(1)} async-done(((bf16[12,128,128]{2,1,0:T(8,128)(2,1)}), bf16[12,128,128]{2,1,0:T(8,128)(2,1)S(1)}, u32[]{:S(2)}, u32[]{:S(2)}) %all-to-all-start.2) | async-done | bytes 393248 | tf_op jit(solution)/shard_map/all_to_all | solution.py:27
  37.2 7.7 %collective-permute-start.5 = (bf16[12,128,128]{2,1,0:T(8,128)(2,1)S(1)}, bf16[12,128,128]{2,1,0:T(8,128)(2,1)S(1)}, u32[]{:S(2)}, u32[]{:S(2)}) collective-permute-start(bf16[12,128,128]{2,1,0:T(8,128)(2,1)S(1)} %all-to-all-done.2.refs_1_), channel_id=1, source_target_pairs={{0,96},{48,144},{96,0},{144,48},{1,97},{49,145},{97,1},{145,49},{2... | collective-permute-start | bytes 1179656 | tf_op jit(solution)/shard_map/ppermute | solution.py:302
  45.0 2.7 %collective-permute-start.4 = (bf16[12,128,128]{2,1,0:T(8,128)(2,1)S(1)}, bf16[12,128,128]{2,1,0:T(8,128)(2,1)S(1)}, u32[]{:S(2)}, u32[]{:S(2)}) collective-permute-start(bf16[12,128,128]{2,1,0:T(8,128)(2,1)S(1)} %all-to-all-done.2.refs_1_), channel_id=1, source_target_pairs={{0,48},{48,96},{96,144},{144,0},{1,49},{49,97},{97,145},{145,1},{2... | collective-permute-start | bytes 1179656 | tf_op jit(solution)/shard_map/ppermute | solution.py:302
  47.7 9.9 %collective-permute-done.2.refs_4_.refs_8_.refs_5_ = bf16[3088,128]{1,0:T(8,128)(2,1)S(1)} collective-permute-done((bf16[3088,128]{1,0:T(8,128)(2,1)S(1)}, bf16[3088,128]{1,0:T(8,128)(2,1)S(1)}, u32[]{:S(2)}, u32[]{:S(2)}) %collective-permute-start.2) | collective-permute-done | bytes 790560 | tf_op jit(solution)/shard_map/ppermute | solution.py:297
  57.6 6.2 %collective-permute-start.3 = (bf16[12,128,128]{2,1,0:T(8,128)(2,1)S(1)}, bf16[12,128,128]{2,1,0:T(8,128)(2,1)S(1)}, u32[]{:S(2)}, u32[]{:S(2)}) collective-permute-start(bf16[12,128,128]{2,1,0:T(8,128)(2,1)S(1)} %all-to-all-done.2.refs_1_), channel_id=1, source_target_pairs={{0,144},{48,0},{96,48},{144,96},{1,145},{49,1},{97,49},{145,97},{2... | collective-permute-start | bytes 1179656 | tf_op jit(solution)/shard_map/ppermute | solution.py:302
  63.8 5.9 %collective-permute-done.4.refs_6_.refs_3_ = bf16[12,128,128]{2,1,0:T(8,128)(2,1)S(1)} collective-permute-done((bf16[12,128,128]{2,1,0:T(8,128)(2,1)S(1)}, bf16[12,128,128]{2,1,0:T(8,128)(2,1)S(1)}, u32[]{:S(2)}, u32[]{:S(2)}) %collective-permute-start.4) | collective-permute-done | bytes 393248 | tf_op jit(solution)/shard_map/ppermute | solution.py:302
  69.7 9.1 %collective-permute-done.3.refs_5_.refs_2_ = bf16[12,128,128]{2,1,0:T(8,128)(2,1)S(1)} collective-permute-done((bf16[12,128,128]{2,1,0:T(8,128)(2,1)S(1)}, bf16[12,128,128]{2,1,0:T(8,128)(2,1)S(1)}, u32[]{:S(2)}, u32[]{:S(2)}) %collective-permute-start.3) | collective-permute-done | bytes 393248 | tf_op jit(solution)/shard_map/ppermute | solution.py:302
  78.8 2.2 %forward_tiles.1 = bf16[16,128,128]{2,1,0:T(8,128)(2,1)S(1)} custom-call(s32[4,128]{1,0:T(4,128)S(1)} %tile_codes.1.refs_0_, bf16[12,128,128]{2,1,0:T(8,128)(2,1)S(1)} %all-to-all-done.2.refs_1_, bf16[12,128,128]{2,1,0:T(8,128)(2,1)S(1)} %collective-permute-done.3.refs_5_.refs_2_, bf16[12,128,128]{2,1,0:T(8,128)(2,1)S(1)} %collective-permute-done.4.refs_6_.refs_3_, ...), custom_call_target="tpu_custom_call" | custom-call | tf_op jit(solution)/shard_map/forward_tiles/pallas_call | solution.py:315
  81.1 12.8 %all_to_all.30.refs_0_ = bf16[16,128,128]{2,1,0:T(8,128)(2,1)S(1)} all-to-all(bf16[16,128,128]{2,1,0:T(8,128)(2,1)S(1)} %forward_tiles.1), channel_id=1, replica_groups=mesh['ylo'=2,'core'=2,'yhi'=4,'x'=4,'z'=12] {'ylo','core','x'}, dimensions={0} | all-to-all | bytes 1048576 | tf_op jit(solution)/shard_map/all_to_all | solution.py:336
  93.9 1.1 dense_layer.1
  95.0 16.1 %all_to_all.31.refs_1_ = bf16[16,176,128]{2,1,0:T(8,128)(2,1)S(1)} all-to-all(bf16[16,176,128]{2,1,0:T(8,128)(2,1)S(1)} %get-tuple-element.22), channel_id=1, replica_groups=mesh['ylo'=2,'core'=2,'yhi'=4,'x'=4,'z'=12] {'ylo','core','x'}, dimensions={0} | all-to-all | bytes 1441792 | tf_op jit(solution)/shard_map/all_to_all | solution.py:351
  111.1 3.5 %backward_tiles.1 = (bf16[12,128,128]{2,1,0:T(8,128)(2,1)S(1)}, bf16[12,128,128]{2,1,0:T(8,128)(2,1)}, bf16[12,112,128]{2,1,0:T(8,128)(2,1)}, bf16[12,128,128]{2,1,0:T(8,128)(2,1)}, bf16[12,64,128]{2,1,0:T(8,128)(2,1)}) custom-call(s32[4,128]{1,0:T(4,128)S(1)} %tile_codes.1.refs_0_, bf16[16,176,128]{2,1,0:T(8,128)(2,1)S(1)} %all_to_all.31.refs_1_, ...), custom_call_target="tpu_custom_call" | custom-call | tf_op jit(solution)/shard_map/backward_tiles/pallas_call | solution.py:354
  114.6 3.8 %collective-permute-start.7 = (bf16[12,128,128]{2,1,0:T(8,128)(2,1)}, bf16[12,128,128]{2,1,0:T(8,128)(2,1)S(1)}, u32[]{:S(2)}, u32[]{:S(2)}) collective-permute-start(bf16[12,128,128]{2,1,0:T(8,128)(2,1)} %get-tuple-element.25), channel_id=1, source_target_pairs={{0,144},{48,0},{96,48},{144,96},{1,145},{49,1},{97,49},{145,97},{2... | collective-permute-start | bytes 1179656 | tf_op jit(solution)/shard_map/ppermute | solution.py:385
  118.4 3.0 %collective-permute-start.8 = (bf16[12,128,128]{2,1,0:T(8,128)(2,1)}, bf16[12,128,128]{2,1,0:T(8,128)(2,1)S(1)}, u32[]{:S(2)}, u32[]{:S(2)}) collective-permute-start(bf16[12,128,128]{2,1,0:T(8,128)(2,1)} %get-tuple-element.26), channel_id=1, source_target_pairs={{0,48},{48,96},{96,144},{144,0},{1,49},{49,97},{97,145},{145,1},{2... | collective-permute-start | bytes 1179656 | tf_op jit(solution)/shard_map/ppermute | solution.py:385
  121.4 5.0 %collective-permute-start.6 = (bf16[12,112,128]{2,1,0:T(8,128)(2,1)}, bf16[12,112,128]{2,1,0:T(8,128)(2,1)S(1)}, u32[]{:S(2)}, u32[]{:S(2)}) collective-permute-start(bf16[12,112,128]{2,1,0:T(8,128)(2,1)} %get-tuple-element.24), channel_id=1, source_target_pairs={{0,96},{48,144},{96,0},{144,48},{1,97},{49,145},{97,1},{145,49},{2... | collective-permute-start | bytes 1032200 | tf_op jit(solution)/shard_map/ppermute | solution.py:385
  126.3 27.9 %conditional.1 = (bf16[288,128]{1,0:T(8,128)(2,1)S(1)}) conditional(s32[]{:T(128)} %convert_element_type.4, () %tuple.14, bf16[12,64,128]{2,1,0:T(8,128)(2,1)} %get-tuple-element.27), branch_computations={%region_0.1_spmd, %region_1.2_spmd} | conditional | bytes 524296 | solution.py:411
  126.4 20.0 %all_to_all.28.refs_0_ = bf16[12,64,128]{2,1,0:T(8,128)(2,1)S(1)} all-to-all(bf16[12,64,128]{2,1,0:T(8,128)(2,1)} %param.1), channel_id=1, replica_groups=mesh['ylo'=2,'core'=2,'yhi'=4,'x'=4,'z'=12] {'z'}, dimensions={0} | all-to-all | bytes 393216 | tf_op jit(solution)/shard_map/cond/branch_1_fun/all_to_all | solution.py:388
  146.4 7.9 %all_to_all.29.refs_0_ = bf16[8,32,128]{2,1,0:T(8,128)(2,1)S(1)} all-to-all(bf16[8,32,128]{2,1,0:T(8,128)(2,1)S(1)} %get-tuple-element.4), channel_id=1, replica_groups=mesh['ylo'=2,'core'=2,'yhi'=4,'x'=4,'z'=12] {'core','x'}, dimensions={0} | all-to-all | bytes 131072 | tf_op jit(solution)/shard_map/cond/branch_1_fun/all_to_all | solution.py:401
  154.3 0.9 middle_sums.1
  155.2 9.0 %all-to-all-start.5 = ((bf16[12,128,128]{2,1,0:T(8,128)(2,1)}), bf16[12,128,128]{2,1,0:T(8,128)(2,1)S(1)}, u32[]{:S(2)}, u32[]{:S(2)}) async-start(bf16[12,128,128]{2,1,0:T(8,128)(2,1)} %middle_sums.1), calls=%async_computation.5 | async-start | bytes 786432 | tf_op jit(solution)/shard_map/all_to_all | solution.py:427
  164.3 14.5 %all-gather = bf16[1152,128]{1,0:T(8,128)(2,1)S(1)} all-gather(bf16[288,128]{1,0:T(8,128)(2,1)S(1)} %get-tuple-element.34.refs_4_), channel_id=2, replica_groups=mesh['ylo'=2,'core'=2,'yhi'=4,'x'=4,'z'=12] {'yhi'}, dimensions={0}, use_global_device_ids=true | all-gather | bytes 368640 | tf_op jit(solution)/shard_map/all_gather | solution.py:426
  178.8 5.2 %all-to-all-done.5.refs_1_ = bf16[12,128,128]{2,1,0:T(8,128)(2,1)S(1)} async-done(((bf16[12,128,128]{2,1,0:T(8,128)(2,1)}), bf16[12,128,128]{2,1,0:T(8,128)(2,1)S(1)}, u32[]{:S(2)}, u32[]{:S(2)}) %all-to-all-start.5) | async-done | bytes 393248 | tf_op jit(solution)/shard_map/all_to_all | solution.py:427
  184.0 0.7 last_sums.1
  (22 shorter events, 0.1 us)
Async XLA Ops:
  0.6 17.7 %copy-start.4 = (s32[1,1,48]{2,1,0:T(1,128)S(1)}, s32[1,1,48]{2,1,0:T(1,128)}, u32[]{:S(2)}) copy-start(s32[1,1,48]{2,1,0:T(1,128)} %param.12) | copy-start | bytes 580
  0.6 17.7 %copy-start.5 = (s32[1,1,48]{2,1,0:T(1,128)S(1)}, s32[1,1,48]{2,1,0:T(1,128)}, u32[]{:S(2)}) copy-start(s32[1,1,48]{2,1,0:T(1,128)} %param.11) | copy-start | bytes 580
  0.7 17.8 %copy-start.3 = (bf16[1,1,48,64,128]{4,3,2,1,0:T(8,128)(2,1)S(1)}, bf16[1,1,48,64,128]{4,3,2,1,0:T(8,128)(2,1)}, u32[]{:S(2)}) copy-start(bf16[1,1,48,64,128]{4,3,2,1,0:T(8,128)(2,1)} %param.14) | copy-start | bytes 2359300
  2.3 34.9 %all-to-all-start.2 = ((bf16[12,128,128]{2,1,0:T(8,128)(2,1)}), bf16[12,128,128]{2,1,0:T(8,128)(2,1)S(1)}, u32[]{:S(2)}, u32[]{:S(2)}) async-start(bf16[12,128,128]{2,1,0:T(8,128)(2,1)} %broadcast_in_dim.16), calls=%async_computation.2 | async-start | bytes 786432 | tf_op jit(solution)/shard_map/all_to_all | solution.py:27
  18.5 39.1 %collective-permute-start.2 = (bf16[3088,128]{1,0:T(8,128)(2,1)S(1)}, bf16[3088,128]{1,0:T(8,128)(2,1)S(1)}, u32[]{:S(2)}, u32[]{:S(2)}) collective-permute-start(bf16[3088,128]{1,0:T(8,128)(2,1)S(1)} %pad_maximum_fusion.refs_1_.refs_5_.refs_2_), channel_id=1, source_target_pairs={{0,36},{12,0},{24,12},{36,24},{1,37},{13,1},{25,13},{37,25},{2,38}... | collective-permute-start | bytes 2371592 | tf_op jit(solution)/shard_map/ppermute | solution.py:297
  21.2 42.6 %collective-permute-start.1 = (bf16[3088,128]{1,0:T(8,128)(2,1)S(1)}, bf16[3088,128]{1,0:T(8,128)(2,1)S(1)}, u32[]{:S(2)}, u32[]{:S(2)}) collective-permute-start(bf16[3088,128]{1,0:T(8,128)(2,1)S(1)} %pad_maximum_fusion.refs_1_.refs_5_.refs_2_), channel_id=1, source_target_pairs={{0,12},{12,24},{24,36},{36,0},{1,13},{13,25},{25,37},{37,1},{2,14}... | collective-permute-start | bytes 2371592 | tf_op jit(solution)/shard_map/ppermute | solution.py:297
  25.6 38.2 %collective-permute-start = (bf16[3088,128]{1,0:T(8,128)(2,1)S(1)}, bf16[3088,128]{1,0:T(8,128)(2,1)S(1)}, u32[]{:S(2)}, u32[]{:S(2)}) collective-permute-start(bf16[3088,128]{1,0:T(8,128)(2,1)S(1)} %pad_maximum_fusion.refs_1_.refs_5_.refs_2_), channel_id=1, source_target_pairs={{0,24},{12,36},{24,0},{36,12},{1,25},{13,37},{25,1},{37,13},{2,26}... | collective-permute-start | bytes 2371592 | tf_op jit(solution)/shard_map/ppermute | solution.py:297
  37.2 26.6 %collective-permute-start.5 = (bf16[12,128,128]{2,1,0:T(8,128)(2,1)S(1)}, bf16[12,128,128]{2,1,0:T(8,128)(2,1)S(1)}, u32[]{:S(2)}, u32[]{:S(2)}) collective-permute-start(bf16[12,128,128]{2,1,0:T(8,128)(2,1)S(1)} %all-to-all-done.2.refs_1_), channel_id=1, source_target_pairs={{0,96},{48,144},{96,0},{144,48},{1,97},{49,145},{97,1},{145,49},{2... | collective-permute-start | bytes 1179656 | tf_op jit(solution)/shard_map/ppermute | solution.py:302
  45.0 24.7 %collective-permute-start.4 = (bf16[12,128,128]{2,1,0:T(8,128)(2,1)S(1)}, bf16[12,128,128]{2,1,0:T(8,128)(2,1)S(1)}, u32[]{:S(2)}, u32[]{:S(2)}) collective-permute-start(bf16[12,128,128]{2,1,0:T(8,128)(2,1)S(1)} %all-to-all-done.2.refs_1_), channel_id=1, source_target_pairs={{0,48},{48,96},{96,144},{144,0},{1,49},{49,97},{97,145},{145,1},{2... | collective-permute-start | bytes 1179656 | tf_op jit(solution)/shard_map/ppermute | solution.py:302
  57.6 21.2 %collective-permute-start.3 = (bf16[12,128,128]{2,1,0:T(8,128)(2,1)S(1)}, bf16[12,128,128]{2,1,0:T(8,128)(2,1)S(1)}, u32[]{:S(2)}, u32[]{:S(2)}) collective-permute-start(bf16[12,128,128]{2,1,0:T(8,128)(2,1)S(1)} %all-to-all-done.2.refs_1_), channel_id=1, source_target_pairs={{0,144},{48,0},{96,48},{144,96},{1,145},{49,1},{97,49},{145,97},{2... | collective-permute-start | bytes 1179656 | tf_op jit(solution)/shard_map/ppermute | solution.py:302
  81.0 12.9 %copy-start = (bf16[128,256]{1,0:T(8,128)(2,1)S(1)}, bf16[128,256]{1,0:T(8,128)(2,1)}, u32[]{:S(2)}) copy-start(bf16[128,256]{1,0:T(8,128)(2,1)} %refs_1_.1) | copy-start | bytes 196612
  81.1 12.9 %copy-start.1 = (bf16[128,256]{1,0:T(8,128)(2,1)S(1)}, bf16[128,256]{1,0:T(8,128)(2,1)}, u32[]{:S(2)}) copy-start(bf16[128,256]{1,0:T(8,128)(2,1)} %refs_3_.1) | copy-start | bytes 196612
  81.1 12.8 %copy-start.2 = (f32[256]{0:T(256)S(1)}, f32[256]{0:T(256)}, u32[]{:S(2)}) copy-start(f32[256]{0:T(256)} %param.16) | copy-start | bytes 3076
  114.6 39.7 %collective-permute-start.7 = (bf16[12,128,128]{2,1,0:T(8,128)(2,1)}, bf16[12,128,128]{2,1,0:T(8,128)(2,1)S(1)}, u32[]{:S(2)}, u32[]{:S(2)}) collective-permute-start(bf16[12,128,128]{2,1,0:T(8,128)(2,1)} %get-tuple-element.25), channel_id=1, source_target_pairs={{0,144},{48,0},{96,48},{144,96},{1,145},{49,1},{97,49},{145,97},{2... | collective-permute-start | bytes 1179656 | tf_op jit(solution)/shard_map/ppermute | solution.py:385
  118.4 35.9 %collective-permute-start.8 = (bf16[12,128,128]{2,1,0:T(8,128)(2,1)}, bf16[12,128,128]{2,1,0:T(8,128)(2,1)S(1)}, u32[]{:S(2)}, u32[]{:S(2)}) collective-permute-start(bf16[12,128,128]{2,1,0:T(8,128)(2,1)} %get-tuple-element.26), channel_id=1, source_target_pairs={{0,48},{48,96},{96,144},{144,0},{1,49},{49,97},{97,145},{145,1},{2... | collective-permute-start | bytes 1179656 | tf_op jit(solution)/shard_map/ppermute | solution.py:385
  121.4 32.9 %collective-permute-start.6 = (bf16[12,112,128]{2,1,0:T(8,128)(2,1)}, bf16[12,112,128]{2,1,0:T(8,128)(2,1)S(1)}, u32[]{:S(2)}, u32[]{:S(2)}) collective-permute-start(bf16[12,112,128]{2,1,0:T(8,128)(2,1)} %get-tuple-element.24), channel_id=1, source_target_pairs={{0,96},{48,144},{96,0},{144,48},{1,97},{49,145},{97,1},{145,49},{2... | collective-permute-start | bytes 1032200 | tf_op jit(solution)/shard_map/ppermute | solution.py:385
  155.2 28.7 %all-to-all-start.5 = ((bf16[12,128,128]{2,1,0:T(8,128)(2,1)}), bf16[12,128,128]{2,1,0:T(8,128)(2,1)S(1)}, u32[]{:S(2)}, u32[]{:S(2)}) async-start(bf16[12,128,128]{2,1,0:T(8,128)(2,1)} %middle_sums.1), calls=%async_computation.5 | async-start | bytes 786432 | tf_op jit(solution)/shard_map/all_to_all | solution.py:427

commit v16 on v15

--- a/solution.py
+++ b/solution.py
@@ -304,11 +304,11 @@
     codes = pl.pallas_call(
         lambda *refs: codes_kernel(*refs, across=across, top=slots * height),
         out_shape=jax.ShapeDtypeStruct((across, lanes), jnp.int32),
-        in_specs=[in_smem()] + [in_vmem()] * across + [any_place()] * (far - 1),
+        in_specs=[in_smem()] + [in_vmem()] * across,
         out_specs=in_vmem(),
         compiler_params=params,
         name="tile_codes",
-    )(here.reshape(1), *buffers, *lines[1:])
+    )(here.reshape(1), *buffers)
 
     scratch_tiles = pltpu.VMEM((across * slots + group, height, tile_width), jnp.bfloat16)
     scratch_list = pltpu.SMEM((across * slots + group,), jnp.int32)

time: 186 us -> 186 us (level)
  the two profiles are of different devices: /device:TPU:6 before, /device:TPU:16 now
where the time goes in v16:
time: 186 us; the launch traced here: 185 us
  blocking collectives  72.4 us (39%)
  starting transfers between devices  53.8 us (29%)
  waiting for transfers between devices  46.9 us (25%)
  Pallas kernels  8.34 us (4%)
    all_to_all x1, blocking collectives, gather_gradients(): arrived = lax.all_to_all(value, 'z', 0, 0, tiled=True)  19 us
    ppermute x3, waiting for transfers between devices, local(): lines.append(lax.ppermute(lines[0], 'yhi', ring(far, shift)))  16 us
    all_to_all x1, blocking collectives, local(): partials = lax.all_to_all(partial, team_axes, 0, 0, tiled=True)  15.9 us
    all_to_all x1, blocking collectives, local(): spreads = lax.all_to_all(message, team_axes, 0, 0, tiled=True)  15.6 us
    all_to_all x1, starting transfers between devices, spread_out(): return lax.all_to_all(copies, axes, 0, 0, tiled=True)  15.2 us
    ppermute x3, waiting for transfers between devices, local(): buffers.append(lax.ppermute(own, 'x', ring(across, shift)))  14.7 us
    all_gather x1, blocking collectives, local(): pieces = lax.all_gather(gradients, 'yhi', axis=0)  14.1 us
    ppermute x3, starting transfers between devices, local(): lines.append(lax.ppermute(outs[shift], 'yhi', ring(far, -shift)))  12.6 us
  transfers between devices with their start and end apart: 11, of which 6 were waited for; matrix products, arithmetic and copies ran while one was open for 0% of the time, Pallas kernels for 0%

profile of v16, /device:TPU:16, one launch (start us, length us, event | category | flops | bytes accessed | tf_op | source)
XLA Modules:
  0.0 184.9 jit_solution(6885443892479474766)
XLA Ops:
  0.7 1.7 broadcast_in_dim.16
  2.3 15.2 %all-to-all-start.2 = ((bf16[12,128,128]{2,1,0:T(8,128)(2,1)}), bf16[12,128,128]{2,1,0:T(8,128)(2,1)S(1)}, u32[]{:S(2)}, u32[]{:S(2)}) async-start(bf16[12,128,128]{2,1,0:T(8,128)(2,1)} %broadcast_in_dim.16), calls=%async_computation.2 | async-start | bytes 786432 | tf_op jit(solution)/shard_map/all_to_all | solution.py:27
  18.1 0.1 maximum_bitcast_fusion
  18.2 0.1 copy.12
  18.4 0.1 fusion.8
  18.5 4.7 %collective-permute-start.2 = (bf16[3088,128]{1,0:T(8,128)(2,1)S(1)}, bf16[3088,128]{1,0:T(8,128)(2,1)S(1)}, u32[]{:S(2)}, u32[]{:S(2)}) collective-permute-start(bf16[3088,128]{1,0:T(8,128)(2,1)S(1)} %pad_maximum_fusion.refs_1_.refs_5_.refs_2_), channel_id=1, source_target_pairs={{0,36},{12,0},{24,12},{36,24},{1,37},{13,1},{25,13},{37,25},{2,38}... | collective-permute-start | bytes 2371592 | tf_op jit(solution)/shard_map/ppermute | solution.py:297
  23.2 1.9 %collective-permute-start.1 = (bf16[3088,128]{1,0:T(8,128)(2,1)S(1)}, bf16[3088,128]{1,0:T(8,128)(2,1)S(1)}, u32[]{:S(2)}, u32[]{:S(2)}) collective-permute-start(bf16[3088,128]{1,0:T(8,128)(2,1)S(1)} %pad_maximum_fusion.refs_1_.refs_5_.refs_2_), channel_id=1, source_target_pairs={{0,12},{12,24},{24,36},{36,0},{1,13},{13,25},{25,37},{37,1},{2,14}... | collective-permute-start | bytes 2371592 | tf_op jit(solution)/shard_map/ppermute | solution.py:297
  25.1 4.2 %collective-permute-start = (bf16[3088,128]{1,0:T(8,128)(2,1)S(1)}, bf16[3088,128]{1,0:T(8,128)(2,1)S(1)}, u32[]{:S(2)}, u32[]{:S(2)}) collective-permute-start(bf16[3088,128]{1,0:T(8,128)(2,1)S(1)} %pad_maximum_fusion.refs_1_.refs_5_.refs_2_), channel_id=1, source_target_pairs={{0,24},{12,36},{24,0},{36,12},{1,25},{13,37},{25,1},{37,13},{2,26}... | collective-permute-start | bytes 2371592 | tf_op jit(solution)/shard_map/ppermute | solution.py:297
  29.3 7.9 %all-to-all-done.2.refs_1_ = bf16[12,128,128]{2,1,0:T(8,128)(2,1)S(1)} async-done(((bf16[12,128,128]{2,1,0:T(8,128)(2,1)}), bf16[12,128,128]{2,1,0:T(8,128)(2,1)S(1)}, u32[]{:S(2)}, u32[]{:S(2)}) %all-to-all-start.2) | async-done | bytes 393248 | tf_op jit(solution)/shard_map/all_to_all | solution.py:27
  37.2 5.9 %collective-permute-start.5 = (bf16[12,128,128]{2,1,0:T(8,128)(2,1)S(1)}, bf16[12,128,128]{2,1,0:T(8,128)(2,1)S(1)}, u32[]{:S(2)}, u32[]{:S(2)}) collective-permute-start(bf16[12,128,128]{2,1,0:T(8,128)(2,1)S(1)} %all-to-all-done.2.refs_1_), channel_id=1, source_target_pairs={{0,96},{48,144},{96,0},{144,48},{1,97},{49,145},{97,1},{145,49},{2... | collective-permute-start | bytes 1179656 | tf_op jit(solution)/shard_map/ppermute | solution.py:302
  43.2 1.9 %collective-permute-start.4 = (bf16[12,128,128]{2,1,0:T(8,128)(2,1)S(1)}, bf16[12,128,128]{2,1,0:T(8,128)(2,1)S(1)}, u32[]{:S(2)}, u32[]{:S(2)}) collective-permute-start(bf16[12,128,128]{2,1,0:T(8,128)(2,1)S(1)} %all-to-all-done.2.refs_1_), channel_id=1, source_target_pairs={{0,48},{48,96},{96,144},{144,0},{1,49},{49,97},{97,145},{145,1},{2... | collective-permute-start | bytes 1179656 | tf_op jit(solution)/shard_map/ppermute | solution.py:302
  45.1 11.6 %collective-permute-done.2.refs_4_.refs_8_.refs_5_ = bf16[3088,128]{1,0:T(8,128)(2,1)S(1)} collective-permute-done((bf16[3088,128]{1,0:T(8,128)(2,1)S(1)}, bf16[3088,128]{1,0:T(8,128)(2,1)S(1)}, u32[]{:S(2)}, u32[]{:S(2)}) %collective-permute-start.2) | collective-permute-done | bytes 790560 | tf_op jit(solution)/shard_map/ppermute | solution.py:297
  56.7 2.2 %collective-permute-start.3 = (bf16[12,128,128]{2,1,0:T(8,128)(2,1)S(1)}, bf16[12,128,128]{2,1,0:T(8,128)(2,1)S(1)}, u32[]{:S(2)}, u32[]{:S(2)}) collective-permute-start(bf16[12,128,128]{2,1,0:T(8,128)(2,1)S(1)} %all-to-all-done.2.refs_1_), channel_id=1, source_target_pairs={{0,144},{48,0},{96,48},{144,96},{1,145},{49,1},{97,49},{145,97},{2... | collective-permute-start | bytes 1179656 | tf_op jit(solution)/shard_map/ppermute | solution.py:302
  59.0 3.1 %collective-permute-done.1.refs_3_.refs_7_.refs_4_ = bf16[3088,128]{1,0:T(8,128)(2,1)S(1)} collective-permute-done((bf16[3088,128]{1,0:T(8,128)(2,1)S(1)}, bf16[3088,128]{1,0:T(8,128)(2,1)S(1)}, u32[]{:S(2)}, u32[]{:S(2)}) %collective-permute-start.1) | collective-permute-done | bytes 790560 | tf_op jit(solution)/shard_map/ppermute | solution.py:297
  62.1 16.0 %collective-permute-done.4.refs_3_ = bf16[12,128,128]{2,1,0:T(8,128)(2,1)S(1)} collective-permute-done((bf16[12,128,128]{2,1,0:T(8,128)(2,1)S(1)}, bf16[12,128,128]{2,1,0:T(8,128)(2,1)S(1)}, u32[]{:S(2)}, u32[]{:S(2)}) %collective-permute-start.4) | collective-permute-done | bytes 393248 | tf_op jit(solution)/shard_map/ppermute | solution.py:302
  78.1 2.1 %forward_tiles.1 = bf16[16,128,128]{2,1,0:T(8,128)(2,1)S(1)} custom-call(s32[4,128]{1,0:T(4,128)S(1)} %tile_codes.1.refs_0_, bf16[12,128,128]{2,1,0:T(8,128)(2,1)S(1)} %all-to-all-done.2.refs_1_, bf16[12,128,128]{2,1,0:T(8,128)(2,1)S(1)} %collective-permute-done.3.refs_2_, bf16[12,128,128]{2,1,0:T(8,128)(2,1)S(1)} %collective-permute-done.4.refs_3_, ...), custom_call_target="tpu_custom_call" | custom-call | tf_op jit(solution)/shard_map/forward_tiles/pallas_call | solution.py:315
  80.2 15.9 %all_to_all.30.refs_0_ = bf16[16,128,128]{2,1,0:T(8,128)(2,1)S(1)} all-to-all(bf16[16,128,128]{2,1,0:T(8,128)(2,1)S(1)} %forward_tiles.1), channel_id=1, replica_groups=mesh['ylo'=2,'core'=2,'yhi'=4,'x'=4,'z'=12] {'ylo','core','x'}, dimensions={0} | all-to-all | bytes 1048576 | tf_op jit(solution)/shard_map/all_to_all | solution.py:336
  96.1 1.1 dense_layer.1
  97.2 15.6 %all_to_all.31.refs_1_ = bf16[16,176,128]{2,1,0:T(8,128)(2,1)S(1)} all-to-all(bf16[16,176,128]{2,1,0:T(8,128)(2,1)S(1)} %get-tuple-element.22), channel_id=1, replica_groups=mesh['ylo'=2,'core'=2,'yhi'=4,'x'=4,'z'=12] {'ylo','core','x'}, dimensions={0} | all-to-all | bytes 1441792 | tf_op jit(solution)/shard_map/all_to_all | solution.py:351
  112.8 3.4 %backward_tiles.1 = (bf16[12,128,128]{2,1,0:T(8,128)(2,1)S(1)}, bf16[12,128,128]{2,1,0:T(8,128)(2,1)}, bf16[12,112,128]{2,1,0:T(8,128)(2,1)}, bf16[12,128,128]{2,1,0:T(8,128)(2,1)}, bf16[12,64,128]{2,1,0:T(8,128)(2,1)}) custom-call(s32[4,128]{1,0:T(4,128)S(1)} %tile_codes.1.refs_0_, bf16[16,176,128]{2,1,0:T(8,128)(2,1)S(1)} %all_to_all.31.refs_1_, ...), custom_call_target="tpu_custom_call" | custom-call | tf_op jit(solution)/shard_map/backward_tiles/pallas_call | solution.py:354
  116.3 2.7 %collective-permute-start.7 = (bf16[12,128,128]{2,1,0:T(8,128)(2,1)}, bf16[12,128,128]{2,1,0:T(8,128)(2,1)S(1)}, u32[]{:S(2)}, u32[]{:S(2)}) collective-permute-start(bf16[12,128,128]{2,1,0:T(8,128)(2,1)} %get-tuple-element.25), channel_id=1, source_target_pairs={{0,144},{48,0},{96,48},{144,96},{1,145},{49,1},{97,49},{145,97},{2... | collective-permute-start | bytes 1179656 | tf_op jit(solution)/shard_map/ppermute | solution.py:385
  119.0 5.2 %collective-permute-start.8 = (bf16[12,128,128]{2,1,0:T(8,128)(2,1)}, bf16[12,128,128]{2,1,0:T(8,128)(2,1)S(1)}, u32[]{:S(2)}, u32[]{:S(2)}) collective-permute-start(bf16[12,128,128]{2,1,0:T(8,128)(2,1)} %get-tuple-element.26), channel_id=1, source_target_pairs={{0,48},{48,96},{96,144},{144,0},{1,49},{49,97},{97,145},{145,1},{2... | collective-permute-start | bytes 1179656 | tf_op jit(solution)/shard_map/ppermute | solution.py:385
  124.2 4.7 %collective-permute-start.6 = (bf16[12,112,128]{2,1,0:T(8,128)(2,1)}, bf16[12,112,128]{2,1,0:T(8,128)(2,1)S(1)}, u32[]{:S(2)}, u32[]{:S(2)}) collective-permute-start(bf16[12,112,128]{2,1,0:T(8,128)(2,1)} %get-tuple-element.24), channel_id=1, source_target_pairs={{0,96},{48,144},{96,0},{144,48},{1,97},{49,145},{97,1},{145,49},{2... | collective-permute-start | bytes 1032200 | tf_op jit(solution)/shard_map/ppermute | solution.py:385
  128.9 26.8 %conditional.1 = (bf16[288,128]{1,0:T(8,128)(2,1)S(1)}) conditional(s32[]{:T(128)} %convert_element_type.4, () %tuple.14, bf16[12,64,128]{2,1,0:T(8,128)(2,1)} %get-tuple-element.27), branch_computations={%region_0.1_spmd, %region_1.2_spmd} | conditional | bytes 524296 | solution.py:411
  128.9 19.0 %all_to_all.28.refs_0_ = bf16[12,64,128]{2,1,0:T(8,128)(2,1)S(1)} all-to-all(bf16[12,64,128]{2,1,0:T(8,128)(2,1)} %param.1), channel_id=1, replica_groups=mesh['ylo'=2,'core'=2,'yhi'=4,'x'=4,'z'=12] {'z'}, dimensions={0} | all-to-all | bytes 393216 | tf_op jit(solution)/shard_map/cond/branch_1_fun/all_to_all | solution.py:388
  148.0 7.7 %all_to_all.29.refs_0_ = bf16[8,32,128]{2,1,0:T(8,128)(2,1)S(1)} all-to-all(bf16[8,32,128]{2,1,0:T(8,128)(2,1)S(1)} %get-tuple-element.4), channel_id=1, replica_groups=mesh['ylo'=2,'core'=2,'yhi'=4,'x'=4,'z'=12] {'core','x'}, dimensions={0} | all-to-all | bytes 131072 | tf_op jit(solution)/shard_map/cond/branch_1_fun/all_to_all | solution.py:401
  155.7 3.2 %collective-permute-done.6.refs_1_ = bf16[12,112,128]{2,1,0:T(8,128)(2,1)S(1)} collective-permute-done((bf16[12,112,128]{2,1,0:T(8,128)(2,1)}, bf16[12,112,128]{2,1,0:T(8,128)(2,1)S(1)}, u32[]{:S(2)}, u32[]{:S(2)}) %collective-permute-start.6) | collective-permute-done | bytes 344096 | tf_op jit(solution)/shard_map/ppermute | solution.py:385
  158.9 0.9 middle_sums.1
  159.8 5.2 %all-to-all-start.5 = ((bf16[12,128,128]{2,1,0:T(8,128)(2,1)}), bf16[12,128,128]{2,1,0:T(8,128)(2,1)S(1)}, u32[]{:S(2)}, u32[]{:S(2)}) async-start(bf16[12,128,128]{2,1,0:T(8,128)(2,1)} %middle_sums.1), calls=%async_computation.5 | async-start | bytes 786432 | tf_op jit(solution)/shard_map/all_to_all | solution.py:427
  165.0 14.1 %all-gather = bf16[1152,128]{1,0:T(8,128)(2,1)S(1)} all-gather(bf16[288,128]{1,0:T(8,128)(2,1)S(1)} %get-tuple-element.34.refs_4_), channel_id=2, replica_groups=mesh['ylo'=2,'core'=2,'yhi'=4,'x'=4,'z'=12] {'yhi'}, dimensions={0}, use_global_device_ids=true | all-gather | bytes 368640 | tf_op jit(solution)/shard_map/all_gather | solution.py:426
  179.1 5.1 %all-to-all-done.5.refs_1_ = bf16[12,128,128]{2,1,0:T(8,128)(2,1)S(1)} async-done(((bf16[12,128,128]{2,1,0:T(8,128)(2,1)}), bf16[12,128,128]{2,1,0:T(8,128)(2,1)S(1)}, u32[]{:S(2)}, u32[]{:S(2)}) %all-to-all-start.5) | async-done | bytes 393248 | tf_op jit(solution)/shard_map/all_to_all | solution.py:427
  184.2 0.7 last_sums.1
  (22 shorter events, 0.2 us)
Async XLA Ops:
  0.6 17.7 %copy-start.4 = (s32[1,1,48]{2,1,0:T(1,128)S(1)}, s32[1,1,48]{2,1,0:T(1,128)}, u32[]{:S(2)}) copy-start(s32[1,1,48]{2,1,0:T(1,128)} %param.12) | copy-start | bytes 580
  0.6 17.7 %copy-start.5 = (s32[1,1,48]{2,1,0:T(1,128)S(1)}, s32[1,1,48]{2,1,0:T(1,128)}, u32[]{:S(2)}) copy-start(s32[1,1,48]{2,1,0:T(1,128)} %param.11) | copy-start | bytes 580
  0.7 17.8 %copy-start.3 = (bf16[1,1,48,64,128]{4,3,2,1,0:T(8,128)(2,1)S(1)}, bf16[1,1,48,64,128]{4,3,2,1,0:T(8,128)(2,1)}, u32[]{:S(2)}) copy-start(bf16[1,1,48,64,128]{4,3,2,1,0:T(8,128)(2,1)} %param.14) | copy-start | bytes 2359300
  2.3 34.9 %all-to-all-start.2 = ((bf16[12,128,128]{2,1,0:T(8,128)(2,1)}), bf16[12,128,128]{2,1,0:T(8,128)(2,1)S(1)}, u32[]{:S(2)}, u32[]{:S(2)}) async-start(bf16[12,128,128]{2,1,0:T(8,128)(2,1)} %broadcast_in_dim.16), calls=%async_computation.2 | async-start | bytes 786432 | tf_op jit(solution)/shard_map/all_to_all | solution.py:27
  18.5 38.2 %collective-permute-start.2 = (bf16[3088,128]{1,0:T(8,128)(2,1)S(1)}, bf16[3088,128]{1,0:T(8,128)(2,1)S(1)}, u32[]{:S(2)}, u32[]{:S(2)}) collective-permute-start(bf16[3088,128]{1,0:T(8,128)(2,1)S(1)} %pad_maximum_fusion.refs_1_.refs_5_.refs_2_), channel_id=1, source_target_pairs={{0,36},{12,0},{24,12},{36,24},{1,37},{13,1},{25,13},{37,25},{2,38}... | collective-permute-start | bytes 2371592 | tf_op jit(solution)/shard_map/ppermute | solution.py:297
  23.2 38.9 %collective-permute-start.1 = (bf16[3088,128]{1,0:T(8,128)(2,1)S(1)}, bf16[3088,128]{1,0:T(8,128)(2,1)S(1)}, u32[]{:S(2)}, u32[]{:S(2)}) collective-permute-start(bf16[3088,128]{1,0:T(8,128)(2,1)S(1)} %pad_maximum_fusion.refs_1_.refs_5_.refs_2_), channel_id=1, source_target_pairs={{0,12},{12,24},{24,36},{36,0},{1,13},{13,25},{25,37},{37,1},{2,14}... | collective-permute-start | bytes 2371592 | tf_op jit(solution)/shard_map/ppermute | solution.py:297
  25.1 36.9 %collective-permute-start = (bf16[3088,128]{1,0:T(8,128)(2,1)S(1)}, bf16[3088,128]{1,0:T(8,128)(2,1)S(1)}, u32[]{:S(2)}, u32[]{:S(2)}) collective-permute-start(bf16[3088,128]{1,0:T(8,128)(2,1)S(1)} %pad_maximum_fusion.refs_1_.refs_5_.refs_2_), channel_id=1, source_target_pairs={{0,24},{12,36},{24,0},{36,12},{1,25},{13,37},{25,1},{37,13},{2,26}... | collective-permute-start | bytes 2371592 | tf_op jit(solution)/shard_map/ppermute | solution.py:297
  37.2 24.8 %collective-permute-start.5 = (bf16[12,128,128]{2,1,0:T(8,128)(2,1)S(1)}, bf16[12,128,128]{2,1,0:T(8,128)(2,1)S(1)}, u32[]{:S(2)}, u32[]{:S(2)}) collective-permute-start(bf16[12,128,128]{2,1,0:T(8,128)(2,1)S(1)} %all-to-all-done.2.refs_1_), channel_id=1, source_target_pairs={{0,96},{48,144},{96,0},{144,48},{1,97},{49,145},{97,1},{145,49},{2... | collective-permute-start | bytes 1179656 | tf_op jit(solution)/shard_map/ppermute | solution.py:302
  43.2 34.9 %collective-permute-start.4 = (bf16[12,128,128]{2,1,0:T(8,128)(2,1)S(1)}, bf16[12,128,128]{2,1,0:T(8,128)(2,1)S(1)}, u32[]{:S(2)}, u32[]{:S(2)}) collective-permute-start(bf16[12,128,128]{2,1,0:T(8,128)(2,1)S(1)} %all-to-all-done.2.refs_1_), channel_id=1, source_target_pairs={{0,48},{48,96},{96,144},{144,0},{1,49},{49,97},{97,145},{145,1},{2... | collective-permute-start | bytes 1179656 | tf_op jit(solution)/shard_map/ppermute | solution.py:302
  56.7 21.3 %collective-permute-start.3 = (bf16[12,128,128]{2,1,0:T(8,128)(2,1)S(1)}, bf16[12,128,128]{2,1,0:T(8,128)(2,1)S(1)}, u32[]{:S(2)}, u32[]{:S(2)}) collective-permute-start(bf16[12,128,128]{2,1,0:T(8,128)(2,1)S(1)} %all-to-all-done.2.refs_1_), channel_id=1, source_target_pairs={{0,144},{48,0},{96,48},{144,96},{1,145},{49,1},{97,49},{145,97},{2... | collective-permute-start | bytes 1179656 | tf_op jit(solution)/shard_map/ppermute | solution.py:302
  80.2 15.9 %copy-start = (bf16[128,256]{1,0:T(8,128)(2,1)S(1)}, bf16[128,256]{1,0:T(8,128)(2,1)}, u32[]{:S(2)}) copy-start(bf16[128,256]{1,0:T(8,128)(2,1)} %refs_1_.1) | copy-start | bytes 196612
  80.2 15.9 %copy-start.1 = (bf16[128,256]{1,0:T(8,128)(2,1)S(1)}, bf16[128,256]{1,0:T(8,128)(2,1)}, u32[]{:S(2)}) copy-start(bf16[128,256]{1,0:T(8,128)(2,1)} %refs_3_.1) | copy-start | bytes 196612
  80.2 15.9 %copy-start.2 = (f32[256]{0:T(256)S(1)}, f32[256]{0:T(256)}, u32[]{:S(2)}) copy-start(f32[256]{0:T(256)} %param.16) | copy-start | bytes 3076
  116.3 42.6 %collective-permute-start.7 = (bf16[12,128,128]{2,1,0:T(8,128)(2,1)}, bf16[12,128,128]{2,1,0:T(8,128)(2,1)S(1)}, u32[]{:S(2)}, u32[]{:S(2)}) collective-permute-start(bf16[12,128,128]{2,1,0:T(8,128)(2,1)} %get-tuple-element.25), channel_id=1, source_target_pairs={{0,144},{48,0},{96,48},{144,96},{1,145},{49,1},{97,49},{145,97},{2... | collective-permute-start | bytes 1179656 | tf_op jit(solution)/shard_map/ppermute | solution.py:385
  119.0 39.9 %collective-permute-start.8 = (bf16[12,128,128]{2,1,0:T(8,128)(2,1)}, bf16[12,128,128]{2,1,0:T(8,128)(2,1)S(1)}, u32[]{:S(2)}, u32[]{:S(2)}) collective-permute-start(bf16[12,128,128]{2,1,0:T(8,128)(2,1)} %get-tuple-element.26), channel_id=1, source_target_pairs={{0,48},{48,96},{96,144},{144,0},{1,49},{49,97},{97,145},{145,1},{2... | collective-permute-start | bytes 1179656 | tf_op jit(solution)/shard_map/ppermute | solution.py:385
  124.2 34.6 %collective-permute-start.6 = (bf16[12,112,128]{2,1,0:T(8,128)(2,1)}, bf16[12,112,128]{2,1,0:T(8,128)(2,1)S(1)}, u32[]{:S(2)}, u32[]{:S(2)}) collective-permute-start(bf16[12,112,128]{2,1,0:T(8,128)(2,1)} %get-tuple-element.24), channel_id=1, source_target_pairs={{0,96},{48,144},{96,0},{144,48},{1,97},{49,145},{97,1},{145,49},{2... | collective-permute-start | bytes 1032200 | tf_op jit(solution)/shard_map/ppermute | solution.py:385
  159.8 24.4 %all-to-all-start.5 = ((bf16[12,128,128]{2,1,0:T(8,128)(2,1)}), bf16[12,128,128]{2,1,0:T(8,128)(2,1)S(1)}, u32[]{:S(2)}, u32[]{:S(2)}) async-start(bf16[12,128,128]{2,1,0:T(8,128)(2,1)} %middle_sums.1), calls=%async_computation.5 | async-start | bytes 786432 | tf_op jit(solution)/shard_map/all_to_all | solution.py:427
